TPU v7x, 32 devices: a whole 2x2x4 slice. The times are simulated.
32 devices in a mesh: shard: 2 (over y), ctx: 8 (over z, x), tp: 2 (over core).
Axes of the slice: x: 2, y: 2, z: 4, core: 2. Of those that a mesh axis runs over, the one named last changes fastest.
Arguments:
- tokens: bfloat16 [8192, 1024], P(('shard', 'ctx')), may hold values from -6 to 6
- cotangent: bfloat16 [8192, 1024], P(('shard', 'ctx')), may hold values from -6 to 6
- seq_lengths: int32 [2, 4], P('shard'), may hold values from 512 to 2048, as said below
- part_order: int32 [8, 2], replicated, may hold values from 0 to 15, as said below
- w_query: bfloat16 [1024, 2048], P('shard', 'tp'), may hold values from -0.1875 to 0.1875
- key_weight: bfloat16 [1024, 1024], P('shard', 'tp'), may hold values from -0.1875 to 0.1875
- value_weight: bfloat16 [1024, 1024], P('shard', 'tp'), may hold values from -0.1875 to 0.1875
- w_out: bfloat16 [2048, 1024], P('tp', 'shard'), may hold values from -1.5 to 1.5
- w_gate: bfloat16 [1024, 3072], P('shard', 'tp'), may hold values from -0.1875 to 0.1875
- w_up: bfloat16 [1024, 3072], P('shard', 'tp'), may hold values from -0.1875 to 0.1875
- w_down: bfloat16 [3072, 1024], P('tp', 'shard'), may hold values from -0.109375 to 0.109375
- gain_in: bfloat16 [1024], P('shard'), may hold values from 0.25 to 1.75
- gain_post: bfloat16 [1024], P('shard'), may hold values from 0.25 to 1.75
- gain_q: bfloat16 [128], P('shard'), may hold values from 0.25 to 1.75
- gain_k: bfloat16 [128], P('shard'), may hold values from 0.25 to 1.75
Outputs:
- mixed: bfloat16 [8192, 1024], P(('shard', 'ctx'))
- input_grad: float32 [8192, 1024], P(('shard', 'ctx'))
- grad_query: float32 [1024, 2048], P('shard', 'tp')
- grad_key: float32 [1024, 1024], P('shard', 'tp')
- grad_value: float32 [1024, 1024], P('shard', 'tp')
- grad_out: float32 [2048, 1024], P('tp', 'shard')
- grad_gate: float32 [1024, 3072], P('shard', 'tp')
- grad_up: float32 [1024, 3072], P('shard', 'tp')
- grad_down: float32 [3072, 1024], P('tp', 'shard')
- grad_gain_in: float32 [1024], P('shard')
- grad_gain_post: float32 [1024], P('shard')
- grad_gain_q: float32 [128], P('shard')
- grad_gain_k: float32 [128], P('shard')
Inputs may be any that keep to these rules, and one draw needn't show every extreme that they name: `seq_lengths`: in each row the 4 lengths add up to 4096; one is 2048 and stands first or last, one is exactly 512, and the other two add up to 1536 with neither under 4096 // 8. Row c names the parts of 256 packed places that device c of ctx holds, in the order of its rows: part_order[c, 0] takes each value of 0 to 7 once over the rows, and part_order[c, 1] = 15 - part_order[c, 0].
All inputs are finite; a program needn't handle non-finite values.
Results may differ from a plain program's by a relative error of at most 0.024.
Values may be sent and summed in bfloat16 or wider, within the bound.
No kernel may reach another device: no remote copies, remote signals or barrier semaphores. Data moves between devices by JAX's collectives and lax.ppermute only.
A program may use at most 128 MiB of HBM per device.

v0:
```python
import math

import jax
import jax.numpy as jnp
from jax import lax
from jax.sharding import PartitionSpec as P

EPS = 1e-06
THETA = 1000000.0
MASKED = -1e30


def from_behind(x, axis, by):
    count = lax.axis_size(axis)
    return lax.ppermute(x, axis, [(i, (i + by) % count) for i in range(count)])


def rms_parts(values):
    factor = lax.rsqrt(jnp.mean(values * values, axis=-1, keepdims=True) + EPS)
    return (values * factor, factor)


def rms_back(grad_hat, normal, factor):
    return factor * (grad_hat - normal * jnp.mean(grad_hat * normal, axis=-1, keepdims=True))


def rotate(values, cosine, sine_table):
    middle = values.shape[-1] // 2
    return (
        values * cosine
        + jnp.concatenate([-values[..., middle:], values[..., :middle]], axis=-1) * sine_table
    )


def rotate_back(grads_in, cosine, sine_table):
    middle = grads_in.shape[-1] // 2
    moved = grads_in * sine_table
    return grads_in * cosine + jnp.concatenate([moved[..., middle:], -moved[..., :middle]], axis=-1)


def place_of(row_index, flat_parts, starts, part_rows):
    slot_id = row_index // part_rows
    matches = slot_id[:, None] == jnp.arange(flat_parts.shape[0], dtype=jnp.int32)[None, :]
    part_id = jnp.sum(jnp.where(matches, flat_parts[None, :], 0), axis=1)
    place_id = part_id * part_rows + row_index % part_rows
    member = jnp.sum((place_id[:, None] >= starts[None, 1:]).astype(jnp.int32), axis=1)
    return (place_id, member)


def visible_scores(q_group, key_block, q_place, q_member, k_place, k_member, score_scale):
    scores = (
        jnp.einsum("tagd,kad->agtk", q_group, key_block, preferred_element_type=jnp.float32)
        * score_scale
    )
    visible = (q_member[:, None] == k_member[None, :]) & (k_place[None, :] <= q_place[:, None])
    return (scores, visible[None, None])


def tensor_total(partial_sum):
    return lax.psum(partial_sum.astype(jnp.bfloat16), "tp").astype(jnp.float32)


def pass_grads(key_grads):
    return from_behind(key_grads.astype(jnp.bfloat16), "ctx", 1).astype(key_grads.dtype)


def body(
    tokens,
    cotangent,
    seq_lengths,
    part_order,
    w_query,
    key_weight,
    value_weight,
    w_out,
    w_gate,
    w_up,
    w_down,
    gain_in,
    gain_post,
    gain_q,
    gain_k,
):
    gathered = (
        lax.all_gather(w_query, "shard", axis=0, tiled=True),
        lax.all_gather(key_weight, "shard", axis=0, tiled=True),
        lax.all_gather(value_weight, "shard", axis=0, tiled=True),
        lax.all_gather(w_out, "shard", axis=1, tiled=True),
        lax.all_gather(w_gate, "shard", axis=0, tiled=True),
        lax.all_gather(w_up, "shard", axis=0, tiled=True),
        lax.all_gather(w_down, "shard", axis=1, tiled=True),
        lax.all_gather(gain_in, "shard", axis=0, tiled=True),
        lax.all_gather(gain_post, "shard", axis=0, tiled=True),
        lax.all_gather(gain_q, "shard", axis=0, tiled=True),
        lax.all_gather(gain_k, "shard", axis=0, tiled=True),
    )
    full_query, full_key, full_value, full_out, full_gate, full_up, full_down = gathered[:7]
    scale_in = gathered[7].astype(jnp.float32)
    scale_post = gathered[8].astype(jnp.float32)
    scale_q = gathered[9].astype(jnp.float32)
    scale_k = gathered[10].astype(jnp.float32)
    token_rows = tokens.shape[0]
    head_size = scale_q.shape[0]
    local_heads = full_query.shape[1] // head_size
    local_kv = full_key.shape[1] // head_size
    group_size = local_heads // local_kv
    score_scale = head_size ** (-0.5)
    ctx_count = lax.axis_size("ctx")
    ctx_index = lax.axis_index("ctx")
    part_rows = token_rows // 2
    flat_parts = part_order.reshape(-1)
    lengths = seq_lengths[0]
    starts = jnp.cumsum(lengths) - lengths
    own_rows = ctx_index * token_rows + jnp.arange(token_rows, dtype=jnp.int32)
    q_place, q_member = place_of(own_rows, flat_parts, starts, part_rows)
    doc_match = q_member[:, None] == jnp.arange(starts.shape[0], dtype=jnp.int32)[None, :]
    doc_begin = jnp.sum(jnp.where(doc_match, starts[None, :], 0), axis=1)
    frequency = THETA ** (-jnp.arange(0, head_size, 2, dtype=jnp.float32) / head_size)
    angles = (q_place - doc_begin).astype(jnp.float32)[:, None] * frequency[None, :]
    cosine = jnp.concatenate([jnp.cos(angles), jnp.cos(angles)], axis=-1)[:, None, :]
    sine_table = jnp.concatenate([jnp.sin(angles), jnp.sin(angles)], axis=-1)[:, None, :]
    inputs = tokens.astype(jnp.float32)
    normal_one, factor_one = rms_parts(inputs)
    normed_input = (normal_one * scale_in).astype(jnp.bfloat16)
    q_pre = jnp.dot(normed_input, full_query, preferred_element_type=jnp.float32).reshape(
        token_rows, local_heads, head_size
    )
    k_pre = jnp.dot(normed_input, full_key, preferred_element_type=jnp.float32).reshape(
        token_rows, local_kv, head_size
    )
    value_row_block = (
        jnp.dot(normed_input, full_value, preferred_element_type=jnp.float32)
        .astype(jnp.bfloat16)
        .reshape(token_rows, local_kv, head_size)
    )
    q_hat, q_factor = rms_parts(q_pre)
    k_hat, k_factor = rms_parts(k_pre)
    queries = rotate(q_hat * scale_q, cosine, sine_table).astype(jnp.bfloat16)
    key_row_block = rotate(k_hat * scale_k, cosine, sine_table).astype(jnp.bfloat16)
    q_group = queries.reshape(token_rows, local_kv, group_size, head_size)
    key_value = jnp.stack([key_row_block, value_row_block])
    start_state = (
        jnp.zeros((local_kv, group_size, token_rows, head_size), jnp.float32),
        jnp.full((local_kv, group_size, token_rows), MASKED, jnp.float32),
        jnp.zeros((local_kv, group_size, token_rows), jnp.float32),
    )
    running = start_state
    arrived = lax.all_gather(key_value, "ctx", axis=1, tiled=True)
    arrived_rows = arrived.shape[1]
    block_rows = math.gcd(arrived_rows, 512)
    count_blocks = arrived_rows // block_rows
    row_index = jnp.arange(arrived_rows, dtype=jnp.int32)
    k_place, k_member = place_of(row_index, flat_parts, starts, part_rows)
    blocks = (
        arrived[0].reshape(count_blocks, block_rows, local_kv, head_size),
        arrived[1].reshape(count_blocks, block_rows, local_kv, head_size),
        k_place.reshape(count_blocks, block_rows),
        k_member.reshape(count_blocks, block_rows),
    )

    def fold_one_block(state, block_data):
        acc_out, highest, row_sums = state
        key_block, value_block, place_block, member_block = block_data
        scores, visible = visible_scores(
            q_group, key_block, q_place, q_member, place_block, member_block, score_scale
        )
        new_high = jnp.maximum(highest, jnp.max(jnp.where(visible, scores, MASKED), axis=-1))
        fading = jnp.exp(highest - new_high)
        weights = jnp.where(visible, jnp.exp(scores - new_high[..., None]), 0.0)
        row_sums = row_sums * fading + jnp.sum(weights, axis=-1)
        acc_out = acc_out * fading[..., None] + jnp.einsum(
            "agtk,kad->agtd",
            weights.astype(jnp.bfloat16),
            value_block,
            preferred_element_type=jnp.float32,
        )
        return ((acc_out, new_high, row_sums), None)

    running, unused = lax.scan(fold_one_block, running, blocks)
    acc_out, highest, row_sums = running
    log_sums = highest + jnp.log(row_sums)
    attended = (acc_out / row_sums[..., None]).transpose(2, 0, 1, 3)
    attn_out = attended.reshape(token_rows, local_heads * head_size).astype(jnp.bfloat16)
    residual = inputs + tensor_total(
        jnp.dot(attn_out, full_out, preferred_element_type=jnp.float32)
    )
    normal_two, factor_two = rms_parts(residual)
    normed_two = (normal_two * scale_post).astype(jnp.bfloat16)
    gate_act = jnp.dot(normed_two, full_gate, preferred_element_type=jnp.float32)
    upward = jnp.dot(normed_two, full_up, preferred_element_type=jnp.float32)
    sigma = jax.nn.sigmoid(gate_act)
    silu_act = gate_act * sigma
    hidden = (silu_act * upward).astype(jnp.bfloat16)
    outputs = residual + tensor_total(
        jnp.dot(hidden, full_down, preferred_element_type=jnp.float32)
    )
    mixed = outputs.astype(jnp.bfloat16)
    grad_down = jnp.einsum("tf,td->fd", hidden, cotangent, preferred_element_type=jnp.float32)
    d_hidden = jnp.einsum("td,fd->tf", cotangent, full_down, preferred_element_type=jnp.float32)
    d_gate = (d_hidden * upward * sigma * (1.0 + gate_act * (1.0 - sigma))).astype(jnp.bfloat16)
    d_up = (d_hidden * silu_act).astype(jnp.bfloat16)
    grad_gate = jnp.einsum("td,tf->df", normed_two, d_gate, preferred_element_type=jnp.float32)
    grad_up = jnp.einsum("td,tf->df", normed_two, d_up, preferred_element_type=jnp.float32)
    d_normed_part = jnp.einsum(
        "tf,df->td", d_gate, full_gate, preferred_element_type=jnp.float32
    ) + jnp.einsum("tf,df->td", d_up, full_up, preferred_element_type=jnp.float32)
    d_normed_two = lax.psum(d_normed_part.astype(jnp.bfloat16), "tp").astype(jnp.float32)
    grad_post = jnp.sum(d_normed_two * normal_two, axis=0)
    d_residual = cotangent.astype(jnp.float32) + rms_back(
        d_normed_two * scale_post, normal_two, factor_two
    )
    d_branch = d_residual.astype(jnp.bfloat16)
    grad_out = jnp.einsum("tc,td->cd", attn_out, d_branch, preferred_element_type=jnp.float32)
    d_attn = jnp.einsum("td,cd->tc", d_branch, full_out, preferred_element_type=jnp.float32).astype(
        jnp.bfloat16
    )
    grad_attn = d_attn.reshape(token_rows, local_kv, group_size, head_size)
    delta = jnp.sum(grad_attn.astype(jnp.float32) * attended, axis=-1).transpose(1, 2, 0)

    def accumulate(held, owner, query_grad):
        row_index = owner * token_rows + jnp.arange(token_rows, dtype=jnp.int32)
        k_place, k_member = place_of(row_index, flat_parts, starts, part_rows)
        block_rows = math.gcd(token_rows, 512)
        count_blocks = token_rows // block_rows
        blocks = (
            held[0].reshape(count_blocks, block_rows, local_kv, head_size),
            held[1].reshape(count_blocks, block_rows, local_kv, head_size),
            k_place.reshape(count_blocks, block_rows),
            k_member.reshape(count_blocks, block_rows),
        )

        def accumulate_one_block(query_sum, block_data):
            key_block, value_block, place_block, member_block = block_data
            scores, visible = visible_scores(
                q_group, key_block, q_place, q_member, place_block, member_block, score_scale
            )
            weights = jnp.where(visible, jnp.exp(scores - log_sums[..., None]), 0.0)
            value_grad = jnp.einsum(
                "agtk,tagd->kad",
                weights.astype(jnp.bfloat16),
                grad_attn,
                preferred_element_type=jnp.float32,
            )
            weight_grad = jnp.einsum(
                "tagd,kad->agtk", grad_attn, value_block, preferred_element_type=jnp.float32
            )
            score_grad = (weights * (weight_grad - delta[..., None])).astype(jnp.bfloat16)
            query_sum = (
                query_sum
                + jnp.einsum(
                    "agtk,kad->tagd", score_grad, key_block, preferred_element_type=jnp.float32
                )
                * score_scale
            )
            key_grad = (
                jnp.einsum(
                    "agtk,tagd->kad", score_grad, q_group, preferred_element_type=jnp.float32
                )
                * score_scale
            )
            return (query_sum, (key_grad, value_grad))

        query_grad, (key_parts, value_parts) = lax.scan(accumulate_one_block, query_grad, blocks)
        block_sum = jnp.stack(
            [
                key_parts.reshape(token_rows, local_kv, head_size),
                value_parts.reshape(token_rows, local_kv, head_size),
            ]
        )
        return (query_grad, block_sum)

    query_grad = jnp.zeros((token_rows, local_kv, group_size, head_size), jnp.float32)
    query_grad, key_grads = accumulate(key_value, ctx_index, query_grad)

    def next_turn(step, carried):
        held, query_grad, key_grads = carried
        key_grads = pass_grads(key_grads)
        held = from_behind(held, "ctx", 1)
        owner = (ctx_index - step) % ctx_count
        query_grad, block_sum = accumulate(held, owner, query_grad)
        return (held, query_grad, key_grads + block_sum)

    held, query_grad, key_grads = lax.fori_loop(
        1, ctx_count, next_turn, (key_value, query_grad, key_grads)
    )
    key_grads = pass_grads(key_grads)
    d_q_rot = rotate_back(
        query_grad.reshape(token_rows, local_heads, head_size), cosine, sine_table
    )
    d_k_rot = rotate_back(key_grads[0], cosine, sine_table)
    gq_part = jnp.sum(d_q_rot * q_hat, axis=(0, 1))
    gk_part = jnp.sum(d_k_rot * k_hat, axis=(0, 1))
    d_q_pre = (
        rms_back(d_q_rot * scale_q, q_hat, q_factor)
        .astype(jnp.bfloat16)
        .reshape(token_rows, local_heads * head_size)
    )
    d_k_pre = (
        rms_back(d_k_rot * scale_k, k_hat, k_factor)
        .astype(jnp.bfloat16)
        .reshape(token_rows, local_kv * head_size)
    )
    d_values = key_grads[1].astype(jnp.bfloat16).reshape(token_rows, local_kv * head_size)
    grad_query = jnp.einsum("td,tc->dc", normed_input, d_q_pre, preferred_element_type=jnp.float32)
    grad_key = jnp.einsum("td,tc->dc", normed_input, d_k_pre, preferred_element_type=jnp.float32)
    grad_value = jnp.einsum("td,tc->dc", normed_input, d_values, preferred_element_type=jnp.float32)
    d_normed_heads = (
        jnp.einsum("tc,dc->td", d_q_pre, full_query, preferred_element_type=jnp.float32)
        + jnp.einsum("tc,dc->td", d_k_pre, full_key, preferred_element_type=jnp.float32)
        + jnp.einsum("tc,dc->td", d_values, full_value, preferred_element_type=jnp.float32)
    )
    d_normed, gq_total, gk_total = (
        lax.psum(d_normed_heads.astype(jnp.bfloat16), "tp").astype(jnp.float32),
        lax.psum(gq_part.astype(jnp.bfloat16), "tp").astype(jnp.float32),
        lax.psum(gk_part.astype(jnp.bfloat16), "tp").astype(jnp.float32),
    )
    grad_in_gain = jnp.sum(d_normed * normal_one, axis=0)
    input_grad = d_residual + rms_back(d_normed * scale_in, normal_one, factor_one)
    shares = (
        lax.psum_scatter(
            grad_query.astype(jnp.bfloat16), "shard", scatter_dimension=0, tiled=True
        ).astype(jnp.float32),
        lax.psum_scatter(
            grad_key.astype(jnp.bfloat16), "shard", scatter_dimension=0, tiled=True
        ).astype(jnp.float32),
        lax.psum_scatter(
            grad_value.astype(jnp.bfloat16), "shard", scatter_dimension=0, tiled=True
        ).astype(jnp.float32),
        lax.psum_scatter(
            grad_out.astype(jnp.bfloat16), "shard", scatter_dimension=1, tiled=True
        ).astype(jnp.float32),
        lax.psum_scatter(
            grad_gate.astype(jnp.bfloat16), "shard", scatter_dimension=0, tiled=True
        ).astype(jnp.float32),
        lax.psum_scatter(
            grad_up.astype(jnp.bfloat16), "shard", scatter_dimension=0, tiled=True
        ).astype(jnp.float32),
        lax.psum_scatter(
            grad_down.astype(jnp.bfloat16), "shard", scatter_dimension=1, tiled=True
        ).astype(jnp.float32),
        lax.psum_scatter(
            grad_in_gain.astype(jnp.bfloat16), "shard", scatter_dimension=0, tiled=True
        ).astype(jnp.float32),
        lax.psum_scatter(
            grad_post.astype(jnp.bfloat16), "shard", scatter_dimension=0, tiled=True
        ).astype(jnp.float32),
        lax.psum_scatter(
            gq_total.astype(jnp.bfloat16), "shard", scatter_dimension=0, tiled=True
        ).astype(jnp.float32),
        lax.psum_scatter(
            gk_total.astype(jnp.bfloat16), "shard", scatter_dimension=0, tiled=True
        ).astype(jnp.float32),
    )
    owned = (
        lax.psum(shares[0].astype(jnp.bfloat16), "ctx").astype(jnp.float32),
        lax.psum(shares[1].astype(jnp.bfloat16), "ctx").astype(jnp.float32),
        lax.psum(shares[2].astype(jnp.bfloat16), "ctx").astype(jnp.float32),
        lax.psum(shares[3].astype(jnp.bfloat16), "ctx").astype(jnp.float32),
        lax.psum(shares[4].astype(jnp.bfloat16), "ctx").astype(jnp.float32),
        lax.psum(shares[5].astype(jnp.bfloat16), "ctx").astype(jnp.float32),
        lax.psum(shares[6].astype(jnp.bfloat16), "ctx").astype(jnp.float32),
        lax.psum(shares[7].astype(jnp.bfloat16), "ctx").astype(jnp.float32),
        lax.psum(shares[8].astype(jnp.bfloat16), "ctx").astype(jnp.float32),
        lax.psum(shares[9].astype(jnp.bfloat16), "ctx").astype(jnp.float32),
        lax.psum(shares[10].astype(jnp.bfloat16), "ctx").astype(jnp.float32),
    )
    return (
        mixed,
        input_grad,
        owned[0],
        owned[1],
        owned[2],
        owned[3],
        owned[4],
        owned[5],
        owned[6],
        owned[7],
        owned[8],
        owned[9],
        owned[10],
    )


def solution(mesh):
    placed = (
        P(("shard", "ctx"), None),
        P(("shard", "ctx"), None),
        P("shard", None),
        P(),
        P("shard", "tp"),
        P("shard", "tp"),
        P("shard", "tp"),
        P("tp", "shard"),
        P("shard", "tp"),
        P("shard", "tp"),
        P("tp", "shard"),
        P("shard"),
        P("shard"),
        P("shard"),
        P("shard"),
    )
    return jax.shard_map(
        body,
        mesh=mesh,
        in_specs=placed,
        out_specs=(
            P(("shard", "ctx"), None),
            P(("shard", "ctx"), None),
            P("shard", "tp"),
            P("shard", "tp"),
            P("shard", "tp"),
            P("tp", "shard"),
            P("shard", "tp"),
            P("shard", "tp"),
            P("tp", "shard"),
            P("shard"),
            P("shard"),
            P("shard"),
            P("shard"),
        ),
        check_vma=False,
    )
```

profile of v0, /device:TPU:0, one launch (start us, length us, event | category | flops | bytes accessed | tf_op | source)
XLA Modules:
  0.0 1546.4 jit_solution(1866756767634180681)
XLA Ops:
  41.2 15.4 all-gather.13.cloned.1.call-done
  65.4 25.9 %all-gather.17.cloned.1.call-done = bf16[1024,1024]{1,0:T(8,128)(2,1)} async-done(((bf16[512,1024]{1,0:T(8,128)(2,1)}), bf16[1024,1024]{1,0:T(8,128)(2,1)}) %all-gather.17.cloned.1.call-update) | async-done | bytes 2097168 | tf_op jit(solution)/shard_map/all_gather | solution.py:85
  116.5 101.8 %all-gather.15.cloned.1.call-done = bf16[2,4096,4,128]{3,1,2,0:T(8,128)(2,1)} async-done(((bf16[2,512,4,128]{3,1,2,0:T(8,128)(2,1)}), bf16[2,4096,4,128]{3,1,2,0:T(8,128)(2,1)}) %all-gather.15.cloned.1.call-update) | async-done | bytes 8388624 | tf_op jit(solution)/shard_map/all_gather | solution.py:148
  224.1 137.1 %while.56 = (s32[]{:T(128)}, f32[4,2,512,128]{3,2,1,0:T(8,128)}, f32[4,2,512]{2,1,0:T(2,128)S(1)}, f32[4,2,512]{2,1,0:T(2,128)S(1)}, s32[512]{0:T(512)S(1)}, /*i...) while((s32[]{:T(128)}, f32[4,2,512,128]{3,2,1,0:T(8,128)}, ...), condition=%wide.region_12.13_spmd.clone, body=%wide.region_9.12_spmd.clone.sunk | while | flops 1099190272 | bytes 66340004 | solution.py:179
  392.2 44.6 %all-gather.21.cloned.1.call-done = bf16[1024,1536]{1,0:T(8,128)(2,1)} async-done(((bf16[512,1536]{1,0:T(8,128)(2,1)}), bf16[1024,1536]{1,0:T(8,128)(2,1)}) %all-gather.21.cloned.1.call-update) | async-done | bytes 3145744 | tf_op jit(solution)/shard_map/all_gather | solution.py:89
  442.5 40.9 %all-gather.23.cloned.1.call-done = bf16[1024,1536]{1,0:T(8,128)(2,1)} async-done(((bf16[512,1536]{1,0:T(8,128)(2,1)}), bf16[1024,1536]{1,0:T(8,128)(2,1)}) %all-gather.23.cloned.1.call-update) | async-done | bytes 3145744 | tf_op jit(solution)/shard_map/all_gather | solution.py:90
  489.1 40.9 %all-gather.25.cloned.1.call-done = bf16[1536,1024]{1,0:T(8,128)(2,1)} async-done(((bf16[1536,512]{1,0:T(8,128)(2,1)}), bf16[1536,1024]{1,0:T(8,128)(2,1)}) %all-gather.25.cloned.1.call-update) | async-done | bytes 3145744 | tf_op jit(solution)/shard_map/all_gather | solution.py:91
  552.5 11.3 all-reduce.19.cloned.1.call-done
  596.6 355.5 %while.57 = (s32[]{:T(128)}, bf16[2,512,4,128]{3,1,2,0:T(8,128)(2,1)}, f32[512,4,2,128]{3,0,2,1:T(8,128)S(1)}, bf16[2,512,4,128]{3,1,2,0:T(8,128)(2,1)}, s32[512...) while((s32[]{:T(128)}, ...), condition=%wide.wide.region_22.23_spmd, body=%wide.wide.region_19.22_spmd.sunk | while | flops 2709563904 | bytes 69540360 | solution.py:283
  600.9 25.2 %collective-permute-done = bf16[2,512,4,128]{3,1,2,0:T(8,128)(2,1)} collective-permute-done((bf16[2,512,4,128]{3,1,2,0:T(8,128)(2,1)}, bf16[2,512,4,128]{3,1,2,0:T(8,128)(2,1)}, u32[]{:S(2)}, u32[]{:S(2)}) %collective-permute-start) | collective-permute-done | bytes 1048608 | tf_op jit(solution)/shard_map/while/body/eval_jaxpr/ppermute | solution.py:15
  652.4 27.2 %collective-permute-done = bf16[2,512,4,128]{3,1,2,0:T(8,128)(2,1)} collective-permute-done((bf16[2,512,4,128]{3,1,2,0:T(8,128)(2,1)}, bf16[2,512,4,128]{3,1,2,0:T(8,128)(2,1)}, u32[]{:S(2)}, u32[]{:S(2)}) %collective-permute-start) | collective-permute-done | bytes 1048608 | tf_op jit(solution)/shard_map/while/body/eval_jaxpr/ppermute | solution.py:15
  703.6 28.5 %collective-permute-done = bf16[2,512,4,128]{3,1,2,0:T(8,128)(2,1)} collective-permute-done((bf16[2,512,4,128]{3,1,2,0:T(8,128)(2,1)}, bf16[2,512,4,128]{3,1,2,0:T(8,128)(2,1)}, u32[]{:S(2)}, u32[]{:S(2)}) %collective-permute-start) | collective-permute-done | bytes 1048608 | tf_op jit(solution)/shard_map/while/body/eval_jaxpr/ppermute | solution.py:15
  755.2 28.5 %collective-permute-done = bf16[2,512,4,128]{3,1,2,0:T(8,128)(2,1)} collective-permute-done((bf16[2,512,4,128]{3,1,2,0:T(8,128)(2,1)}, bf16[2,512,4,128]{3,1,2,0:T(8,128)(2,1)}, u32[]{:S(2)}, u32[]{:S(2)}) %collective-permute-start) | collective-permute-done | bytes 1048608 | tf_op jit(solution)/shard_map/while/body/eval_jaxpr/ppermute | solution.py:15
  805.9 28.5 %collective-permute-done = bf16[2,512,4,128]{3,1,2,0:T(8,128)(2,1)} collective-permute-done((bf16[2,512,4,128]{3,1,2,0:T(8,128)(2,1)}, bf16[2,512,4,128]{3,1,2,0:T(8,128)(2,1)}, u32[]{:S(2)}, u32[]{:S(2)}) %collective-permute-start) | collective-permute-done | bytes 1048608 | tf_op jit(solution)/shard_map/while/body/eval_jaxpr/ppermute | solution.py:15
  855.7 28.5 %collective-permute-done = bf16[2,512,4,128]{3,1,2,0:T(8,128)(2,1)} collective-permute-done((bf16[2,512,4,128]{3,1,2,0:T(8,128)(2,1)}, bf16[2,512,4,128]{3,1,2,0:T(8,128)(2,1)}, u32[]{:S(2)}, u32[]{:S(2)}) %collective-permute-start) | collective-permute-done | bytes 1048608 | tf_op jit(solution)/shard_map/while/body/eval_jaxpr/ppermute | solution.py:15
  904.6 28.5 %collective-permute-done = bf16[2,512,4,128]{3,1,2,0:T(8,128)(2,1)} collective-permute-done((bf16[2,512,4,128]{3,1,2,0:T(8,128)(2,1)}, bf16[2,512,4,128]{3,1,2,0:T(8,128)(2,1)}, u32[]{:S(2)}, u32[]{:S(2)}) %collective-permute-start) | collective-permute-done | bytes 1048608 | tf_op jit(solution)/shard_map/while/body/eval_jaxpr/ppermute | solution.py:15
  952.9 21.2 %collective-permute-done.2 = bf16[2,512,4,128]{3,1,2,0:T(8,128)(2,1)S(1)} collective-permute-done((bf16[2,512,4,128]{3,1,2,0:T(8,128)(2,1)}, bf16[2,512,4,128]{3,1,2,0:T(8,128)(2,1)S(1)}, u32[]{:S(2)}, u32[]{:S(2)}) %collective-permute-start.2) | collective-permute-done | bytes 1048608 | tf_op jit(solution)/shard_map/ppermute | solution.py:15
  1062.8 34.6 %reduce-scatter.8.cloned.1.call-done = bf16[512,1024]{1,0:T(8,128)(2,1)} async-done(((bf16[1024,1024]{1,0:T(8,128)(2,1)}), bf16[512,1024]{1,0:T(8,128)(2,1)}) %reduce-scatter.8.cloned.1.call-update) | async-done | bytes 1048592 | tf_op jit(solution)/shard_map/reduce_scatter | solution.py:320
  1097.5 46.0 %reduce-scatter.16.cloned.1.call-done = bf16[512,1536]{1,0:T(8,128)(2,1)} async-done(((bf16[1024,1536]{1,0:T(8,128)(2,1)}), bf16[512,1536]{1,0:T(8,128)(2,1)}) %reduce-scatter.16.cloned.1.call-update) | async-done | bytes 1572880 | tf_op jit(solution)/shard_map/reduce_scatter | solution.py:332
  1143.5 46.1 %reduce-scatter.18.cloned.1.call-done = bf16[512,1536]{1,0:T(8,128)(2,1)} async-done(((bf16[1024,1536]{1,0:T(8,128)(2,1)}), bf16[512,1536]{1,0:T(8,128)(2,1)}) %reduce-scatter.18.cloned.1.call-update) | async-done | bytes 1572880 | tf_op jit(solution)/shard_map/reduce_scatter | solution.py:335
  1189.7 46.0 %reduce-scatter.20.cloned.1.call-done = bf16[1536,512]{1,0:T(8,128)(2,1)} async-done(((bf16[1536,1024]{1,0:T(8,128)(2,1)}), bf16[1536,512]{1,0:T(8,128)(2,1)}) %reduce-scatter.20.cloned.1.call-update) | async-done | bytes 1572880 | tf_op jit(solution)/shard_map/reduce_scatter | solution.py:338
  1237.1 22.9 %all-reduce.23.cloned.1.call-done = (bf16[512,1024]{1,0:T(8,128)(2,1)}, bf16[512,1024]{1,0:T(8,128)(2,1)}) async-done(((bf16[512,1024]{1,0:T(8,128)(2,1)}, bf16[512,1024]{1,0:T(8,128)(2,1)}), (bf16[512,1024]{1,0:T(8,128)(2,1)}, bf16[512,1024]{1,0:T(8,128)(2,1)})) %all-reduce.23.cloned.1.call-update) | async-done | bytes 2097168 | tf_op jit(solution)/shard_map/psum | solution.py:60
  1269.8 22.2 %all-reduce.6 = (bf16[512]{0:T(512)(128)(2,1)S(1)}, bf16[512]{0:T(512)(128)(2,1)S(1)}, bf16[64]{0:T(256)(128)(2,1)S(1)}, bf16[64]{0:T(256)(128)(2,1)S(1)}) all-reduce(bf16[512]{0:T(512)(128)(2,1)S(1)} %dynamic-slice.8, bf16[512]{0:T(512)(128)(2,1)S(1)} %dynamic-slice.10, ...), channel_id=1, replica_groups=mesh['shard'=2,'ctx'=8,'tp'=2] {'ctx'}, use_global_device_ids=true, to_apply=%region_43.44 | all-reduce | flops 1152 | bytes 4608 | tf_op jit(solution)/shard_map/psum | solution.py:362
  1298.6 227.9 %all-reduce.21.cloned.1.call-done = (bf16[512,1024]{1,0:T(8,128)(2,1)}, bf16[512,512]{1,0:T(8,128)(2,1)}, bf16[512,512]{1,0:T(8,128)(2,1)}, bf16[1024,512]{1,0:T...) async-done(((bf16[512,1024]{1,0:T(8,128)(2,1)}, bf16[512,512]{1,0:T(8,128)(2,1)}, bf16[512,512]{1,0:T(8,128)(2,1)}, ...) | async-done | bytes 7864336 | tf_op jit(solution)/shard_map/psum | solution.py:355
  (544 shorter events, 585.2 us)
Async XLA Ops:
  8.0 48.6 %all-gather.13.cloned.1.call-start = ((), (), s32[]{:S(2)}) async-start(), calls=%async_computation.8 | async-start | bytes 1572864 | tf_op jit(solution)/shard_map/all_gather | solution.py:87
  8.7 82.6 %all-gather.17.cloned.1.call-start = ((), (), s32[]{:S(2)}) async-start(), calls=%async_computation.10 | async-start | bytes 3145728 | tf_op jit(solution)/shard_map/all_gather | solution.py:85
  9.5 208.8 %all-gather.15.cloned.1.call-start = ((), (), s32[]{:S(2)}) async-start(), calls=%async_computation.9 | async-start | bytes 9437184 | tf_op jit(solution)/shard_map/all_gather | solution.py:148
  63.9 303.0 %all-gather.19.cloned.1.call-start = ((), (), s32[]{:S(2)}) async-start(), calls=%async_computation.11 | async-start | bytes 3145728 | tf_op jit(solution)/shard_map/all_gather | solution.py:88
  64.5 324.6 %all-reduce.17.cloned.1.call-start = ((), (), s32[]{:S(2)}) async-start(), calls=%async_computation.12 | async-start | bytes 2097152 | tf_op jit(solution)/shard_map/psum | solution.py:60
  371.1 65.7 %all-gather.21.cloned.1.call-start = ((), (), s32[]{:S(2)}) async-start(), calls=%async_computation.13 | async-start | bytes 4718592 | tf_op jit(solution)/shard_map/all_gather | solution.py:89
  371.9 111.6 %all-gather.23.cloned.1.call-start = ((), (), s32[]{:S(2)}) async-start(), calls=%async_computation.14 | async-start | bytes 4718592 | tf_op jit(solution)/shard_map/all_gather | solution.py:90
  372.6 157.4 %all-gather.25.cloned.1.call-start = ((), (), s32[]{:S(2)}) async-start(), calls=%async_computation.15 | async-start | bytes 4718592 | tf_op jit(solution)/shard_map/all_gather | solution.py:91
  373.3 190.5 %all-reduce.19.cloned.1.call-start = ((), (), s32[]{:S(2)}) async-start(), calls=%async_computation.16 | async-start | bytes 2097152 | tf_op jit(solution)/shard_map/psum | solution.py:207
  544.1 513.9 %reduce-scatter.10.cloned.1.call-start = ((), (), s32[]{:S(2)}) async-start(), calls=%async_computation.18 | async-start | bytes 1572864 | tf_op jit(solution)/shard_map/reduce_scatter | solution.py:323
  598.8 49.2 %collective-permute-start.1 = (bf16[2,512,4,128]{3,1,2,0:T(8,128)(2,1)}, bf16[2,512,4,128]{3,1,2,0:T(8,128)(2,1)}, u32[]{:S(2)}, u32[]{:S(2)}) collective-permute-start(bf16[2,512,4,128]{3,1,2,0:T(8,128)(2,1)} %get-tuple-element.1077), channel_id=1, source_target_pairs={{0,2},{2,4},{4,6},{6,8},{8,10},{10,12},{12,14},{14,0},{1,3},{3,5},... | collective-permute-start | bytes 3145736 | tf_op jit(solution)/shard_map/while/body/eval_jaxpr/ppermute | solution.py:15
  650.4 50.1 %collective-permute-start.1 = (bf16[2,512,4,128]{3,1,2,0:T(8,128)(2,1)}, bf16[2,512,4,128]{3,1,2,0:T(8,128)(2,1)}, u32[]{:S(2)}, u32[]{:S(2)}) collective-permute-start(bf16[2,512,4,128]{3,1,2,0:T(8,128)(2,1)} %get-tuple-element.1077), channel_id=1, source_target_pairs={{0,2},{2,4},{4,6},{6,8},{8,10},{10,12},{12,14},{14,0},{1,3},{3,5},... | collective-permute-start | bytes 3145736 | tf_op jit(solution)/shard_map/while/body/eval_jaxpr/ppermute | solution.py:15
  703.0 49.2 %collective-permute-start.1 = (bf16[2,512,4,128]{3,1,2,0:T(8,128)(2,1)}, bf16[2,512,4,128]{3,1,2,0:T(8,128)(2,1)}, u32[]{:S(2)}, u32[]{:S(2)}) collective-permute-start(bf16[2,512,4,128]{3,1,2,0:T(8,128)(2,1)} %get-tuple-element.1077), channel_id=1, source_target_pairs={{0,2},{2,4},{4,6},{6,8},{8,10},{10,12},{12,14},{14,0},{1,3},{3,5},... | collective-permute-start | bytes 3145736 | tf_op jit(solution)/shard_map/while/body/eval_jaxpr/ppermute | solution.py:15
  754.7 48.3 %collective-permute-start.1 = (bf16[2,512,4,128]{3,1,2,0:T(8,128)(2,1)}, bf16[2,512,4,128]{3,1,2,0:T(8,128)(2,1)}, u32[]{:S(2)}, u32[]{:S(2)}) collective-permute-start(bf16[2,512,4,128]{3,1,2,0:T(8,128)(2,1)} %get-tuple-element.1077), channel_id=1, source_target_pairs={{0,2},{2,4},{4,6},{6,8},{8,10},{10,12},{12,14},{14,0},{1,3},{3,5},... | collective-permute-start | bytes 3145736 | tf_op jit(solution)/shard_map/while/body/eval_jaxpr/ppermute | solution.py:15
  805.4 47.3 %collective-permute-start.1 = (bf16[2,512,4,128]{3,1,2,0:T(8,128)(2,1)}, bf16[2,512,4,128]{3,1,2,0:T(8,128)(2,1)}, u32[]{:S(2)}, u32[]{:S(2)}) collective-permute-start(bf16[2,512,4,128]{3,1,2,0:T(8,128)(2,1)} %get-tuple-element.1077), channel_id=1, source_target_pairs={{0,2},{2,4},{4,6},{6,8},{8,10},{10,12},{12,14},{14,0},{1,3},{3,5},... | collective-permute-start | bytes 3145736 | tf_op jit(solution)/shard_map/while/body/eval_jaxpr/ppermute | solution.py:15
  855.2 46.4 %collective-permute-start.1 = (bf16[2,512,4,128]{3,1,2,0:T(8,128)(2,1)}, bf16[2,512,4,128]{3,1,2,0:T(8,128)(2,1)}, u32[]{:S(2)}, u32[]{:S(2)}) collective-permute-start(bf16[2,512,4,128]{3,1,2,0:T(8,128)(2,1)} %get-tuple-element.1077), channel_id=1, source_target_pairs={{0,2},{2,4},{4,6},{6,8},{8,10},{10,12},{12,14},{14,0},{1,3},{3,5},... | collective-permute-start | bytes 3145736 | tf_op jit(solution)/shard_map/while/body/eval_jaxpr/ppermute | solution.py:15
  989.0 69.1 %reduce-scatter.12.cloned.1.call-start = ((), (), s32[]{:S(2)}) async-start(), calls=%async_computation.19 | async-start | bytes 1572864 | tf_op jit(solution)/shard_map/reduce_scatter | solution.py:326
  994.2 68.6 %reduce-scatter.14.cloned.1.call-start = ((), (), s32[]{:S(2)}) async-start(), calls=%async_computation.20 | async-start | bytes 3145728 | tf_op jit(solution)/shard_map/reduce_scatter | solution.py:329
  999.4 98.1 %reduce-scatter.8.cloned.1.call-start = ((), (), s32[]{:S(2)}) async-start(), calls=%async_computation.17 | async-start | bytes 3145728 | tf_op jit(solution)/shard_map/reduce_scatter | solution.py:320
  1030.5 113.0 %reduce-scatter.16.cloned.1.call-start = ((), (), s32[]{:S(2)}) async-start(), calls=%async_computation.21 | async-start | bytes 4718592 | tf_op jit(solution)/shard_map/reduce_scatter | solution.py:332
  1036.7 153.0 %reduce-scatter.18.cloned.1.call-start = ((), (), s32[]{:S(2)}) async-start(), calls=%async_computation.22 | async-start | bytes 4718592 | tf_op jit(solution)/shard_map/reduce_scatter | solution.py:335
  1042.0 193.8 %reduce-scatter.20.cloned.1.call-start = ((), (), s32[]{:S(2)}) async-start(), calls=%async_computation.23 | async-start | bytes 4718592 | tf_op jit(solution)/shard_map/reduce_scatter | solution.py:338
  1048.1 211.9 %all-reduce.23.cloned.1.call-start = ((), (), s32[]{:S(2)}) async-start(), calls=%async_computation.25 | async-start | bytes 4194304 | tf_op jit(solution)/shard_map/psum | solution.py:60
  1058.0 468.5 %all-reduce.21.cloned.1.call-start = ((), (), s32[]{:S(2)}) async-start(), calls=%async_computation.24 | async-start | bytes 15728640 | tf_op jit(solution)/shard_map/psum | solution.py:355
  (95 other events, 1956.6 us)
Sparse Core Ops, SparseCore 0:
  9.6 24.0 all-gather.10
  35.3 21.2 all-gather.12
  58.2 33.1 all-gather.16
  93.3 124.8 all-gather.14
  219.7 31.2 all-gather.18
  371.2 17.8 all-reduce.16
  390.7 46.1 all-gather.20
  438.5 44.9 all-gather.22
  485.1 44.9 all-gather.24
  544.2 19.5 all-reduce.18
  989.1 17.0 reduce-scatter.9
  1008.4 20.3 reduce-scatter.11
  1031.0 31.8 reduce-scatter.13
  1065.6 31.8 reduce-scatter.7
  1100.1 43.3 reduce-scatter.15
  1146.3 43.3 reduce-scatter.17
  1192.3 43.3 reduce-scatter.19
  1238.6 21.2 all-reduce.22
  1265.4 261.0 all-reduce.20
where the time goes:
time: 1550 us
  waiting for transfers between devices  981 us (63%)
  matrix products  272 us (18%)
  other arithmetic  133 us (9%)
  local copies, waits for them, and re-layouts  91.2 us (6%)
  blocking collectives  44.3 us (3%)
  between operations  17.2 us (1%)
    ppermute x15, waiting for transfers between devices, from_behind(): return lax.ppermute(x, axis, [(i, (i + by) % count) for i in range(count)])  246 us
    psum x1, waiting for transfers between devices, body(): lax.psum(shares[0].astype(jnp.bfloat16), 'ctx').astype(jnp.float32)  228 us
    all_gather x1, waiting for transfers between devices, body(): arrived = lax.all_gather(key_value, 'ctx', axis=1, tiled=True)  102 us
    dot_general x16, matrix products, visible_scores(): jnp.einsum('tagd,kad->agtk', q_group, key_block, preferred_element_type=j...  68.2 us
    reduce_scatter x1, waiting for transfers between devices, body(): lax.psum_scatter(grad_up.astype(jnp.bfloat16), 'shard', scatter_dimension...  46.1 us
    reduce_scatter x1, waiting for transfers between devices, body(): lax.psum_scatter(grad_gate.astype(jnp.bfloat16), 'shard', scatter_dimensi...  46 us
    reduce_scatter x1, waiting for transfers between devices, body(): lax.psum_scatter(grad_down.astype(jnp.bfloat16), 'shard', scatter_dimensi...  46 us
    all_gather x1, waiting for transfers between devices, body(): lax.all_gather(w_gate, 'shard', axis=0, tiled=True)  44.6 us
  transfers between devices with their start and end apart: 34, of which 31 were waited for; matrix products, arithmetic and copies ran while one was open for 25% of the time, Pallas kernels for 0%

commit v1 on v0

v1 whole, which is shorter than its diff:
```python
import functools

import jax
import jax.numpy as jnp
from jax import lax
from jax.experimental import pallas as pl
from jax.experimental.pallas import tpu as pltpu
from jax.sharding import PartitionSpec as P

EPS = 1e-06
THETA = 1000000.0
LOG2E = 1.4426950408889634
HEAD = 128
BF16 = jnp.bfloat16
F32 = jnp.float32
VMEM_LIMIT = 48 * 1024 * 1024


def rms_parts(values):
    factor = lax.rsqrt(jnp.mean(values * values, axis=-1, keepdims=True) + EPS)
    return (values * factor, factor)


def rms_back(grad_hat, normal, factor):
    return factor * (grad_hat - normal * jnp.mean(grad_hat * normal, axis=-1, keepdims=True))


def dot(a, b):
    return jnp.dot(a, b, preferred_element_type=F32)


def dot_nt(a, b):
    return lax.dot_general(a, b, (((1,), (1,)), ((), ())), preferred_element_type=F32)


def dot_tn(a, b):
    return lax.dot_general(a, b, (((0,), (0,)), ((), ())), preferred_element_type=F32)


def after(value, *earlier):
    return lax.optimization_barrier((value,) + earlier)[0]


def pieces_of(own, axis):
    count = lax.axis_size(axis)
    return [own] + [
        lax.ppermute(own, axis, [((i + j) % count, i) for i in range(count)])
        for j in range(1, count)
    ]


def join(pieces, dim, index):
    count = len(pieces)
    if count == 1:
        return pieces[0]
    if count == 2:
        return jnp.where(
            index == 0, jnp.concatenate(pieces, dim), jnp.concatenate(pieces[::-1], dim)
        )
    size = pieces[0].shape[dim]
    shape = list(pieces[0].shape)
    shape[dim] = size * count
    whole = jnp.zeros(shape, pieces[0].dtype)
    for j, piece in enumerate(pieces):
        whole = lax.dynamic_update_slice_in_dim(whole, piece, (index + j) % count * size, dim)
    return whole


def pair_total(partial):
    count = lax.axis_size("tp")
    partial = partial.astype(BF16)
    if count != 2:
        return lax.psum(partial, "tp").astype(F32)
    other = lax.ppermute(partial, "tp", [(0, 1), (1, 0)])
    return partial.astype(F32) + other.astype(F32)


def to_shard_owner(grad, dim):
    count = lax.axis_size("shard")
    index = lax.axis_index("shard")
    if count != 2:
        return lax.psum_scatter(grad, "shard", scatter_dimension=dim, tiled=True).astype(F32)
    size = grad.shape[dim] // 2
    sent = lax.dynamic_slice_in_dim(grad, (1 - index) * size, size, dim)
    kept = lax.dynamic_slice_in_dim(grad, index * size, size, dim)
    other = lax.ppermute(sent, "shard", [(0, 1), (1, 0)])
    return kept.astype(F32) + other.astype(F32)


def ctx_total(value):
    count = lax.axis_size("ctx")
    index = lax.axis_index("ctx")
    levels = [1 << b for b in range(count.bit_length() - 1)]
    for level in levels:
        bit = (index // level) % 2
        size = value.shape[0] // 2
        sent = lax.dynamic_slice_in_dim(value, (1 - bit) * size, size, 0).astype(BF16)
        kept = lax.dynamic_slice_in_dim(value, bit * size, size, 0)
        other = lax.ppermute(sent, "ctx", [(i, i ^ level) for i in range(count)])
        value = kept + other.astype(F32)
    value = value.astype(BF16)
    for level in levels[::-1]:
        bit = (index // level) % 2
        other = lax.ppermute(value, "ctx", [(i, i ^ level) for i in range(count)])
        value = join([value, other], 0, bit)
    return value.astype(F32)


def rope_kernel(roped, pre_ref, cos_ref, sin_ref, gain_ref, out_ref):
    pre = pre_ref[...]

    @pl.when(pl.program_id(0) < roped)
    def _():
        factor = lax.rsqrt(jnp.mean(pre * pre, axis=-1, keepdims=True) + EPS)
        scaled = pre * factor * gain_ref[...]
        turned = pltpu.roll(scaled, HEAD // 2, 1)
        out_ref[...] = (scaled * cos_ref[...] + turned * sin_ref[...]).astype(BF16)

    @pl.when(pl.program_id(0) >= roped)
    def _():
        out_ref[...] = pre.astype(BF16)


def rope(pre, roped, cosine, sine, gain):
    rows, width = pre.shape
    column = pl.BlockSpec((rows, HEAD), lambda h: (0, h))
    table = pl.BlockSpec((rows, HEAD), lambda h: (0, 0))
    return pl.pallas_call(
        functools.partial(rope_kernel, roped),
        grid=(width // HEAD,),
        in_specs=[column, table, table, pl.BlockSpec((1, HEAD), lambda h: (0, 0))],
        out_specs=column,
        out_shape=jax.ShapeDtypeStruct((rows, width), BF16),
        compiler_params=pltpu.CompilerParams(vmem_limit_bytes=VMEM_LIMIT),
    )(pre, cosine, sine, gain)


def rope_back_kernel(grad_ref, pre_ref, cos_ref, sin_ref, gain_ref, out_ref, sum_ref):
    pre = pre_ref[...]
    grad = grad_ref[...]
    factor = lax.rsqrt(jnp.mean(pre * pre, axis=-1, keepdims=True) + EPS)
    hat = pre * factor
    back = grad * cos_ref[...] - pltpu.roll(grad, HEAD // 2, 1) * sin_ref[...]
    terms = jnp.sum(back * hat, axis=0, keepdims=True)

    @pl.when(pl.program_id(0) == 0)
    def _():
        sum_ref[...] = terms

    @pl.when(pl.program_id(0) > 0)
    def _():
        sum_ref[...] += terms

    back = back * gain_ref[...]
    inner = jnp.mean(back * hat, axis=-1, keepdims=True)
    out_ref[...] = (factor * (back - hat * inner)).astype(BF16)


def rope_back(grad, pre, cosine, sine, gain):
    rows, width = grad.shape
    column = pl.BlockSpec((rows, HEAD), lambda h: (0, h))
    table = pl.BlockSpec((rows, HEAD), lambda h: (0, 0))
    one_row = pl.BlockSpec((1, HEAD), lambda h: (0, 0))
    return pl.pallas_call(
        rope_back_kernel,
        grid=(width // HEAD,),
        in_specs=[column, column, table, table, one_row],
        out_specs=[column, one_row],
        out_shape=[
            jax.ShapeDtypeStruct((rows, width), BF16),
            jax.ShapeDtypeStruct((1, HEAD), F32),
        ],
        compiler_params=pltpu.CompilerParams(vmem_limit_bytes=VMEM_LIMIT),
    )(grad, pre, cosine, sine, gain)


def doc_begins(meta_ref, docs, place):
    begin = jnp.zeros_like(place)
    for i in range(1, docs):
        start = meta_ref[i]
        begin = jnp.where(place >= start, start, begin)
    return begin


def block_mask(meta_ref, docs, shape, half, q_part, k_part, diagonal):
    row = lax.broadcasted_iota(jnp.int32, (shape[0], 1), 0)
    q_place = q_part * half + jnp.where(row >= half, row - half, row)
    begin = doc_begins(meta_ref, docs, q_place) - k_part * half
    column = lax.broadcasted_iota(jnp.int32, shape, 1)
    visible = column >= begin
    if diagonal:
        visible = visible & (column <= q_place - k_part * half)
    return visible


def any_visible(meta_ref, docs, half, q_part, k_part):
    return (k_part + 1) * half > doc_begins(meta_ref, docs, q_part * half)


def two_heads(ref, start, half):
    rows = pl.ds(start, half)
    return jnp.concatenate([ref[rows, :HEAD], ref[rows, HEAD:]], axis=0)


def forward_kernel(docs, count, meta_ref, q_ref, k_ref, v_ref, *refs):
    others = refs[: 2 * (count - 1)]
    out_ref, out16_ref, lse_ref, acc_ref = refs[2 * (count - 1) :]
    half = q_ref.shape[0] // 2
    factor = HEAD**-0.5 * LOG2E
    ones = jnp.ones((half, HEAD), BF16)
    own = meta_ref[0]

    def block(start, keys, values, q_part, k_part, diagonal):
        scores = dot_nt(two_heads(q_ref, start, half), keys)
        visible = block_mask(meta_ref, docs, scores.shape, half, q_part, k_part, diagonal)
        weights = jnp.where(visible, jnp.exp2(scores * factor), 0.0).astype(BF16)
        return dot(weights, jnp.concatenate([values, ones], axis=1))

    for e in range(2):
        rows = pl.ds(e * half, half)
        part = own if e == 0 else 2 * count - 1 - own
        acc_ref[e] = block(e * half, k_ref[rows, :], v_ref[rows, :], part, part, True)
    for d in range(count - 1):
        side = meta_ref[docs + 2 * d]
        k_part = meta_ref[docs + 2 * d + 1]
        q_part = jnp.where(side == 0, own, 2 * count - 1 - own)

        @pl.when(any_visible(meta_ref, docs, half, q_part, k_part))
        def _():
            start = pl.multiple_of(side * half, half)
            acc_ref[side] += block(
                start, others[2 * d][...], others[2 * d + 1][...], q_part, k_part, False
            )

    for e in range(2):
        total = acc_ref[e]
        sums = total[:, HEAD:]
        result = total[:, :HEAD] / sums
        lse = jnp.log2(sums)
        for a in range(2):
            part = slice(a * half, (a + 1) * half)
            place = (pl.ds(e * half, half), slice(a * HEAD, (a + 1) * HEAD))
            out_ref[place] = result[part]
            out16_ref[place] = result[part].astype(BF16)
            lse_ref[place] = lse[part]


def backward_kernel(docs, count, meta_ref, q_ref, g_ref, o_ref, lse_ref, k_ref, v_ref, *refs):
    others = refs[: 2 * (count - 1)]
    dq_ref, dkv_ref = refs[2 * (count - 1) : 2 * count]
    given = refs[2 * count : 3 * count - 1]
    acc_ref, stats_ref, delta_ref = refs[3 * count - 1 :]
    half = q_ref.shape[0] // 2
    scale = HEAD**-0.5
    own = meta_ref[0]

    for e in range(2):
        grads = two_heads(g_ref, e * half, half).astype(F32)
        delta = jnp.sum(grads * two_heads(o_ref, e * half, half), axis=1, keepdims=True)
        delta_ref[e] = jnp.broadcast_to(delta, (2 * half, HEAD))
        stats_ref[e] = two_heads(lse_ref, e * half, half)

    def block(side, start, keys, values, q_part, k_part, diagonal):
        queries = two_heads(q_ref, start, half)
        grads = two_heads(g_ref, start, half)
        scores = dot_nt(queries, keys)
        repeat = half // HEAD
        lse = jnp.concatenate([stats_ref[side]] * repeat, axis=1)
        delta = jnp.concatenate([delta_ref[side]] * repeat, axis=1)
        visible = block_mask(meta_ref, docs, scores.shape, half, q_part, k_part, diagonal)
        weights = jnp.where(visible, jnp.exp2(scores * (scale * LOG2E) - lse), 0.0)
        d_weights = dot_nt(grads, values)
        d_scores = (weights * (d_weights - delta)).astype(BF16)
        d_values = dot_tn(weights.astype(BF16), grads)
        d_keys = dot_tn(d_scores, queries) * scale
        return dot(d_scores, keys) * scale, d_keys, d_values

    for e in range(2):
        rows = pl.ds(e * half, half)
        part = own if e == 0 else 2 * count - 1 - own
        d_queries, d_keys, d_values = block(
            e, e * half, k_ref[rows, :], v_ref[rows, :], part, part, True
        )
        acc_ref[e] = d_queries
        dkv_ref[0, rows, :] = d_keys
        dkv_ref[1, rows, :] = d_values
    for d in range(count - 1):
        side = meta_ref[docs + 2 * d]
        k_part = meta_ref[docs + 2 * d + 1]
        q_part = jnp.where(side == 0, own, 2 * count - 1 - own)
        seen = any_visible(meta_ref, docs, half, q_part, k_part)

        @pl.when(seen)
        def _():
            start = pl.multiple_of(side * half, half)
            d_queries, d_keys, d_values = block(
                side, start, others[2 * d][...], others[2 * d + 1][...], q_part, k_part, False
            )
            acc_ref[side] += d_queries
            given[d][0] = d_keys.astype(BF16)
            given[d][1] = d_values.astype(BF16)

        @pl.when(jnp.logical_not(seen))
        def _():
            given[d][...] = jnp.zeros_like(given[d])

    for e in range(2):
        for a in range(2):
            dq_ref[pl.ds(e * half, half), a * HEAD : (a + 1) * HEAD] = acc_ref[
                e, a * half : (a + 1) * half, :
            ]


def key_value_specs(rows, half, kv_heads, count):
    own = [
        pl.BlockSpec((rows, HEAD), lambda h, m: (0, h)),
        pl.BlockSpec((rows, HEAD), lambda h, m: (0, kv_heads + h)),
    ]
    other = [
        pl.BlockSpec((half, HEAD), lambda h, m: (0, h)),
        pl.BlockSpec((half, HEAD), lambda h, m: (0, kv_heads + h)),
    ]
    return own + other * (count - 1)


def twice(arrays):
    return [a for a in arrays for _ in range(2)]


def attend(meta, docs, queries, key_value, others):
    rows, width = queries.shape
    half = rows // 2
    count = len(others) + 1
    kv_heads = key_value.shape[1] // (2 * HEAD)
    column = pl.BlockSpec((rows, 2 * HEAD), lambda h, m: (0, h))
    return pl.pallas_call(
        functools.partial(forward_kernel, docs, count),
        grid_spec=pltpu.PrefetchScalarGridSpec(
            num_scalar_prefetch=1,
            grid=(kv_heads,),
            in_specs=[column] + key_value_specs(rows, half, kv_heads, count),
            out_specs=[column] * 3,
            scratch_shapes=[pltpu.VMEM((2, 2 * half, 2 * HEAD), F32)],
        ),
        out_shape=[
            jax.ShapeDtypeStruct((rows, width), F32),
            jax.ShapeDtypeStruct((rows, width), BF16),
            jax.ShapeDtypeStruct((rows, width), F32),
        ],
        compiler_params=pltpu.CompilerParams(vmem_limit_bytes=VMEM_LIMIT),
        cost_estimate=pl.CostEstimate(
            flops=(count + 1) * half * half * width * 4,
            bytes_accessed=rows * width * 16,
            transcendentals=(count + 1) * half * half * width // HEAD,
        ),
    )(meta, queries, key_value, key_value, *twice(others))


def attend_back(meta, docs, queries, grads, outs, lse, key_value, others):
    rows, width = queries.shape
    half = rows // 2
    count = len(others) + 1
    kv_width = key_value.shape[1] // 2
    kv_heads = kv_width // HEAD
    column = pl.BlockSpec((rows, 2 * HEAD), lambda h, m: (0, h))
    result = pl.pallas_call(
        functools.partial(backward_kernel, docs, count),
        grid_spec=pltpu.PrefetchScalarGridSpec(
            num_scalar_prefetch=1,
            grid=(kv_heads,),
            in_specs=[column] * 4 + key_value_specs(rows, half, kv_heads, count),
            out_specs=[column, pl.BlockSpec((2, rows, HEAD), lambda h, m: (0, 0, h))]
            + [pl.BlockSpec((2, half, HEAD), lambda h, m: (0, 0, h))] * (count - 1),
            scratch_shapes=[pltpu.VMEM((2, 2 * half, HEAD), F32)] * 3,
        ),
        out_shape=[
            jax.ShapeDtypeStruct((rows, width), F32),
            jax.ShapeDtypeStruct((2, rows, kv_width), F32),
        ]
        + [jax.ShapeDtypeStruct((2, half, kv_width), BF16)] * (count - 1),
        compiler_params=pltpu.CompilerParams(vmem_limit_bytes=VMEM_LIMIT),
        cost_estimate=pl.CostEstimate(
            flops=(count + 1) * half * half * width * 10,
            bytes_accessed=rows * width * 24,
            transcendentals=(count + 1) * half * half * width // HEAD,
        ),
    )(meta, queries, grads, outs, lse, key_value, key_value, *twice(others))
    return result[0], result[1], result[2:]


def body(
    tokens,
    cotangent,
    seq_lengths,
    part_order,
    w_query,
    key_weight,
    value_weight,
    w_out,
    w_gate,
    w_up,
    w_down,
    gain_in,
    gain_post,
    gain_q,
    gain_k,
):
    shard_count = lax.axis_size("shard")
    shard = lax.axis_index("shard")
    count = lax.axis_size("ctx")
    ctx = lax.axis_index("ctx")
    rows, model = tokens.shape
    half = rows // 2
    depth = model // shard_count
    docs = seq_lengths.shape[1]
    kv_width = key_weight.shape[1]

    kv_pieces = pieces_of(jnp.concatenate([key_weight, value_weight], axis=1), "shard")
    packed = jnp.concatenate([gain_in, gain_post, gain_q, gain_k])
    gains = lax.all_gather(packed, "shard", axis=0).astype(F32)
    cuts = [0, depth, 2 * depth, 2 * depth + gain_q.shape[0], packed.shape[0]]
    scale_in, scale_post, scale_q, scale_k = (
        gains[:, lo:hi].reshape(1, -1) for lo, hi in zip(cuts[:-1], cuts[1:])
    )

    q_pieces = pieces_of(after(w_query, kv_pieces[-1]), "shard")
    out_pieces = pieces_of(after(w_out, q_pieces[-1]), "shard")
    gate_pieces = pieces_of(after(w_gate, q_pieces[-1]), "shard")
    up_pieces = pieces_of(after(w_up, out_pieces[-1]), "shard")
    down_pieces = pieces_of(after(w_down, out_pieces[-1]), "shard")

    lengths = seq_lengths[0]
    starts = jnp.cumsum(lengths) - lengths
    parts = part_order[:, 0]
    part = parts[ctx]
    other_parts = [parts[ctx ^ d] for d in range(1, count)]
    sides = [jnp.where(p < part, 0, 1).astype(jnp.int32) for p in other_parts]
    held_parts = [jnp.where(p < part, p, 2 * count - 1 - p) for p in other_parts]
    meta = jnp.stack(
        [part]
        + [starts[i] for i in range(1, docs)]
        + [v for pair in zip(sides, held_parts) for v in pair]
    ).astype(jnp.int32)
    places = jnp.concatenate(
        [p * half + jnp.arange(half, dtype=jnp.int32) for p in (part, 2 * count - 1 - part)]
    )
    begins = jnp.zeros_like(places)
    for i in range(1, docs):
        begins = jnp.where(places >= starts[i], starts[i], begins)
    frequency = THETA ** (-jnp.arange(0, HEAD, 2, dtype=F32) / HEAD)
    angles = (places - begins).astype(F32)[:, None] * frequency[None, :]
    cosine, sine = jnp.cos(angles), jnp.sin(angles)
    cosine = jnp.concatenate([cosine, cosine], axis=-1)
    sine = jnp.concatenate([-sine, sine], axis=-1)

    inputs = tokens.astype(F32)
    normal_one, factor_one = rms_parts(inputs)
    normed_input = (normal_one * scale_in).astype(BF16)

    def project(pieces):
        total = None
        for j, piece in enumerate(pieces):
            at = (shard + j) % shard_count * depth
            term = dot(lax.dynamic_slice_in_dim(normed_input, at, depth, 1), piece)
            total = term if total is None else total + term
        return total

    kv_pre = project(kv_pieces)
    key_value = rope(kv_pre, kv_width // HEAD, cosine, sine, scale_k)
    held = []
    for d in range(1, count):
        start = jnp.where(part < other_parts[d - 1], 0, half)
        sent = lax.dynamic_slice_in_dim(key_value, start, half, 0)
        held.append(lax.ppermute(sent, "ctx", [(i, i ^ d) for i in range(count)]))
    q_pre = project(q_pieces)
    queries = rope(q_pre, q_pre.shape[1] // HEAD, cosine, sine, scale_q)
    attended, attn_out, lse = attend(meta, docs, queries, key_value, held)

    full_out = join(out_pieces, 1, shard)
    full_gate = join(gate_pieces, 0, shard)
    full_up = join(up_pieces, 0, shard)
    full_down = join(down_pieces, 1, shard)
    full_kv = join(kv_pieces, 0, shard)
    full_query = join(q_pieces, 0, shard)

    residual = inputs + pair_total(dot(attn_out, full_out))
    normal_two, factor_two = rms_parts(residual)
    normed_two = (normal_two * scale_post).astype(BF16)
    gate_act = dot(normed_two, full_gate)
    upward = dot(normed_two, full_up)
    sigma = jax.nn.sigmoid(gate_act)
    silu_act = gate_act * sigma
    hidden = (silu_act * upward).astype(BF16)
    mixed = (residual + pair_total(dot(hidden, full_down))).astype(BF16)
    grad_down = dot_tn(hidden, cotangent).astype(BF16)
    d_hidden = dot_nt(cotangent, full_down)
    d_gate = (d_hidden * upward * sigma * (1.0 + gate_act * (1.0 - sigma))).astype(BF16)
    d_up = (d_hidden * silu_act).astype(BF16)
    grad_gate = dot_tn(normed_two, d_gate).astype(BF16)
    grad_up = dot_tn(normed_two, d_up).astype(BF16)
    d_normed_two = pair_total(dot_nt(d_gate, full_gate) + dot_nt(d_up, full_up))
    grad_post = jnp.sum(d_normed_two * normal_two, axis=0)
    d_residual = cotangent.astype(F32) + rms_back(
        d_normed_two * scale_post, normal_two, factor_two
    )

    d_branch = d_residual.astype(BF16)
    d_attn = dot_nt(d_branch, full_out).astype(BF16)
    d_queries, d_kv, given = attend_back(
        meta, docs, queries, d_attn, attended, lse, key_value, held
    )
    returned = [
        lax.ppermute(g, "ctx", [(i, i ^ d) for i in range(count)])
        for d, g in zip(range(1, count), given)
    ]
    grad_out = dot_tn(attn_out, d_branch).astype(BF16)
    d_q_pre, gq_part = rope_back(d_queries, q_pre, cosine, sine, scale_q)
    grad_query = dot_tn(normed_input, d_q_pre).astype(BF16)

    first = sum(
        jnp.where(part < p, g.astype(F32), 0.0) for p, g in zip(other_parts, returned)
    )
    second = sum(
        jnp.where(part < p, 0.0, g.astype(F32)) for p, g in zip(other_parts, returned)
    )
    d_kv = d_kv + jnp.concatenate([first, second], axis=1)
    d_k_pre, gk_part = rope_back(d_kv[0], kv_pre, cosine, sine, scale_k)
    d_kv_pre = jnp.concatenate([d_k_pre, d_kv[1].astype(BF16)], axis=1)
    grad_kv = dot_tn(normed_input, d_kv_pre).astype(BF16)
    d_normed = pair_total(dot_nt(d_q_pre, full_query) + dot_nt(d_kv_pre, full_kv))
    grad_in = jnp.sum(d_normed * normal_one, axis=0)
    input_grad = d_residual + rms_back(d_normed * scale_in, normal_one, factor_one)

    once = jnp.where(lax.axis_index("tp") == 0, 1.0, 0.0)
    gain_grads = lax.psum(
        jnp.concatenate([grad_in * once, grad_post * once, gq_part[0], gk_part[0]]),
        ("shard", "ctx", "tp"),
    )
    own_gains = []
    for lo, size in ((0, model), (model, model), (2 * model, HEAD), (2 * model + HEAD, HEAD)):
        size = size // shard_count
        own_gains.append(lax.dynamic_slice_in_dim(gain_grads, lo + shard * size, size, 0))

    owned_down = ctx_total(to_shard_owner(grad_down, 1))
    owned_gate = ctx_total(to_shard_owner(grad_gate, 0))
    owned_up = ctx_total(to_shard_owner(grad_up, 0))
    owned_out = ctx_total(to_shard_owner(grad_out, 1))
    owned_query = ctx_total(to_shard_owner(grad_query, 0))
    owned_kv = ctx_total(to_shard_owner(grad_kv, 0))
    return (
        mixed,
        input_grad,
        owned_query,
        owned_kv[:, :kv_width],
        owned_kv[:, kv_width:],
        owned_out,
        owned_gate,
        owned_up,
        owned_down,
        *own_gains,
    )


def solution(mesh):
    placed = (
        P(("shard", "ctx"), None),
        P(("shard", "ctx"), None),
        P("shard", None),
        P(),
        P("shard", "tp"),
        P("shard", "tp"),
        P("shard", "tp"),
        P("tp", "shard"),
        P("shard", "tp"),
        P("shard", "tp"),
        P("tp", "shard"),
        P("shard"),
        P("shard"),
        P("shard"),
        P("shard"),
    )
    return jax.shard_map(
        body,
        mesh=mesh,
        in_specs=placed,
        out_specs=(
            P(("shard", "ctx"), None),
            P(("shard", "ctx"), None),
            P("shard", "tp"),
            P("shard", "tp"),
            P("shard", "tp"),
            P("tp", "shard"),
            P("shard", "tp"),
            P("shard", "tp"),
            P("tp", "shard"),
            P("shard"),
            P("shard"),
            P("shard"),
            P("shard"),
        ),
        check_vma=False,
    )
```

time: 1550 us -> 858 us (0.55)
  waiting for transfers between devices: 981 us -> 439 us
  matrix products: 272 us -> 65.3 us
  starting transfers between devices: 6.49 us -> 109 us
  other arithmetic: 133 us -> 47.1 us
  local copies, waits for them, and re-layouts: 91.2 us -> 26.2 us
  Pallas kernels: 0 us -> 57.6 us
  blocking collectives: 44.3 us -> 71.3 us
    all_gather x8 -> x0, waiting for transfers between devices: 279 us -> none  [the longest x1 102 us: body(): arrived = lax.all_gather(key_value, 'ctx', axis=1, tiled=True)]
    psum x4 -> x0, waiting for transfers between devices: 273 us -> none  [the longest x1 228 us: body(): lax.psum(shares[0].astype(jnp.bfloat16), 'ctx').astype(jnp.float32)]
    dot_general x77 -> x20, matrix products: 272 us -> 65.3 us  [the longest x8 27.9 us: dot(): return jnp.dot(a, b, preferred_element_type=F32)]
    ppermute x15 -> x66, waiting for transfers between devices: 246 us -> 439 us  [the longest x18 106 us: ctx_total(): other = lax.ppermute(value, 'ctx', [(i, i ^ level) for i in range(count)])]
    reduce_scatter x7 -> x0, waiting for transfers between devices: 178 us -> none  [the longest x1 46.1 us: body(): lax.psum_scatter(grad_up.astype(jnp.bfloat16), 'shard', scatter_dimension...]
    ppermute x15 -> x66, starting transfers between devices: 4.66 us -> 109 us  [the longest x7 32.2 us: body(): lax.ppermute(g, 'ctx', [(i, i ^ d) for i in range(count)])]
    pallas_call x0 -> x6, Pallas kernels: none -> 57.6 us  [the longest x1 29.1 us: attend_back(): pl.pallas_call(functools.partial(backward_kernel, docs, count), grid_spec...]
    reduce_sum x31 -> x1, other arithmetic: 51.2 us -> 0.87 us  [body(): grad_in = jnp.sum(d_normed * normal_one, axis=0)]
  transfers between devices with their start and end apart: 34 -> 66, of which waited for: 31 -> 32; matrix products, arithmetic and copies ran while one was open for 25% -> 13% of each run, Pallas kernels for 0% -> 3%
where the time goes in v1:
time: 858 us; the launch traced here: 845 us
  waiting for transfers between devices  439 us (51%)
  starting transfers between devices  109 us (13%)
  blocking collectives  71.3 us (8%)
  matrix products  65.3 us (8%)
  Pallas kernels  57.6 us (7%)
  other arithmetic  47.1 us (5%)
  between operations  29.2 us (3%)
  local copies, waits for them, and re-layouts  26.2 us (3%)
    ppermute x18, waiting for transfers between devices, ctx_total(): other = lax.ppermute(value, 'ctx', [(i, i ^ level) for i in range(count)])  106 us
    ppermute x6, waiting for transfers between devices, pieces_of(): lax.ppermute(own, axis, [((i + j) % count, i) for i in range(count)])  93.2 us
    ppermute x6, waiting for transfers between devices, to_shard_owner(): other = lax.ppermute(sent, 'shard', [(0, 1), (1, 0)])  75.6 us
    ppermute x7, waiting for transfers between devices, body(): lax.ppermute(g, 'ctx', [(i, i ^ d) for i in range(count)])  57.1 us
    ppermute x7, waiting for transfers between devices, body(): held.append(lax.ppermute(sent, 'ctx', [(i, i ^ d) for i in range(count)]))  55.2 us
    ppermute x18, waiting for transfers between devices, ctx_total(): other = lax.ppermute(sent, 'ctx', [(i, i ^ level) for i in range(count)])  50.6 us
    psum x1, blocking collectives, body(): lax.psum(jnp.concatenate([grad_in * once, grad_post * once, gq_part[0], g...  48.2 us
    ppermute x7, starting transfers between devices, body(): lax.ppermute(g, 'ctx', [(i, i ^ d) for i in range(count)])  32.2 us
  transfers between devices with their start and end apart: 66, of which 32 were waited for; matrix products, arithmetic and copies ran while one was open for 13% of the time, Pallas kernels for 3%

profile of v1, /device:TPU:0, one launch (start us, length us, event | category | flops | bytes accessed | tf_op | source)
XLA Modules:
  0.0 845.1 jit_solution(13626083267093529521)
XLA Ops:
  6.2 23.2 %all-gather.1 = bf16[2,1,1152]{2,1,0:T(2,128)(2,1)S(1)} all-gather(bf16[1,1,1152]{2,1,0:T(2,128)(2,1)S(1)} %reshape.161), channel_id=2, replica_groups=mesh['shard'=2,'ctx'=8,'tp'=2] {'shard'}, dimensions={0}, use_global_device_ids=true | all-gather | bytes 6912 | tf_op jit(solution)/shard_map/all_gather | solution.py:420
  98.5 43.0 %collective-permute-done.5.refs_6_.refs_7_ = bf16[256,1024]{1,0:T(8,128)(2,1)S(1)} collective-permute-done((bf16[256,1024]{1,0:T(8,128)(2,1)}, bf16[256,1024]{1,0:T(8,128)(2,1)S(1)}, u32[]{:S(2)}, u32[]{:S(2)}) %collective-permute-start.5) | collective-permute-done | bytes 524320 | tf_op jit(solution)/shard_map/ppermute | solution.py:474
  141.5 12.2 %collective-permute-done.6.refs_8_.refs_9_ = bf16[256,1024]{1,0:T(8,128)(2,1)S(1)} collective-permute-done((bf16[256,1024]{1,0:T(8,128)(2,1)}, bf16[256,1024]{1,0:T(8,128)(2,1)S(1)}, u32[]{:S(2)}, u32[]{:S(2)}) %collective-permute-start.6) | collective-permute-done | bytes 524320 | tf_op jit(solution)/shard_map/ppermute | solution.py:474
  153.7 17.5 %shard_map.248 = (f32[512,1024]{1,0:T(8,128)}, bf16[512,1024]{1,0:T(8,128)(2,1)S(1)}, f32[512,1024]{1,0:T(8,128)}) custom-call(s32[18]{0:T(128)S(1)} %stack.59.meta_ref, bf16[512,1024]{1,0:T(8,128)(2,1)S(1)} %shard_map.246.q_ref, bf16[512,1024]{1,0:T(8,128)(2,1)} %copy-done, bf16[512,1024]{1,0:T(8,128)(2,1)} %copy-done, ...), custom_call_target="tpu_custom_call" | custom-call | flops 2415919104 | bytes 8388608 | tf_op jit(solution)/shard_map/pallas_call | solution.py:336
  181.8 31.8 %collective-permute-done.12 = bf16[512,1536]{1,0:T(8,128)(2,1)} collective-permute-done((bf16[512,1536]{1,0:T(8,128)(2,1)}, bf16[512,1536]{1,0:T(8,128)(2,1)}, u32[]{:S(2)}, u32[]{:S(2)}) %collective-permute-start.12) | collective-permute-done | bytes 1572896 | tf_op jit(solution)/shard_map/ppermute | solution.py:47
  217.7 29.6 %collective-permute-done.13 = bf16[1536,512]{1,0:T(8,128)(2,1)} collective-permute-done((bf16[1536,512]{1,0:T(8,128)(2,1)}, bf16[1536,512]{1,0:T(8,128)(2,1)}, u32[]{:S(2)}, u32[]{:S(2)}) %collective-permute-start.13) | collective-permute-done | bytes 1572896 | tf_op jit(solution)/shard_map/ppermute | solution.py:47
  252.7 27.9 %collective-permute-done.11 = bf16[512,1536]{1,0:T(8,128)(2,1)S(1)} collective-permute-done((bf16[512,1536]{1,0:T(8,128)(2,1)}, bf16[512,1536]{1,0:T(8,128)(2,1)S(1)}, u32[]{:S(2)}, u32[]{:S(2)}) %collective-permute-start.11) | collective-permute-done | bytes 1572896 | tf_op jit(solution)/shard_map/ppermute | solution.py:47
  318.4 29.1 %shard_map.249 = (f32[512,1024]{1,0:T(8,128)}, f32[2,512,512]{2,1,0:T(8,128)}, bf16[2,256,512]{2,1,0:T(8,128)(2,1)S(1)}, bf16[2,256,512]{2,1,0:T(8,128)(2,1)S(1)...) custom-call(s32[18]{0:T(128)S(1)} %stack.59.meta_ref, ...), custom_call_target="tpu_custom_call" | custom-call | flops 6039797760 | bytes 12582912 | tf_op jit(solution)/shard_map/pallas_call | solution.py:366
  347.5 10.4 %collective-permute-start.17 = (bf16[2,256,512]{2,1,0:T(8,128)(2,1)S(1)}, bf16[2,256,512]{2,1,0:T(8,128)(2,1)}, u32[]{:S(2)}, u32[]{:S(2)}) collective-permute-start(bf16[2,256,512]{2,1,0:T(8,128)(2,1)S(1)} %get-tuple-element.46), channel_id=1, source_target_pairs={{0,4},{2,6},{4,0},{6,2},{8,12},{10,14},{12,8},{14,10},{1,5},{3,7},... | collective-permute-start | bytes 1572872 | tf_op jit(solution)/shard_map/ppermute | solution.py:513
  366.5 16.9 %collective-permute-start.19 = (bf16[2,256,512]{2,1,0:T(8,128)(2,1)S(1)}, bf16[2,256,512]{2,1,0:T(8,128)(2,1)S(1)}, u32[]{:S(2)}, u32[]{:S(2)}) collective-permute-start(bf16[2,256,512]{2,1,0:T(8,128)(2,1)S(1)} %get-tuple-element.48), channel_id=1, source_target_pairs={{0,8},{2,10},{4,12},{6,14},{8,0},{10,2},{12,4},{14,6},{1,9},{3,11}... | collective-permute-start | bytes 1572872 | tf_op jit(solution)/shard_map/ppermute | solution.py:513
  395.4 45.9 %collective-permute-done.19 = bf16[2,256,512]{2,1,0:T(8,128)(2,1)S(1)} collective-permute-done((bf16[2,256,512]{2,1,0:T(8,128)(2,1)S(1)}, bf16[2,256,512]{2,1,0:T(8,128)(2,1)S(1)}, u32[]{:S(2)}, u32[]{:S(2)}) %collective-permute-start.19) | collective-permute-done | bytes 524320 | tf_op jit(solution)/shard_map/ppermute | solution.py:513
  441.3 11.2 %collective-permute-done.20 = bf16[2,256,512]{2,1,0:T(8,128)(2,1)S(1)} collective-permute-done((bf16[2,256,512]{2,1,0:T(8,128)(2,1)S(1)}, bf16[2,256,512]{2,1,0:T(8,128)(2,1)S(1)}, u32[]{:S(2)}, u32[]{:S(2)}) %collective-permute-start.20) | collective-permute-done | bytes 524320 | tf_op jit(solution)/shard_map/ppermute | solution.py:513
  469.0 9.7 %collective-permute-done.52 = bf16[512,1536]{1,0:T(8,128)(2,1)} collective-permute-done((bf16[512,1536]{1,0:T(8,128)(2,1)S(1)}, bf16[512,1536]{1,0:T(8,128)(2,1)}, u32[]{:S(2)}, u32[]{:S(2)}) %collective-permute-start.52) | collective-permute-done | bytes 1572896 | tf_op jit(solution)/shard_map/ppermute | solution.py:86
  480.9 31.5 %collective-permute-done.45 = bf16[512,1536]{1,0:T(8,128)(2,1)} collective-permute-done((bf16[512,1536]{1,0:T(8,128)(2,1)}, bf16[512,1536]{1,0:T(8,128)(2,1)}, u32[]{:S(2)}, u32[]{:S(2)}) %collective-permute-start.45) | collective-permute-done | bytes 1572896 | tf_op jit(solution)/shard_map/ppermute | solution.py:86
  516.8 34.4 %collective-permute-done.24 = bf16[512,1024]{1,0:T(8,128)(2,1)} collective-permute-done((bf16[512,1024]{1,0:T(8,128)(2,1)}, bf16[512,1024]{1,0:T(8,128)(2,1)}, u32[]{:S(2)}, u32[]{:S(2)}) %collective-permute-start.24) | collective-permute-done | bytes 1048608 | tf_op jit(solution)/shard_map/ppermute | solution.py:86
  561.7 10.0 %collective-permute-done.46 = bf16[256,1536]{1,0:T(8,128)(2,1)S(1)} collective-permute-done((bf16[256,1536]{1,0:T(8,128)(2,1)S(1)}, bf16[256,1536]{1,0:T(8,128)(2,1)S(1)}, u32[]{:S(2)}, u32[]{:S(2)}) %collective-permute-start.46) | collective-permute-done | bytes 786464 | tf_op jit(solution)/shard_map/ppermute | solution.py:99
  577.0 48.2 %psum.7 = f32[2304]{0:T(1024)S(1)} all-reduce(f32[2304]{0:T(1024)S(1)} %pad_maximum_fusion.5), channel_id=1, replica_groups=mesh['shard'=2,'ctx'=8,'tp'=2] {'shard','ctx','tp'}, use_global_device_ids=true, to_apply=%region_7.8 | all-reduce | flops 2304 | bytes 18432 | tf_op jit(solution)/shard_map/psum | solution.py:535
  645.3 10.8 %collective-permute-done.40 = bf16[256,512]{1,0:T(8,128)(2,1)S(1)} collective-permute-done((bf16[256,512]{1,0:T(8,128)(2,1)S(1)}, bf16[256,512]{1,0:T(8,128)(2,1)S(1)}, u32[]{:S(2)}, u32[]{:S(2)}) %collective-permute-start.40) | collective-permute-done | bytes 262176 | tf_op jit(solution)/shard_map/ppermute | solution.py:99
  663.1 14.8 %collective-permute-done.48 = bf16[64,1536]{1,0:T(8,128)(2,1)S(1)} collective-permute-done((bf16[64,1536]{1,0:T(8,128)(2,1)S(1)}, bf16[64,1536]{1,0:T(8,128)(2,1)S(1)}, u32[]{:S(2)}, u32[]{:S(2)}) %collective-permute-start.48) | collective-permute-done | bytes 196640 | tf_op jit(solution)/shard_map/ppermute | solution.py:99
  691.9 9.3 %collective-permute-start.33 = (bf16[128,1024]{1,0:T(8,128)(2,1)S(1)}, bf16[128,1024]{1,0:T(8,128)(2,1)S(1)}, u32[]{:S(2)}, u32[]{:S(2)}) collective-permute-start(bf16[128,1024]{1,0:T(8,128)(2,1)S(1)} %dynamic-slice_convert_fusion.10), channel_id=1, source_target_pairs={{0,4},{2,6},{4,0},{6,2},{8,12},{10,14},{12,8},{14,10},{1,5},{3,7},... | collective-permute-start | bytes 786440 | tf_op jit(solution)/shard_map/ppermute | solution.py:99
  718.0 30.6 %collective-permute-done.43 = bf16[256,512]{1,0:T(8,128)(2,1)S(1)} collective-permute-done((bf16[256,512]{1,0:T(8,128)(2,1)S(1)}, bf16[256,512]{1,0:T(8,128)(2,1)S(1)}, u32[]{:S(2)}, u32[]{:S(2)}) %collective-permute-start.43) | collective-permute-done | bytes 262176 | tf_op jit(solution)/shard_map/ppermute | solution.py:104
  785.8 15.1 %collective-permute-done.65 = bf16[768,512]{1,0:T(8,128)(2,1)S(1)} collective-permute-done((bf16[768,512]{1,0:T(8,128)(2,1)S(1)}, bf16[768,512]{1,0:T(8,128)(2,1)S(1)}, u32[]{:S(2)}, u32[]{:S(2)}) %collective-permute-start.65) | collective-permute-done | bytes 786464 | tf_op jit(solution)/shard_map/ppermute | solution.py:104
  803.0 14.7 %collective-permute-done.58 = bf16[256,1536]{1,0:T(8,128)(2,1)S(1)} collective-permute-done((bf16[256,1536]{1,0:T(8,128)(2,1)S(1)}, bf16[256,1536]{1,0:T(8,128)(2,1)S(1)}, u32[]{:S(2)}, u32[]{:S(2)}) %collective-permute-start.58) | collective-permute-done | bytes 786464 | tf_op jit(solution)/shard_map/ppermute | solution.py:104
  820.1 14.6 %collective-permute-done.51 = bf16[256,1536]{1,0:T(8,128)(2,1)S(1)} collective-permute-done((bf16[256,1536]{1,0:T(8,128)(2,1)S(1)}, bf16[256,1536]{1,0:T(8,128)(2,1)S(1)}, u32[]{:S(2)}, u32[]{:S(2)}) %collective-permute-start.51) | collective-permute-done | bytes 786464 | tf_op jit(solution)/shard_map/ppermute | solution.py:104
  (362 shorter events, 273.6 us)
Async XLA Ops:
  63.3 108.0 %collective-permute-start.9 = (bf16[1024,512]{1,0:T(8,128)(2,1)}, bf16[1024,512]{1,0:T(8,128)(2,1)}, u32[]{:S(2)}, u32[]{:S(2)}) collective-permute-start(bf16[1024,512]{1,0:T(8,128)(2,1)} %param.22), channel_id=1, source_target_pairs={{16,0},{0,16},{17,1},{1,17},{18,2},{2,18},{19,3},{3,19},{20,4},{4,... | collective-permute-start | bytes 3145736 | tf_op jit(solution)/shard_map/ppermute | solution.py:47
  85.3 68.4 %collective-permute-start.6 = (bf16[256,1024]{1,0:T(8,128)(2,1)}, bf16[256,1024]{1,0:T(8,128)(2,1)S(1)}, u32[]{:S(2)}, u32[]{:S(2)}) collective-permute-start(bf16[256,1024]{1,0:T(8,128)(2,1)} %get-tuple-element.72), channel_id=1, source_target_pairs={{0,10},{2,8},{4,14},{6,12},{8,2},{10,0},{12,6},{14,4},{1,11},{3,9}... | collective-permute-start | bytes 1572872 | tf_op jit(solution)/shard_map/ppermute | solution.py:474
  86.6 67.1 %collective-permute-start.7 = (bf16[256,1024]{1,0:T(8,128)(2,1)}, bf16[256,1024]{1,0:T(8,128)(2,1)S(1)}, u32[]{:S(2)}, u32[]{:S(2)}) collective-permute-start(bf16[256,1024]{1,0:T(8,128)(2,1)} %get-tuple-element.71), channel_id=1, source_target_pairs={{0,12},{2,14},{4,8},{6,10},{8,4},{10,6},{12,0},{14,2},{1,13},{3,15... | collective-permute-start | bytes 1572872 | tf_op jit(solution)/shard_map/ppermute | solution.py:474
  90.2 63.5 %collective-permute-start.8 = (bf16[256,1024]{1,0:T(8,128)(2,1)}, bf16[256,1024]{1,0:T(8,128)(2,1)S(1)}, u32[]{:S(2)}, u32[]{:S(2)}) collective-permute-start(bf16[256,1024]{1,0:T(8,128)(2,1)} %get-tuple-element.70), channel_id=1, source_target_pairs={{0,14},{2,12},{4,10},{6,8},{8,6},{10,4},{12,2},{14,0},{1,15},{3,13... | collective-permute-start | bytes 1572872 | tf_op jit(solution)/shard_map/ppermute | solution.py:474
  176.1 71.2 %collective-permute-start.13 = (bf16[1536,512]{1,0:T(8,128)(2,1)}, bf16[1536,512]{1,0:T(8,128)(2,1)}, u32[]{:S(2)}, u32[]{:S(2)}) collective-permute-start(bf16[1536,512]{1,0:T(8,128)(2,1)} %param.25), channel_id=1, source_target_pairs={{16,0},{0,16},{17,1},{1,17},{18,2},{2,18},{19,3},{3,19},{20,4},{4,... | collective-permute-start | bytes 4718600 | tf_op jit(solution)/shard_map/ppermute | solution.py:47
  178.1 102.4 %collective-permute-start.11 = (bf16[512,1536]{1,0:T(8,128)(2,1)}, bf16[512,1536]{1,0:T(8,128)(2,1)S(1)}, u32[]{:S(2)}, u32[]{:S(2)}) collective-permute-start(bf16[512,1536]{1,0:T(8,128)(2,1)} %param.23), channel_id=1, source_target_pairs={{16,0},{0,16},{17,1},{1,17},{18,2},{2,18},{19,3},{3,19},{20,4},{4,... | collective-permute-start | bytes 4718600 | tf_op jit(solution)/shard_map/ppermute | solution.py:47
  366.5 74.7 %collective-permute-start.19 = (bf16[2,256,512]{2,1,0:T(8,128)(2,1)S(1)}, bf16[2,256,512]{2,1,0:T(8,128)(2,1)S(1)}, u32[]{:S(2)}, u32[]{:S(2)}) collective-permute-start(bf16[2,256,512]{2,1,0:T(8,128)(2,1)S(1)} %get-tuple-element.48), channel_id=1, source_target_pairs={{0,8},{2,10},{4,12},{6,14},{8,0},{10,2},{12,4},{14,6},{1,9},{3,11}... | collective-permute-start | bytes 1572872 | tf_op jit(solution)/shard_map/ppermute | solution.py:513
  383.5 69.0 %collective-permute-start.20 = (bf16[2,256,512]{2,1,0:T(8,128)(2,1)S(1)}, bf16[2,256,512]{2,1,0:T(8,128)(2,1)S(1)}, u32[]{:S(2)}, u32[]{:S(2)}) collective-permute-start(bf16[2,256,512]{2,1,0:T(8,128)(2,1)S(1)} %get-tuple-element.49), channel_id=1, source_target_pairs={{0,10},{2,8},{4,14},{6,12},{8,2},{10,0},{12,6},{14,4},{1,11},{3,9}... | collective-permute-start | bytes 1572872 | tf_op jit(solution)/shard_map/ppermute | solution.py:513
  384.8 67.7 %collective-permute-start.21 = (bf16[2,256,512]{2,1,0:T(8,128)(2,1)S(1)}, bf16[2,256,512]{2,1,0:T(8,128)(2,1)S(1)}, u32[]{:S(2)}, u32[]{:S(2)}) collective-permute-start(bf16[2,256,512]{2,1,0:T(8,128)(2,1)S(1)} %get-tuple-element.50), channel_id=1, source_target_pairs={{0,12},{2,14},{4,8},{6,10},{8,4},{10,6},{12,0},{14,2},{1,13},{3,15... | collective-permute-start | bytes 1572872 | tf_op jit(solution)/shard_map/ppermute | solution.py:513
  387.3 67.2 %collective-permute-start.22 = (bf16[2,256,512]{2,1,0:T(8,128)(2,1)S(1)}, bf16[2,256,512]{2,1,0:T(8,128)(2,1)S(1)}, u32[]{:S(2)}, u32[]{:S(2)}) collective-permute-start(bf16[2,256,512]{2,1,0:T(8,128)(2,1)S(1)} %get-tuple-element.51), channel_id=1, source_target_pairs={{0,14},{2,12},{4,10},{6,8},{8,6},{10,4},{12,2},{14,0},{1,15},{3,13... | collective-permute-start | bytes 1572872 | tf_op jit(solution)/shard_map/ppermute | solution.py:513
  393.1 73.6 %collective-permute-start.59 = (bf16[1536,512]{1,0:T(8,128)(2,1)}, bf16[1536,512]{1,0:T(8,128)(2,1)}, u32[]{:S(2)}, u32[]{:S(2)}) collective-permute-start(bf16[1536,512]{1,0:T(8,128)(2,1)} %constant_dynamic-slice_fusion), channel_id=1, source_target_pairs={{0,16},{16,0},{1,17},{17,1},{2,18},{18,2},{3,19},{19,3},{4,20},{20... | collective-permute-start | bytes 4718600 | tf_op jit(solution)/shard_map/ppermute | solution.py:86
  452.5 59.9 %collective-permute-start.45 = (bf16[512,1536]{1,0:T(8,128)(2,1)}, bf16[512,1536]{1,0:T(8,128)(2,1)}, u32[]{:S(2)}, u32[]{:S(2)}) collective-permute-start(bf16[512,1536]{1,0:T(8,128)(2,1)} %constant_dynamic-slice_fusion.2), channel_id=1, source_target_pairs={{0,16},{16,0},{1,17},{17,1},{2,18},{18,2},{3,19},{19,3},{4,20},{20... | collective-permute-start | bytes 4718600 | tf_op jit(solution)/shard_map/ppermute | solution.py:86
  452.5 101.3 %collective-permute-start.38 = (bf16[1024,512]{1,0:T(8,128)(2,1)}, bf16[1024,512]{1,0:T(8,128)(2,1)}, u32[]{:S(2)}, u32[]{:S(2)}) collective-permute-start(bf16[1024,512]{1,0:T(8,128)(2,1)} %constant_dynamic-slice_fusion.3), channel_id=1, source_target_pairs={{0,16},{16,0},{1,17},{17,1},{2,18},{18,2},{3,19},{19,3},{4,20},{20... | collective-permute-start | bytes 3145736 | tf_op jit(solution)/shard_map/ppermute | solution.py:86
  454.5 96.7 %collective-permute-start.24 = (bf16[512,1024]{1,0:T(8,128)(2,1)}, bf16[512,1024]{1,0:T(8,128)(2,1)}, u32[]{:S(2)}, u32[]{:S(2)}) collective-permute-start(bf16[512,1024]{1,0:T(8,128)(2,1)} %constant_dynamic-slice_fusion.5), channel_id=1, source_target_pairs={{0,16},{16,0},{1,17},{17,1},{2,18},{18,2},{3,19},{19,3},{4,20},{20... | collective-permute-start | bytes 3145736 | tf_op jit(solution)/shard_map/ppermute | solution.py:86
  466.7 108.5 %collective-permute-start.23 = (bf16[512,1024]{1,0:T(8,128)(2,1)S(1)}, bf16[512,1024]{1,0:T(8,128)(2,1)S(1)}, u32[]{:S(2)}, u32[]{:S(2)}) collective-permute-start(bf16[512,1024]{1,0:T(8,128)(2,1)S(1)} %add_convert_fusion), channel_id=1, source_target_pairs={{0,1},{1,0},{2,3},{3,2},{4,5},{5,4},{6,7},{7,6},{8,9},{9,8},{10,11... | collective-permute-start | bytes 3145736 | tf_op jit(solution)/shard_map/ppermute | solution.py:74
  478.7 79.4 %collective-permute-start.60 = (bf16[768,512]{1,0:T(8,128)(2,1)S(1)}, bf16[768,512]{1,0:T(8,128)(2,1)S(1)}, u32[]{:S(2)}, u32[]{:S(2)}) collective-permute-start(bf16[768,512]{1,0:T(8,128)(2,1)S(1)} %dynamic-slice_convert_fusion), channel_id=1, source_target_pairs={{0,2},{2,0},{4,6},{6,4},{8,10},{10,8},{12,14},{14,12},{1,3},{3,1},... | collective-permute-start | bytes 2359304 | tf_op jit(solution)/shard_map/ppermute | solution.py:99
  553.8 76.1 %collective-permute-start.31 = (bf16[512,1024]{1,0:T(8,128)(2,1)}, bf16[512,1024]{1,0:T(8,128)(2,1)}, u32[]{:S(2)}, u32[]{:S(2)}) collective-permute-start(bf16[512,1024]{1,0:T(8,128)(2,1)} %constant_dynamic-slice_fusion.4), channel_id=1, source_target_pairs={{0,16},{16,0},{1,17},{17,1},{2,18},{18,2},{3,19},{19,3},{4,20},{20... | collective-permute-start | bytes 3145736 | tf_op jit(solution)/shard_map/ppermute | solution.py:86
  558.1 74.3 %collective-permute-start.39 = (bf16[512,512]{1,0:T(8,128)(2,1)}, bf16[512,512]{1,0:T(8,128)(2,1)}, u32[]{:S(2)}, u32[]{:S(2)}) collective-permute-start(bf16[512,512]{1,0:T(8,128)(2,1)} %dynamic-slice_convert_fusion.3), channel_id=1, source_target_pairs={{0,2},{2,0},{4,6},{6,4},{8,10},{10,8},{12,14},{14,12},{1,3},{3,1},... | collective-permute-start | bytes 1572872 | tf_op jit(solution)/shard_map/ppermute | solution.py:99
  559.6 76.4 %collective-permute-start.25 = (bf16[256,1024]{1,0:T(8,128)(2,1)S(1)}, bf16[256,1024]{1,0:T(8,128)(2,1)}, u32[]{:S(2)}, u32[]{:S(2)}) collective-permute-start(bf16[256,1024]{1,0:T(8,128)(2,1)S(1)} %dynamic-slice_convert_fusion.5), channel_id=1, source_target_pairs={{0,2},{2,0},{4,6},{6,4},{8,10},{10,8},{12,14},{14,12},{1,3},{3,1},... | collective-permute-start | bytes 1572872 | tf_op jit(solution)/shard_map/ppermute | solution.py:99
  571.7 67.5 %collective-permute-start.61 = (bf16[384,512]{1,0:T(8,128)(2,1)}, bf16[384,512]{1,0:T(8,128)(2,1)}, u32[]{:S(2)}, u32[]{:S(2)}) collective-permute-start(bf16[384,512]{1,0:T(8,128)(2,1)} %dynamic-slice_convert_fusion.6), channel_id=1, source_target_pairs={{0,4},{2,6},{4,0},{6,2},{8,12},{10,14},{12,8},{14,10},{1,5},{3,7},... | collective-permute-start | bytes 1179656 | tf_op jit(solution)/shard_map/ppermute | solution.py:99
  575.1 65.8 %collective-permute-start.54 = (bf16[128,1536]{1,0:T(8,128)(2,1)S(1)}, bf16[128,1536]{1,0:T(8,128)(2,1)}, u32[]{:S(2)}, u32[]{:S(2)}) collective-permute-start(bf16[128,1536]{1,0:T(8,128)(2,1)S(1)} %dynamic-slice_convert_fusion.7), channel_id=1, source_target_pairs={{0,4},{2,6},{4,0},{6,2},{8,12},{10,14},{12,8},{14,10},{1,5},{3,7},... | collective-permute-start | bytes 1179656 | tf_op jit(solution)/shard_map/ppermute | solution.py:99
  701.3 61.9 %collective-permute-start.64 = (bf16[384,512]{1,0:T(8,128)(2,1)S(1)}, bf16[384,512]{1,0:T(8,128)(2,1)S(1)}, u32[]{:S(2)}, u32[]{:S(2)}) collective-permute-start(bf16[384,512]{1,0:T(8,128)(2,1)S(1)} %maximum_select_fusion.30), channel_id=1, source_target_pairs={{0,4},{2,6},{4,0},{6,2},{8,12},{10,14},{12,8},{14,10},{1,5},{3,7},... | collective-permute-start | bytes 1179656 | tf_op jit(solution)/shard_map/ppermute | solution.py:104
  710.3 60.5 %collective-permute-start.57 = (bf16[128,1536]{1,0:T(8,128)(2,1)S(1)}, bf16[128,1536]{1,0:T(8,128)(2,1)S(1)}, u32[]{:S(2)}, u32[]{:S(2)}) collective-permute-start(bf16[128,1536]{1,0:T(8,128)(2,1)S(1)} %maximum_select_fusion.29), channel_id=1, source_target_pairs={{0,4},{2,6},{4,0},{6,2},{8,12},{10,14},{12,8},{14,10},{1,5},{3,7},... | collective-permute-start | bytes 1179656 | tf_op jit(solution)/shard_map/ppermute | solution.py:104
  779.3 63.4 %collective-permute-start.37 = (bf16[256,1024]{1,0:T(8,128)(2,1)S(1)}, bf16[256,1024]{1,0:T(8,128)(2,1)S(1)}, u32[]{:S(2)}, u32[]{:S(2)}) collective-permute-start(bf16[256,1024]{1,0:T(8,128)(2,1)S(1)} %maximum_select_fusion.26), channel_id=1, source_target_pairs={{0,2},{2,0},{4,6},{6,4},{8,10},{10,8},{12,14},{14,12},{1,3},{3,1},... | collective-permute-start | bytes 1572872 | tf_op jit(solution)/shard_map/ppermute | solution.py:104
  (99 other events, 2186.7 us)

commit v2 on v1

--- a/solution.py
+++ b/solution.py
@@ -349,7 +349,7 @@
         ],
         compiler_params=pltpu.CompilerParams(vmem_limit_bytes=VMEM_LIMIT),
         cost_estimate=pl.CostEstimate(
-            flops=(count + 1) * half * half * width * 4,
+            flops=(count + 1) * half * half * width * 16,
             bytes_accessed=rows * width * 16,
             transcendentals=(count + 1) * half * half * width // HEAD,
         ),
@@ -380,12 +380,12 @@
         + [jax.ShapeDtypeStruct((2, half, kv_width), BF16)] * (count - 1),
         compiler_params=pltpu.CompilerParams(vmem_limit_bytes=VMEM_LIMIT),
         cost_estimate=pl.CostEstimate(
-            flops=(count + 1) * half * half * width * 10,
+            flops=(count + 1) * half * half * width * 40,
             bytes_accessed=rows * width * 24,
             transcendentals=(count + 1) * half * half * width // HEAD,
         ),
     )(meta, queries, grads, outs, lse, key_value, key_value, *twice(others))
-    return result[0], result[1], result[2:]
+    return result[0], result[1], list(result[2:])
 
 
 def body(
@@ -414,20 +414,37 @@
     depth = model // shard_count
     docs = seq_lengths.shape[1]
     kv_width = key_weight.shape[1]
-
-    kv_pieces = pieces_of(jnp.concatenate([key_weight, value_weight], axis=1), "shard")
+    units = w_gate.shape[1]
+
     packed = jnp.concatenate([gain_in, gain_post, gain_q, gain_k])
-    gains = lax.all_gather(packed, "shard", axis=0).astype(F32)
-    cuts = [0, depth, 2 * depth, 2 * depth + gain_q.shape[0], packed.shape[0]]
+    lines = -(-packed.shape[0] // (2 * kv_width * 16)) * 16
+    packed = jnp.pad(packed, (0, lines * 2 * kv_width - packed.shape[0]))
+    kv_own = jnp.concatenate(
+        [
+            jnp.concatenate([key_weight, value_weight], axis=1),
+            packed.reshape(lines, 2 * kv_width),
+        ],
+        axis=0,
+    )
+    first_pieces = pieces_of(kv_own, "shard")
+    kv_pieces = [piece[:depth] for piece in first_pieces]
+    cuts = [0, depth, 2 * depth, 2 * depth + gain_q.shape[0]]
+    cuts = cuts + [cuts[-1] + gain_k.shape[0]]
+    gain_pieces = [
+        [piece[depth:].reshape(-1)[lo:hi].astype(F32) for piece in first_pieces]
+        for lo, hi in zip(cuts[:-1], cuts[1:])
+    ]
     scale_in, scale_post, scale_q, scale_k = (
-        gains[:, lo:hi].reshape(1, -1) for lo, hi in zip(cuts[:-1], cuts[1:])
-    )
-
-    q_pieces = pieces_of(after(w_query, kv_pieces[-1]), "shard")
+        join(pieces, 0, shard).reshape(1, -1) for pieces in gain_pieces
+    )
+
+    q_pieces = pieces_of(after(w_query, first_pieces[-1]), "shard")
+    gate_up = jnp.concatenate([w_gate, w_up], axis=1)
+    full_gate_up = lax.all_gather(
+        after(gate_up, first_pieces[-1]), "shard", axis=0, tiled=True
+    )
     out_pieces = pieces_of(after(w_out, q_pieces[-1]), "shard")
-    gate_pieces = pieces_of(after(w_gate, q_pieces[-1]), "shard")
-    up_pieces = pieces_of(after(w_up, out_pieces[-1]), "shard")
-    down_pieces = pieces_of(after(w_down, out_pieces[-1]), "shard")
+    down_pieces = pieces_of(after(w_down, q_pieces[-1]), "shard")
 
     lengths = seq_lengths[0]
     starts = jnp.cumsum(lengths) - lengths
@@ -461,7 +478,8 @@
         total = None
         for j, piece in enumerate(pieces):
             at = (shard + j) % shard_count * depth
-            term = dot(lax.dynamic_slice_in_dim(normed_input, at, depth, 1), piece)
+            part_in = lax.dynamic_slice_in_dim(normal_one, at, depth, 1)
+            term = dot((part_in * gain_pieces[0][j][None, :]).astype(BF16), piece)
             total = term if total is None else total + term
         return total
 
@@ -474,11 +492,10 @@
         held.append(lax.ppermute(sent, "ctx", [(i, i ^ d) for i in range(count)]))
     q_pre = project(q_pieces)
     queries = rope(q_pre, q_pre.shape[1] // HEAD, cosine, sine, scale_q)
+    queries = after(queries, full_gate_up)
     attended, attn_out, lse = attend(meta, docs, queries, key_value, held)
 
     full_out = join(out_pieces, 1, shard)
-    full_gate = join(gate_pieces, 0, shard)
-    full_up = join(up_pieces, 0, shard)
     full_down = join(down_pieces, 1, shard)
     full_kv = join(kv_pieces, 0, shard)
     full_query = join(q_pieces, 0, shard)
@@ -486,8 +503,9 @@
     residual = inputs + pair_total(dot(attn_out, full_out))
     normal_two, factor_two = rms_parts(residual)
     normed_two = (normal_two * scale_post).astype(BF16)
-    gate_act = dot(normed_two, full_gate)
-    upward = dot(normed_two, full_up)
+    gate_upward = dot(normed_two, full_gate_up)
+    gate_act = gate_upward[:, :units]
+    upward = gate_upward[:, units:]
     sigma = jax.nn.sigmoid(gate_act)
     silu_act = gate_act * sigma
     hidden = (silu_act * upward).astype(BF16)
@@ -496,19 +514,24 @@
     d_hidden = dot_nt(cotangent, full_down)
     d_gate = (d_hidden * upward * sigma * (1.0 + gate_act * (1.0 - sigma))).astype(BF16)
     d_up = (d_hidden * silu_act).astype(BF16)
-    grad_gate = dot_tn(normed_two, d_gate).astype(BF16)
-    grad_up = dot_tn(normed_two, d_up).astype(BF16)
-    d_normed_two = pair_total(dot_nt(d_gate, full_gate) + dot_nt(d_up, full_up))
+    d_gate_up = jnp.concatenate([d_gate, d_up], axis=1)
+    grad_gate_up = dot_tn(normed_two, d_gate_up).astype(BF16)
+    d_normed_two = pair_total(dot_nt(d_gate_up, full_gate_up))
+    shared_down = to_shard_owner(grad_down, 1).astype(BF16)
+    shared_gate_up = to_shard_owner(grad_gate_up, 0).astype(BF16)
+    owned_down = lax.psum(shared_down, "ctx")
+    owned_gate_up = lax.psum(after(shared_gate_up, owned_down), "ctx")
     grad_post = jnp.sum(d_normed_two * normal_two, axis=0)
     d_residual = cotangent.astype(F32) + rms_back(
         d_normed_two * scale_post, normal_two, factor_two
     )
 
     d_branch = d_residual.astype(BF16)
-    d_attn = dot_nt(d_branch, full_out).astype(BF16)
+    d_attn = after(dot_nt(d_branch, full_out).astype(BF16), shared_down)
     d_queries, d_kv, given = attend_back(
         meta, docs, queries, d_attn, attended, lse, key_value, held
     )
+    given = given[:-2] + [after(g, shared_gate_up) for g in given[-2:]]
     returned = [
         lax.ppermute(g, "ctx", [(i, i ^ d) for i in range(count)])
         for d, g in zip(range(1, count), given)
@@ -516,6 +539,11 @@
     grad_out = dot_tn(attn_out, d_branch).astype(BF16)
     d_q_pre, gq_part = rope_back(d_queries, q_pre, cosine, sine, scale_q)
     grad_query = dot_tn(normed_input, d_q_pre).astype(BF16)
+    shared_out = to_shard_owner(grad_out, 1).astype(BF16)
+    shared_query = to_shard_owner(grad_query, 0).astype(BF16)
+    owned_out, owned_query = lax.psum(
+        (after(shared_out, owned_gate_up), after(shared_query, owned_gate_up)), "ctx"
+    )
 
     first = sum(
         jnp.where(part < p, g.astype(F32), 0.0) for p, g in zip(other_parts, returned)
@@ -531,9 +559,12 @@
     grad_in = jnp.sum(d_normed * normal_one, axis=0)
     input_grad = d_residual + rms_back(d_normed * scale_in, normal_one, factor_one)
 
+    owned_kv = ctx_total(to_shard_owner(grad_kv, 0))
+
     once = jnp.where(lax.axis_index("tp") == 0, 1.0, 0.0)
+    gain_grads = jnp.concatenate([grad_in * once, grad_post * once, gq_part[0], gk_part[0]])
     gain_grads = lax.psum(
-        jnp.concatenate([grad_in * once, grad_post * once, gq_part[0], gk_part[0]]),
+        after(gain_grads, owned_query),
         ("shard", "ctx", "tp"),
     )
     own_gains = []
@@ -541,22 +572,16 @@
         size = size // shard_count
         own_gains.append(lax.dynamic_slice_in_dim(gain_grads, lo + shard * size, size, 0))
 
-    owned_down = ctx_total(to_shard_owner(grad_down, 1))
-    owned_gate = ctx_total(to_shard_owner(grad_gate, 0))
-    owned_up = ctx_total(to_shard_owner(grad_up, 0))
-    owned_out = ctx_total(to_shard_owner(grad_out, 1))
-    owned_query = ctx_total(to_shard_owner(grad_query, 0))
-    owned_kv = ctx_total(to_shard_owner(grad_kv, 0))
     return (
         mixed,
         input_grad,
-        owned_query,
+        owned_query.astype(F32),
         owned_kv[:, :kv_width],
         owned_kv[:, kv_width:],
-        owned_out,
-        owned_gate,
-        owned_up,
-        owned_down,
+        owned_out.astype(F32),
+        owned_gate_up[:, :units].astype(F32),
+        owned_gate_up[:, units:].astype(F32),
+        owned_down.astype(F32),
         *own_gains,
     )
 

time: 858 us -> 791 us (0.922)
  starting transfers between devices: 109 us -> 62 us
  blocking collectives: 71.3 us -> 40.2 us
  between operations: 29.2 us -> 43.4 us
  matrix products: 65.3 us -> 54.9 us
  waiting for transfers between devices: 439 us -> 449 us
    psum x0 -> x3, waiting for transfers between devices: none -> 208 us  [the longest x1 81.4 us: body(): owned_gate_up = lax.psum(after(shared_gate_up, owned_down), 'ctx')]
    ppermute x18 -> x3, waiting for transfers between devices: 106 us -> 18.9 us  [ctx_total(): other = lax.ppermute(value, 'ctx', [(i, i ^ level) for i in range(count)])]
    ppermute x7, waiting for transfers between devices: 55.2 us -> 21.9 us  [body(): held.append(lax.ppermute(sent, 'ctx', [(i, i ^ d) for i in range(count)]))]
    ppermute x6 -> x4, waiting for transfers between devices: 93.2 us -> 63.9 us  [pieces_of(): lax.ppermute(own, axis, [((i + j) % count, i) for i in range(count)])]
    ppermute x7, starting transfers between devices: 11.2 us -> 36.9 us  [body(): held.append(lax.ppermute(sent, 'ctx', [(i, i ^ d) for i in range(count)]))]
    ppermute x18 -> x3, starting transfers between devices: 29 us -> 3.65 us  [ctx_total(): other = lax.ppermute(sent, 'ctx', [(i, i ^ level) for i in range(count)])]
    ppermute x7, starting transfers between devices: 32.2 us -> 8.41 us  [body(): lax.ppermute(g, 'ctx', [(i, i ^ d) for i in range(count)])]
    all_gather x1 -> x0, blocking collectives: 23.2 us -> none  [body(): gains = lax.all_gather(packed, 'shard', axis=0).astype(F32)]
  transfers between devices with their start and end apart: 66 -> 37, of which waited for: 32 -> 18; matrix products, arithmetic and copies ran while one was open for 13% -> 12% of each run, Pallas kernels for 3% -> 7%
where the time goes in v2:
time: 791 us; the launch traced here: 786 us
  waiting for transfers between devices  449 us (57%)
  starting transfers between devices  62 us (8%)
  Pallas kernels  57.5 us (7%)
  matrix products  54.9 us (7%)
  other arithmetic  47.5 us (6%)
  between operations  43.4 us (5%)
  blocking collectives  40.2 us (5%)
  local copies, waits for them, and re-layouts  32.1 us (4%)
    psum x1, waiting for transfers between devices, body(): owned_gate_up = lax.psum(after(shared_gate_up, owned_down), 'ctx')  81.4 us
    psum x1, waiting for transfers between devices, body(): lax.psum((after(shared_out, owned_gate_up), after(shared_query, owned_gat...  78.6 us
    ppermute x4, waiting for transfers between devices, pieces_of(): lax.ppermute(own, axis, [((i + j) % count, i) for i in range(count)])  63.9 us
    ppermute x5, waiting for transfers between devices, to_shard_owner(): other = lax.ppermute(sent, 'shard', [(0, 1), (1, 0)])  56.6 us
    psum x1, waiting for transfers between devices, body(): owned_down = lax.psum(shared_down, 'ctx')  47.6 us
    ppermute x7, waiting for transfers between devices, body(): lax.ppermute(g, 'ctx', [(i, i ^ d) for i in range(count)])  40.8 us
    psum x1, blocking collectives, body(): lax.psum(after(gain_grads, owned_query), ('shard', 'ctx', 'tp'))  40.2 us
    ppermute x3, waiting for transfers between devices, ctx_total(): other = lax.ppermute(sent, 'ctx', [(i, i ^ level) for i in range(count)])  38.3 us
  transfers between devices with their start and end apart: 37, of which 18 were waited for; matrix products, arithmetic and copies ran while one was open for 12% of the time, Pallas kernels for 7%

profile of v2, /device:TPU:0, one launch (start us, length us, event | category | flops | bytes accessed | tf_op | source)
XLA Modules:
  0.0 786.1 jit_solution(2114792104725483742)
XLA Ops:
  18.6 22.1 %collective-permute-done = bf16[528,1024]{1,0:T(8,128)(2,1)} collective-permute-done((bf16[528,1024]{1,0:T(8,128)(2,1)}, bf16[528,1024]{1,0:T(8,128)(2,1)}, u32[]{:S(2)}, u32[]{:S(2)}) %collective-permute-start) | collective-permute-done | bytes 1081376 | tf_op jit(solution)/shard_map/ppermute | solution.py:47
  92.8 13.5 %collective-permute-done.1 = bf16[512,1024]{1,0:T(8,128)(2,1)S(1)} collective-permute-done((bf16[512,1024]{1,0:T(8,128)(2,1)}, bf16[512,1024]{1,0:T(8,128)(2,1)S(1)}, u32[]{:S(2)}, u32[]{:S(2)}) %collective-permute-start.1) | collective-permute-done | bytes 1048608 | tf_op jit(solution)/shard_map/ppermute | solution.py:47
  108.9 25.1 %collective-permute-start.3 = (bf16[256,1024]{1,0:T(8,128)(2,1)}, bf16[256,1024]{1,0:T(8,128)(2,1)}, u32[]{:S(2)}, u32[]{:S(2)}) collective-permute-start(bf16[256,1024]{1,0:T(8,128)(2,1)} %get-tuple-element.93), channel_id=1, source_target_pairs={{0,4},{2,6},{4,0},{6,2},{8,12},{10,14},{12,8},{14,10},{1,5},{3,7},... | collective-permute-start | bytes 1572872 | tf_op jit(solution)/shard_map/ppermute | solution.py:492
  137.5 17.6 %collective-permute-done.6.refs_8_.refs_9_ = bf16[256,1024]{1,0:T(8,128)(2,1)S(1)} collective-permute-done((bf16[256,1024]{1,0:T(8,128)(2,1)}, bf16[256,1024]{1,0:T(8,128)(2,1)S(1)}, u32[]{:S(2)}, u32[]{:S(2)}) %collective-permute-start.6) | collective-permute-done | bytes 524320 | tf_op jit(solution)/shard_map/ppermute | solution.py:492
  169.9 17.4 %shard_map.248 = (f32[512,1024]{1,0:T(8,128)}, bf16[512,1024]{1,0:T(8,128)(2,1)S(1)}, f32[512,1024]{1,0:T(8,128)}) custom-call(s32[18]{0:T(128)S(1)} %stack.59.meta_ref, bf16[512,1024]{1,0:T(8,128)(2,1)S(1)} %copy-done.5, bf16[512,1024]{1,0:T(8,128)(2,1)} %copy-done, bf16[512,1024]{1,0:T(8,128)(2,1)} %copy-done, ...), custom_call_target="tpu_custom_call" | custom-call | flops 9663676416 | bytes 8388608 | tf_op jit(solution)/shard_map/pallas_call | solution.py:336
  187.3 4.8 convolution_convert_fusion.7
  200.9 28.3 %collective-permute-done.11 = bf16[1536,512]{1,0:T(8,128)(2,1)S(1)} collective-permute-done((bf16[1536,512]{1,0:T(8,128)(2,1)}, bf16[1536,512]{1,0:T(8,128)(2,1)S(1)}, u32[]{:S(2)}, u32[]{:S(2)}) %collective-permute-start.11) | collective-permute-done | bytes 1572896 | tf_op jit(solution)/shard_map/ppermute | solution.py:47
  233.4 5.7 convolution_convert_fusion
  239.2 6.0 fusion.19
  257.9 5.2 convolution_convert_fusion.5.g_ref
  263.1 25.3 %collective-permute-done.14 = bf16[1536,512]{1,0:T(8,128)(2,1)S(1)} collective-permute-done((bf16[1536,512]{1,0:T(8,128)(2,1)S(1)}, bf16[1536,512]{1,0:T(8,128)(2,1)S(1)}, u32[]{:S(2)}, u32[]{:S(2)}) %collective-permute-start.14) | collective-permute-done | bytes 1572896 | tf_op jit(solution)/shard_map/ppermute | solution.py:86
  290.2 29.2 %shard_map.249 = (f32[512,1024]{1,0:T(8,128)}, f32[2,512,512]{2,1,0:T(8,128)}, bf16[2,256,512]{2,1,0:T(8,128)(2,1)}, bf16[2,256,512]{2,1,0:T(8,128)(2,1)}, bf16[...) custom-call(s32[18]{0:T(128)S(1)} %stack.59.meta_ref, ...), custom_call_target="tpu_custom_call" | custom-call | flops 24159191040 | bytes 12582912 | tf_op jit(solution)/shard_map/pallas_call | solution.py:366
  323.7 31.3 %collective-permute-done.20 = bf16[512,3072]{1,0:T(8,128)(2,1)} collective-permute-done((bf16[512,3072]{1,0:T(8,128)(2,1)}, bf16[512,3072]{1,0:T(8,128)(2,1)}, u32[]{:S(2)}, u32[]{:S(2)}) %collective-permute-start.20) | collective-permute-done | bytes 3145760 | tf_op jit(solution)/shard_map/ppermute | solution.py:86
  355.0 4.7 add_convert_fusion
  359.8 4.9 collective-permute-start.22
  376.6 40.8 %collective-permute-done.19 = bf16[2,256,512]{2,1,0:T(8,128)(2,1)} collective-permute-done((bf16[2,256,512]{2,1,0:T(8,128)(2,1)}, bf16[2,256,512]{2,1,0:T(8,128)(2,1)}, u32[]{:S(2)}, u32[]{:S(2)}) %collective-permute-start.19) | collective-permute-done | bytes 524320 | tf_op jit(solution)/shard_map/ppermute | solution.py:536
  432.6 47.6 %all-reduce.6.cloned.1.call-done = bf16[1536,512]{1,0:T(8,128)(2,1)} async-done(((bf16[1536,512]{1,0:T(8,128)(2,1)}), bf16[1536,512]{1,0:T(8,128)(2,1)}) %all-reduce.6.cloned.1.call-update) | async-done | bytes 1572880 | tf_op jit(solution)/shard_map/psum | solution.py:522
  499.1 14.5 %collective-permute-done.26 = bf16[256,1024]{1,0:T(8,128)(2,1)S(1)} collective-permute-done((bf16[256,1024]{1,0:T(8,128)(2,1)S(1)}, bf16[256,1024]{1,0:T(8,128)(2,1)S(1)}, u32[]{:S(2)}, u32[]{:S(2)}) %collective-permute-start.26) | collective-permute-done | bytes 524320 | tf_op jit(solution)/shard_map/ppermute | solution.py:99
  517.9 15.3 %collective-permute-done.27 = bf16[128,1024]{1,0:T(8,128)(2,1)S(1)} collective-permute-done((bf16[128,1024]{1,0:T(8,128)(2,1)S(1)}, bf16[128,1024]{1,0:T(8,128)(2,1)S(1)}, u32[]{:S(2)}, u32[]{:S(2)}) %collective-permute-start.27) | collective-permute-done | bytes 262176 | tf_op jit(solution)/shard_map/ppermute | solution.py:99
  533.9 8.6 %collective-permute-done.28 = bf16[64,1024]{1,0:T(8,128)(2,1)S(1)} collective-permute-done((bf16[64,1024]{1,0:T(8,128)(2,1)S(1)}, bf16[64,1024]{1,0:T(8,128)(2,1)S(1)}, u32[]{:S(2)}, u32[]{:S(2)}) %collective-permute-start.28) | collective-permute-done | bytes 131104 | tf_op jit(solution)/shard_map/ppermute | solution.py:99
  542.6 81.4 %all-reduce.8.cloned.1.call-done = bf16[512,3072]{1,0:T(8,128)(2,1)} async-done(((bf16[512,3072]{1,0:T(8,128)(2,1)}), bf16[512,3072]{1,0:T(8,128)(2,1)}) %all-reduce.8.cloned.1.call-update) | async-done | bytes 3145744 | tf_op jit(solution)/shard_map/psum | solution.py:523
  637.6 15.3 %collective-permute-done.31 = bf16[256,1024]{1,0:T(8,128)(2,1)S(1)} collective-permute-done((bf16[256,1024]{1,0:T(8,128)(2,1)S(1)}, bf16[256,1024]{1,0:T(8,128)(2,1)S(1)}, u32[]{:S(2)}, u32[]{:S(2)}) %collective-permute-start.31) | collective-permute-done | bytes 524320 | tf_op jit(solution)/shard_map/ppermute | solution.py:104
  654.8 78.6 %all-reduce.10.cloned.1.call-done = (bf16[512,1024]{1,0:T(8,128)(2,1)}, bf16[1024,512]{1,0:T(8,128)(2,1)}) async-done(((bf16[512,1024]{1,0:T(8,128)(2,1)}, bf16[1024,512]{1,0:T(8,128)(2,1)}), (bf16[512,1024]{1,0:T(8,128)(2,1)}, bf16[1024,512]{1,0:T(8,128)(2,1)})) %all-reduce.10.cloned.1.call-update) | async-done | bytes 2097168 | tf_op jit(solution)/shard_map/psum | solution.py:544
  737.9 40.2 %psum.39 = f32[2304]{0:T(1024)S(1)} all-reduce(f32[2304]{0:T(1024)S(1)} %pad_maximum_fusion.12), channel_id=1, replica_groups=mesh['shard'=2,'ctx'=8,'tp'=2] {'shard','ctx','tp'}, use_global_device_ids=true, to_apply=%region_11.12 | all-reduce | flops 2304 | bytes 18432 | tf_op jit(solution)/shard_map/psum | solution.py:566
  (258 shorter events, 159.2 us)
Async XLA Ops:
  7.2 155.0 %all-gather.2.cloned.1.call-start = ((), (), s32[]{:S(2)}) async-start(), calls=%async_computation | async-start | bytes 9437184 | tf_op jit(solution)/shard_map/all_gather | solution.py:443
  40.8 439.4 %all-reduce.6.cloned.1.call-start = ((), (), s32[]{:S(2)}) async-start(), calls=%async_computation.1 | async-start | bytes 3145728 | tf_op jit(solution)/shard_map/psum | solution.py:522
  58.1 48.2 %collective-permute-start.1 = (bf16[512,1024]{1,0:T(8,128)(2,1)}, bf16[512,1024]{1,0:T(8,128)(2,1)S(1)}, u32[]{:S(2)}, u32[]{:S(2)}) collective-permute-start(bf16[512,1024]{1,0:T(8,128)(2,1)} %param.19), channel_id=1, source_target_pairs={{16,0},{0,16},{17,1},{1,17},{18,2},{2,18},{19,3},{3,19},{20,4},{4,... | collective-permute-start | bytes 3145736 | tf_op jit(solution)/shard_map/ppermute | solution.py:47
  66.2 42.8 %collective-permute-start.8 = (bf16[256,1024]{1,0:T(8,128)(2,1)}, bf16[256,1024]{1,0:T(8,128)(2,1)S(1)}, u32[]{:S(2)}, u32[]{:S(2)}) collective-permute-start(bf16[256,1024]{1,0:T(8,128)(2,1)} %get-tuple-element.88), channel_id=1, source_target_pairs={{0,14},{2,12},{4,10},{6,8},{8,6},{10,4},{12,2},{14,0},{1,15},{3,13... | collective-permute-start | bytes 1572872 | tf_op jit(solution)/shard_map/ppermute | solution.py:492
  70.7 63.3 %collective-permute-start.7 = (bf16[256,1024]{1,0:T(8,128)(2,1)}, bf16[256,1024]{1,0:T(8,128)(2,1)S(1)}, u32[]{:S(2)}, u32[]{:S(2)}) collective-permute-start(bf16[256,1024]{1,0:T(8,128)(2,1)} %get-tuple-element.89), channel_id=1, source_target_pairs={{0,12},{2,14},{4,8},{6,10},{8,4},{10,6},{12,0},{14,2},{1,13},{3,15... | collective-permute-start | bytes 1572872 | tf_op jit(solution)/shard_map/ppermute | solution.py:492
  70.9 84.1 %collective-permute-start.6 = (bf16[256,1024]{1,0:T(8,128)(2,1)}, bf16[256,1024]{1,0:T(8,128)(2,1)S(1)}, u32[]{:S(2)}, u32[]{:S(2)}) collective-permute-start(bf16[256,1024]{1,0:T(8,128)(2,1)} %get-tuple-element.90), channel_id=1, source_target_pairs={{0,10},{2,8},{4,14},{6,12},{8,2},{10,0},{12,6},{14,4},{1,11},{3,9}... | collective-permute-start | bytes 1572872 | tf_op jit(solution)/shard_map/ppermute | solution.py:492
  90.5 75.0 %collective-permute-start.5 = (bf16[256,1024]{1,0:T(8,128)(2,1)}, bf16[256,1024]{1,0:T(8,128)(2,1)}, u32[]{:S(2)}, u32[]{:S(2)}) collective-permute-start(bf16[256,1024]{1,0:T(8,128)(2,1)} %get-tuple-element.91), channel_id=1, source_target_pairs={{0,8},{2,10},{4,12},{6,14},{8,0},{10,2},{12,4},{14,6},{1,9},{3,11}... | collective-permute-start | bytes 1572872 | tf_op jit(solution)/shard_map/ppermute | solution.py:492
  106.3 59.2 %collective-permute-start.4 = (bf16[256,1024]{1,0:T(8,128)(2,1)}, bf16[256,1024]{1,0:T(8,128)(2,1)}, u32[]{:S(2)}, u32[]{:S(2)}) collective-permute-start(bf16[256,1024]{1,0:T(8,128)(2,1)} %get-tuple-element.92), channel_id=1, source_target_pairs={{0,6},{2,4},{4,2},{6,0},{8,14},{10,12},{12,10},{14,8},{1,7},{3,5},... | collective-permute-start | bytes 1572872 | tf_op jit(solution)/shard_map/ppermute | solution.py:492
  108.9 57.6 %collective-permute-start.3 = (bf16[256,1024]{1,0:T(8,128)(2,1)}, bf16[256,1024]{1,0:T(8,128)(2,1)}, u32[]{:S(2)}, u32[]{:S(2)}) collective-permute-start(bf16[256,1024]{1,0:T(8,128)(2,1)} %get-tuple-element.93), channel_id=1, source_target_pairs={{0,4},{2,6},{4,0},{6,2},{8,12},{10,14},{12,8},{14,10},{1,5},{3,7},... | collective-permute-start | bytes 1572872 | tf_op jit(solution)/shard_map/ppermute | solution.py:492
  251.1 37.3 %collective-permute-start.14 = (bf16[1536,512]{1,0:T(8,128)(2,1)S(1)}, bf16[1536,512]{1,0:T(8,128)(2,1)S(1)}, u32[]{:S(2)}, u32[]{:S(2)}) collective-permute-start(bf16[1536,512]{1,0:T(8,128)(2,1)S(1)} %constant_dynamic-slice_fusion.4), channel_id=1, source_target_pairs={{0,16},{16,0},{1,17},{17,1},{2,18},{18,2},{3,19},{19,3},{4,20},{20... | collective-permute-start | bytes 4718600 | tf_op jit(solution)/shard_map/ppermute | solution.py:86
  253.3 101.7 %collective-permute-start.20 = (bf16[512,3072]{1,0:T(8,128)(2,1)}, bf16[512,3072]{1,0:T(8,128)(2,1)}, u32[]{:S(2)}, u32[]{:S(2)}) collective-permute-start(bf16[512,3072]{1,0:T(8,128)(2,1)} %constant_dynamic-slice_fusion.3), channel_id=1, source_target_pairs={{0,16},{16,0},{1,17},{17,1},{2,18},{18,2},{3,19},{19,3},{4,20},{20... | collective-permute-start | bytes 9437192 | tf_op jit(solution)/shard_map/ppermute | solution.py:86
  320.2 39.5 %collective-permute-start.15 = (bf16[2,256,512]{2,1,0:T(8,128)(2,1)}, bf16[2,256,512]{2,1,0:T(8,128)(2,1)}, u32[]{:S(2)}, u32[]{:S(2)}) collective-permute-start(bf16[2,256,512]{2,1,0:T(8,128)(2,1)} %get-tuple-element.53), channel_id=1, source_target_pairs={{0,2},{2,0},{4,6},{6,4},{8,10},{10,8},{12,14},{14,12},{1,3},{3,1},... | collective-permute-start | bytes 1572872 | tf_op jit(solution)/shard_map/ppermute | solution.py:536
  321.9 37.9 %collective-permute-start.16 = (bf16[2,256,512]{2,1,0:T(8,128)(2,1)}, bf16[2,256,512]{2,1,0:T(8,128)(2,1)}, u32[]{:S(2)}, u32[]{:S(2)}) collective-permute-start(bf16[2,256,512]{2,1,0:T(8,128)(2,1)} %get-tuple-element.54), channel_id=1, source_target_pairs={{0,4},{2,6},{4,0},{6,2},{8,12},{10,14},{12,8},{14,10},{1,5},{3,7},... | collective-permute-start | bytes 1572872 | tf_op jit(solution)/shard_map/ppermute | solution.py:536
  321.9 54.4 %collective-permute-start.17 = (bf16[2,256,512]{2,1,0:T(8,128)(2,1)}, bf16[2,256,512]{2,1,0:T(8,128)(2,1)}, u32[]{:S(2)}, u32[]{:S(2)}) collective-permute-start(bf16[2,256,512]{2,1,0:T(8,128)(2,1)} %get-tuple-element.55), channel_id=1, source_target_pairs={{0,6},{2,4},{4,2},{6,0},{8,14},{10,12},{12,10},{14,8},{1,7},{3,5},... | collective-permute-start | bytes 1572872 | tf_op jit(solution)/shard_map/ppermute | solution.py:536
  323.7 52.9 %collective-permute-start.18 = (bf16[2,256,512]{2,1,0:T(8,128)(2,1)}, bf16[2,256,512]{2,1,0:T(8,128)(2,1)}, u32[]{:S(2)}, u32[]{:S(2)}) collective-permute-start(bf16[2,256,512]{2,1,0:T(8,128)(2,1)} %get-tuple-element.56), channel_id=1, source_target_pairs={{0,8},{2,10},{4,12},{6,14},{8,0},{10,2},{12,4},{14,6},{1,9},{3,11}... | collective-permute-start | bytes 1572872 | tf_op jit(solution)/shard_map/ppermute | solution.py:536
  355.0 62.5 %collective-permute-start.19 = (bf16[2,256,512]{2,1,0:T(8,128)(2,1)}, bf16[2,256,512]{2,1,0:T(8,128)(2,1)}, u32[]{:S(2)}, u32[]{:S(2)}) collective-permute-start(bf16[2,256,512]{2,1,0:T(8,128)(2,1)} %get-tuple-element.57), channel_id=1, source_target_pairs={{0,10},{2,8},{4,14},{6,12},{8,2},{10,0},{12,6},{14,4},{1,11},{3,9}... | collective-permute-start | bytes 1572872 | tf_op jit(solution)/shard_map/ppermute | solution.py:536
  359.7 57.7 %collective-permute-start.21 = (bf16[2,256,512]{2,1,0:T(8,128)(2,1)}, bf16[2,256,512]{2,1,0:T(8,128)(2,1)}, u32[]{:S(2)}, u32[]{:S(2)}) collective-permute-start(bf16[2,256,512]{2,1,0:T(8,128)(2,1)} %copy-done.13), channel_id=1, source_target_pairs={{0,12},{2,14},{4,8},{6,10},{8,4},{10,6},{12,0},{14,2},{1,13},{3,15... | collective-permute-start | bytes 1572872 | tf_op jit(solution)/shard_map/ppermute | solution.py:536
  359.8 57.7 %collective-permute-start.22 = (bf16[2,256,512]{2,1,0:T(8,128)(2,1)S(1)}, bf16[2,256,512]{2,1,0:T(8,128)(2,1)}, u32[]{:S(2)}, u32[]{:S(2)}) collective-permute-start(bf16[2,256,512]{2,1,0:T(8,128)(2,1)S(1)} %get-tuple-element.61), channel_id=1, source_target_pairs={{0,14},{2,12},{4,10},{6,8},{8,6},{10,4},{12,2},{14,0},{1,15},{3,13... | collective-permute-start | bytes 1572872 | tf_op jit(solution)/shard_map/ppermute | solution.py:536
  370.3 253.7 %all-reduce.8.cloned.1.call-start = ((), (), s32[]{:S(2)}) async-start(), calls=%async_computation.2 | async-start | bytes 6291456 | tf_op jit(solution)/shard_map/psum | solution.py:523
  376.2 115.7 %collective-permute-start.32 = (bf16[1024,512]{1,0:T(8,128)(2,1)}, bf16[1024,512]{1,0:T(8,128)(2,1)}, u32[]{:S(2)}, u32[]{:S(2)}) collective-permute-start(bf16[1024,512]{1,0:T(8,128)(2,1)} %constant_dynamic-slice_fusion), channel_id=1, source_target_pairs={{0,16},{16,0},{1,17},{17,1},{2,18},{18,2},{3,19},{19,3},{4,20},{20... | collective-permute-start | bytes 3145736 | tf_op jit(solution)/shard_map/ppermute | solution.py:86
  427.4 60.9 %collective-permute-start.25 = (bf16[512,1024]{1,0:T(8,128)(2,1)}, bf16[512,1024]{1,0:T(8,128)(2,1)}, u32[]{:S(2)}, u32[]{:S(2)}) collective-permute-start(bf16[512,1024]{1,0:T(8,128)(2,1)} %constant_dynamic-slice_fusion.1), channel_id=1, source_target_pairs={{0,16},{16,0},{1,17},{17,1},{2,18},{18,2},{3,19},{19,3},{4,20},{20... | collective-permute-start | bytes 3145736 | tf_op jit(solution)/shard_map/ppermute | solution.py:86
  432.3 62.1 %collective-permute-start.24 = (bf16[512,1024]{1,0:T(8,128)(2,1)}, bf16[512,1024]{1,0:T(8,128)(2,1)}, u32[]{:S(2)}, u32[]{:S(2)}) collective-permute-start(bf16[512,1024]{1,0:T(8,128)(2,1)} %constant_dynamic-slice_fusion.2), channel_id=1, source_target_pairs={{0,16},{16,0},{1,17},{17,1},{2,18},{18,2},{3,19},{19,3},{4,20},{20... | collective-permute-start | bytes 3145736 | tf_op jit(solution)/shard_map/ppermute | solution.py:86
  480.2 253.2 %all-reduce.10.cloned.1.call-start = ((), (), s32[]{:S(2)}) async-start(), calls=%async_computation.3 | async-start | bytes 4194304 | tf_op jit(solution)/shard_map/psum | solution.py:544
  542.5 81.5 %collective-permute-start.29 = (bf16[64,1024]{1,0:T(8,128)(2,1)S(1)}, bf16[64,1024]{1,0:T(8,128)(2,1)S(1)}, u32[]{:S(2)}, u32[]{:S(2)}) collective-permute-start(bf16[64,1024]{1,0:T(8,128)(2,1)S(1)} %add_convert_fusion.6), channel_id=1, source_target_pairs={{0,8},{2,10},{4,12},{6,14},{8,0},{10,2},{12,4},{14,6},{1,9},{3,11}... | collective-permute-start | bytes 393224 | tf_op jit(solution)/shard_map/ppermute | solution.py:104
  (64 other events, 991.9 us)
Sparse Core Ops, SparseCore 0:
  40.9 104.3 all-gather.1
  370.4 109.6 all-reduce.5
  484.3 139.6 all-reduce.7
  628.6 104.7 all-reduce.9

commit v3 on v2

--- a/solution.py
+++ b/solution.py
@@ -37,8 +37,8 @@
     return lax.dot_general(a, b, (((0,), (0,)), ((), ())), preferred_element_type=F32)
 
 
-def after(value, *earlier):
-    return lax.optimization_barrier((value,) + earlier)[0]
+def tie(*values):
+    return lax.optimization_barrier(values)
 
 
 def pieces_of(own, axis):
@@ -75,64 +75,86 @@
     return partial.astype(F32) + other.astype(F32)
 
 
-def to_shard_owner(grad, dim):
+def swap(value, axis, level=1):
+    count = lax.axis_size(axis)
+    return lax.ppermute(value, axis, [(i, i ^ level) for i in range(count)])
+
+
+def to_shard_owner(grad):
     count = lax.axis_size("shard")
     index = lax.axis_index("shard")
     if count != 2:
-        return lax.psum_scatter(grad, "shard", scatter_dimension=dim, tiled=True).astype(F32)
-    size = grad.shape[dim] // 2
-    sent = lax.dynamic_slice_in_dim(grad, (1 - index) * size, size, dim)
-    kept = lax.dynamic_slice_in_dim(grad, index * size, size, dim)
-    other = lax.ppermute(sent, "shard", [(0, 1), (1, 0)])
-    return kept.astype(F32) + other.astype(F32)
-
-
-def ctx_total(value):
-    count = lax.axis_size("ctx")
-    index = lax.axis_index("ctx")
-    levels = [1 << b for b in range(count.bit_length() - 1)]
-    for level in levels:
-        bit = (index // level) % 2
-        size = value.shape[0] // 2
-        sent = lax.dynamic_slice_in_dim(value, (1 - bit) * size, size, 0).astype(BF16)
-        kept = lax.dynamic_slice_in_dim(value, bit * size, size, 0)
-        other = lax.ppermute(sent, "ctx", [(i, i ^ level) for i in range(count)])
-        value = kept + other.astype(F32)
+        return lax.psum_scatter(grad, "shard", scatter_dimension=0, tiled=True).astype(F32)
+    size = grad.shape[0] // 2
+    sent = lax.dynamic_slice_in_dim(grad, (1 - index) * size, size, 0)
+    kept = lax.dynamic_slice_in_dim(grad, index * size, size, 0)
+    return kept.astype(F32) + swap(sent, "shard").astype(F32)
+
+
+def bit_of(level):
+    return (lax.axis_index("ctx") // level) % 2
+
+
+def halve(value, level):
+    bit = bit_of(level)
+    size = value.shape[0] // 2
+    sent = lax.dynamic_slice_in_dim(value, (1 - bit) * size, size, 0).astype(BF16)
+    kept = lax.dynamic_slice_in_dim(value, bit * size, size, 0)
+    return kept + swap(sent, "ctx", level).astype(F32)
+
+
+def double(value, level):
     value = value.astype(BF16)
-    for level in levels[::-1]:
-        bit = (index // level) % 2
-        other = lax.ppermute(value, "ctx", [(i, i ^ level) for i in range(count)])
-        value = join([value, other], 0, bit)
-    return value.astype(F32)
-
-
-def rope_kernel(roped, pre_ref, cos_ref, sin_ref, gain_ref, out_ref):
+    return join([value, swap(value, "ctx", level)], 0, bit_of(level))
+
+
+def chain_step(value, levels, step):
+    if step < len(levels):
+        return halve(value, levels[step])
+    return double(value, levels[2 * len(levels) - 1 - step])
+
+
+def rope_kernel(pre_ref, cos_ref, sin_ref, gain_ref, out_ref):
     pre = pre_ref[...]
-
+    factor = lax.rsqrt(jnp.mean(pre * pre, axis=-1, keepdims=True) + EPS)
+    scaled = pre * factor * gain_ref[...]
+    turned = pltpu.roll(scaled, HEAD // 2, 1)
+    out_ref[...] = (scaled * cos_ref[...] + turned * sin_ref[...]).astype(BF16)
+
+
+def rope_and_copy_kernel(roped, pre_ref, plain_ref, cos_ref, sin_ref, gain_ref, out_ref):
     @pl.when(pl.program_id(0) < roped)
     def _():
-        factor = lax.rsqrt(jnp.mean(pre * pre, axis=-1, keepdims=True) + EPS)
-        scaled = pre * factor * gain_ref[...]
-        turned = pltpu.roll(scaled, HEAD // 2, 1)
-        out_ref[...] = (scaled * cos_ref[...] + turned * sin_ref[...]).astype(BF16)
+        rope_kernel(pre_ref, cos_ref, sin_ref, gain_ref, out_ref)
 
     @pl.when(pl.program_id(0) >= roped)
     def _():
-        out_ref[...] = pre.astype(BF16)
-
-
-def rope(pre, roped, cosine, sine, gain):
+        out_ref[...] = plain_ref[...].astype(BF16)
+
+
+def rope(pre, cosine, sine, gain, plain=None):
     rows, width = pre.shape
+    heads = width // HEAD
+    table = pl.BlockSpec((rows, HEAD), lambda h: (0, 0))
+    tables = [table, table, pl.BlockSpec((1, HEAD), lambda h: (0, 0))]
     column = pl.BlockSpec((rows, HEAD), lambda h: (0, h))
-    table = pl.BlockSpec((rows, HEAD), lambda h: (0, 0))
+    if plain is None:
+        kernel, steps, columns, values = rope_kernel, heads, [column], [pre]
+    else:
+        kernel, steps = functools.partial(rope_and_copy_kernel, heads), 2 * heads
+        columns = [
+            pl.BlockSpec((rows, HEAD), lambda h: (0, jnp.minimum(h, heads - 1))),
+            pl.BlockSpec((rows, HEAD), lambda h: (0, jnp.maximum(h - heads, 0))),
+        ]
+        values = [pre, plain]
     return pl.pallas_call(
-        functools.partial(rope_kernel, roped),
-        grid=(width // HEAD,),
-        in_specs=[column, table, table, pl.BlockSpec((1, HEAD), lambda h: (0, 0))],
+        kernel,
+        grid=(steps,),
+        in_specs=columns + tables,
         out_specs=column,
-        out_shape=jax.ShapeDtypeStruct((rows, width), BF16),
+        out_shape=jax.ShapeDtypeStruct((rows, steps * HEAD), BF16),
         compiler_params=pltpu.CompilerParams(vmem_limit_bytes=VMEM_LIMIT),
-    )(pre, cosine, sine, gain)
+    )(*values, cosine, sine, gain)
 
 
 def rope_back_kernel(grad_ref, pre_ref, cos_ref, sin_ref, gain_ref, out_ref, sum_ref):
@@ -197,6 +219,16 @@
     return (k_part + 1) * half > doc_begins(meta_ref, docs, q_part * half)
 
 
+def all_visible(meta_ref, docs, half, q_part, k_part):
+    return k_part * half >= doc_begins(meta_ref, docs, q_part * half + half - 1)
+
+
+def masked(weights, *mask_args):
+    if mask_args[-1] is None:
+        return weights
+    return jnp.where(block_mask(*mask_args), weights, 0.0)
+
+
 def two_heads(ref, start, half):
     rows = pl.ds(start, half)
     return jnp.concatenate([ref[rows, :HEAD], ref[rows, HEAD:]], axis=0)
@@ -212,8 +244,9 @@
 
     def block(start, keys, values, q_part, k_part, diagonal):
         scores = dot_nt(two_heads(q_ref, start, half), keys)
-        visible = block_mask(meta_ref, docs, scores.shape, half, q_part, k_part, diagonal)
-        weights = jnp.where(visible, jnp.exp2(scores * factor), 0.0).astype(BF16)
+        weights = jnp.exp2(scores * factor)
+        weights = masked(weights, meta_ref, docs, scores.shape, half, q_part, k_part, diagonal)
+        weights = weights.astype(BF16)
         return dot(weights, jnp.concatenate([values, ones], axis=1))
 
     for e in range(2):
@@ -225,12 +258,16 @@
         k_part = meta_ref[docs + 2 * d + 1]
         q_part = jnp.where(side == 0, own, 2 * count - 1 - own)
 
-        @pl.when(any_visible(meta_ref, docs, half, q_part, k_part))
-        def _():
+        def add(mask):
             start = pl.multiple_of(side * half, half)
             acc_ref[side] += block(
-                start, others[2 * d][...], others[2 * d + 1][...], q_part, k_part, False
+                start, others[2 * d][...], others[2 * d + 1][...], q_part, k_part, mask
             )
+
+        seen = any_visible(meta_ref, docs, half, q_part, k_part)
+        whole = all_visible(meta_ref, docs, half, q_part, k_part)
+        pl.when(whole)(functools.partial(add, None))
+        pl.when(seen & jnp.logical_not(whole))(functools.partial(add, False))
 
     for e in range(2):
         total = acc_ref[e]
@@ -267,8 +304,8 @@
         repeat = half // HEAD
         lse = jnp.concatenate([stats_ref[side]] * repeat, axis=1)
         delta = jnp.concatenate([delta_ref[side]] * repeat, axis=1)
-        visible = block_mask(meta_ref, docs, scores.shape, half, q_part, k_part, diagonal)
-        weights = jnp.where(visible, jnp.exp2(scores * (scale * LOG2E) - lse), 0.0)
+        weights = jnp.exp2(scores * (scale * LOG2E) - lse)
+        weights = masked(weights, meta_ref, docs, scores.shape, half, q_part, k_part, diagonal)
         d_weights = dot_nt(grads, values)
         d_scores = (weights * (d_weights - delta)).astype(BF16)
         d_values = dot_tn(weights.astype(BF16), grads)
@@ -289,16 +326,19 @@
         k_part = meta_ref[docs + 2 * d + 1]
         q_part = jnp.where(side == 0, own, 2 * count - 1 - own)
         seen = any_visible(meta_ref, docs, half, q_part, k_part)
-
-        @pl.when(seen)
-        def _():
+        whole = all_visible(meta_ref, docs, half, q_part, k_part)
+
+        def add(mask):
             start = pl.multiple_of(side * half, half)
             d_queries, d_keys, d_values = block(
-                side, start, others[2 * d][...], others[2 * d + 1][...], q_part, k_part, False
+                side, start, others[2 * d][...], others[2 * d + 1][...], q_part, k_part, mask
             )
             acc_ref[side] += d_queries
             given[d][0] = d_keys.astype(BF16)
             given[d][1] = d_values.astype(BF16)
+
+        pl.when(whole)(functools.partial(add, None))
+        pl.when(seen & jnp.logical_not(whole))(functools.partial(add, False))
 
         @pl.when(jnp.logical_not(seen))
         def _():
@@ -415,36 +455,26 @@
     docs = seq_lengths.shape[1]
     kv_width = key_weight.shape[1]
     units = w_gate.shape[1]
+    heads_width = w_out.shape[0]
 
     packed = jnp.concatenate([gain_in, gain_post, gain_q, gain_k])
-    lines = -(-packed.shape[0] // (2 * kv_width * 16)) * 16
-    packed = jnp.pad(packed, (0, lines * 2 * kv_width - packed.shape[0]))
-    kv_own = jnp.concatenate(
-        [
-            jnp.concatenate([key_weight, value_weight], axis=1),
-            packed.reshape(lines, 2 * kv_width),
-        ],
-        axis=0,
-    )
-    first_pieces = pieces_of(kv_own, "shard")
-    kv_pieces = [piece[:depth] for piece in first_pieces]
-    cuts = [0, depth, 2 * depth, 2 * depth + gain_q.shape[0]]
-    cuts = cuts + [cuts[-1] + gain_k.shape[0]]
+    packed_pieces = pieces_of(packed, "shard")
+    k_pieces = pieces_of(key_weight, "shard")
+    v_pieces = pieces_of(value_weight, "shard")
+    cuts = [0, depth, 2 * depth, 2 * depth + gain_q.shape[0], packed.shape[0]]
     gain_pieces = [
-        [piece[depth:].reshape(-1)[lo:hi].astype(F32) for piece in first_pieces]
+        [piece[lo:hi].astype(F32) for piece in packed_pieces]
         for lo, hi in zip(cuts[:-1], cuts[1:])
     ]
     scale_in, scale_post, scale_q, scale_k = (
         join(pieces, 0, shard).reshape(1, -1) for pieces in gain_pieces
     )
-
-    q_pieces = pieces_of(after(w_query, first_pieces[-1]), "shard")
-    gate_up = jnp.concatenate([w_gate, w_up], axis=1)
-    full_gate_up = lax.all_gather(
-        after(gate_up, first_pieces[-1]), "shard", axis=0, tiled=True
-    )
-    out_pieces = pieces_of(after(w_out, q_pieces[-1]), "shard")
-    down_pieces = pieces_of(after(w_down, q_pieces[-1]), "shard")
+    own_units = jnp.concatenate([w_gate, w_up, w_down.T], axis=1)
+    w_query, own_units, v_pieces[-1] = tie(w_query, own_units, v_pieces[-1])
+    q_pieces = pieces_of(w_query, "shard")
+    full_units = lax.all_gather(own_units, "shard", axis=0, tiled=True)
+    w_out, q_pieces[-1] = tie(w_out, q_pieces[-1])
+    out_pieces = pieces_of(w_out, "shard")
 
     lengths = seq_lengths[0]
     starts = jnp.cumsum(lengths) - lengths
@@ -474,30 +504,35 @@
     normal_one, factor_one = rms_parts(inputs)
     normed_input = (normal_one * scale_in).astype(BF16)
 
+    parts_in = []
+    for j in range(shard_count):
+        at = (shard + j) % shard_count * depth
+        part_in = lax.dynamic_slice_in_dim(normal_one, at, depth, 1)
+        parts_in.append((part_in * gain_pieces[0][j][None, :]).astype(BF16))
+
     def project(pieces):
-        total = None
-        for j, piece in enumerate(pieces):
-            at = (shard + j) % shard_count * depth
-            part_in = lax.dynamic_slice_in_dim(normal_one, at, depth, 1)
-            term = dot((part_in * gain_pieces[0][j][None, :]).astype(BF16), piece)
-            total = term if total is None else total + term
-        return total
-
-    kv_pre = project(kv_pieces)
-    key_value = rope(kv_pre, kv_width // HEAD, cosine, sine, scale_k)
+        return sum(dot(part_in, piece) for part_in, piece in zip(parts_in, pieces))
+
+    k_pieces[-1], cosine, sine, meta, parts_in[-1], scale_k = tie(
+        k_pieces[-1], cosine, sine, meta, parts_in[-1], scale_k
+    )
+    k_pre = project(k_pieces)
+    key_value = rope(k_pre, cosine, sine, scale_k, project(v_pieces))
     held = []
     for d in range(1, count):
         start = jnp.where(part < other_parts[d - 1], 0, half)
         sent = lax.dynamic_slice_in_dim(key_value, start, half, 0)
         held.append(lax.ppermute(sent, "ctx", [(i, i ^ d) for i in range(count)]))
     q_pre = project(q_pieces)
-    queries = rope(q_pre, q_pre.shape[1] // HEAD, cosine, sine, scale_q)
-    queries = after(queries, full_gate_up)
+    queries = rope(q_pre, cosine, sine, scale_q)
+    queries, out_pieces[-1] = tie(queries, out_pieces[-1])
     attended, attn_out, lse = attend(meta, docs, queries, key_value, held)
 
     full_out = join(out_pieces, 1, shard)
-    full_down = join(down_pieces, 1, shard)
-    full_kv = join(kv_pieces, 0, shard)
+    full_gate_up = full_units[:, : 2 * units]
+    full_down_t = full_units[:, 2 * units :]
+    full_key = join(k_pieces, 0, shard)
+    full_value = join(v_pieces, 0, shard)
     full_query = join(q_pieces, 0, shard)
 
     residual = inputs + pair_total(dot(attn_out, full_out))
@@ -509,41 +544,62 @@
     sigma = jax.nn.sigmoid(gate_act)
     silu_act = gate_act * sigma
     hidden = (silu_act * upward).astype(BF16)
-    mixed = (residual + pair_total(dot(hidden, full_down))).astype(BF16)
-    grad_down = dot_tn(hidden, cotangent).astype(BF16)
-    d_hidden = dot_nt(cotangent, full_down)
+    grad_down = dot_tn(cotangent, hidden).astype(BF16)
+    cotangent, grad_down = tie(cotangent, grad_down)
+    d_hidden = dot(cotangent, full_down_t)
     d_gate = (d_hidden * upward * sigma * (1.0 + gate_act * (1.0 - sigma))).astype(BF16)
     d_up = (d_hidden * silu_act).astype(BF16)
     d_gate_up = jnp.concatenate([d_gate, d_up], axis=1)
     grad_gate_up = dot_tn(normed_two, d_gate_up).astype(BF16)
+    d_gate_up, grad_gate_up = tie(d_gate_up, grad_gate_up)
     d_normed_two = pair_total(dot_nt(d_gate_up, full_gate_up))
-    shared_down = to_shard_owner(grad_down, 1).astype(BF16)
-    shared_gate_up = to_shard_owner(grad_gate_up, 0).astype(BF16)
-    owned_down = lax.psum(shared_down, "ctx")
-    owned_gate_up = lax.psum(after(shared_gate_up, owned_down), "ctx")
+    hidden, d_normed_two = tie(hidden, d_normed_two)
+    mixed_part = dot_nt(hidden, full_down_t)
+    mixed = (residual + pair_total(mixed_part)).astype(BF16)
+    shared_down = to_shard_owner(grad_down)
+    shared_gate_up = to_shard_owner(grad_gate_up)
     grad_post = jnp.sum(d_normed_two * normal_two, axis=0)
     d_residual = cotangent.astype(F32) + rms_back(
         d_normed_two * scale_post, normal_two, factor_two
     )
 
     d_branch = d_residual.astype(BF16)
-    d_attn = after(dot_nt(d_branch, full_out).astype(BF16), shared_down)
+    d_attn, shared_down = tie(dot_nt(d_branch, full_out).astype(BF16), shared_down)
     d_queries, d_kv, given = attend_back(
         meta, docs, queries, d_attn, attended, lse, key_value, held
     )
-    given = given[:-2] + [after(g, shared_gate_up) for g in given[-2:]]
-    returned = [
-        lax.ppermute(g, "ctx", [(i, i ^ d) for i in range(count)])
-        for d, g in zip(range(1, count), given)
-    ]
-    grad_out = dot_tn(attn_out, d_branch).astype(BF16)
+    levels = [1 << b for b in range(count.bit_length() - 1)]
+    turned = levels[1:] + levels[:1]
+    half_down = halve(shared_down, levels[0])
+    d_queries, half_down, *given = tie(d_queries, half_down, *given)
+    returned = {}
+
+    def give_back(turns):
+        for d in turns:
+            returned[d] = lax.ppermute(given[d - 1], "ctx", [(i, i ^ d) for i in range(count)])
+
+    def settle(turns, *values):
+        done = tie(*(returned[d] for d in turns), *values)
+        returned.update(zip(turns, done))
+        return done[len(turns) :]
+
+    far = [d for d in range(1, count) if d >= count // 2]
+    near = [d for d in range(1, count) if d < count // 2]
+    early = far[: len(far) // 2] + near[: (len(near) + 1) // 2]
+    late = far[len(far) // 2 :] + near[(len(near) + 1) // 2 :]
+    give_back(early)
+    grad_out = dot_tn(d_branch, attn_out).astype(BF16)
+    given = list(given)
+    d_queries, shared_gate_up, grad_out, *given = settle(
+        early, d_queries, shared_gate_up, grad_out, *given
+    )
+    give_back(late)
+    half_gate_up = halve(shared_gate_up, levels[0])
     d_q_pre, gq_part = rope_back(d_queries, q_pre, cosine, sine, scale_q)
     grad_query = dot_tn(normed_input, d_q_pre).astype(BF16)
-    shared_out = to_shard_owner(grad_out, 1).astype(BF16)
-    shared_query = to_shard_owner(grad_query, 0).astype(BF16)
-    owned_out, owned_query = lax.psum(
-        (after(shared_out, owned_gate_up), after(shared_query, owned_gate_up)), "ctx"
-    )
+    out_query = to_shard_owner(jnp.concatenate([grad_out, grad_query], axis=1))
+    (half_gate_up,) = settle(late, half_gate_up)
+    returned = [returned[d] for d in range(1, count)]
 
     first = sum(
         jnp.where(part < p, g.astype(F32), 0.0) for p, g in zip(other_parts, returned)
@@ -552,36 +608,65 @@
         jnp.where(part < p, 0.0, g.astype(F32)) for p, g in zip(other_parts, returned)
     )
     d_kv = d_kv + jnp.concatenate([first, second], axis=1)
-    d_k_pre, gk_part = rope_back(d_kv[0], kv_pre, cosine, sine, scale_k)
-    d_kv_pre = jnp.concatenate([d_k_pre, d_kv[1].astype(BF16)], axis=1)
+    d_k_pre, gk_part = rope_back(d_kv[0], k_pre, cosine, sine, scale_k)
+    d_v_pre = d_kv[1].astype(BF16)
+    d_kv_pre = jnp.concatenate([d_k_pre, d_v_pre], axis=1)
     grad_kv = dot_tn(normed_input, d_kv_pre).astype(BF16)
-    d_normed = pair_total(dot_nt(d_q_pre, full_query) + dot_nt(d_kv_pre, full_kv))
+
+    steps = 2 * len(levels)
+    unit_chain = jnp.concatenate([half_gate_up, half_down], axis=1)
+    (unit_chain,) = tie(unit_chain)
+    unit_chain = chain_step(unit_chain, levels, 1)
+    rest_chain = jnp.concatenate([out_query, to_shard_owner(grad_kv)], axis=1)
+    d_normed = pair_total(
+        dot_nt(d_q_pre, full_query) + dot_nt(d_k_pre, full_key) + dot_nt(d_v_pre, full_value)
+    )
     grad_in = jnp.sum(d_normed * normal_one, axis=0)
     input_grad = d_residual + rms_back(d_normed * scale_in, normal_one, factor_one)
-
-    owned_kv = ctx_total(to_shard_owner(grad_kv, 0))
-
     once = jnp.where(lax.axis_index("tp") == 0, 1.0, 0.0)
     gain_grads = jnp.concatenate([grad_in * once, grad_post * once, gq_part[0], gk_part[0]])
-    gain_grads = lax.psum(
-        after(gain_grads, owned_query),
-        ("shard", "ctx", "tp"),
+    gain_grads = gain_grads.reshape(-1, HEAD)
+    gain_steps = [("tp", 1)] + [("ctx", level) for level in levels]
+    if shard_count == 2:
+        gain_steps = gain_steps + [("shard", 1)]
+    else:
+        gain_grads = lax.psum(gain_grads, "shard")
+
+    for step in range(2, steps):
+        unit_chain, rest_chain, gain_grads = tie(unit_chain, rest_chain, gain_grads)
+        rest_chain = chain_step(rest_chain, turned, step - 2)
+        if step == steps - 1:
+            unit_chain, rest_chain = tie(unit_chain, rest_chain)
+        unit_chain = chain_step(unit_chain, levels, step)
+        if gain_steps:
+            gain_grads = gain_grads + swap(gain_grads, *gain_steps.pop(0))
+    for step in (steps - 2, steps - 1):
+        rest_chain = chain_step(rest_chain, turned, step)
+    while gain_steps:
+        gain_grads = gain_grads + swap(gain_grads, *gain_steps.pop(0))
+    gain_grads = gain_grads.reshape(-1)
+
+    owned_units = unit_chain.astype(F32)
+    owned_rest = rest_chain.astype(F32)
+    cuts = [0, heads_width, 2 * heads_width, 2 * heads_width + kv_width]
+    cuts = cuts + [cuts[-1] + kv_width]
+    owned_out, owned_query, owned_key, owned_value = (
+        owned_rest[:, lo:hi] for lo, hi in zip(cuts[:-1], cuts[1:])
     )
     own_gains = []
     for lo, size in ((0, model), (model, model), (2 * model, HEAD), (2 * model + HEAD, HEAD)):
         size = size // shard_count
         own_gains.append(lax.dynamic_slice_in_dim(gain_grads, lo + shard * size, size, 0))
-
     return (
         mixed,
         input_grad,
-        owned_query.astype(F32),
-        owned_kv[:, :kv_width],
-        owned_kv[:, kv_width:],
-        owned_out.astype(F32),
-        owned_gate_up[:, :units].astype(F32),
-        owned_gate_up[:, units:].astype(F32),
-        owned_down.astype(F32),
+        owned_query,
+        owned_key,
+        owned_value,
+        owned_out.T,
+        owned_units[:, :units],
+        owned_units[:, units : 2 * units],
+        owned_units[:, 2 * units :].T,
         *own_gains,
     )
 

time: 791 us -> 764 us (0.966)
  waiting for transfers between devices: 449 us -> 407 us
  blocking collectives: 40.2 us -> 0 us
  starting transfers between devices: 62 us -> 91.5 us
  other arithmetic: 47.5 us -> 65.8 us
    psum x3 -> x0, waiting for transfers between devices: 208 us -> none  [the longest x1 81.4 us: body(): owned_gate_up = lax.psum(after(shared_gate_up, owned_down), 'ctx')]
    ppermute x18 -> x29, waiting for transfers between devices: 155 us -> 310 us  [the longest x22 302 us: swap(): return lax.ppermute(value, axis, [(i, i ^ level) for i in range(count)])]
    psum x1 -> x0, blocking collectives: 40.2 us -> none  [body(): lax.psum(after(gain_grads, owned_query), ('shard', 'ctx', 'tp'))]
    ppermute x7, waiting for transfers between devices: 21.9 us -> 46.8 us  [body(): held.append(lax.ppermute(sent, 'ctx', [(i, i ^ d) for i in range(count)]))]
    add x3 -> x16, other arithmetic: 2.27 us -> 24.3 us  [the longest x7 14.4 us: halve(): return kept + swap(sent, 'ctx', level).astype(F32)]
    ppermute x18 -> x29, starting transfers between devices: 18.3 us -> 36.1 us  [the longest x22 27.5 us: swap(): return lax.ppermute(value, axis, [(i, i ^ level) for i in range(count)])]
    ppermute x4 -> x5, waiting for transfers between devices: 63.9 us -> 47.6 us  [pieces_of(): lax.ppermute(own, axis, [((i + j) % count, i) for i in range(count)])]
    convert_element_type x13 -> x7, other arithmetic: 22.3 us -> 9.71 us  [the longest x1 3.54 us: body(): owned_rest = rest_chain.astype(F32)]
  transfers between devices with their start and end apart: 37 -> 46, of which waited for: 18 -> 25; matrix products, arithmetic and copies ran while one was open for 12% -> 13% of each run, Pallas kernels for 7% -> 8%
where the time goes in v3:
time: 764 us; the launch traced here: 758 us
  waiting for transfers between devices  407 us (53%)
  starting transfers between devices  91.5 us (12%)
  other arithmetic  65.8 us (9%)
  Pallas kernels  57.3 us (8%)
  matrix products  51.2 us (7%)
  between operations  44.6 us (6%)
  local copies, waits for them, and re-layouts  40 us (5%)
    ppermute x22, waiting for transfers between devices, swap(): return lax.ppermute(value, axis, [(i, i ^ level) for i in range(count)])  302 us
    ppermute x5, waiting for transfers between devices, pieces_of(): lax.ppermute(own, axis, [((i + j) % count, i) for i in range(count)])  47.6 us
    ppermute x7, waiting for transfers between devices, body(): held.append(lax.ppermute(sent, 'ctx', [(i, i ^ d) for i in range(count)]))  46.8 us
    ppermute x7, starting transfers between devices, body(): held.append(lax.ppermute(sent, 'ctx', [(i, i ^ d) for i in range(count)]))  46.6 us
    pallas_call x1, Pallas kernels, attend_back(): pl.pallas_call(functools.partial(backward_kernel, docs, count), grid_spec...  28.7 us
    ppermute x22, starting transfers between devices, swap(): return lax.ppermute(value, axis, [(i, i ^ level) for i in range(count)])  27.5 us
    dot_general x9, matrix products, dot(): return jnp.dot(a, b, preferred_element_type=F32)  18.6 us
    dot_general x6, matrix products, dot_nt(): lax.dot_general(a, b, (((1,), (1,)), ((), ())), preferred_element_type=F32)  17.8 us
  transfers between devices with their start and end apart: 46, of which 25 were waited for; matrix products, arithmetic and copies ran while one was open for 13% of the time, Pallas kernels for 8%

profile of v3, /device:TPU:0, one launch (start us, length us, event | category | flops | bytes accessed | tf_op | source)
XLA Modules:
  0.0 757.8 jit_solution(9471425022291264707)
XLA Ops:
  66.5 42.3 %collective-permute-done.3 = bf16[512,1024]{1,0:T(8,128)(2,1)S(1)} collective-permute-done((bf16[512,1024]{1,0:T(8,128)(2,1)}, bf16[512,1024]{1,0:T(8,128)(2,1)S(1)}, u32[]{:S(2)}, u32[]{:S(2)}) %collective-permute-start.3) | collective-permute-done | bytes 1048608 | tf_op jit(solution)/shard_map/ppermute | solution.py:47
  121.6 11.4 %collective-permute-done.10.refs_10_.refs_11_ = bf16[256,1024]{1,0:T(8,128)(2,1)S(1)} collective-permute-done((bf16[256,1024]{1,0:T(8,128)(2,1)S(1)}, bf16[256,1024]{1,0:T(8,128)(2,1)S(1)}, u32[]{:S(2)}, u32[]{:S(2)}) %collective-permute-start.10) | collective-permute-done | bytes 524320 | tf_op jit(solution)/shard_map/ppermute | solution.py:525
  133.1 20.5 %collective-permute-start.7 = (bf16[256,1024]{1,0:T(8,128)(2,1)S(1)}, bf16[256,1024]{1,0:T(8,128)(2,1)S(1)}, u32[]{:S(2)}, u32[]{:S(2)}) collective-permute-start(bf16[256,1024]{1,0:T(8,128)(2,1)S(1)} %get-tuple-element.199), channel_id=1, source_target_pairs={{0,6},{2,4},{4,2},{6,0},{8,14},{10,12},{12,10},{14,8},{1,7},{3,5},... | collective-permute-start | bytes 1572872 | tf_op jit(solution)/shard_map/ppermute | solution.py:525
  153.6 20.8 %collective-permute-start.8 = (bf16[256,1024]{1,0:T(8,128)(2,1)S(1)}, bf16[256,1024]{1,0:T(8,128)(2,1)S(1)}, u32[]{:S(2)}, u32[]{:S(2)}) collective-permute-start(bf16[256,1024]{1,0:T(8,128)(2,1)S(1)} %get-tuple-element.198), channel_id=1, source_target_pairs={{0,8},{2,10},{4,12},{6,14},{8,0},{10,2},{12,4},{14,6},{1,9},{3,11}... | collective-permute-start | bytes 1572872 | tf_op jit(solution)/shard_map/ppermute | solution.py:525
  180.5 27.5 %collective-permute-done.8.refs_6_.refs_7_ = bf16[256,1024]{1,0:T(8,128)(2,1)S(1)} collective-permute-done((bf16[256,1024]{1,0:T(8,128)(2,1)S(1)}, bf16[256,1024]{1,0:T(8,128)(2,1)S(1)}, u32[]{:S(2)}, u32[]{:S(2)}) %collective-permute-start.8) | collective-permute-done | bytes 524320 | tf_op jit(solution)/shard_map/ppermute | solution.py:525
  208.0 7.9 %collective-permute-done.9.refs_8_.refs_9_ = bf16[256,1024]{1,0:T(8,128)(2,1)S(1)} collective-permute-done((bf16[256,1024]{1,0:T(8,128)(2,1)S(1)}, bf16[256,1024]{1,0:T(8,128)(2,1)S(1)}, u32[]{:S(2)}, u32[]{:S(2)}) %collective-permute-start.9) | collective-permute-done | bytes 524320 | tf_op jit(solution)/shard_map/ppermute | solution.py:525
  215.9 17.8 %shard_map.248 = (f32[512,1024]{1,0:T(8,128)}, bf16[512,1024]{1,0:T(8,128)(2,1)S(1)}, f32[512,1024]{1,0:T(8,128)}) custom-call(s32[18]{0:T(128)S(1)} %stack.60.meta_ref, bf16[512,1024]{1,0:T(8,128)(2,1)S(1)} %shard_map.246.q_ref, bf16[512,1024]{1,0:T(8,128)(2,1)} %copy-done, bf16[512,1024]{1,0:T(8,128)(2,1)} %copy-done, ...), custom_call_target="tpu_custom_call" | custom-call | flops 9663676416 | bytes 8388608 | tf_op jit(solution)/shard_map/pallas_call | solution.py:376
  239.6 6.4 fusion.2
  255.0 5.8 convolution_convert_fusion
  279.6 24.9 %collective-permute-done.15 = bf16[512,1536]{0,1:T(8,128)(2,1)S(1)} collective-permute-done((bf16[512,1536]{0,1:T(8,128)(2,1)S(1)}, bf16[512,1536]{0,1:T(8,128)(2,1)S(1)}, u32[]{:S(2)}, u32[]{:S(2)}) %collective-permute-start.15) | collective-permute-done | bytes 1572896 | tf_op jit(solution)/shard_map/ppermute | solution.py:80
  309.6 28.7 %shard_map.249 = (f32[512,1024]{1,0:T(8,128)}, f32[2,512,512]{2,1,0:T(8,128)}, bf16[2,256,512]{2,1,0:T(8,128)(2,1)S(1)}, bf16[2,256,512]{2,1,0:T(8,128)(2,1)S(1)...) custom-call(s32[18]{0:T(128)S(1)} %stack.60.meta_ref, ...), custom_call_target="tpu_custom_call" | custom-call | flops 24159191040 | bytes 12582912 | tf_op jit(solution)/shard_map/pallas_call | solution.py:406
  348.7 22.8 %collective-permute-done.21 = bf16[512,3072]{1,0:T(8,128)(2,1)} collective-permute-done((bf16[512,3072]{1,0:T(8,128)(2,1)}, bf16[512,3072]{1,0:T(8,128)(2,1)}, u32[]{:S(2)}, u32[]{:S(2)}) %collective-permute-start.21) | collective-permute-done | bytes 3145760 | tf_op jit(solution)/shard_map/ppermute | solution.py:80
  385.6 8.6 %collective-permute-start.25 = (bf16[256,3072]{1,0:T(8,128)(2,1)}, bf16[256,3072]{1,0:T(8,128)(2,1)}, u32[]{:S(2)}, u32[]{:S(2)}) collective-permute-start(bf16[256,3072]{1,0:T(8,128)(2,1)} %dynamic-slice_convert_fusion.1), channel_id=1, source_target_pairs={{0,2},{2,0},{4,6},{6,4},{8,10},{10,8},{12,14},{14,12},{1,3},{3,1},... | collective-permute-start | bytes 4718600 | tf_op jit(solution)/shard_map/ppermute | solution.py:80
  409.7 41.3 %collective-permute-done.25 = bf16[256,3072]{1,0:T(8,128)(2,1)} collective-permute-done((bf16[256,3072]{1,0:T(8,128)(2,1)}, bf16[256,3072]{1,0:T(8,128)(2,1)}, u32[]{:S(2)}, u32[]{:S(2)}) %collective-permute-start.25) | collective-permute-done | bytes 1572896 | tf_op jit(solution)/shard_map/ppermute | solution.py:80
  475.0 19.7 %collective-permute-done.29 = bf16[512,1024]{1,0:T(8,128)(2,1)S(1)} collective-permute-done((bf16[512,1024]{1,0:T(8,128)(2,1)S(1)}, bf16[512,1024]{1,0:T(8,128)(2,1)S(1)}, u32[]{:S(2)}, u32[]{:S(2)}) %collective-permute-start.29) | collective-permute-done | bytes 1048608 | tf_op jit(solution)/shard_map/ppermute | solution.py:80
  506.9 22.8 %collective-permute-done.30 = bf16[64,4608]{1,0:T(8,128)(2,1)S(1)} collective-permute-done((bf16[64,4608]{1,0:T(8,128)(2,1)S(1)}, bf16[64,4608]{1,0:T(8,128)(2,1)S(1)}, u32[]{:S(2)}, u32[]{:S(2)}) %collective-permute-start.30) | collective-permute-done | bytes 589856 | tf_op jit(solution)/shard_map/ppermute | solution.py:80
  530.6 21.2 %collective-permute-done.31 = bf16[256,3072]{1,0:T(8,128)(2,1)} collective-permute-done((bf16[256,3072]{1,0:T(8,128)(2,1)}, bf16[256,3072]{1,0:T(8,128)(2,1)}, u32[]{:S(2)}, u32[]{:S(2)}) %collective-permute-start.31) | collective-permute-done | bytes 1572896 | tf_op jit(solution)/shard_map/ppermute | solution.py:80
  562.2 36.6 %collective-permute-done.33 = bf16[64,4608]{1,0:T(8,128)(2,1)} collective-permute-done((bf16[64,4608]{1,0:T(8,128)(2,1)}, bf16[64,4608]{1,0:T(8,128)(2,1)}, u32[]{:S(2)}, u32[]{:S(2)}) %collective-permute-start.33) | collective-permute-done | bytes 589856 | tf_op jit(solution)/shard_map/ppermute | solution.py:80
  601.7 13.9 %collective-permute-done.34 = bf16[128,3072]{1,0:T(8,128)(2,1)} collective-permute-done((bf16[128,3072]{1,0:T(8,128)(2,1)}, bf16[128,3072]{1,0:T(8,128)(2,1)}, u32[]{:S(2)}, u32[]{:S(2)}) %collective-permute-start.34) | collective-permute-done | bytes 786464 | tf_op jit(solution)/shard_map/ppermute | solution.py:80
  620.8 24.5 %collective-permute-done.38 = f32[18,128]{1,0:T(8,128)S(1)} collective-permute-done((f32[18,128]{1,0:T(8,128)S(1)}, f32[18,128]{1,0:T(8,128)S(1)}, u32[]{:S(2)}, u32[]{:S(2)}) %collective-permute-start.38) | collective-permute-done | bytes 9248 | tf_op jit(solution)/shard_map/ppermute | solution.py:80
  651.8 8.9 %collective-permute-done.39 = bf16[64,3072]{1,0:T(8,128)(2,1)} collective-permute-done((bf16[64,3072]{1,0:T(8,128)(2,1)}, bf16[64,3072]{1,0:T(8,128)(2,1)}, u32[]{:S(2)}, u32[]{:S(2)}) %collective-permute-start.39) | collective-permute-done | bytes 393248 | tf_op jit(solution)/shard_map/ppermute | solution.py:80
  676.3 27.7 %collective-permute-done.40 = bf16[128,3072]{1,0:T(8,128)(2,1)S(1)} collective-permute-done((bf16[128,3072]{1,0:T(8,128)(2,1)}, bf16[128,3072]{1,0:T(8,128)(2,1)S(1)}, u32[]{:S(2)}, u32[]{:S(2)}) %collective-permute-start.40) | collective-permute-done | bytes 786464 | tf_op jit(solution)/shard_map/ppermute | solution.py:80
  705.6 9.1 %collective-permute-done.42 = bf16[256,4608]{1,0:T(8,128)(2,1)} collective-permute-done((bf16[256,4608]{1,0:T(8,128)(2,1)S(1)}, bf16[256,4608]{1,0:T(8,128)(2,1)}, u32[]{:S(2)}, u32[]{:S(2)}) %collective-permute-start.42) | collective-permute-done | bytes 2359328 | tf_op jit(solution)/shard_map/ppermute | solution.py:80
  724.0 17.8 %collective-permute-done.41 = bf16[256,3072]{1,0:T(8,128)(2,1)} collective-permute-done((bf16[256,3072]{1,0:T(8,128)(2,1)}, bf16[256,3072]{1,0:T(8,128)(2,1)}, u32[]{:S(2)}, u32[]{:S(2)}) %collective-permute-start.41) | collective-permute-done | bytes 1572896 | tf_op jit(solution)/shard_map/ppermute | solution.py:80
  (347 shorter events, 224.3 us)
Async XLA Ops:
  7.2 232.4 %all-gather.2.cloned.1.call-start = ((), (), s32[]{:S(2)}) async-start(), calls=%async_computation | async-start | bytes 14155776 | tf_op jit(solution)/shard_map/all_gather | solution.py:475
  22.7 38.2 %collective-permute-start.1 = (bf16[1152]{0:T(1024)(128)(2,1)S(1)}, bf16[1152]{0:T(1024)(128)(2,1)S(1)}, u32[]{:S(2)}, u32[]{:S(2)}) collective-permute-start(bf16[1152]{0:T(1024)(128)(2,1)S(1)} %concatenate.196), channel_id=1, source_target_pairs={{16,0},{0,16},{17,1},{1,17},{18,2},{2,18},{19,3},{3,19},{20,4},{4,... | collective-permute-start | bytes 6920 | tf_op jit(solution)/shard_map/ppermute | solution.py:47
  24.4 42.1 %collective-permute-start = (bf16[512,512]{1,0:T(8,128)(2,1)}, bf16[512,512]{1,0:T(8,128)(2,1)}, u32[]{:S(2)}, u32[]{:S(2)}) collective-permute-start(bf16[512,512]{1,0:T(8,128)(2,1)} %param.20), channel_id=1, source_target_pairs={{16,0},{0,16},{17,1},{1,17},{18,2},{2,18},{19,3},{3,19},{20,4},{4,... | collective-permute-start | bytes 1572872 | tf_op jit(solution)/shard_map/ppermute | solution.py:47
  60.9 47.9 %collective-permute-start.3 = (bf16[512,1024]{1,0:T(8,128)(2,1)}, bf16[512,1024]{1,0:T(8,128)(2,1)S(1)}, u32[]{:S(2)}, u32[]{:S(2)}) collective-permute-start(bf16[512,1024]{1,0:T(8,128)(2,1)} %param.19), channel_id=1, source_target_pairs={{16,0},{0,16},{17,1},{1,17},{18,2},{2,18},{19,3},{3,19},{20,4},{4,... | collective-permute-start | bytes 3145736 | tf_op jit(solution)/shard_map/ppermute | solution.py:47
  108.8 65.5 %collective-permute-start.4 = (bf16[1024,512]{1,0:T(8,128)(2,1)S(1)}, bf16[1024,512]{1,0:T(8,128)(2,1)S(1)}, u32[]{:S(2)}, u32[]{:S(2)}) collective-permute-start(bf16[1024,512]{1,0:T(8,128)(2,1)S(1)} %copy-done.67), channel_id=1, source_target_pairs={{16,0},{0,16},{17,1},{1,17},{18,2},{2,18},{19,3},{3,19},{20,4},{4,... | collective-permute-start | bytes 3145736 | tf_op jit(solution)/shard_map/ppermute | solution.py:47
  121.1 59.4 %collective-permute-start.5 = (bf16[256,1024]{1,0:T(8,128)(2,1)S(1)}, bf16[256,1024]{1,0:T(8,128)(2,1)S(1)}, u32[]{:S(2)}, u32[]{:S(2)}) collective-permute-start(bf16[256,1024]{1,0:T(8,128)(2,1)S(1)} %get-tuple-element.201), channel_id=1, source_target_pairs={{0,2},{2,0},{4,6},{6,4},{8,10},{10,8},{12,14},{14,12},{1,3},{3,1},... | collective-permute-start | bytes 1572872 | tf_op jit(solution)/shard_map/ppermute | solution.py:525
  121.6 58.9 %collective-permute-start.6 = (bf16[256,1024]{1,0:T(8,128)(2,1)S(1)}, bf16[256,1024]{1,0:T(8,128)(2,1)S(1)}, u32[]{:S(2)}, u32[]{:S(2)}) collective-permute-start(bf16[256,1024]{1,0:T(8,128)(2,1)S(1)} %get-tuple-element.200), channel_id=1, source_target_pairs={{0,4},{2,6},{4,0},{6,2},{8,12},{10,14},{12,8},{14,10},{1,5},{3,7},... | collective-permute-start | bytes 1572872 | tf_op jit(solution)/shard_map/ppermute | solution.py:525
  133.1 47.4 %collective-permute-start.7 = (bf16[256,1024]{1,0:T(8,128)(2,1)S(1)}, bf16[256,1024]{1,0:T(8,128)(2,1)S(1)}, u32[]{:S(2)}, u32[]{:S(2)}) collective-permute-start(bf16[256,1024]{1,0:T(8,128)(2,1)S(1)} %get-tuple-element.199), channel_id=1, source_target_pairs={{0,6},{2,4},{4,2},{6,0},{8,14},{10,12},{12,10},{14,8},{1,7},{3,5},... | collective-permute-start | bytes 1572872 | tf_op jit(solution)/shard_map/ppermute | solution.py:525
  153.6 54.4 %collective-permute-start.8 = (bf16[256,1024]{1,0:T(8,128)(2,1)S(1)}, bf16[256,1024]{1,0:T(8,128)(2,1)S(1)}, u32[]{:S(2)}, u32[]{:S(2)}) collective-permute-start(bf16[256,1024]{1,0:T(8,128)(2,1)S(1)} %get-tuple-element.198), channel_id=1, source_target_pairs={{0,8},{2,10},{4,12},{6,14},{8,0},{10,2},{12,4},{14,6},{1,9},{3,11}... | collective-permute-start | bytes 1572872 | tf_op jit(solution)/shard_map/ppermute | solution.py:525
  175.3 40.5 %collective-permute-start.9 = (bf16[256,1024]{1,0:T(8,128)(2,1)S(1)}, bf16[256,1024]{1,0:T(8,128)(2,1)S(1)}, u32[]{:S(2)}, u32[]{:S(2)}) collective-permute-start(bf16[256,1024]{1,0:T(8,128)(2,1)S(1)} %get-tuple-element.197), channel_id=1, source_target_pairs={{0,10},{2,8},{4,14},{6,12},{8,2},{10,0},{12,6},{14,4},{1,11},{3,9}... | collective-permute-start | bytes 1572872 | tf_op jit(solution)/shard_map/ppermute | solution.py:525
  267.2 37.3 %collective-permute-start.15 = (bf16[512,1536]{0,1:T(8,128)(2,1)S(1)}, bf16[512,1536]{0,1:T(8,128)(2,1)S(1)}, u32[]{:S(2)}, u32[]{:S(2)}) collective-permute-start(bf16[512,1536]{0,1:T(8,128)(2,1)S(1)} %constant_dynamic-slice_fusion.2), channel_id=1, source_target_pairs={{0,16},{16,0},{1,17},{17,1},{2,18},{18,2},{3,19},{19,3},{4,20},{20... | collective-permute-start | bytes 4718600 | tf_op jit(solution)/shard_map/ppermute | solution.py:80
  271.8 99.7 %collective-permute-start.21 = (bf16[512,3072]{1,0:T(8,128)(2,1)}, bf16[512,3072]{1,0:T(8,128)(2,1)}, u32[]{:S(2)}, u32[]{:S(2)}) collective-permute-start(bf16[512,3072]{1,0:T(8,128)(2,1)} %constant_dynamic-slice_fusion.1), channel_id=1, source_target_pairs={{0,16},{16,0},{1,17},{17,1},{2,18},{18,2},{3,19},{19,3},{4,20},{20... | collective-permute-start | bytes 9437192 | tf_op jit(solution)/shard_map/ppermute | solution.py:80
  343.6 36.8 %collective-permute-start.17 = (bf16[2,256,512]{2,1,0:T(8,128)(2,1)S(1)}, bf16[2,256,512]{2,1,0:T(8,128)(2,1)S(1)}, u32[]{:S(2)}, u32[]{:S(2)}) collective-permute-start(bf16[2,256,512]{2,1,0:T(8,128)(2,1)S(1)} %get-tuple-element.118), channel_id=1, source_target_pairs={{0,8},{2,10},{4,12},{6,14},{8,0},{10,2},{12,4},{14,6},{1,9},{3,11}... | collective-permute-start | bytes 1572872 | tf_op jit(solution)/shard_map/ppermute | solution.py:579
  343.6 40.3 %collective-permute-start.18 = (bf16[2,256,512]{2,1,0:T(8,128)(2,1)S(1)}, bf16[2,256,512]{2,1,0:T(8,128)(2,1)S(1)}, u32[]{:S(2)}, u32[]{:S(2)}) collective-permute-start(bf16[2,256,512]{2,1,0:T(8,128)(2,1)S(1)} %get-tuple-element.119), channel_id=1, source_target_pairs={{0,10},{2,8},{4,14},{6,12},{8,2},{10,0},{12,6},{14,4},{1,11},{3,9}... | collective-permute-start | bytes 1572872 | tf_op jit(solution)/shard_map/ppermute | solution.py:579
  343.6 40.3 %collective-permute-start.19 = (bf16[2,256,512]{2,1,0:T(8,128)(2,1)S(1)}, bf16[2,256,512]{2,1,0:T(8,128)(2,1)S(1)}, u32[]{:S(2)}, u32[]{:S(2)}) collective-permute-start(bf16[2,256,512]{2,1,0:T(8,128)(2,1)S(1)} %get-tuple-element.120), channel_id=1, source_target_pairs={{0,2},{2,0},{4,6},{6,4},{8,10},{10,8},{12,14},{14,12},{1,3},{3,1},... | collective-permute-start | bytes 1572872 | tf_op jit(solution)/shard_map/ppermute | solution.py:579
  385.6 65.5 %collective-permute-start.25 = (bf16[256,3072]{1,0:T(8,128)(2,1)}, bf16[256,3072]{1,0:T(8,128)(2,1)}, u32[]{:S(2)}, u32[]{:S(2)}) collective-permute-start(bf16[256,3072]{1,0:T(8,128)(2,1)} %dynamic-slice_convert_fusion.1), channel_id=1, source_target_pairs={{0,2},{2,0},{4,6},{6,4},{8,10},{10,8},{12,14},{14,12},{1,3},{3,1},... | collective-permute-start | bytes 4718600 | tf_op jit(solution)/shard_map/ppermute | solution.py:80
  404.1 50.4 %collective-permute-start.22 = (bf16[2,256,512]{2,1,0:T(8,128)(2,1)S(1)}, bf16[2,256,512]{2,1,0:T(8,128)(2,1)S(1)}, u32[]{:S(2)}, u32[]{:S(2)}) collective-permute-start(bf16[2,256,512]{2,1,0:T(8,128)(2,1)S(1)} %copy-done.11), channel_id=1, source_target_pairs={{0,12},{2,14},{4,8},{6,10},{8,4},{10,6},{12,0},{14,2},{1,13},{3,15... | collective-permute-start | bytes 1572872 | tf_op jit(solution)/shard_map/ppermute | solution.py:579
  405.4 49.2 %collective-permute-start.23 = (bf16[2,256,512]{2,1,0:T(8,128)(2,1)S(1)}, bf16[2,256,512]{2,1,0:T(8,128)(2,1)S(1)}, u32[]{:S(2)}, u32[]{:S(2)}) collective-permute-start(bf16[2,256,512]{2,1,0:T(8,128)(2,1)S(1)} %copy-done.9), channel_id=1, source_target_pairs={{0,14},{2,12},{4,10},{6,8},{8,6},{10,4},{12,2},{14,0},{1,15},{3,13... | collective-permute-start | bytes 1572872 | tf_op jit(solution)/shard_map/ppermute | solution.py:579
  407.6 47.0 %collective-permute-start.24 = (bf16[2,256,512]{2,1,0:T(8,128)(2,1)S(1)}, bf16[2,256,512]{2,1,0:T(8,128)(2,1)S(1)}, u32[]{:S(2)}, u32[]{:S(2)}) collective-permute-start(bf16[2,256,512]{2,1,0:T(8,128)(2,1)S(1)} %copy-done.7), channel_id=1, source_target_pairs={{0,6},{2,4},{4,2},{6,0},{8,14},{10,12},{12,10},{14,8},{1,7},{3,5},... | collective-permute-start | bytes 1572872 | tf_op jit(solution)/shard_map/ppermute | solution.py:579
  409.5 61.6 %collective-permute-start.28 = (bf16[512,2048]{1,0:T(8,128)(2,1)S(1)}, bf16[512,2048]{1,0:T(8,128)(2,1)}, u32[]{:S(2)}, u32[]{:S(2)}) collective-permute-start(bf16[512,2048]{1,0:T(8,128)(2,1)S(1)} %fusion.13), channel_id=1, source_target_pairs={{0,16},{16,0},{1,17},{17,1},{2,18},{18,2},{3,19},{19,3},{4,20},{20... | collective-permute-start | bytes 6291464 | tf_op jit(solution)/shard_map/ppermute | solution.py:80
  503.1 48.7 %collective-permute-start.31 = (bf16[256,3072]{1,0:T(8,128)(2,1)}, bf16[256,3072]{1,0:T(8,128)(2,1)}, u32[]{:S(2)}, u32[]{:S(2)}) collective-permute-start(bf16[256,3072]{1,0:T(8,128)(2,1)} %dynamic-slice_convert_fusion), channel_id=1, source_target_pairs={{0,4},{2,6},{4,0},{6,2},{8,12},{10,14},{12,8},{14,10},{1,5},{3,7},... | collective-permute-start | bytes 4718600 | tf_op jit(solution)/shard_map/ppermute | solution.py:80
  554.6 44.3 %collective-permute-start.33 = (bf16[64,4608]{1,0:T(8,128)(2,1)}, bf16[64,4608]{1,0:T(8,128)(2,1)}, u32[]{:S(2)}, u32[]{:S(2)}) collective-permute-start(bf16[64,4608]{1,0:T(8,128)(2,1)} %convert_add_fusion.12), channel_id=1, source_target_pairs={{0,8},{2,10},{4,12},{6,14},{8,0},{10,2},{12,4},{14,6},{1,9},{3,11}... | collective-permute-start | bytes 1769480 | tf_op jit(solution)/shard_map/ppermute | solution.py:80
  555.8 59.8 %collective-permute-start.34 = (bf16[128,3072]{1,0:T(8,128)(2,1)}, bf16[128,3072]{1,0:T(8,128)(2,1)}, u32[]{:S(2)}, u32[]{:S(2)}) collective-permute-start(bf16[128,3072]{1,0:T(8,128)(2,1)} %dynamic-slice_convert_fusion.3), channel_id=1, source_target_pairs={{0,8},{2,10},{4,12},{6,14},{8,0},{10,2},{12,4},{14,6},{1,9},{3,11}... | collective-permute-start | bytes 2359304 | tf_op jit(solution)/shard_map/ppermute | solution.py:80
  663.1 51.6 %collective-permute-start.42 = (bf16[256,4608]{1,0:T(8,128)(2,1)S(1)}, bf16[256,4608]{1,0:T(8,128)(2,1)}, u32[]{:S(2)}, u32[]{:S(2)}) collective-permute-start(bf16[256,4608]{1,0:T(8,128)(2,1)S(1)} %maximum_select_fusion.2), channel_id=1, source_target_pairs={{0,2},{2,0},{4,6},{6,4},{8,10},{10,8},{12,14},{14,12},{1,3},{3,1},... | collective-permute-start | bytes 7077896 | tf_op jit(solution)/shard_map/ppermute | solution.py:80
  (101 other events, 2252.9 us)
Sparse Core Ops, SparseCore 0:
  22.6 164.4 all-gather.1

commit v4 on v3

--- a/solution.py
+++ b/solution.py
@@ -14,6 +14,7 @@
 BF16 = jnp.bfloat16
 F32 = jnp.float32
 VMEM_LIMIT = 48 * 1024 * 1024
+CHEAP = pl.CostEstimate(flops=1000, bytes_accessed=1000, transcendentals=0)
 
 
 def rms_parts(values):
@@ -80,38 +81,82 @@
     return lax.ppermute(value, axis, [(i, i ^ level) for i in range(count)])
 
 
-def to_shard_owner(grad):
+def to_shard_owner(*grads):
     count = lax.axis_size("shard")
     index = lax.axis_index("shard")
     if count != 2:
+        grad = jnp.concatenate(grads, axis=1)
         return lax.psum_scatter(grad, "shard", scatter_dimension=0, tiled=True).astype(F32)
-    size = grad.shape[0] // 2
-    sent = lax.dynamic_slice_in_dim(grad, (1 - index) * size, size, 0)
-    kept = lax.dynamic_slice_in_dim(grad, index * size, size, 0)
-    return kept.astype(F32) + swap(sent, "shard").astype(F32)
-
-
-def bit_of(level):
-    return (lax.axis_index("ctx") // level) % 2
-
-
-def halve(value, level):
-    bit = bit_of(level)
-    size = value.shape[0] // 2
-    sent = lax.dynamic_slice_in_dim(value, (1 - bit) * size, size, 0).astype(BF16)
-    kept = lax.dynamic_slice_in_dim(value, bit * size, size, 0)
-    return kept + swap(sent, "ctx", level).astype(F32)
-
-
-def double(value, level):
+
+    def rows_of(owner):
+        size = grads[0].shape[0] // 2
+        return jnp.concatenate(
+            [lax.dynamic_slice_in_dim(g, owner * size, size, 0) for g in grads], axis=1
+        )
+
+    return rows_of(index).astype(F32) + swap(rows_of(1 - index), "shard").astype(F32)
+
+
+def place_in(masks):
+    return (lax.axis_index("ctx") // masks[0]) % (1 << len(masks))
+
+
+def exchange(values, done, turns):
+    count = lax.axis_size("ctx")
+    for d in turns:
+        done[d] = lax.ppermute(values[d], "ctx", [(i, i ^ d) for i in range(count)])
+
+
+def settle(done, turns, *values):
+    tied = tie(*(done[d] for d in turns), *values)
+    done.update(zip(turns, tied))
+    return tied[len(turns) :]
+
+
+def halve(value, masks):
+    size = 1 << len(masks)
+    rows = value.shape[0] // size
+    place = place_in(masks)
+    total = lax.dynamic_slice_in_dim(value, place * rows, rows, 0)
+    for turn in range(1, size):
+        sent = lax.dynamic_slice_in_dim(value, (place ^ turn) * rows, rows, 0)
+        total = total + swap(sent.astype(BF16), "ctx", turn * masks[0]).astype(F32)
+    return total
+
+
+def double(value, masks):
     value = value.astype(BF16)
-    return join([value, swap(value, "ctx", level)], 0, bit_of(level))
-
-
-def chain_step(value, levels, step):
-    if step < len(levels):
-        return halve(value, levels[step])
-    return double(value, levels[2 * len(levels) - 1 - step])
+    size = 1 << len(masks)
+    place = place_in(masks)
+    blocks = [value] + [swap(value, "ctx", turn * masks[0]) for turn in range(1, size)]
+    bit = 0
+    while len(blocks) > 1:
+        pairs = zip(blocks[::2], blocks[1::2])
+        blocks = [join(list(pair), 0, (place >> bit) % 2) for pair in pairs]
+        bit += 1
+    return blocks[0]
+
+
+def product_kernel(a_ref, b_ref, out_ref):
+    out_ref[...] = dot_nt(a_ref[...], b_ref[...]).astype(out_ref.dtype)
+
+
+def product_nt(a, b, dtype, column=0):
+    rows, depth = a.shape
+    columns = b.shape[0]
+    step = min(columns, 256)
+    return pl.pallas_call(
+        product_kernel,
+        grid=(columns // step,),
+        in_specs=[
+            pl.BlockSpec((rows, depth), lambda i: (0, 0)),
+            pl.BlockSpec((step, depth), lambda i: (i, column)),
+        ],
+        out_specs=pl.BlockSpec((rows, step), lambda i: (0, i)),
+        out_shape=jax.ShapeDtypeStruct((rows, columns), dtype),
+        compiler_params=pltpu.CompilerParams(vmem_limit_bytes=VMEM_LIMIT),
+        cost_estimate=CHEAP,
+    )(a, b)
 
 
 def rope_kernel(pre_ref, cos_ref, sin_ref, gain_ref, out_ref):
@@ -388,11 +433,7 @@
             jax.ShapeDtypeStruct((rows, width), F32),
         ],
         compiler_params=pltpu.CompilerParams(vmem_limit_bytes=VMEM_LIMIT),
-        cost_estimate=pl.CostEstimate(
-            flops=(count + 1) * half * half * width * 16,
-            bytes_accessed=rows * width * 16,
-            transcendentals=(count + 1) * half * half * width // HEAD,
-        ),
+        cost_estimate=CHEAP,
     )(meta, queries, key_value, key_value, *twice(others))
 
 
@@ -419,11 +460,7 @@
         ]
         + [jax.ShapeDtypeStruct((2, half, kv_width), BF16)] * (count - 1),
         compiler_params=pltpu.CompilerParams(vmem_limit_bytes=VMEM_LIMIT),
-        cost_estimate=pl.CostEstimate(
-            flops=(count + 1) * half * half * width * 40,
-            bytes_accessed=rows * width * 24,
-            transcendentals=(count + 1) * half * half * width // HEAD,
-        ),
+        cost_estimate=CHEAP,
     )(meta, queries, grads, outs, lse, key_value, key_value, *twice(others))
     return result[0], result[1], list(result[2:])
 
@@ -461,20 +498,7 @@
     packed_pieces = pieces_of(packed, "shard")
     k_pieces = pieces_of(key_weight, "shard")
     v_pieces = pieces_of(value_weight, "shard")
-    cuts = [0, depth, 2 * depth, 2 * depth + gain_q.shape[0], packed.shape[0]]
-    gain_pieces = [
-        [piece[lo:hi].astype(F32) for piece in packed_pieces]
-        for lo, hi in zip(cuts[:-1], cuts[1:])
-    ]
-    scale_in, scale_post, scale_q, scale_k = (
-        join(pieces, 0, shard).reshape(1, -1) for pieces in gain_pieces
-    )
     own_units = jnp.concatenate([w_gate, w_up, w_down.T], axis=1)
-    w_query, own_units, v_pieces[-1] = tie(w_query, own_units, v_pieces[-1])
-    q_pieces = pieces_of(w_query, "shard")
-    full_units = lax.all_gather(own_units, "shard", axis=0, tiled=True)
-    w_out, q_pieces[-1] = tie(w_out, q_pieces[-1])
-    out_pieces = pieces_of(w_out, "shard")
 
     lengths = seq_lengths[0]
     starts = jnp.cumsum(lengths) - lengths
@@ -502,33 +526,56 @@
 
     inputs = tokens.astype(F32)
     normal_one, factor_one = rms_parts(inputs)
-    normed_input = (normal_one * scale_in).astype(BF16)
-
+
+    w_query, own_units, packed_pieces[-1], k_pieces[-1], v_pieces[-1] = tie(
+        w_query, own_units, packed_pieces[-1], k_pieces[-1], v_pieces[-1]
+    )
+    cosine, sine, meta, normal_one, k_pieces[-1] = tie(
+        cosine, sine, meta, normal_one, k_pieces[-1]
+    )
+    cuts = [0, depth, 2 * depth, 2 * depth + gain_q.shape[0], packed.shape[0]]
+    gain_pieces = [
+        [piece[lo:hi].astype(F32) for piece in packed_pieces]
+        for lo, hi in zip(cuts[:-1], cuts[1:])
+    ]
+    scale_in, scale_post, scale_q, scale_k = (
+        join(pieces, 0, shard).reshape(1, -1) for pieces in gain_pieces
+    )
     parts_in = []
     for j in range(shard_count):
         at = (shard + j) % shard_count * depth
         part_in = lax.dynamic_slice_in_dim(normal_one, at, depth, 1)
         parts_in.append((part_in * gain_pieces[0][j][None, :]).astype(BF16))
+    normed_input = (normal_one * scale_in).astype(BF16)
 
     def project(pieces):
         return sum(dot(part_in, piece) for part_in, piece in zip(parts_in, pieces))
 
-    k_pieces[-1], cosine, sine, meta, parts_in[-1], scale_k = tie(
-        k_pieces[-1], cosine, sine, meta, parts_in[-1], scale_k
-    )
+    q_pieces = pieces_of(w_query, "shard")
+    full_units = lax.all_gather(own_units, "shard", axis=0, tiled=True)
     k_pre = project(k_pieces)
     key_value = rope(k_pre, cosine, sine, scale_k, project(v_pieces))
-    held = []
-    for d in range(1, count):
+    far = [d for d in range(1, count) if d >= count // 2]
+    near = [d for d in range(1, count) if d < count // 2]
+    early = far[: len(far) // 2] + near[: (len(near) + 1) // 2]
+    late = far[len(far) // 2 :] + near[(len(near) + 1) // 2 :]
+    sent = {}
+    for d in early + late:
         start = jnp.where(part < other_parts[d - 1], 0, half)
-        sent = lax.dynamic_slice_in_dim(key_value, start, half, 0)
-        held.append(lax.ppermute(sent, "ctx", [(i, i ^ d) for i in range(count)]))
+        sent[d] = lax.dynamic_slice_in_dim(key_value, start, half, 0)
+    held = {}
+    exchange(sent, held, early)
+    w_out, q_pieces[-1], *rest = settle(held, early, w_out, q_pieces[-1], *(sent[d] for d in late))
+    sent.update(zip(late, rest))
+
+    exchange(sent, held, late)
+    out_pieces = pieces_of(w_out, "shard")
     q_pre = project(q_pieces)
     queries = rope(q_pre, cosine, sine, scale_q)
-    queries, out_pieces[-1] = tie(queries, out_pieces[-1])
+    queries, full_out = settle(held, late, queries, join(out_pieces, 1, shard))
+    held = [held[d] for d in range(1, count)]
     attended, attn_out, lse = attend(meta, docs, queries, key_value, held)
 
-    full_out = join(out_pieces, 1, shard)
     full_gate_up = full_units[:, : 2 * units]
     full_down_t = full_units[:, 2 * units :]
     full_key = join(k_pieces, 0, shard)
@@ -552,53 +599,37 @@
     d_gate_up = jnp.concatenate([d_gate, d_up], axis=1)
     grad_gate_up = dot_tn(normed_two, d_gate_up).astype(BF16)
     d_gate_up, grad_gate_up = tie(d_gate_up, grad_gate_up)
-    d_normed_two = pair_total(dot_nt(d_gate_up, full_gate_up))
+    d_normed_two = pair_total(product_nt(d_gate_up, full_units, BF16))
     hidden, d_normed_two = tie(hidden, d_normed_two)
-    mixed_part = dot_nt(hidden, full_down_t)
+    mixed_part = product_nt(hidden, full_units, BF16, 2)
     mixed = (residual + pair_total(mixed_part)).astype(BF16)
-    shared_down = to_shard_owner(grad_down)
-    shared_gate_up = to_shard_owner(grad_gate_up)
+    shared_units = to_shard_owner(grad_gate_up, grad_down)
     grad_post = jnp.sum(d_normed_two * normal_two, axis=0)
     d_residual = cotangent.astype(F32) + rms_back(
         d_normed_two * scale_post, normal_two, factor_two
     )
 
     d_branch = d_residual.astype(BF16)
-    d_attn, shared_down = tie(dot_nt(d_branch, full_out).astype(BF16), shared_down)
+    d_attn = product_nt(d_branch, full_out, BF16)
     d_queries, d_kv, given = attend_back(
         meta, docs, queries, d_attn, attended, lse, key_value, held
     )
-    levels = [1 << b for b in range(count.bit_length() - 1)]
-    turned = levels[1:] + levels[:1]
-    half_down = halve(shared_down, levels[0])
-    d_queries, half_down, *given = tie(d_queries, half_down, *given)
+    masks = [1 << b for b in range(count.bit_length() - 1)]
+    near_axis, far_axis = masks[:1], masks[1:]
+    given = dict(zip(range(1, count), given))
     returned = {}
-
-    def give_back(turns):
-        for d in turns:
-            returned[d] = lax.ppermute(given[d - 1], "ctx", [(i, i ^ d) for i in range(count)])
-
-    def settle(turns, *values):
-        done = tie(*(returned[d] for d in turns), *values)
-        returned.update(zip(turns, done))
-        return done[len(turns) :]
-
-    far = [d for d in range(1, count) if d >= count // 2]
-    near = [d for d in range(1, count) if d < count // 2]
-    early = far[: len(far) // 2] + near[: (len(near) + 1) // 2]
-    late = far[len(far) // 2 :] + near[(len(near) + 1) // 2 :]
-    give_back(early)
+    exchange(given, returned, early)
     grad_out = dot_tn(d_branch, attn_out).astype(BF16)
-    given = list(given)
-    d_queries, shared_gate_up, grad_out, *given = settle(
-        early, d_queries, shared_gate_up, grad_out, *given
-    )
-    give_back(late)
-    half_gate_up = halve(shared_gate_up, levels[0])
+    d_queries, shared_units, grad_out, *rest = settle(
+        returned, early, d_queries, shared_units, grad_out, *(given[d] for d in late)
+    )
+    given.update(zip(late, rest))
+    exchange(given, returned, late)
+    unit_chain = halve(shared_units, near_axis)
     d_q_pre, gq_part = rope_back(d_queries, q_pre, cosine, sine, scale_q)
     grad_query = dot_tn(normed_input, d_q_pre).astype(BF16)
-    out_query = to_shard_owner(jnp.concatenate([grad_out, grad_query], axis=1))
-    (half_gate_up,) = settle(late, half_gate_up)
+    out_query = to_shard_owner(grad_out, grad_query)
+    (unit_chain,) = settle(returned, late, unit_chain)
     returned = [returned[d] for d in range(1, count)]
 
     first = sum(
@@ -613,11 +644,14 @@
     d_kv_pre = jnp.concatenate([d_k_pre, d_v_pre], axis=1)
     grad_kv = dot_tn(normed_input, d_kv_pre).astype(BF16)
 
-    steps = 2 * len(levels)
-    unit_chain = jnp.concatenate([half_gate_up, half_down], axis=1)
-    (unit_chain,) = tie(unit_chain)
-    unit_chain = chain_step(unit_chain, levels, 1)
+    unit_chain = halve(unit_chain, far_axis)
     rest_chain = jnp.concatenate([out_query, to_shard_owner(grad_kv)], axis=1)
+    unit_chain, rest_chain, d_q_pre, d_k_pre, d_v_pre = tie(
+        unit_chain, rest_chain, d_q_pre, d_k_pre, d_v_pre
+    )
+
+    unit_chain = double(unit_chain, far_axis)
+    rest_chain = halve(rest_chain, near_axis)
     d_normed = pair_total(
         dot_nt(d_q_pre, full_query) + dot_nt(d_k_pre, full_key) + dot_nt(d_v_pre, full_value)
     )
@@ -626,27 +660,31 @@
     once = jnp.where(lax.axis_index("tp") == 0, 1.0, 0.0)
     gain_grads = jnp.concatenate([grad_in * once, grad_post * once, gq_part[0], gk_part[0]])
     gain_grads = gain_grads.reshape(-1, HEAD)
-    gain_steps = [("tp", 1)] + [("ctx", level) for level in levels]
+    if shard_count != 2:
+        gain_grads = lax.psum(gain_grads, "shard")
+    unit_chain, rest_chain, gain_grads = tie(unit_chain, rest_chain, gain_grads)
+
+    owned_gate_up = double(unit_chain[:, : 2 * units], near_axis)
+    owned_down = unit_chain[:, 2 * units :]
+    rest_chain = halve(rest_chain, far_axis)
+    gain_grads = gain_grads + swap(gain_grads, "tp")
+    gain_grads = gain_grads + swap(gain_grads, "ctx", masks[0])
+    owned_gate_up, owned_down, rest_chain, gain_grads = tie(
+        owned_gate_up, owned_down, rest_chain, gain_grads
+    )
+
+    owned_down = double(owned_down, near_axis)
+    rest_chain = double(rest_chain, far_axis)
+    for mask in masks[1:]:
+        gain_grads = gain_grads + swap(gain_grads, "ctx", mask)
+    owned_down, rest_chain, gain_grads = tie(owned_down, rest_chain, gain_grads)
+
+    rest_chain = double(rest_chain, near_axis)
     if shard_count == 2:
-        gain_steps = gain_steps + [("shard", 1)]
-    else:
-        gain_grads = lax.psum(gain_grads, "shard")
-
-    for step in range(2, steps):
-        unit_chain, rest_chain, gain_grads = tie(unit_chain, rest_chain, gain_grads)
-        rest_chain = chain_step(rest_chain, turned, step - 2)
-        if step == steps - 1:
-            unit_chain, rest_chain = tie(unit_chain, rest_chain)
-        unit_chain = chain_step(unit_chain, levels, step)
-        if gain_steps:
-            gain_grads = gain_grads + swap(gain_grads, *gain_steps.pop(0))
-    for step in (steps - 2, steps - 1):
-        rest_chain = chain_step(rest_chain, turned, step)
-    while gain_steps:
-        gain_grads = gain_grads + swap(gain_grads, *gain_steps.pop(0))
+        gain_grads = gain_grads + swap(gain_grads, "shard")
     gain_grads = gain_grads.reshape(-1)
-
-    owned_units = unit_chain.astype(F32)
+    owned_gate_up = owned_gate_up.astype(F32)
+    owned_down = owned_down.astype(F32)
     owned_rest = rest_chain.astype(F32)
     cuts = [0, heads_width, 2 * heads_width, 2 * heads_width + kv_width]
     cuts = cuts + [cuts[-1] + kv_width]
@@ -664,9 +702,9 @@
         owned_key,
         owned_value,
         owned_out.T,
-        owned_units[:, :units],
-        owned_units[:, units : 2 * units],
-        owned_units[:, 2 * units :].T,
+        owned_gate_up[:, :units],
+        owned_gate_up[:, units:],
+        owned_down.T,
         *own_gains,
     )
 

time: 764 us -> 697 us (0.912)
  starting transfers between devices: 91.5 us -> 51.2 us
  waiting for transfers between devices: 407 us -> 372 us
  matrix products: 51.2 us -> 33.4 us
  local copies, waits for them, and re-layouts: 40 us -> 57.3 us
  Pallas kernels: 57.3 us -> 71.2 us
    ppermute x22 -> x25, waiting for transfers between devices: 302 us -> 266 us  [swap(): return lax.ppermute(value, axis, [(i, i ^ level) for i in range(count)])]
    ppermute x14, starting transfers between devices: 55.1 us -> 20.6 us  [exchange(): done[d] = lax.ppermute(values[d], 'ctx', [(i, i ^ d) for i in range(count)])]
    dot_general x6 -> x3, matrix products: 17.8 us -> 2.93 us  [dot_nt(): lax.dot_general(a, b, (((1,), (1,)), ((), ())), preferred_element_type=F32)]
    pallas_call x0 -> x3, Pallas kernels: none -> 13.1 us  [product_nt(): pl.pallas_call(product_kernel, grid=(columns // step,), in_specs=[pl.Bloc...]
    ppermute x14, waiting for transfers between devices: 55.2 us -> 44.2 us  [exchange(): done[d] = lax.ppermute(values[d], 'ctx', [(i, i ^ d) for i in range(count)])]
    dynamic_slice x4 -> x8, local copies, waits for them, and re-layouts: 5.79 us -> 15.2 us  [the longest x7 14.6 us: rows_of(): lax.dynamic_slice_in_dim(g, owner * size, size, 0)]
    ppermute x5, waiting for transfers between devices: 47.6 us -> 55.4 us  [pieces_of(): lax.ppermute(own, axis, [((i + j) % count, i) for i in range(count)])]
    add x16 -> x11, other arithmetic: 24.3 us -> 18.4 us  [the longest x3 10.7 us: to_shard_owner(): rows_of(index).astype(F32) + swap(rows_of(1 - index), 'shard').astype(F32)]
  transfers between devices with their start and end apart: 46 -> 49, of which waited for: 25 -> 23; matrix products, arithmetic and copies ran while one was open for 13% -> 12% of each run, Pallas kernels for 8% -> 10%
where the time goes in v4:
time: 697 us; the launch traced here: 689 us
  waiting for transfers between devices  372 us (53%)
  Pallas kernels  71.2 us (10%)
  other arithmetic  60 us (9%)
  local copies, waits for them, and re-layouts  57.3 us (8%)
  starting transfers between devices  51.2 us (7%)
  between operations  44.7 us (6%)
  matrix products  33.4 us (5%)
    ppermute x25, waiting for transfers between devices, swap(): return lax.ppermute(value, axis, [(i, i ^ level) for i in range(count)])  266 us
    ppermute x5, waiting for transfers between devices, pieces_of(): lax.ppermute(own, axis, [((i + j) % count, i) for i in range(count)])  55.4 us
    ppermute x14, waiting for transfers between devices, exchange(): done[d] = lax.ppermute(values[d], 'ctx', [(i, i ^ d) for i in range(count)])  44.2 us
    pallas_call x1, Pallas kernels, attend_back(): pl.pallas_call(functools.partial(backward_kernel, docs, count), grid_spec...  29.1 us
    ppermute x25, starting transfers between devices, swap(): return lax.ppermute(value, axis, [(i, i ^ level) for i in range(count)])  24.5 us
    ppermute x14, starting transfers between devices, exchange(): done[d] = lax.ppermute(values[d], 'ctx', [(i, i ^ d) for i in range(count)])  20.6 us
    unnamed x161, local copies, waits for them, and re-layouts  20 us
    pallas_call x1, Pallas kernels, attend(): pl.pallas_call(functools.partial(forward_kernel, docs, count), grid_spec=...  18.2 us
  transfers between devices with their start and end apart: 49, of which 23 were waited for; matrix products, arithmetic and copies ran while one was open for 12% of the time, Pallas kernels for 10%

profile of v4, /device:TPU:0, one launch (start us, length us, event | category | flops | bytes accessed | tf_op | source)
XLA Modules:
  0.0 689.5 jit_solution(14691263250313112128)
XLA Ops:
  20.4 7.6 %collective-permute-done.1 = bf16[512,512]{1,0:T(8,128)(2,1)S(1)} collective-permute-done((bf16[512,512]{1,0:T(8,128)(2,1)}, bf16[512,512]{1,0:T(8,128)(2,1)S(1)}, u32[]{:S(2)}, u32[]{:S(2)}) %collective-permute-start.1) | collective-permute-done | bytes 524320 | tf_op jit(solution)/shard_map/ppermute | solution.py:48
  28.1 9.8 %collective-permute-done.2 = bf16[512,512]{1,0:T(8,128)(2,1)S(1)} collective-permute-done((bf16[512,512]{1,0:T(8,128)(2,1)}, bf16[512,512]{1,0:T(8,128)(2,1)S(1)}, u32[]{:S(2)}, u32[]{:S(2)}) %collective-permute-start.2) | collective-permute-done | bytes 524320 | tf_op jit(solution)/shard_map/ppermute | solution.py:48
  86.7 16.5 %collective-permute-done.6.refs_2_.refs_3_ = bf16[256,1024]{1,0:T(8,128)(2,1)S(1)} collective-permute-done((bf16[256,1024]{1,0:T(8,128)(2,1)S(1)}, bf16[256,1024]{1,0:T(8,128)(2,1)S(1)}, u32[]{:S(2)}, u32[]{:S(2)}) %collective-permute-start.6) | collective-permute-done | bytes 524320 | tf_op jit(solution)/shard_map/ppermute | solution.py:107
  103.7 19.3 %collective-permute-done.4.refs_8_.refs_9_ = bf16[256,1024]{1,0:T(8,128)(2,1)S(1)} collective-permute-done((bf16[256,1024]{1,0:T(8,128)(2,1)S(1)}, bf16[256,1024]{1,0:T(8,128)(2,1)S(1)}, u32[]{:S(2)}, u32[]{:S(2)}) %collective-permute-start.4) | collective-permute-done | bytes 524320 | tf_op jit(solution)/shard_map/ppermute | solution.py:107
  122.9 8.0 %collective-permute-done.3.refs_6_.refs_7_ = bf16[256,1024]{1,0:T(8,128)(2,1)S(1)} collective-permute-done((bf16[256,1024]{1,0:T(8,128)(2,1)S(1)}, bf16[256,1024]{1,0:T(8,128)(2,1)S(1)}, u32[]{:S(2)}, u32[]{:S(2)}) %collective-permute-start.3) | collective-permute-done | bytes 524320 | tf_op jit(solution)/shard_map/ppermute | solution.py:107
  140.0 38.0 %collective-permute-done.11 = bf16[1024,512]{1,0:T(8,128)(2,1)S(1)} collective-permute-done((bf16[1024,512]{1,0:T(8,128)(2,1)S(1)}, bf16[1024,512]{1,0:T(8,128)(2,1)S(1)}, u32[]{:S(2)}, u32[]{:S(2)}) %collective-permute-start.11) | collective-permute-done | bytes 1048608 | tf_op jit(solution)/shard_map/ppermute | solution.py:48
  178.8 18.2 %shard_map.248 = (f32[512,1024]{1,0:T(8,128)}, bf16[512,1024]{1,0:T(8,128)(2,1)S(1)}, f32[512,1024]{1,0:T(8,128)}) custom-call(s32[18]{0:T(128)S(1)} %stack.60.meta_ref, bf16[512,1024]{1,0:T(8,128)(2,1)S(1)} %shard_map.247.q_ref, bf16[512,1024]{1,0:T(8,128)(2,1)} %copy-done, bf16[512,1024]{1,0:T(8,128)(2,1)} %copy-done, ...), custom_call_target="tpu_custom_call" | custom-call | flops 1000 | bytes 1000 | tf_op jit(solution)/shard_map/pallas_call | solution.py:421
  206.0 6.8 fusion
  223.5 5.8 convolution_convert_fusion
  233.9 5.1 constant_dynamic-slice_fusion.8
  242.4 6.8 shard_map.249
  266.2 29.1 %shard_map.252 = (f32[512,1024]{1,0:T(8,128)}, f32[2,512,512]{2,1,0:T(8,128)}, bf16[2,256,512]{2,1,0:T(8,128)(2,1)S(1)}, bf16[2,256,512]{2,1,0:T(8,128)(2,1)S(1)...) custom-call(s32[18]{0:T(128)S(1)} %stack.60.meta_ref, ...), custom_call_target="tpu_custom_call" | custom-call | flops 1000 | bytes 1000 | tf_op jit(solution)/shard_map/pallas_call | solution.py:447
  302.6 43.1 %collective-permute-done.19 = bf16[512,4608]{1,0:T(8,128)(2,1)} collective-permute-done((bf16[512,4608]{1,0:T(8,128)(2,1)}, bf16[512,4608]{1,0:T(8,128)(2,1)}, u32[]{:S(2)}, u32[]{:S(2)}) %collective-permute-start.19) | collective-permute-done | bytes 4718624 | tf_op jit(solution)/shard_map/ppermute | solution.py:81
  345.8 7.4 %convert_add_fusion = f32[512,4608]{1,0:T(8,128)} fusion(bf16[512,4608]{1,0:T(8,128)(2,1)} %collective-permute-done.19, bf16[512,1536]{1,0:T(8,128)(2,1)S(1)} %copy-done.48, bf16[512,3072]{1,0:T(8,128)(2,1)S(1)} %copy-done.44), kind=kLoop, calls=%fused_computation | loop fusion | flops 14155776 | bytes 18874368 | tf_op jit(solution)/shard_map/add | solution.py:97
  367.9 4.7 collective-permute-start.20
  373.2 37.5 %collective-permute-done.27 = bf16[512,2048]{1,0:T(8,128)(2,1)} collective-permute-done((bf16[512,2048]{1,0:T(8,128)(2,1)}, bf16[512,2048]{1,0:T(8,128)(2,1)}, u32[]{:S(2)}, u32[]{:S(2)}) %collective-permute-start.27) | collective-permute-done | bytes 2097184 | tf_op jit(solution)/shard_map/ppermute | solution.py:81
  413.6 29.6 %collective-permute-done.23 = bf16[256,4608]{1,0:T(8,128)(2,1)} collective-permute-done((bf16[256,4608]{1,0:T(8,128)(2,1)}, bf16[256,4608]{1,0:T(8,128)(2,1)}, u32[]{:S(2)}, u32[]{:S(2)}) %collective-permute-start.23) | collective-permute-done | bytes 2359328 | tf_op jit(solution)/shard_map/ppermute | solution.py:81
  461.1 15.2 %collective-permute-done.24 = bf16[64,4608]{1,0:T(8,128)(2,1)} collective-permute-done((bf16[64,4608]{1,0:T(8,128)(2,1)S(1)}, bf16[64,4608]{1,0:T(8,128)(2,1)}, u32[]{:S(2)}, u32[]{:S(2)}) %collective-permute-start.24) | collective-permute-done | bytes 589856 | tf_op jit(solution)/shard_map/ppermute | solution.py:81
  480.3 23.1 %collective-permute-done.25 = bf16[64,4608]{1,0:T(8,128)(2,1)} collective-permute-done((bf16[64,4608]{1,0:T(8,128)(2,1)S(1)}, bf16[64,4608]{1,0:T(8,128)(2,1)}, u32[]{:S(2)}, u32[]{:S(2)}) %collective-permute-start.25) | collective-permute-done | bytes 589856 | tf_op jit(solution)/shard_map/ppermute | solution.py:81
  516.6 19.2 %collective-permute-done.30 = bf16[64,4608]{1,0:T(8,128)(2,1)S(1)} collective-permute-done((bf16[64,4608]{1,0:T(8,128)(2,1)S(1)}, bf16[64,4608]{1,0:T(8,128)(2,1)S(1)}, u32[]{:S(2)}, u32[]{:S(2)}) %collective-permute-start.30) | collective-permute-done | bytes 589856 | tf_op jit(solution)/shard_map/ppermute | solution.py:81
  536.0 19.7 %collective-permute-done.31 = bf16[64,4608]{1,0:T(8,128)(2,1)S(1)} collective-permute-done((bf16[64,4608]{1,0:T(8,128)(2,1)S(1)}, bf16[64,4608]{1,0:T(8,128)(2,1)S(1)}, u32[]{:S(2)}, u32[]{:S(2)}) %collective-permute-start.31) | collective-permute-done | bytes 589856 | tf_op jit(solution)/shard_map/ppermute | solution.py:81
  572.9 20.8 %collective-permute-done.39 = f32[18,128]{1,0:T(8,128)S(1)} collective-permute-done((f32[18,128]{1,0:T(8,128)S(1)}, f32[18,128]{1,0:T(8,128)S(1)}, u32[]{:S(2)}, u32[]{:S(2)}) %collective-permute-start.39) | collective-permute-done | bytes 9248 | tf_op jit(solution)/shard_map/ppermute | solution.py:81
  614.3 23.3 %collective-permute-done.45 = f32[18,128]{1,0:T(8,128)S(1)} collective-permute-done((f32[18,128]{1,0:T(8,128)S(1)}, f32[18,128]{1,0:T(8,128)S(1)}, u32[]{:S(2)}, u32[]{:S(2)}) %collective-permute-start.45) | collective-permute-done | bytes 9248 | tf_op jit(solution)/shard_map/ppermute | solution.py:81
  651.9 22.7 %collective-permute-done.46 = bf16[256,3072]{1,0:T(8,128)(2,1)} collective-permute-done((bf16[256,3072]{1,0:T(8,128)(2,1)S(1)}, bf16[256,3072]{1,0:T(8,128)(2,1)}, u32[]{:S(2)}, u32[]{:S(2)}) %collective-permute-start.46) | collective-permute-done | bytes 1572896 | tf_op jit(solution)/shard_map/ppermute | solution.py:81
  (355 shorter events, 207.7 us)
Async XLA Ops:
  7.2 198.8 %all-gather.2.cloned.1.call-start = ((), (), s32[]{:S(2)}) async-start(), calls=%async_computation | async-start | bytes 14155776 | tf_op jit(solution)/shard_map/all_gather | solution.py:555
  74.3 56.6 %collective-permute-start.7 = (bf16[512,1024]{1,0:T(8,128)(2,1)S(1)}, bf16[512,1024]{1,0:T(8,128)(2,1)S(1)}, u32[]{:S(2)}, u32[]{:S(2)}) collective-permute-start(bf16[512,1024]{1,0:T(8,128)(2,1)S(1)} %copy-done.62), channel_id=1, source_target_pairs={{16,0},{0,16},{17,1},{1,17},{18,2},{2,18},{19,3},{3,19},{20,4},{4,... | collective-permute-start | bytes 3145736 | tf_op jit(solution)/shard_map/ppermute | solution.py:48
  83.8 39.1 %collective-permute-start.4 = (bf16[256,1024]{1,0:T(8,128)(2,1)S(1)}, bf16[256,1024]{1,0:T(8,128)(2,1)S(1)}, u32[]{:S(2)}, u32[]{:S(2)}) collective-permute-start(bf16[256,1024]{1,0:T(8,128)(2,1)S(1)} %get-tuple-element.215), channel_id=1, source_target_pairs={{0,10},{2,8},{4,14},{6,12},{8,2},{10,0},{12,6},{14,4},{1,11},{3,9}... | collective-permute-start | bytes 1572872 | tf_op jit(solution)/shard_map/ppermute | solution.py:107
  86.4 44.5 %collective-permute-start.3 = (bf16[256,1024]{1,0:T(8,128)(2,1)S(1)}, bf16[256,1024]{1,0:T(8,128)(2,1)S(1)}, u32[]{:S(2)}, u32[]{:S(2)}) collective-permute-start(bf16[256,1024]{1,0:T(8,128)(2,1)S(1)} %get-tuple-element.216), channel_id=1, source_target_pairs={{0,8},{2,10},{4,12},{6,14},{8,0},{10,2},{12,4},{14,6},{1,9},{3,11}... | collective-permute-start | bytes 1572872 | tf_op jit(solution)/shard_map/ppermute | solution.py:107
  130.9 47.1 %collective-permute-start.11 = (bf16[1024,512]{1,0:T(8,128)(2,1)S(1)}, bf16[1024,512]{1,0:T(8,128)(2,1)S(1)}, u32[]{:S(2)}, u32[]{:S(2)}) collective-permute-start(bf16[1024,512]{1,0:T(8,128)(2,1)S(1)} %copy-done.59), channel_id=1, source_target_pairs={{16,0},{0,16},{17,1},{1,17},{18,2},{2,18},{19,3},{3,19},{20,4},{4,... | collective-permute-start | bytes 3145736 | tf_op jit(solution)/shard_map/ppermute | solution.py:48
  131.4 47.3 %collective-permute-start.8 = (bf16[256,1024]{1,0:T(8,128)(2,1)S(1)}, bf16[256,1024]{1,0:T(8,128)(2,1)S(1)}, u32[]{:S(2)}, u32[]{:S(2)}) collective-permute-start(bf16[256,1024]{1,0:T(8,128)(2,1)S(1)} %get-tuple-element.97), channel_id=1, source_target_pairs={{0,12},{2,14},{4,8},{6,10},{8,4},{10,6},{12,0},{14,2},{1,13},{3,15... | collective-permute-start | bytes 1572872 | tf_op jit(solution)/shard_map/ppermute | solution.py:107
  135.0 43.7 %collective-permute-start.9 = (bf16[256,1024]{1,0:T(8,128)(2,1)S(1)}, bf16[256,1024]{1,0:T(8,128)(2,1)S(1)}, u32[]{:S(2)}, u32[]{:S(2)}) collective-permute-start(bf16[256,1024]{1,0:T(8,128)(2,1)S(1)} %get-tuple-element.98), channel_id=1, source_target_pairs={{0,14},{2,12},{4,10},{6,8},{8,6},{10,4},{12,2},{14,0},{1,15},{3,13... | collective-permute-start | bytes 1572872 | tf_op jit(solution)/shard_map/ppermute | solution.py:107
  136.1 42.6 %collective-permute-start.10 = (bf16[256,1024]{1,0:T(8,128)(2,1)S(1)}, bf16[256,1024]{1,0:T(8,128)(2,1)S(1)}, u32[]{:S(2)}, u32[]{:S(2)}) collective-permute-start(bf16[256,1024]{1,0:T(8,128)(2,1)S(1)} %get-tuple-element.99), channel_id=1, source_target_pairs={{0,6},{2,4},{4,2},{6,0},{8,14},{10,12},{12,10},{14,8},{1,7},{3,5},... | collective-permute-start | bytes 1572872 | tf_op jit(solution)/shard_map/ppermute | solution.py:107
  241.6 104.2 %collective-permute-start.19 = (bf16[512,4608]{1,0:T(8,128)(2,1)}, bf16[512,4608]{1,0:T(8,128)(2,1)}, u32[]{:S(2)}, u32[]{:S(2)}) collective-permute-start(bf16[512,4608]{1,0:T(8,128)(2,1)} %pad_maximum_fusion.2), channel_id=1, source_target_pairs={{0,16},{16,0},{1,17},{17,1},{2,18},{18,2},{3,19},{19,3},{4,20},{20... | collective-permute-start | bytes 14155784 | tf_op jit(solution)/shard_map/ppermute | solution.py:81
  295.4 57.8 %collective-permute-start.15 = (bf16[2,256,512]{2,1,0:T(8,128)(2,1)S(1)}, bf16[2,256,512]{2,1,0:T(8,128)(2,1)}, u32[]{:S(2)}, u32[]{:S(2)}) collective-permute-start(bf16[2,256,512]{2,1,0:T(8,128)(2,1)S(1)} %get-tuple-element.119), channel_id=1, source_target_pairs={{0,8},{2,10},{4,12},{6,14},{8,0},{10,2},{12,4},{14,6},{1,9},{3,11}... | collective-permute-start | bytes 1572872 | tf_op jit(solution)/shard_map/ppermute | solution.py:107
  295.4 57.7 %collective-permute-start.16 = (bf16[2,256,512]{2,1,0:T(8,128)(2,1)S(1)}, bf16[2,256,512]{2,1,0:T(8,128)(2,1)}, u32[]{:S(2)}, u32[]{:S(2)}) collective-permute-start(bf16[2,256,512]{2,1,0:T(8,128)(2,1)S(1)} %get-tuple-element.120), channel_id=1, source_target_pairs={{0,10},{2,8},{4,14},{6,12},{8,2},{10,0},{12,6},{14,4},{1,11},{3,9}... | collective-permute-start | bytes 1572872 | tf_op jit(solution)/shard_map/ppermute | solution.py:107
  295.8 57.4 %collective-permute-start.17 = (bf16[2,256,512]{2,1,0:T(8,128)(2,1)S(1)}, bf16[2,256,512]{2,1,0:T(8,128)(2,1)}, u32[]{:S(2)}, u32[]{:S(2)}) collective-permute-start(bf16[2,256,512]{2,1,0:T(8,128)(2,1)S(1)} %get-tuple-element.121), channel_id=1, source_target_pairs={{0,2},{2,0},{4,6},{6,4},{8,10},{10,8},{12,14},{14,12},{1,3},{3,1},... | collective-permute-start | bytes 1572872 | tf_op jit(solution)/shard_map/ppermute | solution.py:107
  299.8 53.4 %collective-permute-start.18 = (bf16[2,256,512]{2,1,0:T(8,128)(2,1)S(1)}, bf16[2,256,512]{2,1,0:T(8,128)(2,1)}, u32[]{:S(2)}, u32[]{:S(2)}) collective-permute-start(bf16[2,256,512]{2,1,0:T(8,128)(2,1)S(1)} %get-tuple-element.122), channel_id=1, source_target_pairs={{0,4},{2,6},{4,0},{6,2},{8,12},{10,14},{12,8},{14,10},{1,5},{3,7},... | collective-permute-start | bytes 1572872 | tf_op jit(solution)/shard_map/ppermute | solution.py:107
  363.5 47.2 %collective-permute-start.27 = (bf16[512,2048]{1,0:T(8,128)(2,1)}, bf16[512,2048]{1,0:T(8,128)(2,1)}, u32[]{:S(2)}, u32[]{:S(2)}) collective-permute-start(bf16[512,2048]{1,0:T(8,128)(2,1)} %pad_maximum_fusion.4), channel_id=1, source_target_pairs={{0,16},{16,0},{1,17},{17,1},{2,18},{18,2},{3,19},{19,3},{4,20},{20... | collective-permute-start | bytes 6291464 | tf_op jit(solution)/shard_map/ppermute | solution.py:81
  367.9 75.3 %collective-permute-start.23 = (bf16[256,4608]{1,0:T(8,128)(2,1)}, bf16[256,4608]{1,0:T(8,128)(2,1)}, u32[]{:S(2)}, u32[]{:S(2)}) collective-permute-start(bf16[256,4608]{1,0:T(8,128)(2,1)} %dynamic-slice_convert_fusion), channel_id=1, source_target_pairs={{0,2},{2,0},{4,6},{6,4},{8,10},{10,8},{12,14},{14,12},{1,3},{3,1},... | collective-permute-start | bytes 7077896 | tf_op jit(solution)/shard_map/ppermute | solution.py:81
  367.9 78.9 %collective-permute-start.20 = (bf16[2,256,512]{2,1,0:T(8,128)(2,1)S(1)}, bf16[2,256,512]{2,1,0:T(8,128)(2,1)S(1)}, u32[]{:S(2)}, u32[]{:S(2)}) collective-permute-start(bf16[2,256,512]{2,1,0:T(8,128)(2,1)S(1)} %copy-done.34), channel_id=1, source_target_pairs={{0,12},{2,14},{4,8},{6,10},{8,4},{10,6},{12,0},{14,2},{1,13},{3,15... | collective-permute-start | bytes 1572872 | tf_op jit(solution)/shard_map/ppermute | solution.py:107
  372.6 74.2 %collective-permute-start.21 = (bf16[2,256,512]{2,1,0:T(8,128)(2,1)S(1)}, bf16[2,256,512]{2,1,0:T(8,128)(2,1)S(1)}, u32[]{:S(2)}, u32[]{:S(2)}) collective-permute-start(bf16[2,256,512]{2,1,0:T(8,128)(2,1)S(1)} %copy-done.32), channel_id=1, source_target_pairs={{0,14},{2,12},{4,10},{6,8},{8,6},{10,4},{12,2},{14,0},{1,15},{3,13... | collective-permute-start | bytes 1572872 | tf_op jit(solution)/shard_map/ppermute | solution.py:107
  373.2 73.7 %collective-permute-start.22 = (bf16[2,256,512]{2,1,0:T(8,128)(2,1)S(1)}, bf16[2,256,512]{2,1,0:T(8,128)(2,1)S(1)}, u32[]{:S(2)}, u32[]{:S(2)}) collective-permute-start(bf16[2,256,512]{2,1,0:T(8,128)(2,1)S(1)} %copy-done.30), channel_id=1, source_target_pairs={{0,6},{2,4},{4,2},{6,0},{8,14},{10,12},{12,10},{14,8},{1,7},{3,5},... | collective-permute-start | bytes 1572872 | tf_op jit(solution)/shard_map/ppermute | solution.py:107
  453.3 50.1 %collective-permute-start.25 = (bf16[64,4608]{1,0:T(8,128)(2,1)S(1)}, bf16[64,4608]{1,0:T(8,128)(2,1)}, u32[]{:S(2)}, u32[]{:S(2)}) collective-permute-start(bf16[64,4608]{1,0:T(8,128)(2,1)S(1)} %get-tuple-element.192), channel_id=1, source_target_pairs={{0,8},{2,10},{4,12},{6,14},{8,0},{10,2},{12,4},{14,6},{1,9},{3,11}... | collective-permute-start | bytes 1769480 | tf_op jit(solution)/shard_map/ppermute | solution.py:81
  459.7 45.4 %collective-permute-start.28 = (bf16[512,1024]{1,0:T(8,128)(2,1)S(1)}, bf16[512,1024]{1,0:T(8,128)(2,1)S(1)}, u32[]{:S(2)}, u32[]{:S(2)}) collective-permute-start(bf16[512,1024]{1,0:T(8,128)(2,1)S(1)} %constant_dynamic-slice_fusion), channel_id=1, source_target_pairs={{0,16},{16,0},{1,17},{17,1},{2,18},{18,2},{3,19},{19,3},{4,20},{20... | collective-permute-start | bytes 3145736 | tf_op jit(solution)/shard_map/ppermute | solution.py:81
  508.9 46.9 %collective-permute-start.31 = (bf16[64,4608]{1,0:T(8,128)(2,1)S(1)}, bf16[64,4608]{1,0:T(8,128)(2,1)S(1)}, u32[]{:S(2)}, u32[]{:S(2)}) collective-permute-start(bf16[64,4608]{1,0:T(8,128)(2,1)S(1)} %convert_add_fusion.8), channel_id=1, source_target_pairs={{0,8},{2,10},{4,12},{6,14},{8,0},{10,2},{12,4},{14,6},{1,9},{3,11}... | collective-permute-start | bytes 1769480 | tf_op jit(solution)/shard_map/ppermute | solution.py:81
  514.7 41.8 %collective-permute-start.29 = (bf16[512,1024]{1,0:T(8,128)(2,1)S(1)}, bf16[512,1024]{1,0:T(8,128)(2,1)S(1)}, u32[]{:S(2)}, u32[]{:S(2)}) collective-permute-start(bf16[512,1024]{1,0:T(8,128)(2,1)S(1)} %add_convert_fusion), channel_id=1, source_target_pairs={{0,1},{1,0},{2,3},{3,2},{4,5},{5,4},{6,7},{7,6},{8,9},{9,8},{10,11... | collective-permute-start | bytes 3145736 | tf_op jit(solution)/shard_map/ppermute | solution.py:75
  515.1 42.6 %collective-permute-start.33 = (bf16[256,3072]{1,0:T(8,128)(2,1)S(1)}, bf16[256,3072]{1,0:T(8,128)(2,1)S(1)}, u32[]{:S(2)}, u32[]{:S(2)}) collective-permute-start(bf16[256,3072]{1,0:T(8,128)(2,1)S(1)} %dynamic-slice_convert_fusion.1), channel_id=1, source_target_pairs={{0,2},{2,0},{4,6},{6,4},{8,10},{10,8},{12,14},{14,12},{1,3},{3,1},... | collective-permute-start | bytes 4718600 | tf_op jit(solution)/shard_map/ppermute | solution.py:81
  559.7 38.6 %collective-permute-start.34 = (bf16[256,3072]{1,0:T(8,128)(2,1)}, bf16[256,3072]{1,0:T(8,128)(2,1)}, u32[]{:S(2)}, u32[]{:S(2)}) collective-permute-start(bf16[256,3072]{1,0:T(8,128)(2,1)} %slice.91), channel_id=1, source_target_pairs={{0,2},{2,0},{4,6},{6,4},{8,10},{10,8},{12,14},{14,12},{1,3},{3,1},... | collective-permute-start | bytes 4718600 | tf_op jit(solution)/shard_map/ppermute | solution.py:81
  (105 other events, 1812.0 us)
Sparse Core Ops, SparseCore 0:
  38.8 163.2 all-gather.1

commit v5 on v4

--- a/solution.py
+++ b/solution.py
@@ -81,22 +81,6 @@
     return lax.ppermute(value, axis, [(i, i ^ level) for i in range(count)])
 
 
-def to_shard_owner(*grads):
-    count = lax.axis_size("shard")
-    index = lax.axis_index("shard")
-    if count != 2:
-        grad = jnp.concatenate(grads, axis=1)
-        return lax.psum_scatter(grad, "shard", scatter_dimension=0, tiled=True).astype(F32)
-
-    def rows_of(owner):
-        size = grads[0].shape[0] // 2
-        return jnp.concatenate(
-            [lax.dynamic_slice_in_dim(g, owner * size, size, 0) for g in grads], axis=1
-        )
-
-    return rows_of(index).astype(F32) + swap(rows_of(1 - index), "shard").astype(F32)
-
-
 def place_in(masks):
     return (lax.axis_index("ctx") // masks[0]) % (1 << len(masks))
 
@@ -113,19 +97,50 @@
     return tied[len(turns) :]
 
 
-def halve(value, masks):
+def total(addends):
+    return sum(a.astype(F32) for a in addends).astype(BF16)
+
+
+def rows_at(addends, block, rows):
+    return [lax.dynamic_slice_in_dim(a, block * rows, rows, 0) for a in addends]
+
+
+def halve(addends, masks):
     size = 1 << len(masks)
-    rows = value.shape[0] // size
+    rows = addends[0].shape[0] // size
     place = place_in(masks)
-    total = lax.dynamic_slice_in_dim(value, place * rows, rows, 0)
+    kept = rows_at(addends, place, rows)
     for turn in range(1, size):
-        sent = lax.dynamic_slice_in_dim(value, (place ^ turn) * rows, rows, 0)
-        total = total + swap(sent.astype(BF16), "ctx", turn * masks[0]).astype(F32)
-    return total
+        sent = total(rows_at(addends, place ^ turn, rows))
+        kept = kept + [swap(sent, "ctx", turn * masks[0])]
+    return kept
+
+
+def over_shard(pairs):
+    count = lax.axis_size("shard")
+    index = lax.axis_index("shard")
+    if count != 2:
+        grads = [dot_tn(a, b[:, lo:hi]).astype(BF16) for a, b, lo, hi in pairs]
+        grad = jnp.concatenate(grads, axis=1)
+        return [lax.psum_scatter(grad, "shard", scatter_dimension=0, tiled=True)]
+    away, home = 2 * (1 - index), 2 * index
+    sent = split_product((away, away + 1), pairs)
+    return [split_product((home, home + 1), pairs), swap(sent, "shard")]
+
+
+def over_near_then_shard(pairs, near_axis):
+    count = lax.axis_size("shard")
+    index = lax.axis_index("shard")
+    bit = place_in(near_axis)
+    if count != 2:
+        return halve(over_shard(pairs), near_axis), None
+    sent = split_product((1 - bit, 3 - bit), pairs)
+    addends = [split_product((bit, 2 + bit), pairs), swap(sent, "ctx", near_axis[0])]
+    rows = addends[0].shape[0] // 2
+    return rows_at(addends, index, rows), lambda: rows_at(addends, 1 - index, rows)
 
 
 def double(value, masks):
-    value = value.astype(BF16)
     size = 1 << len(masks)
     place = place_in(masks)
     blocks = [value] + [swap(value, "ctx", turn * masks[0]) for turn in range(1, size)]
@@ -137,26 +152,69 @@
     return blocks[0]
 
 
-def product_kernel(a_ref, b_ref, out_ref):
-    out_ref[...] = dot_nt(a_ref[...], b_ref[...]).astype(out_ref.dtype)
-
-
-def product_nt(a, b, dtype, column=0):
-    rows, depth = a.shape
-    columns = b.shape[0]
+def product_kernel(count, *refs):
+    products = [dot_nt(refs[2 * i][...], refs[2 * i + 1][...]) for i in range(count)]
+    refs[-1][...] = sum(products).astype(BF16)
+
+
+def product_nt(*terms):
+    rows = terms[0][0].shape[0]
+    columns = terms[0][1].shape[0]
     step = min(columns, 256)
+    specs, values = [], []
+    for a, b, column in terms:
+        depth = a.shape[1]
+        specs.append(pl.BlockSpec((rows, depth), lambda i: (0, 0)))
+        specs.append(pl.BlockSpec((step, depth), lambda i, column=column: (i, column)))
+        values += [a, b]
     return pl.pallas_call(
-        product_kernel,
+        functools.partial(product_kernel, len(terms)),
         grid=(columns // step,),
-        in_specs=[
-            pl.BlockSpec((rows, depth), lambda i: (0, 0)),
-            pl.BlockSpec((step, depth), lambda i: (i, column)),
-        ],
+        in_specs=specs,
         out_specs=pl.BlockSpec((rows, step), lambda i: (0, i)),
-        out_shape=jax.ShapeDtypeStruct((rows, columns), dtype),
+        out_shape=jax.ShapeDtypeStruct((rows, columns), BF16),
         compiler_params=pltpu.CompilerParams(vmem_limit_bytes=VMEM_LIMIT),
         cost_estimate=CHEAP,
-    )(a, b)
+    )(*values)
+
+
+def split_product_kernel(spans, which_ref, *refs):
+    j = pl.program_id(1)
+    for i, (lo, hi) in enumerate(spans):
+
+        @pl.when((j >= lo) & (j < hi))
+        def _():
+            refs[-1][...] = dot_tn(refs[2 * i][...], refs[2 * i + 1][...]).astype(BF16)
+
+
+def split_product(which, pairs):
+    tokens, model = pairs[0][0].shape
+    rows = model // 4
+    step = min(hi - lo for a, b, lo, hi in pairs)
+    specs, values, spans, done = [], [], [], 0
+    for a, b, lo, hi in pairs:
+        blocks = (hi - lo) // step
+
+        def column(i, j, w, first=done, base=lo // step, blocks=blocks):
+            return (0, base + jnp.clip(j - first, 0, blocks - 1))
+
+        specs.append(pl.BlockSpec((tokens, rows), lambda i, j, w: (0, w[i])))
+        specs.append(pl.BlockSpec((tokens, step), column))
+        values += [a, b]
+        spans.append((done, done + blocks))
+        done += blocks
+    return pl.pallas_call(
+        functools.partial(split_product_kernel, spans),
+        grid_spec=pltpu.PrefetchScalarGridSpec(
+            num_scalar_prefetch=1,
+            grid=(2, done),
+            in_specs=specs,
+            out_specs=pl.BlockSpec((rows, step), lambda i, j, w: (i, j)),
+        ),
+        out_shape=jax.ShapeDtypeStruct((2 * rows, done * step), BF16),
+        compiler_params=pltpu.CompilerParams(vmem_limit_bytes=VMEM_LIMIT),
+        cost_estimate=CHEAP,
+    )(jnp.stack(which).astype(jnp.int32), *values)
 
 
 def rope_kernel(pre_ref, cos_ref, sin_ref, gain_ref, out_ref):
@@ -167,44 +225,71 @@
     out_ref[...] = (scaled * cos_ref[...] + turned * sin_ref[...]).astype(BF16)
 
 
-def rope_and_copy_kernel(roped, pre_ref, plain_ref, cos_ref, sin_ref, gain_ref, out_ref):
-    @pl.when(pl.program_id(0) < roped)
+def rope(pre, cosine, sine, gain):
+    rows, width = pre.shape
+    table = pl.BlockSpec((rows, HEAD), lambda h: (0, 0))
+    column = pl.BlockSpec((rows, HEAD), lambda h: (0, h))
+    return pl.pallas_call(
+        rope_kernel,
+        grid=(width // HEAD,),
+        in_specs=[column, table, table, pl.BlockSpec((1, HEAD), lambda h: (0, 0))],
+        out_specs=column,
+        out_shape=jax.ShapeDtypeStruct((rows, width), BF16),
+        compiler_params=pltpu.CompilerParams(vmem_limit_bytes=VMEM_LIMIT),
+        cost_estimate=CHEAP,
+    )(pre, cosine, sine, gain)
+
+
+def part_start(meta_ref, docs, d, half):
+    return pl.multiple_of((1 - meta_ref[docs + d]) * half, half)
+
+
+def key_value_kernel(heads, docs, count, meta_ref, key_ref, value_ref, *refs):
+    cos_ref, sin_ref, gain_ref, out_ref = refs[:4]
+    half = out_ref.shape[0] // 2
+
+    @pl.when(pl.program_id(0) < heads)
     def _():
-        rope_kernel(pre_ref, cos_ref, sin_ref, gain_ref, out_ref)
-
-    @pl.when(pl.program_id(0) >= roped)
+        rope_kernel(key_ref, cos_ref, sin_ref, gain_ref, out_ref)
+
+    @pl.when(pl.program_id(0) >= heads)
     def _():
-        out_ref[...] = plain_ref[...].astype(BF16)
-
-
-def rope(pre, cosine, sine, gain, plain=None):
-    rows, width = pre.shape
+        out_ref[...] = value_ref[...].astype(BF16)
+
+    for d, sent_ref in enumerate(refs[4:]):
+        sent_ref[...] = out_ref[pl.ds(part_start(meta_ref, docs, d, half), half), :]
+
+
+def key_value_and_parts(meta, docs, count, key, value, cosine, sine, gain):
+    rows, width = key.shape
     heads = width // HEAD
-    table = pl.BlockSpec((rows, HEAD), lambda h: (0, 0))
-    tables = [table, table, pl.BlockSpec((1, HEAD), lambda h: (0, 0))]
-    column = pl.BlockSpec((rows, HEAD), lambda h: (0, h))
-    if plain is None:
-        kernel, steps, columns, values = rope_kernel, heads, [column], [pre]
-    else:
-        kernel, steps = functools.partial(rope_and_copy_kernel, heads), 2 * heads
-        columns = [
-            pl.BlockSpec((rows, HEAD), lambda h: (0, jnp.minimum(h, heads - 1))),
-            pl.BlockSpec((rows, HEAD), lambda h: (0, jnp.maximum(h - heads, 0))),
-        ]
-        values = [pre, plain]
-    return pl.pallas_call(
-        kernel,
-        grid=(steps,),
-        in_specs=columns + tables,
-        out_specs=column,
-        out_shape=jax.ShapeDtypeStruct((rows, steps * HEAD), BF16),
+    table = pl.BlockSpec((rows, HEAD), lambda h, m: (0, 0))
+    column = pl.BlockSpec((rows, HEAD), lambda h, m: (0, h))
+    part = pl.BlockSpec((rows // 2, HEAD), lambda h, m: (0, h))
+    result = pl.pallas_call(
+        functools.partial(key_value_kernel, heads, docs, count),
+        grid_spec=pltpu.PrefetchScalarGridSpec(
+            num_scalar_prefetch=1,
+            grid=(2 * heads,),
+            in_specs=[
+                pl.BlockSpec((rows, HEAD), lambda h, m: (0, jnp.minimum(h, heads - 1))),
+                pl.BlockSpec((rows, HEAD), lambda h, m: (0, jnp.maximum(h - heads, 0))),
+                table,
+                table,
+                pl.BlockSpec((1, HEAD), lambda h, m: (0, 0)),
+            ],
+            out_specs=[column] + [part] * (count - 1),
+        ),
+        out_shape=[jax.ShapeDtypeStruct((rows, 2 * width), BF16)]
+        + [jax.ShapeDtypeStruct((rows // 2, 2 * width), BF16)] * (count - 1),
         compiler_params=pltpu.CompilerParams(vmem_limit_bytes=VMEM_LIMIT),
-    )(*values, cosine, sine, gain)
-
-
-def rope_back_kernel(grad_ref, pre_ref, cos_ref, sin_ref, gain_ref, out_ref, sum_ref):
+        cost_estimate=CHEAP,
+    )(meta, key, value, cosine, sine, gain)
+    return result[0], dict(zip(range(1, count), result[1:]))
+
+
+def turn_back(grad, pre_ref, cos_ref, sin_ref, gain_ref, out_ref, sum_ref):
     pre = pre_ref[...]
-    grad = grad_ref[...]
     factor = lax.rsqrt(jnp.mean(pre * pre, axis=-1, keepdims=True) + EPS)
     hat = pre * factor
     back = grad * cos_ref[...] - pltpu.roll(grad, HEAD // 2, 1) * sin_ref[...]
@@ -221,6 +306,48 @@
     back = back * gain_ref[...]
     inner = jnp.mean(back * hat, axis=-1, keepdims=True)
     out_ref[...] = (factor * (back - hat * inner)).astype(BF16)
+
+
+def rope_back_kernel(grad_ref, *refs):
+    turn_back(grad_ref[...], *refs)
+
+
+def key_value_back_kernel(docs, meta_ref, own_ref, *refs):
+    returned = refs[:-8]
+    key_ref, cos_ref, sin_ref, gain_ref, d_key_ref, d_value_ref, sum_ref, acc_ref = refs[-8:]
+    half = key_ref.shape[0] // 2
+    acc_ref[...] = own_ref[...]
+    for d, given_ref in enumerate(returned):
+        rows = pl.ds(part_start(meta_ref, docs, d, half), half)
+        acc_ref[:, rows, :] += given_ref[...].astype(F32)
+    d_value_ref[...] = acc_ref[1].astype(BF16)
+    turn_back(acc_ref[0], key_ref, cos_ref, sin_ref, gain_ref, d_key_ref, sum_ref)
+
+
+def key_value_back(meta, docs, own, returned, key, cosine, sine, gain):
+    rows, width = key.shape
+    table = pl.BlockSpec((rows, HEAD), lambda h, m: (0, 0))
+    column = pl.BlockSpec((rows, HEAD), lambda h, m: (0, h))
+    one_row = pl.BlockSpec((1, HEAD), lambda h, m: (0, 0))
+    return pl.pallas_call(
+        functools.partial(key_value_back_kernel, docs),
+        grid_spec=pltpu.PrefetchScalarGridSpec(
+            num_scalar_prefetch=1,
+            grid=(width // HEAD,),
+            in_specs=[pl.BlockSpec((2, rows, HEAD), lambda h, m: (0, 0, h))]
+            + [pl.BlockSpec((2, rows // 2, HEAD), lambda h, m: (0, 0, h))] * len(returned)
+            + [column, table, table, one_row],
+            out_specs=[column, column, one_row],
+            scratch_shapes=[pltpu.VMEM((2, rows, HEAD), F32)],
+        ),
+        out_shape=[
+            jax.ShapeDtypeStruct((rows, width), BF16),
+            jax.ShapeDtypeStruct((rows, width), BF16),
+            jax.ShapeDtypeStruct((1, HEAD), F32),
+        ],
+        compiler_params=pltpu.CompilerParams(vmem_limit_bytes=VMEM_LIMIT),
+        cost_estimate=CHEAP,
+    )(meta, own, *returned, key, cosine, sine, gain)
 
 
 def rope_back(grad, pre, cosine, sine, gain):
@@ -299,8 +426,8 @@
         part = own if e == 0 else 2 * count - 1 - own
         acc_ref[e] = block(e * half, k_ref[rows, :], v_ref[rows, :], part, part, True)
     for d in range(count - 1):
-        side = meta_ref[docs + 2 * d]
-        k_part = meta_ref[docs + 2 * d + 1]
+        side = meta_ref[docs + d]
+        k_part = meta_ref[docs + count - 1 + d]
         q_part = jnp.where(side == 0, own, 2 * count - 1 - own)
 
         def add(mask):
@@ -367,8 +494,8 @@
         dkv_ref[0, rows, :] = d_keys
         dkv_ref[1, rows, :] = d_values
     for d in range(count - 1):
-        side = meta_ref[docs + 2 * d]
-        k_part = meta_ref[docs + 2 * d + 1]
+        side = meta_ref[docs + d]
+        k_part = meta_ref[docs + count - 1 + d]
         q_part = jnp.where(side == 0, own, 2 * count - 1 - own)
         seen = any_visible(meta_ref, docs, half, q_part, k_part)
         whole = all_visible(meta_ref, docs, half, q_part, k_part)
@@ -494,30 +621,41 @@
     units = w_gate.shape[1]
     heads_width = w_out.shape[0]
 
+    masks = [1 << b for b in range(count.bit_length() - 1)]
+    near_axis, far_axis = masks[:1], masks[1:]
+    far = [d for d in range(1, count) if d >= count // 2]
+    near = [d for d in range(1, count) if d < count // 2]
+    crossing = [d for d in far + near if d % 2 == 1]
+    straight = [d for d in far + near if d % 2 == 0]
+
     packed = jnp.concatenate([gain_in, gain_post, gain_q, gain_k])
-    packed_pieces = pieces_of(packed, "shard")
     k_pieces = pieces_of(key_weight, "shard")
     v_pieces = pieces_of(value_weight, "shard")
-    own_units = jnp.concatenate([w_gate, w_up, w_down.T], axis=1)
-
+    packed_pieces = pieces_of(packed, "shard")
+    own_rest = jnp.concatenate([w_query, w_out.T, w_down.T], axis=1)
+    own_gate_up = jnp.concatenate([w_gate, w_up], axis=1)
+
+    turns = jnp.arange(count, dtype=jnp.int32)
+    partner = jnp.bitwise_xor(ctx.astype(jnp.int32), turns)
+    parts = jnp.sum(
+        jnp.where(partner[:, None] == turns[None, :], part_order[:, 0][None, :], 0), axis=1
+    )
+    part = parts[:1]
     lengths = seq_lengths[0]
-    starts = jnp.cumsum(lengths) - lengths
-    parts = part_order[:, 0]
-    part = parts[ctx]
-    other_parts = [parts[ctx ^ d] for d in range(1, count)]
-    sides = [jnp.where(p < part, 0, 1).astype(jnp.int32) for p in other_parts]
-    held_parts = [jnp.where(p < part, p, 2 * count - 1 - p) for p in other_parts]
-    meta = jnp.stack(
-        [part]
-        + [starts[i] for i in range(1, docs)]
-        + [v for pair in zip(sides, held_parts) for v in pair]
+    order = jnp.arange(docs, dtype=jnp.int32)
+    starts = jnp.sum(jnp.where(order[None, :] < order[:, None], lengths[None, :], 0), axis=1)
+    meta = jnp.concatenate(
+        [
+            part,
+            starts[1:],
+            (parts[1:] >= part).astype(jnp.int32),
+            jnp.where(parts[1:] < part, parts[1:], 2 * count - 1 - parts[1:]),
+        ]
     ).astype(jnp.int32)
-    places = jnp.concatenate(
-        [p * half + jnp.arange(half, dtype=jnp.int32) for p in (part, 2 * count - 1 - part)]
-    )
-    begins = jnp.zeros_like(places)
-    for i in range(1, docs):
-        begins = jnp.where(places >= starts[i], starts[i], begins)
+    row = jnp.arange(rows, dtype=jnp.int32)
+    places = jnp.where(row < half, part * half + row, (2 * count - 2 - part) * half + row)
+    reached = places[:, None] >= starts[None, :]
+    begins = jnp.max(jnp.where(reached, starts[None, :], 0), axis=1)
     frequency = THETA ** (-jnp.arange(0, HEAD, 2, dtype=F32) / HEAD)
     angles = (places - begins).astype(F32)[:, None] * frequency[None, :]
     cosine, sine = jnp.cos(angles), jnp.sin(angles)
@@ -527,62 +665,53 @@
     inputs = tokens.astype(F32)
     normal_one, factor_one = rms_parts(inputs)
 
-    w_query, own_units, packed_pieces[-1], k_pieces[-1], v_pieces[-1] = tie(
-        w_query, own_units, packed_pieces[-1], k_pieces[-1], v_pieces[-1]
+    own_rest, own_gate_up, packed_pieces[-1], k_pieces[-1], v_pieces[-1] = tie(
+        own_rest, own_gate_up, packed_pieces[-1], k_pieces[-1], v_pieces[-1]
     )
     cosine, sine, meta, normal_one, k_pieces[-1] = tie(
         cosine, sine, meta, normal_one, k_pieces[-1]
     )
     cuts = [0, depth, 2 * depth, 2 * depth + gain_q.shape[0], packed.shape[0]]
-    gain_pieces = [
-        [piece[lo:hi].astype(F32) for piece in packed_pieces]
+    scale_in, scale_post, scale_q, scale_k = (
+        join([piece[lo:hi] for piece in packed_pieces], 0, shard).astype(F32).reshape(1, -1)
         for lo, hi in zip(cuts[:-1], cuts[1:])
-    ]
-    scale_in, scale_post, scale_q, scale_k = (
-        join(pieces, 0, shard).reshape(1, -1) for pieces in gain_pieces
-    )
-    parts_in = []
-    for j in range(shard_count):
-        at = (shard + j) % shard_count * depth
-        part_in = lax.dynamic_slice_in_dim(normal_one, at, depth, 1)
-        parts_in.append((part_in * gain_pieces[0][j][None, :]).astype(BF16))
+    )
     normed_input = (normal_one * scale_in).astype(BF16)
-
-    def project(pieces):
-        return sum(dot(part_in, piece) for part_in, piece in zip(parts_in, pieces))
-
-    q_pieces = pieces_of(w_query, "shard")
-    full_units = lax.all_gather(own_units, "shard", axis=0, tiled=True)
-    k_pre = project(k_pieces)
-    key_value = rope(k_pre, cosine, sine, scale_k, project(v_pieces))
-    far = [d for d in range(1, count) if d >= count // 2]
-    near = [d for d in range(1, count) if d < count // 2]
-    early = far[: len(far) // 2] + near[: (len(near) + 1) // 2]
-    late = far[len(far) // 2 :] + near[(len(near) + 1) // 2 :]
-    sent = {}
-    for d in early + late:
-        start = jnp.where(part < other_parts[d - 1], 0, half)
-        sent[d] = lax.dynamic_slice_in_dim(key_value, start, half, 0)
+    full_key = join(k_pieces, 0, shard)
+    full_value = join(v_pieces, 0, shard)
+
+    full_gate_up = lax.all_gather(own_gate_up, "shard", axis=0, tiled=True)
+    if shard_count == 2:
+        bit = place_in(near_axis)
+        half_rest = lax.dynamic_slice_in_dim(own_rest, bit * (depth // 2), depth // 2, 0)
+        half_rest = swap(half_rest, "shard")
+    else:
+        half_rest = own_rest
+    k_pre = dot(normed_input, full_key)
+    key_value, sent = key_value_and_parts(
+        meta, docs, count, k_pre, dot(normed_input, full_value), cosine, sine, scale_k
+    )
     held = {}
-    exchange(sent, held, early)
-    w_out, q_pieces[-1], *rest = settle(held, early, w_out, q_pieces[-1], *(sent[d] for d in late))
-    sent.update(zip(late, rest))
-
-    exchange(sent, held, late)
-    out_pieces = pieces_of(w_out, "shard")
-    q_pre = project(q_pieces)
+    exchange(sent, held, crossing)
+    half_rest, *rest = settle(held, crossing, half_rest, *(sent[d] for d in straight))
+    sent.update(zip(straight, rest))
+
+    exchange(sent, held, straight)
+    if shard_count == 2:
+        other_rest = join([half_rest, swap(half_rest, "ctx", near_axis[0])], 0, bit)
+        full_rest = join([own_rest, other_rest], 0, shard)
+    else:
+        full_rest = lax.all_gather(half_rest, "shard", axis=0, tiled=True)
+    full_query = full_rest[:, :heads_width]
+    full_out_t = full_rest[:, heads_width : 2 * heads_width]
+    full_down_t = full_rest[:, 2 * heads_width :]
+    q_pre = dot(normed_input, full_query)
     queries = rope(q_pre, cosine, sine, scale_q)
-    queries, full_out = settle(held, late, queries, join(out_pieces, 1, shard))
+    queries, full_out_t = settle(held, straight, queries, full_out_t)
     held = [held[d] for d in range(1, count)]
     attended, attn_out, lse = attend(meta, docs, queries, key_value, held)
 
-    full_gate_up = full_units[:, : 2 * units]
-    full_down_t = full_units[:, 2 * units :]
-    full_key = join(k_pieces, 0, shard)
-    full_value = join(v_pieces, 0, shard)
-    full_query = join(q_pieces, 0, shard)
-
-    residual = inputs + pair_total(dot(attn_out, full_out))
+    residual = inputs + pair_total(dot_nt(attn_out, full_out_t))
     normal_two, factor_two = rms_parts(residual)
     normed_two = (normal_two * scale_post).astype(BF16)
     gate_upward = dot(normed_two, full_gate_up)
@@ -591,67 +720,64 @@
     sigma = jax.nn.sigmoid(gate_act)
     silu_act = gate_act * sigma
     hidden = (silu_act * upward).astype(BF16)
-    grad_down = dot_tn(cotangent, hidden).astype(BF16)
-    cotangent, grad_down = tie(cotangent, grad_down)
     d_hidden = dot(cotangent, full_down_t)
     d_gate = (d_hidden * upward * sigma * (1.0 + gate_act * (1.0 - sigma))).astype(BF16)
     d_up = (d_hidden * silu_act).astype(BF16)
-    d_gate_up = jnp.concatenate([d_gate, d_up], axis=1)
-    grad_gate_up = dot_tn(normed_two, d_gate_up).astype(BF16)
-    d_gate_up, grad_gate_up = tie(d_gate_up, grad_gate_up)
-    d_normed_two = pair_total(product_nt(d_gate_up, full_units, BF16))
+    middle = units // 2
+    units_a = over_shard([(normed_two, d_gate, 0, units), (normed_two, d_up, 0, middle)])
+    units_b, units_b_away = over_near_then_shard(
+        [(normed_two, d_up, middle, units), (cotangent, hidden, 0, units)], near_axis
+    )
+    d_normed_two = pair_total(
+        product_nt((d_gate, full_gate_up, 0), (d_up, full_gate_up, 1))
+    )
     hidden, d_normed_two = tie(hidden, d_normed_two)
-    mixed_part = product_nt(hidden, full_units, BF16, 2)
+    mixed_part = product_nt((hidden, full_down_t, 0))
     mixed = (residual + pair_total(mixed_part)).astype(BF16)
-    shared_units = to_shard_owner(grad_gate_up, grad_down)
     grad_post = jnp.sum(d_normed_two * normal_two, axis=0)
     d_residual = cotangent.astype(F32) + rms_back(
         d_normed_two * scale_post, normal_two, factor_two
     )
 
     d_branch = d_residual.astype(BF16)
-    d_attn = product_nt(d_branch, full_out, BF16)
+    d_attn = dot(d_branch, full_out_t).astype(BF16)
     d_queries, d_kv, given = attend_back(
         meta, docs, queries, d_attn, attended, lse, key_value, held
     )
-    masks = [1 << b for b in range(count.bit_length() - 1)]
-    near_axis, far_axis = masks[:1], masks[1:]
     given = dict(zip(range(1, count), given))
     returned = {}
-    exchange(given, returned, early)
-    grad_out = dot_tn(d_branch, attn_out).astype(BF16)
-    d_queries, shared_units, grad_out, *rest = settle(
-        returned, early, d_queries, shared_units, grad_out, *(given[d] for d in late)
-    )
-    given.update(zip(late, rest))
-    exchange(given, returned, late)
-    unit_chain = halve(shared_units, near_axis)
+    exchange(given, returned, straight)
+    units_a = halve(units_a, near_axis)
+    if units_b_away is not None:
+        units_b = units_b + [swap(total(units_b_away()), "shard")]
     d_q_pre, gq_part = rope_back(d_queries, q_pre, cosine, sine, scale_q)
-    grad_query = dot_tn(normed_input, d_q_pre).astype(BF16)
-    out_query = to_shard_owner(grad_out, grad_query)
-    (unit_chain,) = settle(returned, late, unit_chain)
+    out_query = over_shard(
+        [(d_branch, attn_out, 0, heads_width), (normed_input, d_q_pre, 0, heads_width)]
+    )
+    units_a[-1], units_b[-1], out_query[0], *rest = settle(
+        returned, straight, units_a[-1], units_b[-1], out_query[0], *(given[d] for d in crossing)
+    )
+    given.update(zip(crossing, rest))
+    exchange(given, returned, crossing)
+    out_query[-1], d_kv = settle(returned, crossing, out_query[-1], d_kv)
     returned = [returned[d] for d in range(1, count)]
 
-    first = sum(
-        jnp.where(part < p, g.astype(F32), 0.0) for p, g in zip(other_parts, returned)
-    )
-    second = sum(
-        jnp.where(part < p, 0.0, g.astype(F32)) for p, g in zip(other_parts, returned)
-    )
-    d_kv = d_kv + jnp.concatenate([first, second], axis=1)
-    d_k_pre, gk_part = rope_back(d_kv[0], k_pre, cosine, sine, scale_k)
-    d_v_pre = d_kv[1].astype(BF16)
-    d_kv_pre = jnp.concatenate([d_k_pre, d_v_pre], axis=1)
-    grad_kv = dot_tn(normed_input, d_kv_pre).astype(BF16)
-
-    unit_chain = halve(unit_chain, far_axis)
-    rest_chain = jnp.concatenate([out_query, to_shard_owner(grad_kv)], axis=1)
-    unit_chain, rest_chain, d_q_pre, d_k_pre, d_v_pre = tie(
-        unit_chain, rest_chain, d_q_pre, d_k_pre, d_v_pre
-    )
-
-    unit_chain = double(unit_chain, far_axis)
-    rest_chain = halve(rest_chain, near_axis)
+    units_a = halve(units_a, far_axis)
+    units_b = halve(units_b, far_axis)
+    out_query = halve(out_query, near_axis)
+    d_k_pre, d_v_pre, gk_part = key_value_back(
+        meta, docs, d_kv, returned, k_pre, cosine, sine, scale_k
+    )
+    key_value_grad = over_shard(
+        [(normed_input, d_k_pre, 0, kv_width), (normed_input, d_v_pre, 0, kv_width)]
+    )
+    units_a, units_b = total(units_a), total(units_b)
+    units_a, units_b, out_query[-1], key_value_grad[-1], d_q_pre, d_k_pre, d_v_pre = tie(
+        units_a, units_b, out_query[-1], key_value_grad[-1], d_q_pre, d_k_pre, d_v_pre
+    )
+
+    units_chain = double(jnp.concatenate([units_a, units_b], axis=1), far_axis)
+    key_value_grad = halve(key_value_grad, near_axis)
     d_normed = pair_total(
         dot_nt(d_q_pre, full_query) + dot_nt(d_k_pre, full_key) + dot_nt(d_v_pre, full_value)
     )
@@ -662,35 +788,35 @@
     gain_grads = gain_grads.reshape(-1, HEAD)
     if shard_count != 2:
         gain_grads = lax.psum(gain_grads, "shard")
-    unit_chain, rest_chain, gain_grads = tie(unit_chain, rest_chain, gain_grads)
-
-    owned_gate_up = double(unit_chain[:, : 2 * units], near_axis)
-    owned_down = unit_chain[:, 2 * units :]
-    rest_chain = halve(rest_chain, far_axis)
+    units_chain, key_value_grad[-1], gain_grads = tie(
+        units_chain, key_value_grad[-1], gain_grads
+    )
+
+    cut = units_chain.shape[1] // 2
+    owned_a = double(units_chain[:, :cut], near_axis)
+    owned_b = units_chain[:, cut:]
+    rest_chain = jnp.concatenate([total(out_query), total(key_value_grad)], axis=1)
+    rest_chain = total(halve([rest_chain], far_axis))
     gain_grads = gain_grads + swap(gain_grads, "tp")
     gain_grads = gain_grads + swap(gain_grads, "ctx", masks[0])
-    owned_gate_up, owned_down, rest_chain, gain_grads = tie(
-        owned_gate_up, owned_down, rest_chain, gain_grads
-    )
-
-    owned_down = double(owned_down, near_axis)
+    owned_a, owned_b, rest_chain, gain_grads = tie(owned_a, owned_b, rest_chain, gain_grads)
+
+    owned_b = double(owned_b, near_axis)
     rest_chain = double(rest_chain, far_axis)
     for mask in masks[1:]:
         gain_grads = gain_grads + swap(gain_grads, "ctx", mask)
-    owned_down, rest_chain, gain_grads = tie(owned_down, rest_chain, gain_grads)
-
-    rest_chain = double(rest_chain, near_axis)
+    owned_b, rest_chain, gain_grads = tie(owned_b, rest_chain, gain_grads)
+
+    owned_rest = double(rest_chain, near_axis).astype(F32)
     if shard_count == 2:
         gain_grads = gain_grads + swap(gain_grads, "shard")
     gain_grads = gain_grads.reshape(-1)
-    owned_gate_up = owned_gate_up.astype(F32)
-    owned_down = owned_down.astype(F32)
-    owned_rest = rest_chain.astype(F32)
     cuts = [0, heads_width, 2 * heads_width, 2 * heads_width + kv_width]
     cuts = cuts + [cuts[-1] + kv_width]
     owned_out, owned_query, owned_key, owned_value = (
         owned_rest[:, lo:hi] for lo, hi in zip(cuts[:-1], cuts[1:])
     )
+    owned_up = jnp.concatenate([owned_a[:, units:], owned_b[:, :middle]], axis=1)
     own_gains = []
     for lo, size in ((0, model), (model, model), (2 * model, HEAD), (2 * model + HEAD, HEAD)):
         size = size // shard_count
@@ -702,9 +828,9 @@
         owned_key,
         owned_value,
         owned_out.T,
-        owned_gate_up[:, :units],
-        owned_gate_up[:, units:],
-        owned_down.T,
+        owned_a[:, :units].astype(F32),
+        owned_up.astype(F32),
+        owned_b[:, middle:].astype(F32).T,
         *own_gains,
     )
 

time: 697 us -> 663 us (0.951)
  waiting for transfers between devices: 372 us -> 291 us
  Pallas kernels: 71.2 us -> 121 us
  starting transfers between devices: 51.2 us -> 90.7 us
  between operations: 44.7 us -> 15.5 us
  local copies, waits for them, and re-layouts: 57.3 us -> 46.8 us
    ppermute x25 -> x33, waiting for transfers between devices: 266 us -> 164 us  [swap(): return lax.ppermute(value, axis, [(i, i ^ level) for i in range(count)])]
    ppermute x14, waiting for transfers between devices: 44.2 us -> 120 us  [exchange(): done[d] = lax.ppermute(values[d], 'ctx', [(i, i ^ d) for i in range(count)])]
    pallas_call x5 -> x13, Pallas kernels: 17.2 us -> 69.7 us  [the longest x8 44.8 us: split_product(): pl.pallas_call(functools.partial(split_product_kernel, spans), grid_spec=...]
    ppermute x5 -> x3, waiting for transfers between devices: 55.4 us -> 4.82 us  [pieces_of(): lax.ppermute(own, axis, [((i + j) % count, i) for i in range(count)])]
    ppermute x25 -> x33, starting transfers between devices: 24.5 us -> 66.1 us  [swap(): return lax.ppermute(value, axis, [(i, i ^ level) for i in range(count)])]
    convert_element_type x6 -> x21, other arithmetic: 3.65 us -> 27.7 us  [the longest x11 18.7 us: total(): return sum((a.astype(F32) for a in addends)).astype(BF16)]
    add x10 -> x0, other arithmetic: 21.6 us -> none  [the longest x3 10.7 us: to_shard_owner(): rows_of(index).astype(F32) + swap(rows_of(1 - index), 'shard').astype(F32)]
    dot_general x5 -> x0, matrix products: 13.9 us -> none  [dot_tn(): lax.dot_general(a, b, (((0,), (0,)), ((), ())), preferred_element_type=F32)]
  transfers between devices with their start and end apart: 49 -> 55, of which waited for: 23 -> 22; matrix products, arithmetic and copies ran while one was open for 12% -> 13% of each run, Pallas kernels for 10% -> 17%
where the time goes in v5:
time: 663 us; the launch traced here: 653 us
  waiting for transfers between devices  291 us (44%)
  Pallas kernels  121 us (18%)
  starting transfers between devices  90.7 us (14%)
  other arithmetic  57.8 us (9%)
  local copies, waits for them, and re-layouts  46.8 us (7%)
  matrix products  29.4 us (4%)
  between operations  15.5 us (2%)
    ppermute x33, waiting for transfers between devices, swap(): return lax.ppermute(value, axis, [(i, i ^ level) for i in range(count)])  164 us
    ppermute x14, waiting for transfers between devices, exchange(): done[d] = lax.ppermute(values[d], 'ctx', [(i, i ^ d) for i in range(count)])  120 us
    ppermute x33, starting transfers between devices, swap(): return lax.ppermute(value, axis, [(i, i ^ level) for i in range(count)])  66.1 us
    pallas_call x8, Pallas kernels, split_product(): pl.pallas_call(functools.partial(split_product_kernel, spans), grid_spec=...  44.8 us
    unnamed x191, local copies, waits for them, and re-layouts  30.4 us
    pallas_call x1, Pallas kernels, attend_back(): pl.pallas_call(functools.partial(backward_kernel, docs, count), grid_spec...  28.8 us
    dot_general x6, matrix products, dot(): return jnp.dot(a, b, preferred_element_type=F32)  21.1 us
    ppermute x14, starting transfers between devices, exchange(): done[d] = lax.ppermute(values[d], 'ctx', [(i, i ^ d) for i in range(count)])  19.1 us
  transfers between devices with their start and end apart: 55, of which 22 were waited for; matrix products, arithmetic and copies ran while one was open for 13% of the time, Pallas kernels for 17%

profile of v5, /device:TPU:0, one launch (start us, length us, event | category | flops | bytes accessed | tf_op | source)
XLA Modules:
  0.0 652.6 jit_solution(5086007480348277855)
XLA Ops:
  46.5 6.9 %shard_map.246 = (bf16[512,1024]{1,0:T(8,128)(2,1)S(1)}, bf16[256,1024]{1,0:T(8,128)(2,1)}, bf16[256,1024]{1,0:T(8,128)(2,1)S(1)}, bf16[256,1024]{1,0:T(8,128)(2...) custom-call(s32[18]{0:T(128)S(1)} %pad_add_fusion.meta_ref, ...), custom_call_target="tpu_custom_call" | custom-call | flops 1000 | bytes 1000 | tf_op jit(solution)/shard_map/pallas_call | solution.py:269
  63.4 31.7 %collective-permute-done.3.refs_8_.refs_9_ = bf16[256,1024]{1,0:T(8,128)(2,1)S(1)} collective-permute-done((bf16[256,1024]{1,0:T(8,128)(2,1)}, bf16[256,1024]{1,0:T(8,128)(2,1)S(1)}, u32[]{:S(2)}, u32[]{:S(2)}) %collective-permute-start.3) | collective-permute-done | bytes 524320 | tf_op jit(solution)/shard_map/ppermute | solution.py:91
  95.1 11.3 %collective-permute-done.5.refs_0_.refs_1_ = bf16[256,1024]{1,0:T(8,128)(2,1)S(1)} collective-permute-done((bf16[256,1024]{1,0:T(8,128)(2,1)}, bf16[256,1024]{1,0:T(8,128)(2,1)S(1)}, u32[]{:S(2)}, u32[]{:S(2)}) %collective-permute-start.5) | collective-permute-done | bytes 524320 | tf_op jit(solution)/shard_map/ppermute | solution.py:91
  112.5 35.0 %collective-permute-done.11 = bf16[256,3584]{1,0:T(8,128)(2,1)} collective-permute-done((bf16[256,3584]{1,0:T(8,128)(2,1)}, bf16[256,3584]{1,0:T(8,128)(2,1)}, u32[]{:S(2)}, u32[]{:S(2)}) %collective-permute-start.11) | collective-permute-done | bytes 1835040 | tf_op jit(solution)/shard_map/ppermute | solution.py:81
  158.8 18.4 %shard_map.248 = (f32[512,1024]{1,0:T(8,128)}, bf16[512,1024]{1,0:T(8,128)(2,1)S(1)}, f32[512,1024]{1,0:T(8,128)}) custom-call(s32[18]{0:T(128)S(1)} %pad_add_fusion.meta_ref, bf16[512,1024]{1,0:T(8,128)(2,1)S(1)} %shard_map.247.q_ref, bf16[512,1024]{1,0:T(8,128)(2,1)} %copy-done.6, bf16[512,1024]{1,0:T(8,128)(2,1)} %copy-done.6, ...), custom_call_target="tpu_custom_call" | custom-call | flops 1000 | bytes 1000 | tf_op jit(solution)/shard_map/pallas_call | solution.py:548
  183.5 5.6 fusion.32
  189.1 5.9 multiply_convert_fusion
  195.0 7.9 %shard_map.249 = bf16[512,1024]{1,0:T(8,128)(2,1)} custom-call(bf16[512,1536]{1,0:T(8,128)(2,1)S(1)} %get-tuple-element.212.refs_0_.refs_1_, bf16[1024,3072]{1,0:T(8,128)(2,1)} %all-gather.2.cloned.1.call-done.refs_1_.refs_3_, bf16[512,1536]{1,0:T(8,128)(2,1)S(1)} %get-tuple-element.211.refs_2_.refs_3_.refs_1_, ...), custom_call_target="tpu_custom_call" | custom-call | flops 1000 | bytes 1000 | tf_op jit(solution)/shard_map/pallas_call | solution.py:170
  206.0 17.3 %shard_map.255 = bf16[512,2304]{1,0:T(8,128)(2,1)} custom-call(s32[2]{0:T(128)S(1)} %get-tuple-element.243.which_ref, bf16[512,1024]{1,0:T(8,128)(2,1)S(1)} %multiply_convert_fusion.3.refs_0_.refs_2_, bf16[512,1536]{1,0:T(8,128)(2,1)S(1)} %copy-done.1, bf16[512,1024]{1,0:T(8,128)(2,1)S(1)} %copy-done.5, bf16[512,1536]{1,0:T(8,128)(2,1)S(1)} %copy-done.10), custom_call_target="tpu_custom_call" | custom-call | flops 1000 | bytes 1000 | tf_op jit(solution)/shard_map/pallas_call | solution.py:206
  250.3 28.8 %shard_map.253 = (f32[512,1024]{1,0:T(8,128)}, f32[2,512,512]{2,1,0:T(8,128)}, bf16[2,256,512]{2,1,0:T(8,128)(2,1)S(1)}, bf16[2,256,512]{2,1,0:T(8,128)(2,1)}, b...) custom-call(s32[18]{0:T(128)S(1)} %pad_add_fusion.meta_ref, ...), custom_call_target="tpu_custom_call" | custom-call | flops 1000 | bytes 1000 | tf_op jit(solution)/shard_map/pallas_call | solution.py:574
  301.2 34.1 %collective-permute-done.16.refs_3_ = bf16[2,256,512]{2,1,0:T(8,128)(2,1)S(1)} collective-permute-done((bf16[2,256,512]{2,1,0:T(8,128)(2,1)S(1)}, bf16[2,256,512]{2,1,0:T(8,128)(2,1)S(1)}, u32[]{:S(2)}, u32[]{:S(2)}) %collective-permute-start.16) | collective-permute-done | bytes 524320 | tf_op jit(solution)/shard_map/ppermute | solution.py:91
  342.4 7.8 %collective-permute-done.18.refs_1_ = bf16[2,256,512]{2,1,0:T(8,128)(2,1)} collective-permute-done((bf16[2,256,512]{2,1,0:T(8,128)(2,1)}, bf16[2,256,512]{2,1,0:T(8,128)(2,1)}, u32[]{:S(2)}, u32[]{:S(2)}) %collective-permute-start.18) | collective-permute-done | bytes 524320 | tf_op jit(solution)/shard_map/ppermute | solution.py:91
  350.2 14.4 %collective-permute-done.21 = bf16[256,2304]{1,0:T(8,128)(2,1)} collective-permute-done((bf16[256,2304]{1,0:T(8,128)(2,1)}, bf16[256,2304]{1,0:T(8,128)(2,1)}, u32[]{:S(2)}, u32[]{:S(2)}) %collective-permute-start.21) | collective-permute-done | bytes 1179680 | tf_op jit(solution)/shard_map/ppermute | solution.py:81
  372.6 28.3 %collective-permute-done.28.refs_4_ = bf16[2,256,512]{2,1,0:T(8,128)(2,1)S(1)} collective-permute-done((bf16[2,256,512]{2,1,0:T(8,128)(2,1)S(1)}, bf16[2,256,512]{2,1,0:T(8,128)(2,1)S(1)}, u32[]{:S(2)}, u32[]{:S(2)}) %collective-permute-start.28) | collective-permute-done | bytes 524320 | tf_op jit(solution)/shard_map/ppermute | solution.py:91
  407.1 6.4 collective-permute-done.30.refs_0_
  413.5 17.1 %collective-permute-start.22 = (bf16[64,2304]{1,0:T(8,128)(2,1)}, bf16[64,2304]{1,0:T(8,128)(2,1)}, u32[]{:S(2)}, u32[]{:S(2)}) collective-permute-start(bf16[64,2304]{1,0:T(8,128)(2,1)} %get-tuple-element.221), channel_id=1, source_target_pairs={{0,4},{2,6},{4,0},{6,2},{8,12},{10,14},{12,8},{14,10},{1,5},{3,7},... | collective-permute-start | bytes 884744 | tf_op jit(solution)/shard_map/ppermute | solution.py:81
  446.2 11.1 %collective-permute-done.23 = bf16[64,2304]{1,0:T(8,128)(2,1)} collective-permute-done((bf16[64,2304]{1,0:T(8,128)(2,1)}, bf16[64,2304]{1,0:T(8,128)(2,1)}, u32[]{:S(2)}, u32[]{:S(2)}) %collective-permute-start.23) | collective-permute-done | bytes 294944 | tf_op jit(solution)/shard_map/ppermute | solution.py:81
  482.0 10.2 %collective-permute-done.36 = bf16[64,4608]{1,0:T(8,128)(2,1)S(1)} collective-permute-done((bf16[64,4608]{1,0:T(8,128)(2,1)S(1)}, bf16[64,4608]{1,0:T(8,128)(2,1)S(1)}, u32[]{:S(2)}, u32[]{:S(2)}) %collective-permute-start.36) | collective-permute-done | bytes 589856 | tf_op jit(solution)/shard_map/ppermute | solution.py:81
  492.5 18.4 %collective-permute-done.37 = bf16[64,4608]{1,0:T(8,128)(2,1)S(1)} collective-permute-done((bf16[64,4608]{1,0:T(8,128)(2,1)S(1)}, bf16[64,4608]{1,0:T(8,128)(2,1)S(1)}, u32[]{:S(2)}, u32[]{:S(2)}) %collective-permute-start.37) | collective-permute-done | bytes 589856 | tf_op jit(solution)/shard_map/ppermute | solution.py:81
  517.5 11.5 %collective-permute-start.41 = (bf16[64,3072]{1,0:T(8,128)(2,1)}, bf16[64,3072]{1,0:T(8,128)(2,1)}, u32[]{:S(2)}, u32[]{:S(2)}) collective-permute-start(bf16[64,3072]{1,0:T(8,128)(2,1)} %get-tuple-element.228), channel_id=1, source_target_pairs={{0,4},{2,6},{4,0},{6,2},{8,12},{10,14},{12,8},{14,10},{1,5},{3,7},... | collective-permute-start | bytes 1179656 | tf_op jit(solution)/shard_map/ppermute | solution.py:81
  543.5 15.6 %collective-permute-done.42 = bf16[64,3072]{1,0:T(8,128)(2,1)} collective-permute-done((bf16[64,3072]{1,0:T(8,128)(2,1)}, bf16[64,3072]{1,0:T(8,128)(2,1)}, u32[]{:S(2)}, u32[]{:S(2)}) %collective-permute-start.42) | collective-permute-done | bytes 393248 | tf_op jit(solution)/shard_map/ppermute | solution.py:81
  563.5 5.8 collective-permute-start.50
  578.2 26.3 %collective-permute-done.51 = f32[18,128]{1,0:T(8,128)S(1)} collective-permute-done((f32[18,128]{1,0:T(8,128)S(1)}, f32[18,128]{1,0:T(8,128)S(1)}, u32[]{:S(2)}, u32[]{:S(2)}) %collective-permute-start.51) | collective-permute-done | bytes 9248 | tf_op jit(solution)/shard_map/ppermute | solution.py:81
  619.6 18.6 %collective-permute-done.52 = bf16[256,3072]{1,0:T(8,128)(2,1)} collective-permute-done((bf16[256,3072]{1,0:T(8,128)(2,1)S(1)}, bf16[256,3072]{1,0:T(8,128)(2,1)}, u32[]{:S(2)}, u32[]{:S(2)}) %collective-permute-start.52) | collective-permute-done | bytes 1572896 | tf_op jit(solution)/shard_map/ppermute | solution.py:81
  (390 shorter events, 242.8 us)
Async XLA Ops:
  7.2 176.3 %all-gather.2.cloned.1.call-start = ((), (), s32[]{:S(2)}) async-start(), calls=%async_computation | async-start | bytes 9437184 | tf_op jit(solution)/shard_map/all_gather | solution.py:683
  36.7 69.7 %collective-permute-start.7 = (bf16[256,3584]{1,0:T(8,128)(2,1)}, bf16[256,3584]{1,0:T(8,128)(2,1)}, u32[]{:S(2)}, u32[]{:S(2)}) collective-permute-start(bf16[256,3584]{1,0:T(8,128)(2,1)} %constant_dynamic-slice_fusion), channel_id=1, source_target_pairs={{0,16},{16,0},{1,17},{17,1},{2,18},{18,2},{3,19},{19,3},{4,20},{20... | collective-permute-start | bytes 5505032 | tf_op jit(solution)/shard_map/ppermute | solution.py:81
  56.8 38.3 %collective-permute-start.3 = (bf16[256,1024]{1,0:T(8,128)(2,1)}, bf16[256,1024]{1,0:T(8,128)(2,1)S(1)}, u32[]{:S(2)}, u32[]{:S(2)}) collective-permute-start(bf16[256,1024]{1,0:T(8,128)(2,1)} %get-tuple-element.104), channel_id=1, source_target_pairs={{0,10},{2,8},{4,14},{6,12},{8,2},{10,0},{12,6},{14,4},{1,11},{3,9}... | collective-permute-start | bytes 1572872 | tf_op jit(solution)/shard_map/ppermute | solution.py:91
  61.6 44.8 %collective-permute-start.5 = (bf16[256,1024]{1,0:T(8,128)(2,1)}, bf16[256,1024]{1,0:T(8,128)(2,1)S(1)}, u32[]{:S(2)}, u32[]{:S(2)}) collective-permute-start(bf16[256,1024]{1,0:T(8,128)(2,1)} %get-tuple-element.106), channel_id=1, source_target_pairs={{0,2},{2,0},{4,6},{6,4},{8,10},{10,8},{12,14},{14,12},{1,3},{3,1},... | collective-permute-start | bytes 1572872 | tf_op jit(solution)/shard_map/ppermute | solution.py:91
  63.1 43.3 %collective-permute-start.6 = (bf16[256,1024]{1,0:T(8,128)(2,1)}, bf16[256,1024]{1,0:T(8,128)(2,1)S(1)}, u32[]{:S(2)}, u32[]{:S(2)}) collective-permute-start(bf16[256,1024]{1,0:T(8,128)(2,1)} %get-tuple-element.107), channel_id=1, source_target_pairs={{0,6},{2,4},{4,2},{6,0},{8,14},{10,12},{12,10},{14,8},{1,7},{3,5},... | collective-permute-start | bytes 1572872 | tf_op jit(solution)/shard_map/ppermute | solution.py:91
  106.4 41.0 %collective-permute-start.11 = (bf16[256,3584]{1,0:T(8,128)(2,1)}, bf16[256,3584]{1,0:T(8,128)(2,1)}, u32[]{:S(2)}, u32[]{:S(2)}) collective-permute-start(bf16[256,3584]{1,0:T(8,128)(2,1)} %collective-permute-done.7), channel_id=1, source_target_pairs={{0,2},{2,0},{4,6},{6,4},{8,10},{10,8},{12,14},{14,12},{1,3},{3,1},... | collective-permute-start | bytes 5505032 | tf_op jit(solution)/shard_map/ppermute | solution.py:81
  108.1 50.6 %collective-permute-start.10 = (bf16[256,1024]{1,0:T(8,128)(2,1)}, bf16[256,1024]{1,0:T(8,128)(2,1)S(1)}, u32[]{:S(2)}, u32[]{:S(2)}) collective-permute-start(bf16[256,1024]{1,0:T(8,128)(2,1)} %copy-done.50), channel_id=1, source_target_pairs={{0,4},{2,6},{4,0},{6,2},{8,12},{10,14},{12,8},{14,10},{1,5},{3,7},... | collective-permute-start | bytes 1572872 | tf_op jit(solution)/shard_map/ppermute | solution.py:91
  108.6 50.1 %collective-permute-start.8 = (bf16[256,1024]{1,0:T(8,128)(2,1)}, bf16[256,1024]{1,0:T(8,128)(2,1)S(1)}, u32[]{:S(2)}, u32[]{:S(2)}) collective-permute-start(bf16[256,1024]{1,0:T(8,128)(2,1)} %copy-done.49), channel_id=1, source_target_pairs={{0,8},{2,10},{4,12},{6,14},{8,0},{10,2},{12,4},{14,6},{1,9},{3,11}... | collective-permute-start | bytes 1572872 | tf_op jit(solution)/shard_map/ppermute | solution.py:91
  112.1 46.5 %collective-permute-start.9 = (bf16[256,1024]{1,0:T(8,128)(2,1)}, bf16[256,1024]{1,0:T(8,128)(2,1)S(1)}, u32[]{:S(2)}, u32[]{:S(2)}) collective-permute-start(bf16[256,1024]{1,0:T(8,128)(2,1)} %copy-done.48), channel_id=1, source_target_pairs={{0,12},{2,14},{4,8},{6,10},{8,4},{10,6},{12,0},{14,2},{1,13},{3,15... | collective-permute-start | bytes 1572872 | tf_op jit(solution)/shard_map/ppermute | solution.py:91
  202.9 40.0 %collective-permute-start.13 = (bf16[512,1024]{1,0:T(8,128)(2,1)}, bf16[512,1024]{1,0:T(8,128)(2,1)}, u32[]{:S(2)}, u32[]{:S(2)}) collective-permute-start(bf16[512,1024]{1,0:T(8,128)(2,1)} %shard_map.249), channel_id=1, source_target_pairs={{0,1},{1,0},{2,3},{3,2},{4,5},{5,4},{6,7},{7,6},{8,9},{9,8},{10,11... | collective-permute-start | bytes 3145736 | tf_op jit(solution)/shard_map/ppermute | solution.py:75
  223.3 68.1 %collective-permute-start.20 = (bf16[512,2304]{1,0:T(8,128)(2,1)}, bf16[512,2304]{1,0:T(8,128)(2,1)}, u32[]{:S(2)}, u32[]{:S(2)}) collective-permute-start(bf16[512,2304]{1,0:T(8,128)(2,1)} %shard_map.255), channel_id=1, source_target_pairs={{0,2},{2,0},{4,6},{6,4},{8,10},{10,8},{12,14},{14,12},{1,3},{3,1},... | collective-permute-start | bytes 7077896 | tf_op jit(solution)/shard_map/ppermute | solution.py:81
  229.8 66.2 %collective-permute-start.15 = (bf16[512,2304]{1,0:T(8,128)(2,1)}, bf16[512,2304]{1,0:T(8,128)(2,1)}, u32[]{:S(2)}, u32[]{:S(2)}) collective-permute-start(bf16[512,2304]{1,0:T(8,128)(2,1)} %shard_map.252), channel_id=1, source_target_pairs={{0,16},{16,0},{1,17},{17,1},{2,18},{18,2},{3,19},{19,3},{4,20},{20... | collective-permute-start | bytes 7077896 | tf_op jit(solution)/shard_map/ppermute | solution.py:81
  291.3 81.2 %collective-permute-start.32 = (bf16[512,2048]{1,0:T(8,128)(2,1)}, bf16[512,2048]{1,0:T(8,128)(2,1)}, u32[]{:S(2)}, u32[]{:S(2)}) collective-permute-start(bf16[512,2048]{1,0:T(8,128)(2,1)} %shard_map.258), channel_id=1, source_target_pairs={{0,16},{16,0},{1,17},{17,1},{2,18},{18,2},{3,19},{19,3},{4,20},{20... | collective-permute-start | bytes 6291464 | tf_op jit(solution)/shard_map/ppermute | solution.py:81
  294.2 70.4 %collective-permute-start.21 = (bf16[256,2304]{1,0:T(8,128)(2,1)}, bf16[256,2304]{1,0:T(8,128)(2,1)}, u32[]{:S(2)}, u32[]{:S(2)}) collective-permute-start(bf16[256,2304]{1,0:T(8,128)(2,1)} %add_convert_fusion), channel_id=1, source_target_pairs={{0,16},{16,0},{1,17},{17,1},{2,18},{18,2},{3,19},{19,3},{4,20},{20... | collective-permute-start | bytes 3538952 | tf_op jit(solution)/shard_map/ppermute | solution.py:81
  298.6 66.0 %collective-permute-start.19 = (bf16[256,2304]{1,0:T(8,128)(2,1)}, bf16[256,2304]{1,0:T(8,128)(2,1)}, u32[]{:S(2)}, u32[]{:S(2)}) collective-permute-start(bf16[256,2304]{1,0:T(8,128)(2,1)} %add_convert_fusion.1), channel_id=1, source_target_pairs={{0,2},{2,0},{4,6},{6,4},{8,10},{10,8},{12,14},{14,12},{1,3},{3,1},... | collective-permute-start | bytes 3538952 | tf_op jit(solution)/shard_map/ppermute | solution.py:81
  300.0 42.4 %collective-permute-start.17 = (bf16[2,256,512]{2,1,0:T(8,128)(2,1)}, bf16[2,256,512]{2,1,0:T(8,128)(2,1)}, u32[]{:S(2)}, u32[]{:S(2)}) collective-permute-start(bf16[2,256,512]{2,1,0:T(8,128)(2,1)} %get-tuple-element.133), channel_id=1, source_target_pairs={{0,12},{2,14},{4,8},{6,10},{8,4},{10,6},{12,0},{14,2},{1,13},{3,15... | collective-permute-start | bytes 1572872 | tf_op jit(solution)/shard_map/ppermute | solution.py:91
  366.7 46.9 %collective-permute-start.30 = (bf16[2,256,512]{2,1,0:T(8,128)(2,1)S(1)}, bf16[2,256,512]{2,1,0:T(8,128)(2,1)S(1)}, u32[]{:S(2)}, u32[]{:S(2)}) collective-permute-start(bf16[2,256,512]{2,1,0:T(8,128)(2,1)S(1)} %copy-done.43), channel_id=1, source_target_pairs={{0,2},{2,0},{4,6},{6,4},{8,10},{10,8},{12,14},{14,12},{1,3},{3,1},... | collective-permute-start | bytes 1572872 | tf_op jit(solution)/shard_map/ppermute | solution.py:91
  368.5 62.1 %collective-permute-start.31 = (bf16[2,256,512]{2,1,0:T(8,128)(2,1)S(1)}, bf16[2,256,512]{2,1,0:T(8,128)(2,1)S(1)}, u32[]{:S(2)}, u32[]{:S(2)}) collective-permute-start(bf16[2,256,512]{2,1,0:T(8,128)(2,1)S(1)} %copy-done.41), channel_id=1, source_target_pairs={{0,6},{2,4},{4,2},{6,0},{8,14},{10,12},{12,10},{14,8},{1,7},{3,5},... | collective-permute-start | bytes 1572872 | tf_op jit(solution)/shard_map/ppermute | solution.py:91
  372.6 67.4 %collective-permute-start.25 = (bf16[64,2304]{1,0:T(8,128)(2,1)S(1)}, bf16[64,2304]{1,0:T(8,128)(2,1)S(1)}, u32[]{:S(2)}, u32[]{:S(2)}) collective-permute-start(bf16[64,2304]{1,0:T(8,128)(2,1)S(1)} %get-tuple-element.218), channel_id=1, source_target_pairs={{0,4},{2,6},{4,0},{6,2},{8,12},{10,14},{12,8},{14,10},{1,5},{3,7},... | collective-permute-start | bytes 884744 | tf_op jit(solution)/shard_map/ppermute | solution.py:81
  400.9 41.4 %collective-permute-start.26 = (bf16[64,2304]{1,0:T(8,128)(2,1)S(1)}, bf16[64,2304]{1,0:T(8,128)(2,1)}, u32[]{:S(2)}, u32[]{:S(2)}) collective-permute-start(bf16[64,2304]{1,0:T(8,128)(2,1)S(1)} %get-tuple-element.220), channel_id=1, source_target_pairs={{0,8},{2,10},{4,12},{6,14},{8,0},{10,2},{12,4},{14,6},{1,9},{3,11}... | collective-permute-start | bytes 884744 | tf_op jit(solution)/shard_map/ppermute | solution.py:81
  400.9 42.8 %collective-permute-start.27 = (bf16[64,2304]{1,0:T(8,128)(2,1)S(1)}, bf16[64,2304]{1,0:T(8,128)(2,1)}, u32[]{:S(2)}, u32[]{:S(2)}) collective-permute-start(bf16[64,2304]{1,0:T(8,128)(2,1)S(1)} %get-tuple-element.219), channel_id=1, source_target_pairs={{0,12},{2,14},{4,8},{6,10},{8,4},{10,6},{12,0},{14,2},{1,13},{3,15... | collective-permute-start | bytes 884744 | tf_op jit(solution)/shard_map/ppermute | solution.py:81
  468.5 42.4 %collective-permute-start.37 = (bf16[64,4608]{1,0:T(8,128)(2,1)S(1)}, bf16[64,4608]{1,0:T(8,128)(2,1)S(1)}, u32[]{:S(2)}, u32[]{:S(2)}) collective-permute-start(bf16[64,4608]{1,0:T(8,128)(2,1)S(1)} %constant_dynamic-update-slice_fusion), channel_id=1, source_target_pairs={{0,8},{2,10},{4,12},{6,14},{8,0},{10,2},{12,4},{14,6},{1,9},{3,11}... | collective-permute-start | bytes 1769480 | tf_op jit(solution)/shard_map/ppermute | solution.py:81
  470.0 40.9 %collective-permute-start.38 = (bf16[64,4608]{1,0:T(8,128)(2,1)S(1)}, bf16[64,4608]{1,0:T(8,128)(2,1)S(1)}, u32[]{:S(2)}, u32[]{:S(2)}) collective-permute-start(bf16[64,4608]{1,0:T(8,128)(2,1)S(1)} %constant_dynamic-update-slice_fusion), channel_id=1, source_target_pairs={{0,12},{2,14},{4,8},{6,10},{8,4},{10,6},{12,0},{14,2},{1,13},{3,15... | collective-permute-start | bytes 1769480 | tf_op jit(solution)/shard_map/ppermute | solution.py:81
  515.6 45.2 %collective-permute-start.40 = (bf16[256,2304]{1,0:T(8,128)(2,1)}, bf16[256,2304]{1,0:T(8,128)(2,1)}, u32[]{:S(2)}, u32[]{:S(2)}) collective-permute-start(bf16[256,2304]{1,0:T(8,128)(2,1)} %get-tuple-element.225), channel_id=1, source_target_pairs={{0,2},{2,0},{4,6},{6,4},{8,10},{10,8},{12,14},{14,12},{1,3},{3,1},... | collective-permute-start | bytes 3538952 | tf_op jit(solution)/shard_map/ppermute | solution.py:81
  (125 other events, 2093.5 us)
Sparse Core Ops, SparseCore 0:
  63.5 82.2 all-gather.1

commit v6 on v5

--- a/solution.py
+++ b/solution.py
@@ -116,28 +116,10 @@
     return kept
 
 
-def over_shard(pairs):
-    count = lax.axis_size("shard")
-    index = lax.axis_index("shard")
-    if count != 2:
-        grads = [dot_tn(a, b[:, lo:hi]).astype(BF16) for a, b, lo, hi in pairs]
-        grad = jnp.concatenate(grads, axis=1)
-        return [lax.psum_scatter(grad, "shard", scatter_dimension=0, tiled=True)]
-    away, home = 2 * (1 - index), 2 * index
-    sent = split_product((away, away + 1), pairs)
-    return [split_product((home, home + 1), pairs), swap(sent, "shard")]
-
-
-def over_near_then_shard(pairs, near_axis):
-    count = lax.axis_size("shard")
-    index = lax.axis_index("shard")
-    bit = place_in(near_axis)
-    if count != 2:
-        return halve(over_shard(pairs), near_axis), None
-    sent = split_product((1 - bit, 3 - bit), pairs)
-    addends = [split_product((bit, 2 + bit), pairs), swap(sent, "ctx", near_axis[0])]
-    rows = addends[0].shape[0] // 2
-    return rows_at(addends, index, rows), lambda: rows_at(addends, 1 - index, rows)
+def scattered(pairs):
+    grads = [dot_tn(a, b[:, lo:hi]).astype(BF16) for a, b, lo, hi in pairs]
+    grad = jnp.concatenate(grads, axis=1)
+    return [lax.psum_scatter(grad, "shard", scatter_dimension=0, tiled=True)]
 
 
 def double(value, masks):
@@ -244,48 +226,82 @@
     return pl.multiple_of((1 - meta_ref[docs + d]) * half, half)
 
 
-def key_value_kernel(heads, docs, count, meta_ref, key_ref, value_ref, *refs):
-    cos_ref, sin_ref, gain_ref, out_ref = refs[:4]
+def key_value_kernel(heads, docs, count, pieces, meta_ref, normal_ref, scale_ref, *refs):
+    weights = refs[: 2 * pieces]
+    cos_ref, sin_ref, gain_ref = refs[2 * pieces : 2 * pieces + 3]
+    key_ref, out_ref, normed_ref = refs[2 * pieces + 3 : 2 * pieces + 6]
+    sent = refs[2 * pieces + 6 :]
     half = out_ref.shape[0] // 2
-
-    @pl.when(pl.program_id(0) < heads)
+    depth = normal_ref.shape[1] // pieces
+    step = pl.program_id(0)
+
+    @pl.when(step == 0)
     def _():
-        rope_kernel(key_ref, cos_ref, sin_ref, gain_ref, out_ref)
-
-    @pl.when(pl.program_id(0) >= heads)
+        normed_ref[...] = (normal_ref[...] * scale_ref[...]).astype(BF16)
+
+    def product(parts):
+        result = None
+        for j, part in enumerate(parts):
+            at = pl.multiple_of(meta_ref[docs + 2 * (count - 1) + j] * depth, HEAD)
+            term = dot(normed_ref[:, pl.ds(at, depth)], part[...])
+            result = term if result is None else result + term
+        return result
+
+    @pl.when(step < heads // 2)
     def _():
-        out_ref[...] = value_ref[...].astype(BF16)
-
-    for d, sent_ref in enumerate(refs[4:]):
+        key_ref[...] = product(weights[:pieces])
+        for a in range(2):
+            lanes = slice(a * HEAD, (a + 1) * HEAD)
+            pre = key_ref[:, lanes]
+            factor = lax.rsqrt(jnp.mean(pre * pre, axis=-1, keepdims=True) + EPS)
+            scaled = pre * factor * gain_ref[...]
+            turned = pltpu.roll(scaled, HEAD // 2, 1)
+            out_ref[:, lanes] = (scaled * cos_ref[...] + turned * sin_ref[...]).astype(BF16)
+
+    @pl.when(step >= heads // 2)
+    def _():
+        out_ref[...] = product(weights[pieces:]).astype(BF16)
+
+    for d, sent_ref in enumerate(sent):
         sent_ref[...] = out_ref[pl.ds(part_start(meta_ref, docs, d, half), half), :]
 
 
-def key_value_and_parts(meta, docs, count, key, value, cosine, sine, gain):
-    rows, width = key.shape
+def key_value_and_parts(meta, docs, count, normal, scale, keys, values, cosine, sine, gain):
+    rows, model = normal.shape
+    depth, width = keys[0].shape
     heads = width // HEAD
-    table = pl.BlockSpec((rows, HEAD), lambda h, m: (0, 0))
-    column = pl.BlockSpec((rows, HEAD), lambda h, m: (0, h))
-    part = pl.BlockSpec((rows // 2, HEAD), lambda h, m: (0, h))
+    half_steps = heads // 2
+    whole = lambda shape: pl.BlockSpec(shape, lambda h, m: (0, 0))
+    column = pl.BlockSpec((rows, 2 * HEAD), lambda h, m: (0, h))
+    key_spec = pl.BlockSpec((depth, 2 * HEAD), lambda h, m: (0, jnp.minimum(h, half_steps - 1)))
+    value_spec = pl.BlockSpec((depth, 2 * HEAD), lambda h, m: (0, jnp.maximum(h - half_steps, 0)))
+    part = pl.BlockSpec((rows // 2, 2 * HEAD), lambda h, m: (0, h))
     result = pl.pallas_call(
-        functools.partial(key_value_kernel, heads, docs, count),
+        functools.partial(key_value_kernel, heads, docs, count, len(keys)),
         grid_spec=pltpu.PrefetchScalarGridSpec(
             num_scalar_prefetch=1,
-            grid=(2 * heads,),
-            in_specs=[
-                pl.BlockSpec((rows, HEAD), lambda h, m: (0, jnp.minimum(h, heads - 1))),
-                pl.BlockSpec((rows, HEAD), lambda h, m: (0, jnp.maximum(h - heads, 0))),
-                table,
-                table,
-                pl.BlockSpec((1, HEAD), lambda h, m: (0, 0)),
-            ],
-            out_specs=[column] + [part] * (count - 1),
+            grid=(heads,),
+            in_specs=[whole((rows, model)), whole((1, model))]
+            + [key_spec] * len(keys)
+            + [value_spec] * len(values)
+            + [whole((rows, HEAD)), whole((rows, HEAD)), whole((1, HEAD))],
+            out_specs=[
+                pl.BlockSpec((rows, 2 * HEAD), lambda h, m: (0, jnp.minimum(h, half_steps - 1))),
+                column,
+                whole((rows, model)),
+            ]
+            + [part] * (count - 1),
         ),
-        out_shape=[jax.ShapeDtypeStruct((rows, 2 * width), BF16)]
+        out_shape=[
+            jax.ShapeDtypeStruct((rows, width), F32),
+            jax.ShapeDtypeStruct((rows, 2 * width), BF16),
+            jax.ShapeDtypeStruct((rows, model), BF16),
+        ]
         + [jax.ShapeDtypeStruct((rows // 2, 2 * width), BF16)] * (count - 1),
         compiler_params=pltpu.CompilerParams(vmem_limit_bytes=VMEM_LIMIT),
         cost_estimate=CHEAP,
-    )(meta, key, value, cosine, sine, gain)
-    return result[0], dict(zip(range(1, count), result[1:]))
+    )(meta, normal, scale, *keys, *values, cosine, sine, gain)
+    return result[0], result[1], result[2], dict(zip(range(1, count), result[3:]))
 
 
 def turn_back(grad, pre_ref, cos_ref, sin_ref, gain_ref, out_ref, sum_ref):
@@ -387,6 +403,17 @@
     return visible
 
 
+def mask_across(meta_ref, docs, shape, half, q_part, k_part, diagonal):
+    column = lax.broadcasted_iota(jnp.int32, (1, shape[1]), 1)
+    q_place = q_part * half + jnp.where(column >= half, column - half, column)
+    begin = doc_begins(meta_ref, docs, q_place) - k_part * half
+    row = lax.broadcasted_iota(jnp.int32, shape, 0)
+    visible = row >= begin
+    if diagonal:
+        visible = visible & (row <= q_place - k_part * half)
+    return visible
+
+
 def any_visible(meta_ref, docs, half, q_part, k_part):
     return (k_part + 1) * half > doc_begins(meta_ref, docs, q_part * half)
 
@@ -466,23 +493,27 @@
     for e in range(2):
         grads = two_heads(g_ref, e * half, half).astype(F32)
         delta = jnp.sum(grads * two_heads(o_ref, e * half, half), axis=1, keepdims=True)
-        delta_ref[e] = jnp.broadcast_to(delta, (2 * half, HEAD))
-        stats_ref[e] = two_heads(lse_ref, e * half, half)
+        delta = jnp.broadcast_to(delta, (2 * half, HEAD))
+        delta_ref[e] = jnp.transpose(delta)[:8]
+        stats_ref[e] = jnp.transpose(two_heads(lse_ref, e * half, half))[:8]
 
     def block(side, start, keys, values, q_part, k_part, diagonal):
         queries = two_heads(q_ref, start, half)
         grads = two_heads(g_ref, start, half)
-        scores = dot_nt(queries, keys)
-        repeat = half // HEAD
-        lse = jnp.concatenate([stats_ref[side]] * repeat, axis=1)
-        delta = jnp.concatenate([delta_ref[side]] * repeat, axis=1)
+        scores = dot_nt(keys, queries)
+        lse = stats_ref[side][:1]
+        delta = delta_ref[side][:1]
         weights = jnp.exp2(scores * (scale * LOG2E) - lse)
-        weights = masked(weights, meta_ref, docs, scores.shape, half, q_part, k_part, diagonal)
-        d_weights = dot_nt(grads, values)
+        if diagonal is not None:
+            visible = mask_across(
+                meta_ref, docs, scores.shape, half, q_part, k_part, diagonal
+            )
+            weights = jnp.where(visible, weights, 0.0)
+        d_weights = dot_nt(values, grads)
         d_scores = (weights * (d_weights - delta)).astype(BF16)
-        d_values = dot_tn(weights.astype(BF16), grads)
-        d_keys = dot_tn(d_scores, queries) * scale
-        return dot(d_scores, keys) * scale, d_keys, d_values
+        d_values = dot(weights.astype(BF16), grads)
+        d_keys = dot(d_scores, queries) * scale
+        return dot_tn(d_scores, keys) * scale, d_keys, d_values
 
     for e in range(2):
         rows = pl.ds(e * half, half)
@@ -579,7 +610,11 @@
             in_specs=[column] * 4 + key_value_specs(rows, half, kv_heads, count),
             out_specs=[column, pl.BlockSpec((2, rows, HEAD), lambda h, m: (0, 0, h))]
             + [pl.BlockSpec((2, half, HEAD), lambda h, m: (0, 0, h))] * (count - 1),
-            scratch_shapes=[pltpu.VMEM((2, 2 * half, HEAD), F32)] * 3,
+            scratch_shapes=[
+                pltpu.VMEM((2, 2 * half, HEAD), F32),
+                pltpu.VMEM((2, 8, 2 * half), F32),
+                pltpu.VMEM((2, 8, 2 * half), F32),
+            ],
         ),
         out_shape=[
             jax.ShapeDtypeStruct((rows, width), F32),
@@ -650,6 +685,7 @@
             starts[1:],
             (parts[1:] >= part).astype(jnp.int32),
             jnp.where(parts[1:] < part, parts[1:], 2 * count - 1 - parts[1:]),
+            (shard + jnp.arange(shard_count, dtype=jnp.int32)) % shard_count,
         ]
     ).astype(jnp.int32)
     row = jnp.arange(rows, dtype=jnp.int32)
@@ -676,7 +712,6 @@
         join([piece[lo:hi] for piece in packed_pieces], 0, shard).astype(F32).reshape(1, -1)
         for lo, hi in zip(cuts[:-1], cuts[1:])
     )
-    normed_input = (normal_one * scale_in).astype(BF16)
     full_key = join(k_pieces, 0, shard)
     full_value = join(v_pieces, 0, shard)
 
@@ -687,9 +722,8 @@
         half_rest = swap(half_rest, "shard")
     else:
         half_rest = own_rest
-    k_pre = dot(normed_input, full_key)
-    key_value, sent = key_value_and_parts(
-        meta, docs, count, k_pre, dot(normed_input, full_value), cosine, sine, scale_k
+    k_pre, key_value, normed_input, sent = key_value_and_parts(
+        meta, docs, count, normal_one, scale_in, k_pieces, v_pieces, cosine, sine, scale_k
     )
     held = {}
     exchange(sent, held, crossing)
@@ -724,10 +758,20 @@
     d_gate = (d_hidden * upward * sigma * (1.0 + gate_act * (1.0 - sigma))).astype(BF16)
     d_up = (d_hidden * silu_act).astype(BF16)
     middle = units // 2
-    units_a = over_shard([(normed_two, d_gate, 0, units), (normed_two, d_up, 0, middle)])
-    units_b, units_b_away = over_near_then_shard(
-        [(normed_two, d_up, middle, units), (cotangent, hidden, 0, units)], near_axis
-    )
+    away, home = (2 - 2 * shard, 3 - 2 * shard), (2 * shard, 2 * shard + 1)
+    bit = place_in(near_axis)
+
+    def pairs_a(normed):
+        return [(normed, d_gate, 0, units), (normed, d_up, 0, middle)]
+
+    def pairs_b(normed, upstream):
+        return [(normed, d_up, middle, units), (upstream, hidden, 0, units)]
+
+    if shard_count == 2:
+        sent_a = split_product(away, pairs_a(normed_two))
+        sent_b = split_product((1 - bit, 3 - bit), pairs_b(normed_two, cotangent))
+        d_gate, d_up, sent_a, sent_b = tie(d_gate, d_up, sent_a, sent_b)
+        got_a, got_b = swap(sent_a, "shard"), swap(sent_b, "ctx", near_axis[0])
     d_normed_two = pair_total(
         product_nt((d_gate, full_gate_up, 0), (d_up, full_gate_up, 1))
     )
@@ -747,16 +791,38 @@
     given = dict(zip(range(1, count), given))
     returned = {}
     exchange(given, returned, straight)
-    units_a = halve(units_a, near_axis)
-    if units_b_away is not None:
-        units_b = units_b + [swap(total(units_b_away()), "shard")]
+    if shard_count == 2:
+        first, second = straight[-1], straight[0]
+        normed_late, returned[first] = tie(normed_two, returned[first])
+        units_a = [split_product(home, pairs_a(normed_late)), got_a]
+        units_a = halve(units_a, near_axis)
+        normed_late, upstream_late, returned[second] = tie(
+            normed_two, cotangent, returned[second]
+        )
+        kept_b = split_product((bit, 2 + bit), pairs_b(normed_late, upstream_late))
+        units_b = [kept_b, got_b]
+        units_b_away = total(rows_at(units_b, 1 - shard, depth // 2))
+        units_b = rows_at(units_b, shard, depth // 2) + [swap(units_b_away, "shard")]
+    else:
+        units_a = halve(scattered(pairs_a(normed_two)), near_axis)
+        units_b = halve(scattered(pairs_b(normed_two, cotangent)), near_axis)
     d_q_pre, gq_part = rope_back(d_queries, q_pre, cosine, sine, scale_q)
-    out_query = over_shard(
-        [(d_branch, attn_out, 0, heads_width), (normed_input, d_q_pre, 0, heads_width)]
-    )
-    units_a[-1], units_b[-1], out_query[0], *rest = settle(
-        returned, straight, units_a[-1], units_b[-1], out_query[0], *(given[d] for d in crossing)
-    )
+    out_pairs = [(d_branch, attn_out, 0, heads_width), (normed_input, d_q_pre, 0, heads_width)]
+    if shard_count == 2:
+        out_query = [split_product(home, out_pairs), split_product(away, out_pairs)]
+    else:
+        out_query = scattered(out_pairs)
+    units_a[-1], units_b[-1], out_query[0], out_query[-1], *rest = settle(
+        returned,
+        straight,
+        units_a[-1],
+        units_b[-1],
+        out_query[0],
+        out_query[-1],
+        *(given[d] for d in crossing),
+    )
+    if shard_count == 2:
+        out_query[-1] = swap(out_query[-1], "shard")
     given.update(zip(crossing, rest))
     exchange(given, returned, crossing)
     out_query[-1], d_kv = settle(returned, crossing, out_query[-1], d_kv)
@@ -768,16 +834,25 @@
     d_k_pre, d_v_pre, gk_part = key_value_back(
         meta, docs, d_kv, returned, k_pre, cosine, sine, scale_k
     )
-    key_value_grad = over_shard(
-        [(normed_input, d_k_pre, 0, kv_width), (normed_input, d_v_pre, 0, kv_width)]
-    )
+    kv_pairs = [(normed_input, d_k_pre, 0, kv_width), (normed_input, d_v_pre, 0, kv_width)]
+    if shard_count == 2:
+        sent_kv = swap(split_product(away, kv_pairs), "shard")
+        key_value_grad = [split_product(home, kv_pairs), sent_kv]
+    else:
+        key_value_grad = scattered(kv_pairs)
     units_a, units_b = total(units_a), total(units_b)
     units_a, units_b, out_query[-1], key_value_grad[-1], d_q_pre, d_k_pre, d_v_pre = tie(
         units_a, units_b, out_query[-1], key_value_grad[-1], d_q_pre, d_k_pre, d_v_pre
     )
 
-    units_chain = double(jnp.concatenate([units_a, units_b], axis=1), far_axis)
+    units_a = double(units_a, far_axis)
     key_value_grad = halve(key_value_grad, near_axis)
+    units_a, units_b, key_value_grad[-1], out_query[-1] = tie(
+        units_a, units_b, key_value_grad[-1], out_query[-1]
+    )
+
+    units_b = double(units_b, far_axis)
+    owned_a = double(units_a, near_axis)
     d_normed = pair_total(
         dot_nt(d_q_pre, full_query) + dot_nt(d_k_pre, full_key) + dot_nt(d_v_pre, full_value)
     )
@@ -788,29 +863,34 @@
     gain_grads = gain_grads.reshape(-1, HEAD)
     if shard_count != 2:
         gain_grads = lax.psum(gain_grads, "shard")
-    units_chain, key_value_grad[-1], gain_grads = tie(
-        units_chain, key_value_grad[-1], gain_grads
-    )
-
-    cut = units_chain.shape[1] // 2
-    owned_a = double(units_chain[:, :cut], near_axis)
-    owned_b = units_chain[:, cut:]
-    rest_chain = jnp.concatenate([total(out_query), total(key_value_grad)], axis=1)
-    rest_chain = total(halve([rest_chain], far_axis))
+    rest_chain = [jnp.concatenate([total(out_query), total(key_value_grad)], axis=1)]
+    units_b, owned_a, rest_chain[0], gain_grads = tie(
+        units_b, owned_a, rest_chain[0], gain_grads
+    )
+
+    owned_b = double(units_b, near_axis)
+    rest_chain = total(halve(rest_chain, far_axis))
     gain_grads = gain_grads + swap(gain_grads, "tp")
     gain_grads = gain_grads + swap(gain_grads, "ctx", masks[0])
-    owned_a, owned_b, rest_chain, gain_grads = tie(owned_a, owned_b, rest_chain, gain_grads)
-
-    owned_b = double(owned_b, near_axis)
-    rest_chain = double(rest_chain, far_axis)
-    for mask in masks[1:]:
+    owned_b, rest_chain, gain_grads = tie(owned_b, rest_chain, gain_grads)
+
+    cut = rest_chain.shape[1] // 2
+    rest_a, rest_b = rest_chain[:, :cut], rest_chain[:, cut:]
+    rest_a = double(rest_a, far_axis)
+    gain_grads = gain_grads + swap(gain_grads, "ctx", masks[1])
+    rest_a, rest_b, gain_grads = tie(rest_a, rest_b, gain_grads)
+
+    rest_b = double(rest_b, far_axis)
+    rest_a = double(rest_a, near_axis)
+    for mask in masks[2:]:
         gain_grads = gain_grads + swap(gain_grads, "ctx", mask)
-    owned_b, rest_chain, gain_grads = tie(owned_b, rest_chain, gain_grads)
-
-    owned_rest = double(rest_chain, near_axis).astype(F32)
+    rest_a, rest_b, gain_grads = tie(rest_a, rest_b, gain_grads)
+
+    rest_b = double(rest_b, near_axis)
     if shard_count == 2:
         gain_grads = gain_grads + swap(gain_grads, "shard")
     gain_grads = gain_grads.reshape(-1)
+    owned_rest = jnp.concatenate([rest_a, rest_b], axis=1).astype(F32)
     cuts = [0, heads_width, 2 * heads_width, 2 * heads_width + kv_width]
     cuts = cuts + [cuts[-1] + kv_width]
     owned_out, owned_query, owned_key, owned_value = (

time: 663 us -> 612 us (0.923)
  waiting for transfers between devices: 291 us -> 247 us
  Pallas kernels: 121 us -> 105 us
  starting transfers between devices: 90.7 us -> 105 us
  matrix products: 29.4 us -> 21 us
    ppermute x14, waiting for transfers between devices: 120 us -> 91.2 us  [exchange(): done[d] = lax.ppermute(values[d], 'ctx', [(i, i ^ d) for i in range(count)])]
    ppermute x33 -> x40, waiting for transfers between devices: 164 us -> 147 us  [swap(): return lax.ppermute(value, axis, [(i, i ^ level) for i in range(count)])]
    pallas_call x8, Pallas kernels: 44.8 us -> 32.8 us  [split_product(): pl.pallas_call(functools.partial(split_product_kernel, spans), grid_spec=...]
    ppermute x33 -> x40, starting transfers between devices: 66.1 us -> 76.9 us  [swap(): return lax.ppermute(value, axis, [(i, i ^ level) for i in range(count)])]
    dot_general x6 -> x4, matrix products: 21.1 us -> 13.9 us  [dot(): return jnp.dot(a, b, preferred_element_type=F32)]
    unnamed x191 -> x180, local copies, waits for them, and re-layouts: 30.4 us -> 27.1 us
  transfers between devices with their start and end apart: 55 -> 62, of which waited for: 22 -> 24; matrix products, arithmetic and copies ran while one was open for 13% -> 14% of each run, Pallas kernels for 17% -> 15%
where the time goes in v6:
time: 612 us; the launch traced here: 603 us
  waiting for transfers between devices  247 us (40%)
  starting transfers between devices  105 us (17%)
  Pallas kernels  105 us (17%)
  other arithmetic  63 us (10%)
  local copies, waits for them, and re-layouts  45.2 us (7%)
  matrix products  21 us (3%)
  between operations  15.6 us (3%)
    ppermute x40, waiting for transfers between devices, swap(): return lax.ppermute(value, axis, [(i, i ^ level) for i in range(count)])  147 us
    ppermute x14, waiting for transfers between devices, exchange(): done[d] = lax.ppermute(values[d], 'ctx', [(i, i ^ d) for i in range(count)])  91.2 us
    ppermute x40, starting transfers between devices, swap(): return lax.ppermute(value, axis, [(i, i ^ level) for i in range(count)])  76.9 us
    pallas_call x8, Pallas kernels, split_product(): pl.pallas_call(functools.partial(split_product_kernel, spans), grid_spec=...  32.8 us
    unnamed x180, local copies, waits for them, and re-layouts  27.1 us
    pallas_call x1, Pallas kernels, attend_back(): pl.pallas_call(functools.partial(backward_kernel, docs, count), grid_spec...  26 us
    ppermute x14, starting transfers between devices, exchange(): done[d] = lax.ppermute(values[d], 'ctx', [(i, i ^ d) for i in range(count)])  23 us
    pallas_call x1, Pallas kernels, attend(): pl.pallas_call(functools.partial(forward_kernel, docs, count), grid_spec=...  18.1 us
  transfers between devices with their start and end apart: 62, of which 24 were waited for; matrix products, arithmetic and copies ran while one was open for 14% of the time, Pallas kernels for 15%

profile of v6, /device:TPU:0, one launch (start us, length us, event | category | flops | bytes accessed | tf_op | source)
XLA Modules:
  0.0 602.7 jit_solution(7654572671098745558)
XLA Ops:
  40.6 8.2 %shard_map.246 = (f32[512,512]{1,0:T(8,128)}, bf16[512,1024]{1,0:T(8,128)(2,1)}, bf16[512,1024]{1,0:T(8,128)(2,1)}, bf16[256,1024]{1,0:T(8,128)(2,1)}, bf16[256,...) custom-call(s32[20]{0:T(128)S(1)} %concatenate.244.meta_ref, ...), custom_call_target="tpu_custom_call" | custom-call | flops 1000 | bytes 1000 | tf_op jit(solution)/shard_map/pallas_call | solution.py:279
  57.8 31.7 %collective-permute-done.3.refs_8_.refs_9_ = bf16[256,1024]{1,0:T(8,128)(2,1)S(1)} collective-permute-done((bf16[256,1024]{1,0:T(8,128)(2,1)}, bf16[256,1024]{1,0:T(8,128)(2,1)S(1)}, u32[]{:S(2)}, u32[]{:S(2)}) %collective-permute-start.3) | collective-permute-done | bytes 524320 | tf_op jit(solution)/shard_map/ppermute | solution.py:91
  89.5 11.3 %collective-permute-done.5.refs_0_.refs_1_ = bf16[256,1024]{1,0:T(8,128)(2,1)S(1)} collective-permute-done((bf16[256,1024]{1,0:T(8,128)(2,1)}, bf16[256,1024]{1,0:T(8,128)(2,1)S(1)}, u32[]{:S(2)}, u32[]{:S(2)}) %collective-permute-start.5) | collective-permute-done | bytes 524320 | tf_op jit(solution)/shard_map/ppermute | solution.py:91
  106.9 35.0 %collective-permute-done.11 = bf16[256,3584]{1,0:T(8,128)(2,1)} collective-permute-done((bf16[256,3584]{1,0:T(8,128)(2,1)}, bf16[256,3584]{1,0:T(8,128)(2,1)}, u32[]{:S(2)}, u32[]{:S(2)}) %collective-permute-start.11) | collective-permute-done | bytes 1835040 | tf_op jit(solution)/shard_map/ppermute | solution.py:81
  156.6 18.1 %shard_map.248 = (f32[512,1024]{1,0:T(8,128)}, bf16[512,1024]{1,0:T(8,128)(2,1)S(1)}, f32[512,1024]{1,0:T(8,128)}) custom-call(s32[20]{0:T(128)S(1)} %concatenate.244.meta_ref, bf16[512,1024]{1,0:T(8,128)(2,1)S(1)} %shard_map.247.q_ref, bf16[512,1024]{1,0:T(8,128)(2,1)} %get-tuple-element.137.k_ref.v_ref, bf16[512,1024]{1,0:T(8,128)(2,1)} %get-tuple-element.137.k_ref.v_ref, ...), custom_call_target="tpu_custom_call" | custom-call | flops 1000 | bytes 1000 | tf_op jit(solution)/shard_map/pallas_call | solution.py:579
  182.4 5.6 fusion.36
  197.8 5.2 shard_map.249
  203.0 5.9 shard_map.251
  217.3 26.0 %shard_map.253 = (f32[512,1024]{1,0:T(8,128)}, f32[2,512,512]{2,1,0:T(8,128)}, bf16[2,256,512]{2,1,0:T(8,128)(2,1)S(1)}, bf16[2,256,512]{2,1,0:T(8,128)(2,1)}, b...) custom-call(s32[20]{0:T(128)S(1)} %concatenate.244.meta_ref, ...), custom_call_target="tpu_custom_call" | custom-call | flops 1000 | bytes 1000 | tf_op jit(solution)/shard_map/pallas_call | solution.py:605
  250.6 21.0 %collective-permute-done.15.refs_1_ = bf16[2,256,512]{2,1,0:T(8,128)(2,1)S(1)} collective-permute-done((bf16[2,256,512]{2,1,0:T(8,128)(2,1)}, bf16[2,256,512]{2,1,0:T(8,128)(2,1)S(1)}, u32[]{:S(2)}, u32[]{:S(2)}) %collective-permute-start.15) | collective-permute-done | bytes 524320 | tf_op jit(solution)/shard_map/ppermute | solution.py:91
  278.0 5.1 shard_map.255
  303.3 9.3 %collective-permute-done.21 = bf16[256,2304]{1,0:T(8,128)(2,1)} collective-permute-done((bf16[256,2304]{1,0:T(8,128)(2,1)S(1)}, bf16[256,2304]{1,0:T(8,128)(2,1)}, u32[]{:S(2)}, u32[]{:S(2)}) %collective-permute-start.21) | collective-permute-done | bytes 1179680 | tf_op jit(solution)/shard_map/ppermute | solution.py:81
  324.9 26.6 %collective-permute-done.28.refs_4_ = bf16[2,256,512]{2,1,0:T(8,128)(2,1)S(1)} collective-permute-done((bf16[2,256,512]{2,1,0:T(8,128)(2,1)}, bf16[2,256,512]{2,1,0:T(8,128)(2,1)S(1)}, u32[]{:S(2)}, u32[]{:S(2)}) %collective-permute-start.28) | collective-permute-done | bytes 524320 | tf_op jit(solution)/shard_map/ppermute | solution.py:91
  351.5 12.3 %collective-permute-start.26 = (bf16[64,2304]{1,0:T(8,128)(2,1)S(1)}, bf16[64,2304]{1,0:T(8,128)(2,1)}, u32[]{:S(2)}, u32[]{:S(2)}) collective-permute-start(bf16[64,2304]{1,0:T(8,128)(2,1)S(1)} %get-tuple-element.254), channel_id=1, source_target_pairs={{0,8},{2,10},{4,12},{6,14},{8,0},{10,2},{12,4},{14,6},{1,9},{3,11}... | collective-permute-start | bytes 884744 | tf_op jit(solution)/shard_map/ppermute | solution.py:81
  370.4 5.2 shard_map.259
  387.5 22.1 %collective-permute-done.23 = bf16[64,2304]{1,0:T(8,128)(2,1)} collective-permute-done((bf16[64,2304]{1,0:T(8,128)(2,1)S(1)}, bf16[64,2304]{1,0:T(8,128)(2,1)}, u32[]{:S(2)}, u32[]{:S(2)}) %collective-permute-start.23) | collective-permute-done | bytes 294944 | tf_op jit(solution)/shard_map/ppermute | solution.py:81
  413.7 14.0 %collective-permute-start.36 = (bf16[64,2304]{1,0:T(8,128)(2,1)S(1)}, bf16[64,2304]{1,0:T(8,128)(2,1)S(1)}, u32[]{:S(2)}, u32[]{:S(2)}) collective-permute-start(bf16[64,2304]{1,0:T(8,128)(2,1)S(1)} %add_convert_fusion.13), channel_id=1, source_target_pairs={{0,4},{2,6},{4,0},{6,2},{8,12},{10,14},{12,8},{14,10},{1,5},{3,7},... | collective-permute-start | bytes 884744 | tf_op jit(solution)/shard_map/ppermute | solution.py:81
  437.2 13.3 %collective-permute-done.37 = bf16[64,2304]{1,0:T(8,128)(2,1)S(1)} collective-permute-done((bf16[64,2304]{1,0:T(8,128)(2,1)S(1)}, bf16[64,2304]{1,0:T(8,128)(2,1)S(1)}, u32[]{:S(2)}, u32[]{:S(2)}) %collective-permute-start.37) | collective-permute-done | bytes 294944 | tf_op jit(solution)/shard_map/ppermute | solution.py:81
  464.7 12.4 %collective-permute-done.41 = bf16[64,2304]{1,0:T(8,128)(2,1)S(1)} collective-permute-done((bf16[64,2304]{1,0:T(8,128)(2,1)S(1)}, bf16[64,2304]{1,0:T(8,128)(2,1)S(1)}, u32[]{:S(2)}, u32[]{:S(2)}) %collective-permute-start.41) | collective-permute-done | bytes 294944 | tf_op jit(solution)/shard_map/ppermute | solution.py:81
  502.1 7.6 %collective-permute-done.49 = f32[18,128]{1,0:T(8,128)S(1)} collective-permute-done((f32[18,128]{1,0:T(8,128)S(1)}, f32[18,128]{1,0:T(8,128)S(1)}, u32[]{:S(2)}, u32[]{:S(2)}) %collective-permute-start.49) | collective-permute-done | bytes 9248 | tf_op jit(solution)/shard_map/ppermute | solution.py:81
  509.8 6.8 %collective-permute-done.46 = bf16[64,3072]{1,0:T(8,128)(2,1)} collective-permute-done((bf16[64,3072]{1,0:T(8,128)(2,1)S(1)}, bf16[64,3072]{1,0:T(8,128)(2,1)}, u32[]{:S(2)}, u32[]{:S(2)}) %collective-permute-start.46) | collective-permute-done | bytes 393248 | tf_op jit(solution)/shard_map/ppermute | solution.py:81
  535.3 7.4 %collective-permute-done.51 = bf16[64,1536]{1,0:T(8,128)(2,1)S(1)} collective-permute-done((bf16[64,1536]{1,0:T(8,128)(2,1)S(1)}, bf16[64,1536]{1,0:T(8,128)(2,1)S(1)}, u32[]{:S(2)}, u32[]{:S(2)}) %collective-permute-start.51) | collective-permute-done | bytes 196640 | tf_op jit(solution)/shard_map/ppermute | solution.py:81
  554.0 10.8 %collective-permute-done.56 = bf16[64,1536]{1,0:T(8,128)(2,1)S(1)} collective-permute-done((bf16[64,1536]{1,0:T(8,128)(2,1)S(1)}, bf16[64,1536]{1,0:T(8,128)(2,1)S(1)}, u32[]{:S(2)}, u32[]{:S(2)}) %collective-permute-start.56) | collective-permute-done | bytes 196640 | tf_op jit(solution)/shard_map/ppermute | solution.py:81
  576.5 5.9 collective-permute-done.59
  (403 shorter events, 260.2 us)
Async XLA Ops:
  7.2 174.2 %all-gather.2.cloned.1.call-start = ((), (), s32[]{:S(2)}) async-start(), calls=%async_computation | async-start | bytes 9437184 | tf_op jit(solution)/shard_map/all_gather | solution.py:718
  36.8 64.0 %collective-permute-start.7 = (bf16[256,3584]{1,0:T(8,128)(2,1)}, bf16[256,3584]{1,0:T(8,128)(2,1)}, u32[]{:S(2)}, u32[]{:S(2)}) collective-permute-start(bf16[256,3584]{1,0:T(8,128)(2,1)} %constant_dynamic-slice_fusion.3), channel_id=1, source_target_pairs={{0,16},{16,0},{1,17},{17,1},{2,18},{18,2},{3,19},{19,3},{4,20},{20... | collective-permute-start | bytes 5505032 | tf_op jit(solution)/shard_map/ppermute | solution.py:81
  51.2 38.3 %collective-permute-start.3 = (bf16[256,1024]{1,0:T(8,128)(2,1)}, bf16[256,1024]{1,0:T(8,128)(2,1)S(1)}, u32[]{:S(2)}, u32[]{:S(2)}) collective-permute-start(bf16[256,1024]{1,0:T(8,128)(2,1)} %get-tuple-element.123), channel_id=1, source_target_pairs={{0,10},{2,8},{4,14},{6,12},{8,2},{10,0},{12,6},{14,4},{1,11},{3,9}... | collective-permute-start | bytes 1572872 | tf_op jit(solution)/shard_map/ppermute | solution.py:91
  54.7 34.8 %collective-permute-start.4 = (bf16[256,1024]{1,0:T(8,128)(2,1)}, bf16[256,1024]{1,0:T(8,128)(2,1)S(1)}, u32[]{:S(2)}, u32[]{:S(2)}) collective-permute-start(bf16[256,1024]{1,0:T(8,128)(2,1)} %get-tuple-element.124), channel_id=1, source_target_pairs={{0,14},{2,12},{4,10},{6,8},{8,6},{10,4},{12,2},{14,0},{1,15},{3,13... | collective-permute-start | bytes 1572872 | tf_op jit(solution)/shard_map/ppermute | solution.py:91
  56.0 44.8 %collective-permute-start.5 = (bf16[256,1024]{1,0:T(8,128)(2,1)}, bf16[256,1024]{1,0:T(8,128)(2,1)S(1)}, u32[]{:S(2)}, u32[]{:S(2)}) collective-permute-start(bf16[256,1024]{1,0:T(8,128)(2,1)} %get-tuple-element.125), channel_id=1, source_target_pairs={{0,2},{2,0},{4,6},{6,4},{8,10},{10,8},{12,14},{14,12},{1,3},{3,1},... | collective-permute-start | bytes 1572872 | tf_op jit(solution)/shard_map/ppermute | solution.py:91
  57.5 43.3 %collective-permute-start.6 = (bf16[256,1024]{1,0:T(8,128)(2,1)}, bf16[256,1024]{1,0:T(8,128)(2,1)S(1)}, u32[]{:S(2)}, u32[]{:S(2)}) collective-permute-start(bf16[256,1024]{1,0:T(8,128)(2,1)} %get-tuple-element.126), channel_id=1, source_target_pairs={{0,6},{2,4},{4,2},{6,0},{8,14},{10,12},{12,10},{14,8},{1,7},{3,5},... | collective-permute-start | bytes 1572872 | tf_op jit(solution)/shard_map/ppermute | solution.py:91
  100.8 41.0 %collective-permute-start.11 = (bf16[256,3584]{1,0:T(8,128)(2,1)}, bf16[256,3584]{1,0:T(8,128)(2,1)}, u32[]{:S(2)}, u32[]{:S(2)}) collective-permute-start(bf16[256,3584]{1,0:T(8,128)(2,1)} %collective-permute-done.7), channel_id=1, source_target_pairs={{0,2},{2,0},{4,6},{6,4},{8,10},{10,8},{12,14},{14,12},{1,3},{3,1},... | collective-permute-start | bytes 5505032 | tf_op jit(solution)/shard_map/ppermute | solution.py:81
  102.5 54.1 %collective-permute-start.10 = (bf16[256,1024]{1,0:T(8,128)(2,1)}, bf16[256,1024]{1,0:T(8,128)(2,1)S(1)}, u32[]{:S(2)}, u32[]{:S(2)}) collective-permute-start(bf16[256,1024]{1,0:T(8,128)(2,1)} %copy-done.49), channel_id=1, source_target_pairs={{0,4},{2,6},{4,0},{6,2},{8,12},{10,14},{12,8},{14,10},{1,5},{3,7},... | collective-permute-start | bytes 1572872 | tf_op jit(solution)/shard_map/ppermute | solution.py:91
  103.0 53.6 %collective-permute-start.8 = (bf16[256,1024]{1,0:T(8,128)(2,1)}, bf16[256,1024]{1,0:T(8,128)(2,1)S(1)}, u32[]{:S(2)}, u32[]{:S(2)}) collective-permute-start(bf16[256,1024]{1,0:T(8,128)(2,1)} %copy-done.48), channel_id=1, source_target_pairs={{0,8},{2,10},{4,12},{6,14},{8,0},{10,2},{12,4},{14,6},{1,9},{3,11}... | collective-permute-start | bytes 1572872 | tf_op jit(solution)/shard_map/ppermute | solution.py:91
  106.5 50.0 %collective-permute-start.9 = (bf16[256,1024]{1,0:T(8,128)(2,1)S(1)}, bf16[256,1024]{1,0:T(8,128)(2,1)S(1)}, u32[]{:S(2)}, u32[]{:S(2)}) collective-permute-start(bf16[256,1024]{1,0:T(8,128)(2,1)S(1)} %copy-done.47), channel_id=1, source_target_pairs={{0,12},{2,14},{4,8},{6,10},{8,4},{10,6},{12,0},{14,2},{1,13},{3,15... | collective-permute-start | bytes 1572872 | tf_op jit(solution)/shard_map/ppermute | solution.py:91
  209.2 73.9 %collective-permute-start.20 = (bf16[512,2304]{1,0:T(8,128)(2,1)}, bf16[512,2304]{1,0:T(8,128)(2,1)}, u32[]{:S(2)}, u32[]{:S(2)}) collective-permute-start(bf16[512,2304]{1,0:T(8,128)(2,1)} %shard_map.250), channel_id=1, source_target_pairs={{0,2},{2,0},{4,6},{6,4},{8,10},{10,8},{12,14},{14,12},{1,3},{3,1},... | collective-permute-start | bytes 7077896 | tf_op jit(solution)/shard_map/ppermute | solution.py:81
  209.2 76.6 %collective-permute-start.16 = (bf16[512,2304]{1,0:T(8,128)(2,1)}, bf16[512,2304]{1,0:T(8,128)(2,1)}, u32[]{:S(2)}, u32[]{:S(2)}) collective-permute-start(bf16[512,2304]{1,0:T(8,128)(2,1)} %shard_map.249), channel_id=1, source_target_pairs={{0,16},{16,0},{1,17},{17,1},{2,18},{18,2},{3,19},{19,3},{4,20},{20... | collective-permute-start | bytes 7077896 | tf_op jit(solution)/shard_map/ppermute | solution.py:81
  247.5 30.5 %collective-permute-start.17 = (bf16[2,256,512]{2,1,0:T(8,128)(2,1)}, bf16[2,256,512]{2,1,0:T(8,128)(2,1)}, u32[]{:S(2)}, u32[]{:S(2)}) collective-permute-start(bf16[2,256,512]{2,1,0:T(8,128)(2,1)} %get-tuple-element.157), channel_id=1, source_target_pairs={{0,8},{2,10},{4,12},{6,14},{8,0},{10,2},{12,4},{14,6},{1,9},{3,11}... | collective-permute-start | bytes 1572872 | tf_op jit(solution)/shard_map/ppermute | solution.py:91
  314.7 53.4 %collective-permute-start.32 = (bf16[512,2048]{1,0:T(8,128)(2,1)}, bf16[512,2048]{1,0:T(8,128)(2,1)}, u32[]{:S(2)}, u32[]{:S(2)}) collective-permute-start(bf16[512,2048]{1,0:T(8,128)(2,1)} %shard_map.258), channel_id=1, source_target_pairs={{0,16},{16,0},{1,17},{17,1},{2,18},{18,2},{3,19},{19,3},{4,20},{20... | collective-permute-start | bytes 6291464 | tf_op jit(solution)/shard_map/ppermute | solution.py:81
  316.1 35.4 %collective-permute-start.28 = (bf16[2,256,512]{2,1,0:T(8,128)(2,1)}, bf16[2,256,512]{2,1,0:T(8,128)(2,1)S(1)}, u32[]{:S(2)}, u32[]{:S(2)}) collective-permute-start(bf16[2,256,512]{2,1,0:T(8,128)(2,1)} %copy-done.43), channel_id=1, source_target_pairs={{0,10},{2,8},{4,14},{6,12},{8,2},{10,0},{12,6},{14,4},{1,11},{3,9}... | collective-permute-start | bytes 1572872 | tf_op jit(solution)/shard_map/ppermute | solution.py:91
  316.1 35.3 %collective-permute-start.29 = (bf16[2,256,512]{2,1,0:T(8,128)(2,1)}, bf16[2,256,512]{2,1,0:T(8,128)(2,1)S(1)}, u32[]{:S(2)}, u32[]{:S(2)}) collective-permute-start(bf16[2,256,512]{2,1,0:T(8,128)(2,1)} %copy-done.42), channel_id=1, source_target_pairs={{0,14},{2,12},{4,10},{6,8},{8,6},{10,4},{12,2},{14,0},{1,15},{3,13... | collective-permute-start | bytes 1572872 | tf_op jit(solution)/shard_map/ppermute | solution.py:91
  318.9 45.0 %collective-permute-start.30 = (bf16[2,256,512]{2,1,0:T(8,128)(2,1)}, bf16[2,256,512]{2,1,0:T(8,128)(2,1)S(1)}, u32[]{:S(2)}, u32[]{:S(2)}) collective-permute-start(bf16[2,256,512]{2,1,0:T(8,128)(2,1)} %copy-done.41), channel_id=1, source_target_pairs={{0,2},{2,0},{4,6},{6,4},{8,10},{10,8},{12,14},{14,12},{1,3},{3,1},... | collective-permute-start | bytes 1572872 | tf_op jit(solution)/shard_map/ppermute | solution.py:91
  320.3 47.7 %collective-permute-start.31 = (bf16[2,256,512]{2,1,0:T(8,128)(2,1)}, bf16[2,256,512]{2,1,0:T(8,128)(2,1)S(1)}, u32[]{:S(2)}, u32[]{:S(2)}) collective-permute-start(bf16[2,256,512]{2,1,0:T(8,128)(2,1)} %copy-done.40), channel_id=1, source_target_pairs={{0,6},{2,4},{4,2},{6,0},{8,14},{10,12},{12,10},{14,8},{1,7},{3,5},... | collective-permute-start | bytes 1572872 | tf_op jit(solution)/shard_map/ppermute | solution.py:91
  351.5 33.1 %collective-permute-start.26 = (bf16[64,2304]{1,0:T(8,128)(2,1)S(1)}, bf16[64,2304]{1,0:T(8,128)(2,1)}, u32[]{:S(2)}, u32[]{:S(2)}) collective-permute-start(bf16[64,2304]{1,0:T(8,128)(2,1)S(1)} %get-tuple-element.254), channel_id=1, source_target_pairs={{0,8},{2,10},{4,12},{6,14},{8,0},{10,2},{12,4},{14,6},{1,9},{3,11}... | collective-permute-start | bytes 884744 | tf_op jit(solution)/shard_map/ppermute | solution.py:81
  368.1 41.5 %collective-permute-start.23 = (bf16[64,2304]{1,0:T(8,128)(2,1)S(1)}, bf16[64,2304]{1,0:T(8,128)(2,1)}, u32[]{:S(2)}, u32[]{:S(2)}) collective-permute-start(bf16[64,2304]{1,0:T(8,128)(2,1)S(1)} %get-tuple-element.257), channel_id=1, source_target_pairs={{0,8},{2,10},{4,12},{6,14},{8,0},{10,2},{12,4},{14,6},{1,9},{3,11}... | collective-permute-start | bytes 884744 | tf_op jit(solution)/shard_map/ppermute | solution.py:81
  379.5 30.1 %collective-permute-start.24 = (bf16[64,2304]{1,0:T(8,128)(2,1)S(1)}, bf16[64,2304]{1,0:T(8,128)(2,1)S(1)}, u32[]{:S(2)}, u32[]{:S(2)}) collective-permute-start(bf16[64,2304]{1,0:T(8,128)(2,1)S(1)} %get-tuple-element.256), channel_id=1, source_target_pairs={{0,12},{2,14},{4,8},{6,10},{8,4},{10,6},{12,0},{14,2},{1,13},{3,15... | collective-permute-start | bytes 884744 | tf_op jit(solution)/shard_map/ppermute | solution.py:81
  384.5 29.1 %collective-permute-start.34 = (bf16[512,1024]{1,0:T(8,128)(2,1)S(1)}, bf16[512,1024]{1,0:T(8,128)(2,1)S(1)}, u32[]{:S(2)}, u32[]{:S(2)}) collective-permute-start(bf16[512,1024]{1,0:T(8,128)(2,1)S(1)} %shard_map.260), channel_id=1, source_target_pairs={{0,16},{16,0},{1,17},{17,1},{2,18},{18,2},{3,19},{19,3},{4,20},{20... | collective-permute-start | bytes 3145736 | tf_op jit(solution)/shard_map/ppermute | solution.py:81
  435.9 41.6 %collective-permute-start.35 = (bf16[512,1024]{1,0:T(8,128)(2,1)S(1)}, bf16[512,1024]{1,0:T(8,128)(2,1)S(1)}, u32[]{:S(2)}, u32[]{:S(2)}) collective-permute-start(bf16[512,1024]{1,0:T(8,128)(2,1)S(1)} %add_convert_fusion.3), channel_id=1, source_target_pairs={{0,1},{1,0},{2,3},{3,2},{4,5},{5,4},{6,7},{7,6},{8,9},{9,8},{10,11... | collective-permute-start | bytes 3145736 | tf_op jit(solution)/shard_map/ppermute | solution.py:75
  485.8 32.5 %collective-permute-start.44 = (bf16[256,2304]{1,0:T(8,128)(2,1)S(1)}, bf16[256,2304]{1,0:T(8,128)(2,1)}, u32[]{:S(2)}, u32[]{:S(2)}) collective-permute-start(bf16[256,2304]{1,0:T(8,128)(2,1)S(1)} %maximum_select_fusion.7), channel_id=1, source_target_pairs={{0,2},{2,0},{4,6},{6,4},{8,10},{10,8},{12,14},{14,12},{1,3},{3,1},... | collective-permute-start | bytes 3538952 | tf_op jit(solution)/shard_map/ppermute | solution.py:81
  (127 other events, 1805.7 us)
Sparse Core Ops, SparseCore 0:
  57.9 88.0 all-gather.1

commit v7 on v6

--- a/solution.py
+++ b/solution.py
@@ -226,18 +226,21 @@
     return pl.multiple_of((1 - meta_ref[docs + d]) * half, half)
 
 
-def key_value_kernel(heads, docs, count, pieces, meta_ref, normal_ref, scale_ref, *refs):
+def key_value_kernel(
+    heads, docs, count, pieces, meta_ref, tokens_ref, factor_ref, scale_ref, *refs
+):
     weights = refs[: 2 * pieces]
     cos_ref, sin_ref, gain_ref = refs[2 * pieces : 2 * pieces + 3]
     key_ref, out_ref, normed_ref = refs[2 * pieces + 3 : 2 * pieces + 6]
     sent = refs[2 * pieces + 6 :]
     half = out_ref.shape[0] // 2
-    depth = normal_ref.shape[1] // pieces
+    depth = tokens_ref.shape[1] // pieces
     step = pl.program_id(0)
 
     @pl.when(step == 0)
     def _():
-        normed_ref[...] = (normal_ref[...] * scale_ref[...]).astype(BF16)
+        normal = tokens_ref[...].astype(F32) * factor_ref[...]
+        normed_ref[...] = (normal * scale_ref[...]).astype(BF16)
 
     def product(parts):
         result = None
@@ -266,8 +269,10 @@
         sent_ref[...] = out_ref[pl.ds(part_start(meta_ref, docs, d, half), half), :]
 
 
-def key_value_and_parts(meta, docs, count, normal, scale, keys, values, cosine, sine, gain):
-    rows, model = normal.shape
+def key_value_and_parts(
+    meta, docs, count, tokens, factor, scale, keys, values, cosine, sine, gain
+):
+    rows, model = tokens.shape
     depth, width = keys[0].shape
     heads = width // HEAD
     half_steps = heads // 2
@@ -281,7 +286,7 @@
         grid_spec=pltpu.PrefetchScalarGridSpec(
             num_scalar_prefetch=1,
             grid=(heads,),
-            in_specs=[whole((rows, model)), whole((1, model))]
+            in_specs=[whole((rows, model)), whole((rows, 1)), whole((1, model))]
             + [key_spec] * len(keys)
             + [value_spec] * len(values)
             + [whole((rows, HEAD)), whole((rows, HEAD)), whole((1, HEAD))],
@@ -300,7 +305,7 @@
         + [jax.ShapeDtypeStruct((rows // 2, 2 * width), BF16)] * (count - 1),
         compiler_params=pltpu.CompilerParams(vmem_limit_bytes=VMEM_LIMIT),
         cost_estimate=CHEAP,
-    )(meta, normal, scale, *keys, *values, cosine, sine, gain)
+    )(meta, tokens, factor, scale, *keys, *values, cosine, sine, gain)
     return result[0], result[1], result[2], dict(zip(range(1, count), result[3:]))
 
 
@@ -701,11 +706,15 @@
     inputs = tokens.astype(F32)
     normal_one, factor_one = rms_parts(inputs)
 
-    own_rest, own_gate_up, packed_pieces[-1], k_pieces[-1], v_pieces[-1] = tie(
-        own_rest, own_gate_up, packed_pieces[-1], k_pieces[-1], v_pieces[-1]
-    )
-    cosine, sine, meta, normal_one, k_pieces[-1] = tie(
-        cosine, sine, meta, normal_one, k_pieces[-1]
+    bit = place_in(near_axis)
+    half_rest = own_rest
+    if shard_count == 2:
+        half_rest = lax.dynamic_slice_in_dim(own_rest, bit * (depth // 2), depth // 2, 0)
+    half_rest, own_gate_up, packed_pieces[-1], k_pieces[-1], v_pieces[-1] = tie(
+        half_rest, own_gate_up, packed_pieces[-1], k_pieces[-1], v_pieces[-1]
+    )
+    cosine, sine, meta, factor_one, k_pieces[-1] = tie(
+        cosine, sine, meta, factor_one, k_pieces[-1]
     )
     cuts = [0, depth, 2 * depth, 2 * depth + gain_q.shape[0], packed.shape[0]]
     scale_in, scale_post, scale_q, scale_k = (
@@ -717,13 +726,19 @@
 
     full_gate_up = lax.all_gather(own_gate_up, "shard", axis=0, tiled=True)
     if shard_count == 2:
-        bit = place_in(near_axis)
-        half_rest = lax.dynamic_slice_in_dim(own_rest, bit * (depth // 2), depth // 2, 0)
         half_rest = swap(half_rest, "shard")
-    else:
-        half_rest = own_rest
     k_pre, key_value, normed_input, sent = key_value_and_parts(
-        meta, docs, count, normal_one, scale_in, k_pieces, v_pieces, cosine, sine, scale_k
+        meta,
+        docs,
+        count,
+        tokens,
+        factor_one,
+        scale_in,
+        k_pieces,
+        v_pieces,
+        cosine,
+        sine,
+        scale_k,
     )
     held = {}
     exchange(sent, held, crossing)
@@ -732,13 +747,18 @@
 
     exchange(sent, held, straight)
     if shard_count == 2:
-        other_rest = join([half_rest, swap(half_rest, "ctx", near_axis[0])], 0, bit)
-        full_rest = join([own_rest, other_rest], 0, shard)
+        query_half, rest_half = half_rest[:, :heads_width], half_rest[:, heads_width:]
+        query_got = swap(query_half, "ctx", near_axis[0])
+        query_got, rest_half = tie(query_got, rest_half)
+        other_query = join([query_half, query_got], 0, bit)
+        other_rest = join([rest_half, swap(rest_half, "ctx", near_axis[0])], 0, bit)
+        full_query = join([own_rest[:, :heads_width], other_query], 0, shard)
+        full_rest = join([own_rest[:, heads_width:], other_rest], 0, shard)
     else:
         full_rest = lax.all_gather(half_rest, "shard", axis=0, tiled=True)
-    full_query = full_rest[:, :heads_width]
-    full_out_t = full_rest[:, heads_width : 2 * heads_width]
-    full_down_t = full_rest[:, 2 * heads_width :]
+        full_query, full_rest = full_rest[:, :heads_width], full_rest[:, heads_width:]
+    full_out_t = full_rest[:, :heads_width]
+    full_down_t = full_rest[:, heads_width:]
     q_pre = dot(normed_input, full_query)
     queries = rope(q_pre, cosine, sine, scale_q)
     queries, full_out_t = settle(held, straight, queries, full_out_t)
@@ -759,7 +779,6 @@
     d_up = (d_hidden * silu_act).astype(BF16)
     middle = units // 2
     away, home = (2 - 2 * shard, 3 - 2 * shard), (2 * shard, 2 * shard + 1)
-    bit = place_in(near_axis)
 
     def pairs_a(normed):
         return [(normed, d_gate, 0, units), (normed, d_up, 0, middle)]
@@ -790,57 +809,66 @@
     )
     given = dict(zip(range(1, count), given))
     returned = {}
+    exchange(given, returned, crossing)
+    normed_late, d_queries = tie(normed_two, d_queries)
+    gates = crossing[:4]
+    if shard_count == 2:
+        normed_b, upstream_b, returned[gates[0]] = tie(
+            normed_late, cotangent, returned[gates[0]]
+        )
+        kept_b = split_product((bit, 2 + bit), pairs_b(normed_b, upstream_b))
+        normed_a, kept_b, returned[gates[1]] = tie(normed_late, kept_b, returned[gates[1]])
+        kept_a = split_product(home, pairs_a(normed_a))
+        d_queries, kept_a = tie(d_queries, kept_a)
+    d_queries, returned[gates[2]] = tie(d_queries, returned[gates[2]])
+    d_q_pre, gq_part = rope_back(d_queries, q_pre, cosine, sine, scale_q)
+    d_q_pre, returned[gates[3]] = tie(d_q_pre, returned[gates[3]])
+    out_pairs = [(d_branch, attn_out, 0, heads_width), (normed_input, d_q_pre, 0, heads_width)]
+    if shard_count == 2:
+        kept_out, sent_out = split_product(home, out_pairs), split_product(away, out_pairs)
+        kept_a, kept_b, kept_out, sent_out, got_a, got_b, *rest = settle(
+            returned,
+            crossing,
+            kept_a,
+            kept_b,
+            kept_out,
+            sent_out,
+            got_a,
+            got_b,
+            *(given[d] for d in straight),
+        )
+        given.update(zip(straight, rest))
     exchange(given, returned, straight)
     if shard_count == 2:
-        first, second = straight[-1], straight[0]
-        normed_late, returned[first] = tie(normed_two, returned[first])
-        units_a = [split_product(home, pairs_a(normed_late)), got_a]
-        units_a = halve(units_a, near_axis)
-        normed_late, upstream_late, returned[second] = tie(
-            normed_two, cotangent, returned[second]
-        )
-        kept_b = split_product((bit, 2 + bit), pairs_b(normed_late, upstream_late))
+        units_a = halve([kept_a, got_a], near_axis)
         units_b = [kept_b, got_b]
         units_b_away = total(rows_at(units_b, 1 - shard, depth // 2))
         units_b = rows_at(units_b, shard, depth // 2) + [swap(units_b_away, "shard")]
+        out_query = [kept_out, swap(sent_out, "shard")]
     else:
         units_a = halve(scattered(pairs_a(normed_two)), near_axis)
         units_b = halve(scattered(pairs_b(normed_two, cotangent)), near_axis)
-    d_q_pre, gq_part = rope_back(d_queries, q_pre, cosine, sine, scale_q)
-    out_pairs = [(d_branch, attn_out, 0, heads_width), (normed_input, d_q_pre, 0, heads_width)]
-    if shard_count == 2:
-        out_query = [split_product(home, out_pairs), split_product(away, out_pairs)]
-    else:
         out_query = scattered(out_pairs)
-    units_a[-1], units_b[-1], out_query[0], out_query[-1], *rest = settle(
-        returned,
-        straight,
-        units_a[-1],
-        units_b[-1],
-        out_query[0],
-        out_query[-1],
-        *(given[d] for d in crossing),
-    )
-    if shard_count == 2:
-        out_query[-1] = swap(out_query[-1], "shard")
-    given.update(zip(crossing, rest))
-    exchange(given, returned, crossing)
-    out_query[-1], d_kv = settle(returned, crossing, out_query[-1], d_kv)
+    units_a[-1], units_b[-1], d_kv = settle(
+        returned, straight, units_a[-1], units_b[-1], d_kv
+    )
     returned = [returned[d] for d in range(1, count)]
 
-    units_a = halve(units_a, far_axis)
-    units_b = halve(units_b, far_axis)
-    out_query = halve(out_query, near_axis)
+    units_sum = halve([jnp.concatenate([total(units_a), total(units_b)], axis=1)], far_axis)
     d_k_pre, d_v_pre, gk_part = key_value_back(
         meta, docs, d_kv, returned, k_pre, cosine, sine, scale_k
     )
+    d_k_pre, d_v_pre, out_query[-1] = tie(d_k_pre, d_v_pre, out_query[-1])
+    out_query = halve(out_query, near_axis)
     kv_pairs = [(normed_input, d_k_pre, 0, kv_width), (normed_input, d_v_pre, 0, kv_width)]
     if shard_count == 2:
         sent_kv = swap(split_product(away, kv_pairs), "shard")
         key_value_grad = [split_product(home, kv_pairs), sent_kv]
     else:
         key_value_grad = scattered(kv_pairs)
-    units_a, units_b = total(units_a), total(units_b)
+    units_sum = total(units_sum)
+    cut = units_sum.shape[1] // 2
+    units_a, units_b = units_sum[:, :cut], units_sum[:, cut:]
     units_a, units_b, out_query[-1], key_value_grad[-1], d_q_pre, d_k_pre, d_v_pre = tie(
         units_a, units_b, out_query[-1], key_value_grad[-1], d_q_pre, d_k_pre, d_v_pre
     )
@@ -863,7 +891,18 @@
     gain_grads = gain_grads.reshape(-1, HEAD)
     if shard_count != 2:
         gain_grads = lax.psum(gain_grads, "shard")
-    rest_chain = [jnp.concatenate([total(out_query), total(key_value_grad)], axis=1)]
+    out_query, key_value_grad = total(out_query), total(key_value_grad)
+    rest_chain = [
+        jnp.concatenate(
+            [
+                out_query[:, :heads_width],
+                key_value_grad[:, :kv_width],
+                out_query[:, heads_width:],
+                key_value_grad[:, kv_width:],
+            ],
+            axis=1,
+        )
+    ]
     units_b, owned_a, rest_chain[0], gain_grads = tie(
         units_b, owned_a, rest_chain[0], gain_grads
     )
@@ -890,12 +929,6 @@
     if shard_count == 2:
         gain_grads = gain_grads + swap(gain_grads, "shard")
     gain_grads = gain_grads.reshape(-1)
-    owned_rest = jnp.concatenate([rest_a, rest_b], axis=1).astype(F32)
-    cuts = [0, heads_width, 2 * heads_width, 2 * heads_width + kv_width]
-    cuts = cuts + [cuts[-1] + kv_width]
-    owned_out, owned_query, owned_key, owned_value = (
-        owned_rest[:, lo:hi] for lo, hi in zip(cuts[:-1], cuts[1:])
-    )
     owned_up = jnp.concatenate([owned_a[:, units:], owned_b[:, :middle]], axis=1)
     own_gains = []
     for lo, size in ((0, model), (model, model), (2 * model, HEAD), (2 * model + HEAD, HEAD)):
@@ -904,10 +937,10 @@
     return (
         mixed,
         input_grad,
-        owned_query,
-        owned_key,
-        owned_value,
-        owned_out.T,
+        rest_b[:, :heads_width].astype(F32),
+        rest_a[:, heads_width:].astype(F32),
+        rest_b[:, heads_width:].astype(F32),
+        rest_a[:, :heads_width].astype(F32).T,
         owned_a[:, :units].astype(F32),
         owned_up.astype(F32),
         owned_b[:, middle:].astype(F32).T,

time: 612 us -> 667 us (1.090)
  waiting for transfers between devices: 247 us -> 301 us
  other arithmetic: 63 us -> 79.6 us
  local copies, waits for them, and re-layouts: 45.2 us -> 32 us
  starting transfers between devices: 105 us -> 114 us
  Pallas kernels: 105 us -> 96.9 us
    ppermute x40 -> x38, waiting for transfers between devices: 147 us -> 179 us  [swap(): return lax.ppermute(value, axis, [(i, i ^ level) for i in range(count)])]
    ppermute x14, starting transfers between devices: 23 us -> 48.8 us  [exchange(): done[d] = lax.ppermute(values[d], 'ctx', [(i, i ^ d) for i in range(count)])]
    select_n x18 -> x19, other arithmetic: 12.3 us -> 34.2 us  [join(): jnp.where(index == 0, jnp.concatenate(pieces, dim), jnp.concatenate(piece...]
    ppermute x14, waiting for transfers between devices: 91.2 us -> 110 us  [exchange(): done[d] = lax.ppermute(values[d], 'ctx', [(i, i ^ d) for i in range(count)])]
    ppermute x40 -> x38, starting transfers between devices: 76.9 us -> 59.4 us  [swap(): return lax.ppermute(value, axis, [(i, i ^ level) for i in range(count)])]
    pallas_call x1, Pallas kernels: 26 us -> 14.4 us  [attend_back(): pl.pallas_call(functools.partial(backward_kernel, docs, count), grid_spec...]
    pallas_call x8, Pallas kernels: 32.8 us -> 43.7 us  [split_product(): pl.pallas_call(functools.partial(split_product_kernel, spans), grid_spec=...]
    unnamed x180 -> x162, local copies, waits for them, and re-layouts: 27.1 us -> 19 us
  transfers between devices with their start and end apart: 62 -> 60, of which waited for: 24 -> 28; matrix products, arithmetic and copies ran while one was open for 14% -> 15% of each run, Pallas kernels for 15% -> 11%
where the time goes in v7:
time: 667 us; the launch traced here: 660 us
  waiting for transfers between devices  301 us (45%)
  starting transfers between devices  114 us (17%)
  Pallas kernels  96.9 us (15%)
  other arithmetic  79.6 us (12%)
  local copies, waits for them, and re-layouts  32 us (5%)
  matrix products  21 us (3%)
  between operations  15.9 us (2%)
    ppermute x38, waiting for transfers between devices, swap(): return lax.ppermute(value, axis, [(i, i ^ level) for i in range(count)])  179 us
    ppermute x14, waiting for transfers between devices, exchange(): done[d] = lax.ppermute(values[d], 'ctx', [(i, i ^ d) for i in range(count)])  110 us
    ppermute x38, starting transfers between devices, swap(): return lax.ppermute(value, axis, [(i, i ^ level) for i in range(count)])  59.4 us
    ppermute x14, starting transfers between devices, exchange(): done[d] = lax.ppermute(values[d], 'ctx', [(i, i ^ d) for i in range(count)])  48.8 us
    pallas_call x8, Pallas kernels, split_product(): pl.pallas_call(functools.partial(split_product_kernel, spans), grid_spec=...  43.7 us
    select_n x19, other arithmetic, join(): jnp.where(index == 0, jnp.concatenate(pieces, dim), jnp.concatenate(piece...  34.2 us
    unnamed x162, local copies, waits for them, and re-layouts  19 us
    convert_element_type x10, other arithmetic, total(): return sum((a.astype(F32) for a in addends)).astype(BF16)  16.2 us
  transfers between devices with their start and end apart: 60, of which 28 were waited for; matrix products, arithmetic and copies ran while one was open for 15% of the time, Pallas kernels for 11%

profile of v7, /device:TPU:0, one launch (start us, length us, event | category | flops | bytes accessed | tf_op | source)
XLA Modules:
  0.0 659.7 jit_solution(6211813187903606248)
XLA Ops:
  28.7 9.3 %collective-permute-done.2.refs_3_ = bf16[512,512]{1,0:T(8,128)(2,1)} collective-permute-done((bf16[512,512]{1,0:T(8,128)(2,1)}, bf16[512,512]{1,0:T(8,128)(2,1)}, u32[]{:S(2)}, u32[]{:S(2)}) %collective-permute-start.2) | collective-permute-done | bytes 524320 | tf_op jit(solution)/shard_map/ppermute | solution.py:48
  55.5 31.2 %collective-permute-done.3.refs_8_.refs_9_ = bf16[256,1024]{1,0:T(8,128)(2,1)S(1)} collective-permute-done((bf16[256,1024]{1,0:T(8,128)(2,1)S(1)}, bf16[256,1024]{1,0:T(8,128)(2,1)S(1)}, u32[]{:S(2)}, u32[]{:S(2)}) %collective-permute-start.3) | collective-permute-done | bytes 524320 | tf_op jit(solution)/shard_map/ppermute | solution.py:91
  86.7 11.5 %collective-permute-done.5.refs_0_.refs_1_ = bf16[256,1024]{1,0:T(8,128)(2,1)S(1)} collective-permute-done((bf16[256,1024]{1,0:T(8,128)(2,1)S(1)}, bf16[256,1024]{1,0:T(8,128)(2,1)S(1)}, u32[]{:S(2)}, u32[]{:S(2)}) %collective-permute-start.5) | collective-permute-done | bytes 524320 | tf_op jit(solution)/shard_map/ppermute | solution.py:91
  111.7 9.4 %collective-permute-done.11 = bf16[256,1024]{1,0:T(8,128)(2,1)S(1)} collective-permute-done((bf16[256,1024]{1,0:T(8,128)(2,1)S(1)}, bf16[256,1024]{1,0:T(8,128)(2,1)S(1)}, u32[]{:S(2)}, u32[]{:S(2)}) %collective-permute-start.11) | collective-permute-done | bytes 524320 | tf_op jit(solution)/shard_map/ppermute | solution.py:81
  133.8 11.3 %collective-permute-done.12 = bf16[256,2560]{1,0:T(8,128)(2,1)} collective-permute-done((bf16[256,2560]{1,0:T(8,128)(2,1)}, bf16[256,2560]{1,0:T(8,128)(2,1)}, u32[]{:S(2)}, u32[]{:S(2)}) %collective-permute-start.12) | collective-permute-done | bytes 1310752 | tf_op jit(solution)/shard_map/ppermute | solution.py:81
  147.9 21.3 %maximum_select_fusion = bf16[1024,2560]{1,0:T(8,128)(2,1)} fusion(bf16[512,2560]{1,0:T(8,128)(2,1)S(1)} %maximum_select_fusion.1, bf16[512,1536]{1,0:T(8,128)(2,1)S(1)} %bitcast.51, bf16[512,1024]{1,0:T(8,128)(2,1)S(1)} %bitcast.53, pred[]{:T(512)S(6)} %eq.88), kind=kLoop, calls=%fused_computation | loop fusion | flops 34078720 | bytes 10485761 | tf_op jit(solution)/shard_map/jit(_where)/select_n | solution.py:58
  171.1 10.3 %shard_map.248 = (f32[512,1024]{1,0:T(8,128)}, bf16[512,1024]{1,0:T(8,128)(2,1)S(1)}, f32[512,1024]{1,0:T(8,128)}) custom-call(s32[20]{0:T(128)S(1)} %concatenate.259.meta_ref, bf16[512,1024]{1,0:T(8,128)(2,1)S(1)} %shard_map.247.q_ref, bf16[512,1024]{1,0:T(8,128)(2,1)} %get-tuple-element.155.k_ref.v_ref, bf16[512,1024]{1,0:T(8,128)(2,1)} %get-tuple-element.155.k_ref.v_ref, ...), custom_call_target="tpu_custom_call" | custom-call | flops 1000 | bytes 1000 | tf_op jit(solution)/shard_map/pallas_call | solution.py:584
  204.6 16.3 %shard_map.250 = bf16[512,2304]{1,0:T(8,128)(2,1)} custom-call(s32[2]{0:T(128)S(1)} %get-tuple-element.325.which_ref, bf16[512,1024]{1,0:T(8,128)(2,1)S(1)} %multiply_convert_fusion.3.refs_0_.refs_2_, bf16[512,1536]{1,0:T(8,128)(2,1)S(1)} %get-tuple-element.167.refs_3_.refs_1_.refs_2_, bf16[512,1024]{1,0:T(8,128)(2,1)S(1)} %copy-done.2, ...), custom_call_target="tpu_custom_call" | custom-call | flops 1000 | bytes 1000 | tf_op jit(solution)/shard_map/pallas_call | solution.py:188
  239.4 14.4 %shard_map.253 = (f32[512,1024]{1,0:T(8,128)}, f32[2,512,512]{2,1,0:T(8,128)}, bf16[2,256,512]{2,1,0:T(8,128)(2,1)}, bf16[2,256,512]{2,1,0:T(8,128)(2,1)}, bf16[...) custom-call(s32[20]{0:T(128)S(1)} %concatenate.259.meta_ref, ...), custom_call_target="tpu_custom_call" | custom-call | flops 1000 | bytes 1000 | tf_op jit(solution)/shard_map/pallas_call | solution.py:610
  253.8 10.6 %collective-permute-start.16 = (bf16[2,256,512]{2,1,0:T(8,128)(2,1)S(1)}, bf16[2,256,512]{2,1,0:T(8,128)(2,1)S(1)}, u32[]{:S(2)}, u32[]{:S(2)}) collective-permute-start(bf16[2,256,512]{2,1,0:T(8,128)(2,1)S(1)} %get-tuple-element.174), channel_id=1, source_target_pairs={{0,10},{2,8},{4,14},{6,12},{8,2},{10,0},{12,6},{14,4},{1,11},{3,9}... | collective-permute-start | bytes 1572872 | tf_op jit(solution)/shard_map/ppermute | solution.py:91
  264.3 9.5 %collective-permute-start.17 = (bf16[2,256,512]{2,1,0:T(8,128)(2,1)}, bf16[2,256,512]{2,1,0:T(8,128)(2,1)}, u32[]{:S(2)}, u32[]{:S(2)}) collective-permute-start(bf16[2,256,512]{2,1,0:T(8,128)(2,1)} %get-tuple-element.178), channel_id=1, source_target_pairs={{0,14},{2,12},{4,10},{6,8},{8,6},{10,4},{12,2},{14,0},{1,15},{3,13... | collective-permute-start | bytes 1572872 | tf_op jit(solution)/shard_map/ppermute | solution.py:91
  275.6 23.9 %collective-permute-done.16.refs_4_ = bf16[2,256,512]{2,1,0:T(8,128)(2,1)S(1)} collective-permute-done((bf16[2,256,512]{2,1,0:T(8,128)(2,1)S(1)}, bf16[2,256,512]{2,1,0:T(8,128)(2,1)S(1)}, u32[]{:S(2)}, u32[]{:S(2)}) %collective-permute-start.16) | collective-permute-done | bytes 524320 | tf_op jit(solution)/shard_map/ppermute | solution.py:91
  320.2 10.3 %collective-permute-done.18.refs_0_ = bf16[2,256,512]{2,1,0:T(8,128)(2,1)} collective-permute-done((bf16[2,256,512]{2,1,0:T(8,128)(2,1)}, bf16[2,256,512]{2,1,0:T(8,128)(2,1)}, u32[]{:S(2)}, u32[]{:S(2)}) %collective-permute-start.18) | collective-permute-done | bytes 524320 | tf_op jit(solution)/shard_map/ppermute | solution.py:91
  358.7 32.7 %collective-permute-done.22.refs_3_ = bf16[2,256,512]{2,1,0:T(8,128)(2,1)S(1)} collective-permute-done((bf16[2,256,512]{2,1,0:T(8,128)(2,1)}, bf16[2,256,512]{2,1,0:T(8,128)(2,1)S(1)}, u32[]{:S(2)}, u32[]{:S(2)}) %collective-permute-start.22) | collective-permute-done | bytes 524320 | tf_op jit(solution)/shard_map/ppermute | solution.py:91
  401.6 9.0 %collective-permute-start.28 = (bf16[64,4608]{1,0:T(8,128)(2,1)}, bf16[64,4608]{1,0:T(8,128)(2,1)}, u32[]{:S(2)}, u32[]{:S(2)}) collective-permute-start(bf16[64,4608]{1,0:T(8,128)(2,1)} %get-tuple-element.298), channel_id=1, source_target_pairs={{0,8},{2,10},{4,12},{6,14},{8,0},{10,2},{12,4},{14,6},{1,9},{3,11}... | collective-permute-start | bytes 1769480 | tf_op jit(solution)/shard_map/ppermute | solution.py:81
  421.6 14.2 %collective-permute-done.30 = bf16[512,2048]{1,0:T(8,128)(2,1)} collective-permute-done((bf16[512,2048]{1,0:T(8,128)(2,1)}, bf16[512,2048]{1,0:T(8,128)(2,1)}, u32[]{:S(2)}, u32[]{:S(2)}) %collective-permute-start.30) | collective-permute-done | bytes 2097184 | tf_op jit(solution)/shard_map/ppermute | solution.py:81
  442.3 9.8 %collective-permute-done.28 = bf16[64,4608]{1,0:T(8,128)(2,1)} collective-permute-done((bf16[64,4608]{1,0:T(8,128)(2,1)}, bf16[64,4608]{1,0:T(8,128)(2,1)}, u32[]{:S(2)}, u32[]{:S(2)}) %collective-permute-start.28) | collective-permute-done | bytes 589856 | tf_op jit(solution)/shard_map/ppermute | solution.py:81
  477.3 10.1 %collective-permute-done.34 = bf16[64,2304]{1,0:T(8,128)(2,1)S(1)} collective-permute-done((bf16[64,2304]{1,0:T(8,128)(2,1)S(1)}, bf16[64,2304]{1,0:T(8,128)(2,1)S(1)}, u32[]{:S(2)}, u32[]{:S(2)}) %collective-permute-start.34) | collective-permute-done | bytes 294944 | tf_op jit(solution)/shard_map/ppermute | solution.py:81
  504.9 10.0 %collective-permute-done.38 = bf16[64,2304]{1,0:T(8,128)(2,1)S(1)} collective-permute-done((bf16[64,2304]{1,0:T(8,128)(2,1)S(1)}, bf16[64,2304]{1,0:T(8,128)(2,1)S(1)}, u32[]{:S(2)}, u32[]{:S(2)}) %collective-permute-start.38) | collective-permute-done | bytes 294944 | tf_op jit(solution)/shard_map/ppermute | solution.py:81
  530.6 9.7 %collective-permute-done.41 = bf16[256,2304]{1,0:T(8,128)(2,1)S(1)} collective-permute-done((bf16[256,2304]{1,0:T(8,128)(2,1)S(1)}, bf16[256,2304]{1,0:T(8,128)(2,1)S(1)}, u32[]{:S(2)}, u32[]{:S(2)}) %collective-permute-start.41) | collective-permute-done | bytes 1179680 | tf_op jit(solution)/shard_map/ppermute | solution.py:81
  549.7 14.5 %collective-permute-done.47 = f32[18,128]{1,0:T(8,128)S(1)} collective-permute-done((f32[18,128]{1,0:T(8,128)S(1)}, f32[18,128]{1,0:T(8,128)S(1)}, u32[]{:S(2)}, u32[]{:S(2)}) %collective-permute-start.47) | collective-permute-done | bytes 9248 | tf_op jit(solution)/shard_map/ppermute | solution.py:81
  564.2 16.2 %collective-permute-done.44 = bf16[64,3072]{1,0:T(8,128)(2,1)S(1)} collective-permute-done((bf16[64,3072]{1,0:T(8,128)(2,1)S(1)}, bf16[64,3072]{1,0:T(8,128)(2,1)S(1)}, u32[]{:S(2)}, u32[]{:S(2)}) %collective-permute-start.44) | collective-permute-done | bytes 393248 | tf_op jit(solution)/shard_map/ppermute | solution.py:81
  586.3 10.7 %collective-permute-done.51 = f32[18,128]{1,0:T(8,128)S(1)} collective-permute-done((f32[18,128]{1,0:T(8,128)S(1)}, f32[18,128]{1,0:T(8,128)S(1)}, u32[]{:S(2)}, u32[]{:S(2)}) %collective-permute-start.51) | collective-permute-done | bytes 9248 | tf_op jit(solution)/shard_map/ppermute | solution.py:81
  636.0 12.0 %collective-permute-done.57 = bf16[256,1536]{1,0:T(8,128)(2,1)} collective-permute-done((bf16[256,1536]{1,0:T(8,128)(2,1)S(1)}, bf16[256,1536]{1,0:T(8,128)(2,1)}, u32[]{:S(2)}, u32[]{:S(2)}) %collective-permute-start.57) | collective-permute-done | bytes 786464 | tf_op jit(solution)/shard_map/ppermute | solution.py:81
  (387 shorter events, 305.7 us)
Async XLA Ops:
  7.2 181.9 %all-gather.2.cloned.1.call-start = ((), (), s32[]{:S(2)}) async-start(), calls=%async_computation | async-start | bytes 9437184 | tf_op jit(solution)/shard_map/all_gather | solution.py:727
  37.9 68.6 %collective-permute-start.7 = (bf16[256,3584]{1,0:T(8,128)(2,1)}, bf16[256,3584]{1,0:T(8,128)(2,1)}, u32[]{:S(2)}, u32[]{:S(2)}) collective-permute-start(bf16[256,3584]{1,0:T(8,128)(2,1)} %fusion.12), channel_id=1, source_target_pairs={{0,16},{16,0},{1,17},{17,1},{2,18},{18,2},{3,19},{19,3},{4,20},{20... | collective-permute-start | bytes 5505032 | tf_op jit(solution)/shard_map/ppermute | solution.py:81
  48.7 37.9 %collective-permute-start.3 = (bf16[256,1024]{1,0:T(8,128)(2,1)S(1)}, bf16[256,1024]{1,0:T(8,128)(2,1)S(1)}, u32[]{:S(2)}, u32[]{:S(2)}) collective-permute-start(bf16[256,1024]{1,0:T(8,128)(2,1)S(1)} %get-tuple-element.139), channel_id=1, source_target_pairs={{0,10},{2,8},{4,14},{6,12},{8,2},{10,0},{12,6},{14,4},{1,11},{3,9}... | collective-permute-start | bytes 1572872 | tf_op jit(solution)/shard_map/ppermute | solution.py:91
  53.7 44.5 %collective-permute-start.5 = (bf16[256,1024]{1,0:T(8,128)(2,1)S(1)}, bf16[256,1024]{1,0:T(8,128)(2,1)S(1)}, u32[]{:S(2)}, u32[]{:S(2)}) collective-permute-start(bf16[256,1024]{1,0:T(8,128)(2,1)S(1)} %get-tuple-element.141), channel_id=1, source_target_pairs={{0,2},{2,0},{4,6},{6,4},{8,10},{10,8},{12,14},{14,12},{1,3},{3,1},... | collective-permute-start | bytes 1572872 | tf_op jit(solution)/shard_map/ppermute | solution.py:91
  55.2 43.0 %collective-permute-start.6 = (bf16[256,1024]{1,0:T(8,128)(2,1)S(1)}, bf16[256,1024]{1,0:T(8,128)(2,1)S(1)}, u32[]{:S(2)}, u32[]{:S(2)}) collective-permute-start(bf16[256,1024]{1,0:T(8,128)(2,1)S(1)} %get-tuple-element.142), channel_id=1, source_target_pairs={{0,6},{2,4},{4,2},{6,0},{8,14},{10,12},{12,10},{14,8},{1,7},{3,5},... | collective-permute-start | bytes 1572872 | tf_op jit(solution)/shard_map/ppermute | solution.py:91
  123.4 47.6 %collective-permute-start.8 = (bf16[256,1024]{1,0:T(8,128)(2,1)}, bf16[256,1024]{1,0:T(8,128)(2,1)S(1)}, u32[]{:S(2)}, u32[]{:S(2)}) collective-permute-start(bf16[256,1024]{1,0:T(8,128)(2,1)} %copy-done.45), channel_id=1, source_target_pairs={{0,8},{2,10},{4,12},{6,14},{8,0},{10,2},{12,4},{14,6},{1,9},{3,11}... | collective-permute-start | bytes 1572872 | tf_op jit(solution)/shard_map/ppermute | solution.py:91
  126.2 44.9 %collective-permute-start.9 = (bf16[256,1024]{1,0:T(8,128)(2,1)}, bf16[256,1024]{1,0:T(8,128)(2,1)S(1)}, u32[]{:S(2)}, u32[]{:S(2)}) collective-permute-start(bf16[256,1024]{1,0:T(8,128)(2,1)} %copy-done.44), channel_id=1, source_target_pairs={{0,12},{2,14},{4,8},{6,10},{8,4},{10,6},{12,0},{14,2},{1,13},{3,15... | collective-permute-start | bytes 1572872 | tf_op jit(solution)/shard_map/ppermute | solution.py:91
  130.9 40.1 %collective-permute-start.10 = (bf16[256,1024]{1,0:T(8,128)(2,1)S(1)}, bf16[256,1024]{1,0:T(8,128)(2,1)S(1)}, u32[]{:S(2)}, u32[]{:S(2)}) collective-permute-start(bf16[256,1024]{1,0:T(8,128)(2,1)S(1)} %copy-done.43), channel_id=1, source_target_pairs={{0,4},{2,6},{4,0},{6,2},{8,12},{10,14},{12,8},{14,10},{1,5},{3,7},... | collective-permute-start | bytes 1572872 | tf_op jit(solution)/shard_map/ppermute | solution.py:91
  227.1 115.5 %collective-permute-start.20 = (bf16[512,2304]{1,0:T(8,128)(2,1)}, bf16[512,2304]{1,0:T(8,128)(2,1)}, u32[]{:S(2)}, u32[]{:S(2)}) collective-permute-start(bf16[512,2304]{1,0:T(8,128)(2,1)} %shard_map.249), channel_id=1, source_target_pairs={{0,16},{16,0},{1,17},{17,1},{2,18},{18,2},{3,19},{19,3},{4,20},{20... | collective-permute-start | bytes 7077896 | tf_op jit(solution)/shard_map/ppermute | solution.py:81
  227.1 115.5 %collective-permute-start.21 = (bf16[512,2304]{1,0:T(8,128)(2,1)}, bf16[512,2304]{1,0:T(8,128)(2,1)}, u32[]{:S(2)}, u32[]{:S(2)}) collective-permute-start(bf16[512,2304]{1,0:T(8,128)(2,1)} %shard_map.250), channel_id=1, source_target_pairs={{0,2},{2,0},{4,6},{6,4},{8,10},{10,8},{12,14},{14,12},{1,3},{3,1},... | collective-permute-start | bytes 7077896 | tf_op jit(solution)/shard_map/ppermute | solution.py:81
  253.8 45.8 %collective-permute-start.16 = (bf16[2,256,512]{2,1,0:T(8,128)(2,1)S(1)}, bf16[2,256,512]{2,1,0:T(8,128)(2,1)S(1)}, u32[]{:S(2)}, u32[]{:S(2)}) collective-permute-start(bf16[2,256,512]{2,1,0:T(8,128)(2,1)S(1)} %get-tuple-element.174), channel_id=1, source_target_pairs={{0,10},{2,8},{4,14},{6,12},{8,2},{10,0},{12,6},{14,4},{1,11},{3,9}... | collective-permute-start | bytes 1572872 | tf_op jit(solution)/shard_map/ppermute | solution.py:91
  264.3 50.8 %collective-permute-start.17 = (bf16[2,256,512]{2,1,0:T(8,128)(2,1)}, bf16[2,256,512]{2,1,0:T(8,128)(2,1)}, u32[]{:S(2)}, u32[]{:S(2)}) collective-permute-start(bf16[2,256,512]{2,1,0:T(8,128)(2,1)} %get-tuple-element.178), channel_id=1, source_target_pairs={{0,14},{2,12},{4,10},{6,8},{8,6},{10,4},{12,2},{14,0},{1,15},{3,13... | collective-permute-start | bytes 1572872 | tf_op jit(solution)/shard_map/ppermute | solution.py:91
  273.8 56.7 %collective-permute-start.18 = (bf16[2,256,512]{2,1,0:T(8,128)(2,1)}, bf16[2,256,512]{2,1,0:T(8,128)(2,1)}, u32[]{:S(2)}, u32[]{:S(2)}) collective-permute-start(bf16[2,256,512]{2,1,0:T(8,128)(2,1)} %get-tuple-element.183), channel_id=1, source_target_pairs={{0,2},{2,0},{4,6},{6,4},{8,10},{10,8},{12,14},{14,12},{1,3},{3,1},... | collective-permute-start | bytes 1572872 | tf_op jit(solution)/shard_map/ppermute | solution.py:91
  345.3 46.7 %collective-permute-start.25 = (bf16[256,2304]{1,0:T(8,128)(2,1)}, bf16[256,2304]{1,0:T(8,128)(2,1)}, u32[]{:S(2)}, u32[]{:S(2)}) collective-permute-start(bf16[256,2304]{1,0:T(8,128)(2,1)} %add_convert_fusion.3), channel_id=1, source_target_pairs={{0,2},{2,0},{4,6},{6,4},{8,10},{10,8},{12,14},{14,12},{1,3},{3,1},... | collective-permute-start | bytes 3538952 | tf_op jit(solution)/shard_map/ppermute | solution.py:81
  349.7 42.3 %collective-permute-start.26 = (bf16[256,2304]{1,0:T(8,128)(2,1)}, bf16[256,2304]{1,0:T(8,128)(2,1)}, u32[]{:S(2)}, u32[]{:S(2)}) collective-permute-start(bf16[256,2304]{1,0:T(8,128)(2,1)} %add_convert_fusion.2), channel_id=1, source_target_pairs={{0,16},{16,0},{1,17},{17,1},{2,18},{18,2},{3,19},{19,3},{4,20},{20... | collective-permute-start | bytes 3538952 | tf_op jit(solution)/shard_map/ppermute | solution.py:81
  349.9 41.4 %collective-permute-start.22 = (bf16[2,256,512]{2,1,0:T(8,128)(2,1)}, bf16[2,256,512]{2,1,0:T(8,128)(2,1)S(1)}, u32[]{:S(2)}, u32[]{:S(2)}) collective-permute-start(bf16[2,256,512]{2,1,0:T(8,128)(2,1)} %get-tuple-element.199), channel_id=1, source_target_pairs={{0,8},{2,10},{4,12},{6,14},{8,0},{10,2},{12,4},{14,6},{1,9},{3,11}... | collective-permute-start | bytes 1572872 | tf_op jit(solution)/shard_map/ppermute | solution.py:91
  391.4 44.4 %collective-permute-start.30 = (bf16[512,2048]{1,0:T(8,128)(2,1)}, bf16[512,2048]{1,0:T(8,128)(2,1)}, u32[]{:S(2)}, u32[]{:S(2)}) collective-permute-start(bf16[512,2048]{1,0:T(8,128)(2,1)} %shard_map.258), channel_id=1, source_target_pairs={{0,16},{16,0},{1,17},{17,1},{2,18},{18,2},{3,19},{19,3},{4,20},{20... | collective-permute-start | bytes 6291464 | tf_op jit(solution)/shard_map/ppermute | solution.py:81
  398.9 42.7 %collective-permute-start.29 = (bf16[64,4608]{1,0:T(8,128)(2,1)}, bf16[64,4608]{1,0:T(8,128)(2,1)}, u32[]{:S(2)}, u32[]{:S(2)}) collective-permute-start(bf16[64,4608]{1,0:T(8,128)(2,1)} %get-tuple-element.299), channel_id=1, source_target_pairs={{0,12},{2,14},{4,8},{6,10},{8,4},{10,6},{12,0},{14,2},{1,13},{3,15... | collective-permute-start | bytes 1769480 | tf_op jit(solution)/shard_map/ppermute | solution.py:81
  401.6 50.6 %collective-permute-start.28 = (bf16[64,4608]{1,0:T(8,128)(2,1)}, bf16[64,4608]{1,0:T(8,128)(2,1)}, u32[]{:S(2)}, u32[]{:S(2)}) collective-permute-start(bf16[64,4608]{1,0:T(8,128)(2,1)} %get-tuple-element.298), channel_id=1, source_target_pairs={{0,8},{2,10},{4,12},{6,14},{8,0},{10,2},{12,4},{14,6},{1,9},{3,11}... | collective-permute-start | bytes 1769480 | tf_op jit(solution)/shard_map/ppermute | solution.py:81
  410.5 41.6 %collective-permute-start.27 = (bf16[64,4608]{1,0:T(8,128)(2,1)}, bf16[64,4608]{1,0:T(8,128)(2,1)}, u32[]{:S(2)}, u32[]{:S(2)}) collective-permute-start(bf16[64,4608]{1,0:T(8,128)(2,1)} %get-tuple-element.297), channel_id=1, source_target_pairs={{0,4},{2,6},{4,0},{6,2},{8,12},{10,14},{12,8},{14,10},{1,5},{3,7},... | collective-permute-start | bytes 1769480 | tf_op jit(solution)/shard_map/ppermute | solution.py:81
  416.0 109.3 %collective-permute-start.15 = (bf16[512,1024]{1,0:T(8,128)(2,1)S(1)}, bf16[512,1024]{1,0:T(8,128)(2,1)}, u32[]{:S(2)}, u32[]{:S(2)}) collective-permute-start(bf16[512,1024]{1,0:T(8,128)(2,1)S(1)} %shard_map.252), channel_id=1, source_target_pairs={{0,1},{1,0},{2,3},{3,2},{4,5},{5,4},{6,7},{7,6},{8,9},{9,8},{10,11... | collective-permute-start | bytes 3145736 | tf_op jit(solution)/shard_map/ppermute | solution.py:75
  477.0 47.4 %collective-permute-start.33 = (bf16[512,1024]{1,0:T(8,128)(2,1)S(1)}, bf16[512,1024]{1,0:T(8,128)(2,1)S(1)}, u32[]{:S(2)}, u32[]{:S(2)}) collective-permute-start(bf16[512,1024]{1,0:T(8,128)(2,1)S(1)} %add_convert_fusion.5), channel_id=1, source_target_pairs={{0,1},{1,0},{2,3},{3,2},{4,5},{5,4},{6,7},{7,6},{8,9},{9,8},{10,11... | collective-permute-start | bytes 3145736 | tf_op jit(solution)/shard_map/ppermute | solution.py:75
  541.0 39.6 %collective-permute-start.42 = (bf16[256,2304]{1,0:T(8,128)(2,1)S(1)}, bf16[256,2304]{1,0:T(8,128)(2,1)S(1)}, u32[]{:S(2)}, u32[]{:S(2)}) collective-permute-start(bf16[256,2304]{1,0:T(8,128)(2,1)S(1)} %maximum_select_fusion.8), channel_id=1, source_target_pairs={{0,2},{2,0},{4,6},{6,4},{8,10},{10,8},{12,14},{14,12},{1,3},{3,1},... | collective-permute-start | bytes 3538952 | tf_op jit(solution)/shard_map/ppermute | solution.py:81
  544.2 36.3 %collective-permute-start.44 = (bf16[64,3072]{1,0:T(8,128)(2,1)S(1)}, bf16[64,3072]{1,0:T(8,128)(2,1)S(1)}, u32[]{:S(2)}, u32[]{:S(2)}) collective-permute-start(bf16[64,3072]{1,0:T(8,128)(2,1)S(1)} %get-tuple-element.304), channel_id=1, source_target_pairs={{0,8},{2,10},{4,12},{6,14},{8,0},{10,2},{12,4},{14,6},{1,9},{3,11}... | collective-permute-start | bytes 1179656 | tf_op jit(solution)/shard_map/ppermute | solution.py:81
  (117 other events, 1728.8 us)
Sparse Core Ops, SparseCore 0:
  39.1 107.1 all-gather.1

commit v8 on v7

--- a/solution.py
+++ b/solution.py
@@ -397,17 +397,6 @@
     return begin
 
 
-def block_mask(meta_ref, docs, shape, half, q_part, k_part, diagonal):
-    row = lax.broadcasted_iota(jnp.int32, (shape[0], 1), 0)
-    q_place = q_part * half + jnp.where(row >= half, row - half, row)
-    begin = doc_begins(meta_ref, docs, q_place) - k_part * half
-    column = lax.broadcasted_iota(jnp.int32, shape, 1)
-    visible = column >= begin
-    if diagonal:
-        visible = visible & (column <= q_place - k_part * half)
-    return visible
-
-
 def mask_across(meta_ref, docs, shape, half, q_part, k_part, diagonal):
     column = lax.broadcasted_iota(jnp.int32, (1, shape[1]), 1)
     q_place = q_part * half + jnp.where(column >= half, column - half, column)
@@ -419,20 +408,6 @@
     return visible
 
 
-def any_visible(meta_ref, docs, half, q_part, k_part):
-    return (k_part + 1) * half > doc_begins(meta_ref, docs, q_part * half)
-
-
-def all_visible(meta_ref, docs, half, q_part, k_part):
-    return k_part * half >= doc_begins(meta_ref, docs, q_part * half + half - 1)
-
-
-def masked(weights, *mask_args):
-    if mask_args[-1] is None:
-        return weights
-    return jnp.where(block_mask(*mask_args), weights, 0.0)
-
-
 def two_heads(ref, start, half):
     rows = pl.ds(start, half)
     return jnp.concatenate([ref[rows, :HEAD], ref[rows, HEAD:]], axis=0)
@@ -440,38 +415,41 @@
 
 def forward_kernel(docs, count, meta_ref, q_ref, k_ref, v_ref, *refs):
     others = refs[: 2 * (count - 1)]
-    out_ref, out16_ref, lse_ref, acc_ref = refs[2 * (count - 1) :]
+    out_ref, out16_ref, lse_ref, acc_ref, begin_ref = refs[2 * (count - 1) :]
     half = q_ref.shape[0] // 2
     factor = HEAD**-0.5 * LOG2E
     ones = jnp.ones((half, HEAD), BF16)
     own = meta_ref[0]
-
-    def block(start, keys, values, q_part, k_part, diagonal):
+    parts = (own, 2 * count - 1 - own)
+
+    @pl.when(pl.program_id(0) == 0)
+    def _():
+        row = lax.broadcasted_iota(jnp.int32, (2 * half, HEAD), 0)
+        for e in range(2):
+            place = parts[e] * half + jnp.where(row >= half, row - half, row)
+            begin_ref[e] = doc_begins(meta_ref, docs, place)
+
+    def block(side, start, keys, values, k_part, diagonal):
         scores = dot_nt(two_heads(q_ref, start, half), keys)
-        weights = jnp.exp2(scores * factor)
-        weights = masked(weights, meta_ref, docs, scores.shape, half, q_part, k_part, diagonal)
-        weights = weights.astype(BF16)
+        column = lax.broadcasted_iota(jnp.int32, scores.shape, 1)
+        begin = begin_ref[side] - k_part * half
+        visible = column >= jnp.concatenate([begin] * (half // HEAD), axis=1)
+        if diagonal:
+            row = lax.broadcasted_iota(jnp.int32, scores.shape, 0)
+            visible = visible & (column <= jnp.where(row >= half, row - half, row))
+        weights = jnp.where(visible, jnp.exp2(scores * factor), 0.0).astype(BF16)
         return dot(weights, jnp.concatenate([values, ones], axis=1))
 
     for e in range(2):
         rows = pl.ds(e * half, half)
-        part = own if e == 0 else 2 * count - 1 - own
-        acc_ref[e] = block(e * half, k_ref[rows, :], v_ref[rows, :], part, part, True)
+        acc_ref[e] = block(e, e * half, k_ref[rows, :], v_ref[rows, :], parts[e], True)
     for d in range(count - 1):
         side = meta_ref[docs + d]
         k_part = meta_ref[docs + count - 1 + d]
-        q_part = jnp.where(side == 0, own, 2 * count - 1 - own)
-
-        def add(mask):
-            start = pl.multiple_of(side * half, half)
-            acc_ref[side] += block(
-                start, others[2 * d][...], others[2 * d + 1][...], q_part, k_part, mask
-            )
-
-        seen = any_visible(meta_ref, docs, half, q_part, k_part)
-        whole = all_visible(meta_ref, docs, half, q_part, k_part)
-        pl.when(whole)(functools.partial(add, None))
-        pl.when(seen & jnp.logical_not(whole))(functools.partial(add, False))
+        start = pl.multiple_of(side * half, half)
+        acc_ref[side] += block(
+            side, start, others[2 * d][...], others[2 * d + 1][...], k_part, False
+        )
 
     for e in range(2):
         total = acc_ref[e]
@@ -509,11 +487,8 @@
         lse = stats_ref[side][:1]
         delta = delta_ref[side][:1]
         weights = jnp.exp2(scores * (scale * LOG2E) - lse)
-        if diagonal is not None:
-            visible = mask_across(
-                meta_ref, docs, scores.shape, half, q_part, k_part, diagonal
-            )
-            weights = jnp.where(visible, weights, 0.0)
+        visible = mask_across(meta_ref, docs, scores.shape, half, q_part, k_part, diagonal)
+        weights = jnp.where(visible, weights, 0.0)
         d_weights = dot_nt(values, grads)
         d_scores = (weights * (d_weights - delta)).astype(BF16)
         d_values = dot(weights.astype(BF16), grads)
@@ -533,24 +508,13 @@
         side = meta_ref[docs + d]
         k_part = meta_ref[docs + count - 1 + d]
         q_part = jnp.where(side == 0, own, 2 * count - 1 - own)
-        seen = any_visible(meta_ref, docs, half, q_part, k_part)
-        whole = all_visible(meta_ref, docs, half, q_part, k_part)
-
-        def add(mask):
-            start = pl.multiple_of(side * half, half)
-            d_queries, d_keys, d_values = block(
-                side, start, others[2 * d][...], others[2 * d + 1][...], q_part, k_part, mask
-            )
-            acc_ref[side] += d_queries
-            given[d][0] = d_keys.astype(BF16)
-            given[d][1] = d_values.astype(BF16)
-
-        pl.when(whole)(functools.partial(add, None))
-        pl.when(seen & jnp.logical_not(whole))(functools.partial(add, False))
-
-        @pl.when(jnp.logical_not(seen))
-        def _():
-            given[d][...] = jnp.zeros_like(given[d])
+        start = pl.multiple_of(side * half, half)
+        d_queries, d_keys, d_values = block(
+            side, start, others[2 * d][...], others[2 * d + 1][...], q_part, k_part, False
+        )
+        acc_ref[side] += d_queries
+        given[d][0] = d_keys.astype(BF16)
+        given[d][1] = d_values.astype(BF16)
 
     for e in range(2):
         for a in range(2):
@@ -588,7 +552,10 @@
             grid=(kv_heads,),
             in_specs=[column] + key_value_specs(rows, half, kv_heads, count),
             out_specs=[column] * 3,
-            scratch_shapes=[pltpu.VMEM((2, 2 * half, 2 * HEAD), F32)],
+            scratch_shapes=[
+                pltpu.VMEM((2, 2 * half, 2 * HEAD), F32),
+                pltpu.VMEM((2, 2 * half, HEAD), jnp.int32),
+            ],
         ),
         out_shape=[
             jax.ShapeDtypeStruct((rows, width), F32),
@@ -747,18 +714,13 @@
 
     exchange(sent, held, straight)
     if shard_count == 2:
-        query_half, rest_half = half_rest[:, :heads_width], half_rest[:, heads_width:]
-        query_got = swap(query_half, "ctx", near_axis[0])
-        query_got, rest_half = tie(query_got, rest_half)
-        other_query = join([query_half, query_got], 0, bit)
-        other_rest = join([rest_half, swap(rest_half, "ctx", near_axis[0])], 0, bit)
-        full_query = join([own_rest[:, :heads_width], other_query], 0, shard)
-        full_rest = join([own_rest[:, heads_width:], other_rest], 0, shard)
+        other_rest = join([half_rest, swap(half_rest, "ctx", near_axis[0])], 0, bit)
+        full_rest = join([own_rest, other_rest], 0, shard)
     else:
         full_rest = lax.all_gather(half_rest, "shard", axis=0, tiled=True)
-        full_query, full_rest = full_rest[:, :heads_width], full_rest[:, heads_width:]
-    full_out_t = full_rest[:, :heads_width]
-    full_down_t = full_rest[:, heads_width:]
+    full_query = full_rest[:, :heads_width]
+    full_out_t = full_rest[:, heads_width : 2 * heads_width]
+    full_down_t = full_rest[:, 2 * heads_width :]
     q_pre = dot(normed_input, full_query)
     queries = rope(q_pre, cosine, sine, scale_q)
     queries, full_out_t = settle(held, straight, queries, full_out_t)
@@ -809,52 +771,46 @@
     )
     given = dict(zip(range(1, count), given))
     returned = {}
-    exchange(given, returned, crossing)
-    normed_late, d_queries = tie(normed_two, d_queries)
-    gates = crossing[:4]
-    if shard_count == 2:
-        normed_b, upstream_b, returned[gates[0]] = tie(
-            normed_late, cotangent, returned[gates[0]]
-        )
-        kept_b = split_product((bit, 2 + bit), pairs_b(normed_b, upstream_b))
-        normed_a, kept_b, returned[gates[1]] = tie(normed_late, kept_b, returned[gates[1]])
-        kept_a = split_product(home, pairs_a(normed_a))
-        d_queries, kept_a = tie(d_queries, kept_a)
-    d_queries, returned[gates[2]] = tie(d_queries, returned[gates[2]])
-    d_q_pre, gq_part = rope_back(d_queries, q_pre, cosine, sine, scale_q)
-    d_q_pre, returned[gates[3]] = tie(d_q_pre, returned[gates[3]])
-    out_pairs = [(d_branch, attn_out, 0, heads_width), (normed_input, d_q_pre, 0, heads_width)]
-    if shard_count == 2:
-        kept_out, sent_out = split_product(home, out_pairs), split_product(away, out_pairs)
-        kept_a, kept_b, kept_out, sent_out, got_a, got_b, *rest = settle(
-            returned,
-            crossing,
-            kept_a,
-            kept_b,
-            kept_out,
-            sent_out,
-            got_a,
-            got_b,
-            *(given[d] for d in straight),
-        )
-        given.update(zip(straight, rest))
     exchange(given, returned, straight)
     if shard_count == 2:
-        units_a = halve([kept_a, got_a], near_axis)
+        first, second = straight[-1], straight[0]
+        normed_late, returned[first] = tie(normed_two, returned[first])
+        units_a = [split_product(home, pairs_a(normed_late)), got_a]
+        units_a = halve(units_a, near_axis)
+        normed_late, upstream_late, returned[second] = tie(
+            normed_two, cotangent, returned[second]
+        )
+        kept_b = split_product((bit, 2 + bit), pairs_b(normed_late, upstream_late))
         units_b = [kept_b, got_b]
         units_b_away = total(rows_at(units_b, 1 - shard, depth // 2))
         units_b = rows_at(units_b, shard, depth // 2) + [swap(units_b_away, "shard")]
-        out_query = [kept_out, swap(sent_out, "shard")]
     else:
         units_a = halve(scattered(pairs_a(normed_two)), near_axis)
         units_b = halve(scattered(pairs_b(normed_two, cotangent)), near_axis)
+    d_q_pre, gq_part = rope_back(d_queries, q_pre, cosine, sine, scale_q)
+    out_pairs = [(d_branch, attn_out, 0, heads_width), (normed_input, d_q_pre, 0, heads_width)]
+    if shard_count == 2:
+        out_query = [split_product(home, out_pairs), split_product(away, out_pairs)]
+    else:
         out_query = scattered(out_pairs)
-    units_a[-1], units_b[-1], d_kv = settle(
-        returned, straight, units_a[-1], units_b[-1], d_kv
-    )
+    units_a[-1], units_b[-1], out_query[0], out_query[-1], *rest = settle(
+        returned,
+        straight,
+        units_a[-1],
+        units_b[-1],
+        out_query[0],
+        out_query[-1],
+        *(given[d] for d in crossing),
+    )
+    if shard_count == 2:
+        out_query[-1] = swap(out_query[-1], "shard")
+    given.update(zip(crossing, rest))
+    exchange(given, returned, crossing)
+    units_sum = jnp.concatenate([total(units_a), total(units_b)], axis=1)
+    units_sum, d_kv = settle(returned, crossing, units_sum, d_kv)
     returned = [returned[d] for d in range(1, count)]
 
-    units_sum = halve([jnp.concatenate([total(units_a), total(units_b)], axis=1)], far_axis)
+    units_sum = halve([units_sum], far_axis)
     d_k_pre, d_v_pre, gk_part = key_value_back(
         meta, docs, d_kv, returned, k_pre, cosine, sine, scale_k
     )

time: 667 us -> 631 us (0.946)
  waiting for transfers between devices: 301 us -> 266 us
  other arithmetic: 79.6 us -> 102 us
  starting transfers between devices: 114 us -> 94.6 us
    ppermute x14, starting transfers between devices: 48.8 us -> 22.4 us  [exchange(): done[d] = lax.ppermute(values[d], 'ctx', [(i, i ^ d) for i in range(count)])]
    select_n x19 -> x18, other arithmetic: 34.2 us -> 56.6 us  [join(): jnp.where(index == 0, jnp.concatenate(pieces, dim), jnp.concatenate(piece...]
    ppermute x38 -> x37, waiting for transfers between devices: 179 us -> 157 us  [swap(): return lax.ppermute(value, axis, [(i, i ^ level) for i in range(count)])]
    pallas_call x8, Pallas kernels: 43.7 us -> 32.3 us  [split_product(): pl.pallas_call(functools.partial(split_product_kernel, spans), grid_spec=...]
    ppermute x14, waiting for transfers between devices: 110 us -> 101 us  [exchange(): done[d] = lax.ppermute(values[d], 'ctx', [(i, i ^ d) for i in range(count)])]
    ppermute x38 -> x37, starting transfers between devices: 59.4 us -> 66.7 us  [swap(): return lax.ppermute(value, axis, [(i, i ^ level) for i in range(count)])]
    unnamed x162 -> x186, local copies, waits for them, and re-layouts: 19 us -> 21.2 us
  transfers between devices with their start and end apart: 60 -> 59, of which waited for: 28 -> 24; matrix products, arithmetic and copies ran while one was open for 15% -> 20% of each run, Pallas kernels for 11% -> 12%
where the time goes in v8:
time: 631 us; the launch traced here: 623 us
  waiting for transfers between devices  266 us (42%)
  other arithmetic  102 us (16%)
  starting transfers between devices  94.6 us (15%)
  Pallas kernels  90.7 us (14%)
  local copies, waits for them, and re-layouts  31.7 us (5%)
  matrix products  22.6 us (4%)
  between operations  16 us (3%)
    ppermute x37, waiting for transfers between devices, swap(): return lax.ppermute(value, axis, [(i, i ^ level) for i in range(count)])  157 us
    ppermute x14, waiting for transfers between devices, exchange(): done[d] = lax.ppermute(values[d], 'ctx', [(i, i ^ d) for i in range(count)])  101 us
    ppermute x37, starting transfers between devices, swap(): return lax.ppermute(value, axis, [(i, i ^ level) for i in range(count)])  66.7 us
    select_n x18, other arithmetic, join(): jnp.where(index == 0, jnp.concatenate(pieces, dim), jnp.concatenate(piece...  56.6 us
    pallas_call x8, Pallas kernels, split_product(): pl.pallas_call(functools.partial(split_product_kernel, spans), grid_spec=...  32.3 us
    ppermute x14, starting transfers between devices, exchange(): done[d] = lax.ppermute(values[d], 'ctx', [(i, i ^ d) for i in range(count)])  22.4 us
    unnamed x186, local copies, waits for them, and re-layouts  21.2 us
    pallas_call x1, Pallas kernels, attend_back(): pl.pallas_call(functools.partial(backward_kernel, docs, count), grid_spec...  19.4 us
  transfers between devices with their start and end apart: 59, of which 24 were waited for; matrix products, arithmetic and copies ran while one was open for 20% of the time, Pallas kernels for 12%

profile of v8, /device:TPU:0, one launch (start us, length us, event | category | flops | bytes accessed | tf_op | source)
XLA Modules:
  0.0 623.4 jit_solution(17101747893742126357)
XLA Ops:
  27.8 6.0 collective-permute-done
  37.7 7.9 %shard_map.246 = (f32[512,512]{1,0:T(8,128)}, bf16[512,1024]{1,0:T(8,128)(2,1)}, bf16[512,1024]{1,0:T(8,128)(2,1)}, bf16[256,1024]{1,0:T(8,128)(2,1)S(1)}, bf16[...) custom-call(s32[20]{0:T(128)S(1)} %concatenate.244.meta_ref, ...), custom_call_target="tpu_custom_call" | custom-call | flops 1000 | bytes 1000 | tf_op jit(solution)/shard_map/pallas_call | solution.py:284
  53.1 31.5 %collective-permute-done.3.refs_8_.refs_9_ = bf16[256,1024]{1,0:T(8,128)(2,1)S(1)} collective-permute-done((bf16[256,1024]{1,0:T(8,128)(2,1)S(1)}, bf16[256,1024]{1,0:T(8,128)(2,1)S(1)}, u32[]{:S(2)}, u32[]{:S(2)}) %collective-permute-start.3) | collective-permute-done | bytes 524320 | tf_op jit(solution)/shard_map/ppermute | solution.py:91
  84.6 11.4 %collective-permute-done.5.refs_0_.refs_1_ = bf16[256,1024]{1,0:T(8,128)(2,1)S(1)} collective-permute-done((bf16[256,1024]{1,0:T(8,128)(2,1)S(1)}, bf16[256,1024]{1,0:T(8,128)(2,1)S(1)}, u32[]{:S(2)}, u32[]{:S(2)}) %collective-permute-start.5) | collective-permute-done | bytes 524320 | tf_op jit(solution)/shard_map/ppermute | solution.py:91
  102.1 34.7 %collective-permute-done.11 = bf16[256,3584]{1,0:T(8,128)(2,1)} collective-permute-done((bf16[256,3584]{1,0:T(8,128)(2,1)}, bf16[256,3584]{1,0:T(8,128)(2,1)}, u32[]{:S(2)}, u32[]{:S(2)}) %collective-permute-start.11) | collective-permute-done | bytes 1835040 | tf_op jit(solution)/shard_map/ppermute | solution.py:81
  140.7 45.0 %maximum_select_fusion = bf16[1024,3584]{1,0:T(8,128)(2,1)} fusion(bf16[512,3584]{1,0:T(8,128)(2,1)S(1)} %maximum_select_fusion.1, bf16[512,1536]{1,0:T(8,128)(2,1)S(1)} %bitcast.51, bf16[512,1024]{1,0:T(8,128)(2,1)S(1)} %bitcast.53, bf16[512,1024]{1,0:T(8,128)(2,1)S(1)} %copy-done.81, pred[]{:T(512)S(6)} %eq.86), kind=kLoop, calls=%fused_computation | loop fusion | flops 62390272 | bytes 14680065 | tf_op jit(solution)/shard_map/jit(_where)/select_n | solution.py:58
  193.2 10.6 %shard_map.248 = (f32[512,1024]{1,0:T(8,128)}, bf16[512,1024]{1,0:T(8,128)(2,1)S(1)}, f32[512,1024]{1,0:T(8,128)}) custom-call(s32[20]{0:T(128)S(1)} %concatenate.244.meta_ref, bf16[512,1024]{1,0:T(8,128)(2,1)S(1)} %shard_map.247.q_ref, bf16[512,1024]{1,0:T(8,128)(2,1)} %get-tuple-element.140.k_ref.v_ref, bf16[512,1024]{1,0:T(8,128)(2,1)} %get-tuple-element.140.k_ref.v_ref, ...), custom_call_target="tpu_custom_call" | custom-call | flops 1000 | bytes 1000 | tf_op jit(solution)/shard_map/pallas_call | solution.py:548
  211.5 5.6 fusion.49
  231.9 6.1 shard_map.251
  246.4 19.4 %shard_map.253 = (f32[512,1024]{1,0:T(8,128)}, f32[2,512,512]{2,1,0:T(8,128)}, bf16[2,256,512]{2,1,0:T(8,128)(2,1)S(1)}, bf16[2,256,512]{2,1,0:T(8,128)(2,1)}, b...) custom-call(s32[20]{0:T(128)S(1)} %concatenate.244.meta_ref, ...), custom_call_target="tpu_custom_call" | custom-call | flops 1000 | bytes 1000 | tf_op jit(solution)/shard_map/pallas_call | solution.py:577
  273.2 21.2 %collective-permute-done.17.refs_1_ = bf16[2,256,512]{2,1,0:T(8,128)(2,1)S(1)} collective-permute-done((bf16[2,256,512]{2,1,0:T(8,128)(2,1)}, bf16[2,256,512]{2,1,0:T(8,128)(2,1)S(1)}, u32[]{:S(2)}, u32[]{:S(2)}) %collective-permute-start.17) | collective-permute-done | bytes 524320 | tf_op jit(solution)/shard_map/ppermute | solution.py:91
  330.0 6.5 %collective-permute-done.21 = bf16[256,2304]{1,0:T(8,128)(2,1)} collective-permute-done((bf16[256,2304]{1,0:T(8,128)(2,1)}, bf16[256,2304]{1,0:T(8,128)(2,1)}, u32[]{:S(2)}, u32[]{:S(2)}) %collective-permute-start.21) | collective-permute-done | bytes 1179680 | tf_op jit(solution)/shard_map/ppermute | solution.py:81
  351.0 23.9 %collective-permute-done.22.refs_4_ = bf16[2,256,512]{2,1,0:T(8,128)(2,1)S(1)} collective-permute-done((bf16[2,256,512]{2,1,0:T(8,128)(2,1)S(1)}, bf16[2,256,512]{2,1,0:T(8,128)(2,1)S(1)}, u32[]{:S(2)}, u32[]{:S(2)}) %collective-permute-start.22) | collective-permute-done | bytes 524320 | tf_op jit(solution)/shard_map/ppermute | solution.py:91
  375.0 12.5 %collective-permute-done.24.refs_0_ = bf16[2,256,512]{2,1,0:T(8,128)(2,1)S(1)} collective-permute-done((bf16[2,256,512]{2,1,0:T(8,128)(2,1)S(1)}, bf16[2,256,512]{2,1,0:T(8,128)(2,1)S(1)}, u32[]{:S(2)}, u32[]{:S(2)}) %collective-permute-start.24) | collective-permute-done | bytes 524320 | tf_op jit(solution)/shard_map/ppermute | solution.py:91
  398.4 5.2 shard_map.259
  416.4 15.3 %collective-permute-done.27 = bf16[64,4608]{1,0:T(8,128)(2,1)} collective-permute-done((bf16[64,4608]{1,0:T(8,128)(2,1)}, bf16[64,4608]{1,0:T(8,128)(2,1)}, u32[]{:S(2)}, u32[]{:S(2)}) %collective-permute-start.27) | collective-permute-done | bytes 589856 | tf_op jit(solution)/shard_map/ppermute | solution.py:81
  438.6 8.8 %collective-permute-start.33 = (bf16[64,2304]{1,0:T(8,128)(2,1)S(1)}, bf16[64,2304]{1,0:T(8,128)(2,1)S(1)}, u32[]{:S(2)}, u32[]{:S(2)}) collective-permute-start(bf16[64,2304]{1,0:T(8,128)(2,1)S(1)} %get-tuple-element.200), channel_id=1, source_target_pairs={{0,4},{2,6},{4,0},{6,2},{8,12},{10,14},{12,8},{14,10},{1,5},{3,7},... | collective-permute-start | bytes 884744 | tf_op jit(solution)/shard_map/ppermute | solution.py:81
  458.7 12.1 %collective-permute-done.34 = bf16[64,2304]{1,0:T(8,128)(2,1)S(1)} collective-permute-done((bf16[64,2304]{1,0:T(8,128)(2,1)S(1)}, bf16[64,2304]{1,0:T(8,128)(2,1)S(1)}, u32[]{:S(2)}, u32[]{:S(2)}) %collective-permute-start.34) | collective-permute-done | bytes 294944 | tf_op jit(solution)/shard_map/ppermute | solution.py:81
  487.0 10.7 %collective-permute-done.38 = bf16[64,2304]{1,0:T(8,128)(2,1)S(1)} collective-permute-done((bf16[64,2304]{1,0:T(8,128)(2,1)S(1)}, bf16[64,2304]{1,0:T(8,128)(2,1)S(1)}, u32[]{:S(2)}, u32[]{:S(2)}) %collective-permute-start.38) | collective-permute-done | bytes 294944 | tf_op jit(solution)/shard_map/ppermute | solution.py:81
  517.5 23.7 %collective-permute-done.46 = f32[18,128]{1,0:T(8,128)S(1)} collective-permute-done((f32[18,128]{1,0:T(8,128)S(1)}, f32[18,128]{1,0:T(8,128)S(1)}, u32[]{:S(2)}, u32[]{:S(2)}) %collective-permute-start.46) | collective-permute-done | bytes 9248 | tf_op jit(solution)/shard_map/ppermute | solution.py:81
  542.2 6.2 %collective-permute-start.47 = (bf16[64,1536]{1,0:T(8,128)(2,1)S(1)}, bf16[64,1536]{1,0:T(8,128)(2,1)S(1)}, u32[]{:S(2)}, u32[]{:S(2)}) collective-permute-start(bf16[64,1536]{1,0:T(8,128)(2,1)S(1)} %get-tuple-element.286), channel_id=1, source_target_pairs={{0,4},{2,6},{4,0},{6,2},{8,12},{10,14},{12,8},{14,10},{1,5},{3,7},... | collective-permute-start | bytes 589832 | tf_op jit(solution)/shard_map/ppermute | solution.py:81
  552.6 8.6 %collective-permute-done.50 = f32[18,128]{1,0:T(8,128)S(1)} collective-permute-done((f32[18,128]{1,0:T(8,128)S(1)}, f32[18,128]{1,0:T(8,128)S(1)}, u32[]{:S(2)}, u32[]{:S(2)}) %collective-permute-start.50) | collective-permute-done | bytes 9248 | tf_op jit(solution)/shard_map/ppermute | solution.py:81
  580.9 10.5 %collective-permute-done.53 = bf16[64,1536]{1,0:T(8,128)(2,1)S(1)} collective-permute-done((bf16[64,1536]{1,0:T(8,128)(2,1)S(1)}, bf16[64,1536]{1,0:T(8,128)(2,1)S(1)}, u32[]{:S(2)}, u32[]{:S(2)}) %collective-permute-start.53) | collective-permute-done | bytes 196640 | tf_op jit(solution)/shard_map/ppermute | solution.py:81
  600.4 11.3 %collective-permute-done.56 = bf16[256,1536]{1,0:T(8,128)(2,1)} collective-permute-done((bf16[256,1536]{1,0:T(8,128)(2,1)S(1)}, bf16[256,1536]{1,0:T(8,128)(2,1)}, u32[]{:S(2)}, u32[]{:S(2)}) %collective-permute-start.56) | collective-permute-done | bytes 786464 | tf_op jit(solution)/shard_map/ppermute | solution.py:81
  (407 shorter events, 252.6 us)
Async XLA Ops:
  7.2 203.3 %all-gather.2.cloned.1.call-start = ((), (), s32[]{:S(2)}) async-start(), calls=%async_computation | async-start | bytes 9437184 | tf_op jit(solution)/shard_map/all_gather | solution.py:694
  33.8 62.3 %collective-permute-start.7 = (bf16[256,3584]{1,0:T(8,128)(2,1)}, bf16[256,3584]{1,0:T(8,128)(2,1)}, u32[]{:S(2)}, u32[]{:S(2)}) collective-permute-start(bf16[256,3584]{1,0:T(8,128)(2,1)} %fusion.16), channel_id=1, source_target_pairs={{0,16},{16,0},{1,17},{17,1},{2,18},{18,2},{3,19},{19,3},{4,20},{20... | collective-permute-start | bytes 5505032 | tf_op jit(solution)/shard_map/ppermute | solution.py:81
  46.5 38.2 %collective-permute-start.3 = (bf16[256,1024]{1,0:T(8,128)(2,1)S(1)}, bf16[256,1024]{1,0:T(8,128)(2,1)S(1)}, u32[]{:S(2)}, u32[]{:S(2)}) collective-permute-start(bf16[256,1024]{1,0:T(8,128)(2,1)S(1)} %get-tuple-element.126), channel_id=1, source_target_pairs={{0,10},{2,8},{4,14},{6,12},{8,2},{10,0},{12,6},{14,4},{1,11},{3,9}... | collective-permute-start | bytes 1572872 | tf_op jit(solution)/shard_map/ppermute | solution.py:91
  50.1 34.6 %collective-permute-start.4 = (bf16[256,1024]{1,0:T(8,128)(2,1)S(1)}, bf16[256,1024]{1,0:T(8,128)(2,1)S(1)}, u32[]{:S(2)}, u32[]{:S(2)}) collective-permute-start(bf16[256,1024]{1,0:T(8,128)(2,1)S(1)} %get-tuple-element.127), channel_id=1, source_target_pairs={{0,14},{2,12},{4,10},{6,8},{8,6},{10,4},{12,2},{14,0},{1,15},{3,13... | collective-permute-start | bytes 1572872 | tf_op jit(solution)/shard_map/ppermute | solution.py:91
  51.4 44.6 %collective-permute-start.5 = (bf16[256,1024]{1,0:T(8,128)(2,1)S(1)}, bf16[256,1024]{1,0:T(8,128)(2,1)S(1)}, u32[]{:S(2)}, u32[]{:S(2)}) collective-permute-start(bf16[256,1024]{1,0:T(8,128)(2,1)S(1)} %get-tuple-element.128), channel_id=1, source_target_pairs={{0,2},{2,0},{4,6},{6,4},{8,10},{10,8},{12,14},{14,12},{1,3},{3,1},... | collective-permute-start | bytes 1572872 | tf_op jit(solution)/shard_map/ppermute | solution.py:91
  52.9 43.2 %collective-permute-start.6 = (bf16[256,1024]{1,0:T(8,128)(2,1)S(1)}, bf16[256,1024]{1,0:T(8,128)(2,1)S(1)}, u32[]{:S(2)}, u32[]{:S(2)}) collective-permute-start(bf16[256,1024]{1,0:T(8,128)(2,1)S(1)} %get-tuple-element.129), channel_id=1, source_target_pairs={{0,6},{2,4},{4,2},{6,0},{8,14},{10,12},{12,10},{14,8},{1,7},{3,5},... | collective-permute-start | bytes 1572872 | tf_op jit(solution)/shard_map/ppermute | solution.py:91
  96.1 40.8 %collective-permute-start.11 = (bf16[256,3584]{1,0:T(8,128)(2,1)}, bf16[256,3584]{1,0:T(8,128)(2,1)}, u32[]{:S(2)}, u32[]{:S(2)}) collective-permute-start(bf16[256,3584]{1,0:T(8,128)(2,1)} %collective-permute-done.7), channel_id=1, source_target_pairs={{0,2},{2,0},{4,6},{6,4},{8,10},{10,8},{12,14},{14,12},{1,3},{3,1},... | collective-permute-start | bytes 5505032 | tf_op jit(solution)/shard_map/ppermute | solution.py:81
  97.7 95.4 %collective-permute-start.10 = (bf16[256,1024]{1,0:T(8,128)(2,1)}, bf16[256,1024]{1,0:T(8,128)(2,1)S(1)}, u32[]{:S(2)}, u32[]{:S(2)}) collective-permute-start(bf16[256,1024]{1,0:T(8,128)(2,1)} %copy-done.61), channel_id=1, source_target_pairs={{0,4},{2,6},{4,0},{6,2},{8,12},{10,14},{12,8},{14,10},{1,5},{3,7},... | collective-permute-start | bytes 1572872 | tf_op jit(solution)/shard_map/ppermute | solution.py:91
  98.2 94.9 %collective-permute-start.8 = (bf16[256,1024]{1,0:T(8,128)(2,1)}, bf16[256,1024]{1,0:T(8,128)(2,1)S(1)}, u32[]{:S(2)}, u32[]{:S(2)}) collective-permute-start(bf16[256,1024]{1,0:T(8,128)(2,1)} %copy-done.60), channel_id=1, source_target_pairs={{0,8},{2,10},{4,12},{6,14},{8,0},{10,2},{12,4},{14,6},{1,9},{3,11}... | collective-permute-start | bytes 1572872 | tf_op jit(solution)/shard_map/ppermute | solution.py:91
  101.8 91.3 %collective-permute-start.9 = (bf16[256,1024]{1,0:T(8,128)(2,1)S(1)}, bf16[256,1024]{1,0:T(8,128)(2,1)S(1)}, u32[]{:S(2)}, u32[]{:S(2)}) collective-permute-start(bf16[256,1024]{1,0:T(8,128)(2,1)S(1)} %copy-done.59), channel_id=1, source_target_pairs={{0,12},{2,14},{4,8},{6,10},{8,4},{10,6},{12,0},{14,2},{1,13},{3,15... | collective-permute-start | bytes 1572872 | tf_op jit(solution)/shard_map/ppermute | solution.py:91
  238.3 67.7 %collective-permute-start.20 = (bf16[512,2304]{1,0:T(8,128)(2,1)}, bf16[512,2304]{1,0:T(8,128)(2,1)}, u32[]{:S(2)}, u32[]{:S(2)}) collective-permute-start(bf16[512,2304]{1,0:T(8,128)(2,1)} %shard_map.250), channel_id=1, source_target_pairs={{0,2},{2,0},{4,6},{6,4},{8,10},{10,8},{12,14},{14,12},{1,3},{3,1},... | collective-permute-start | bytes 7077896 | tf_op jit(solution)/shard_map/ppermute | solution.py:81
  240.0 69.9 %collective-permute-start.18 = (bf16[512,2304]{1,0:T(8,128)(2,1)}, bf16[512,2304]{1,0:T(8,128)(2,1)}, u32[]{:S(2)}, u32[]{:S(2)}) collective-permute-start(bf16[512,2304]{1,0:T(8,128)(2,1)} %shard_map.249), channel_id=1, source_target_pairs={{0,16},{16,0},{1,17},{17,1},{2,18},{18,2},{3,19},{19,3},{4,20},{20... | collective-permute-start | bytes 7077896 | tf_op jit(solution)/shard_map/ppermute | solution.py:81
  269.8 31.1 %collective-permute-start.15 = (bf16[2,256,512]{2,1,0:T(8,128)(2,1)}, bf16[2,256,512]{2,1,0:T(8,128)(2,1)}, u32[]{:S(2)}, u32[]{:S(2)}) collective-permute-start(bf16[2,256,512]{2,1,0:T(8,128)(2,1)} %get-tuple-element.157), channel_id=1, source_target_pairs={{0,8},{2,10},{4,12},{6,14},{8,0},{10,2},{12,4},{14,6},{1,9},{3,11}... | collective-permute-start | bytes 1572872 | tf_op jit(solution)/shard_map/ppermute | solution.py:91
  339.6 35.4 %collective-permute-start.22 = (bf16[2,256,512]{2,1,0:T(8,128)(2,1)S(1)}, bf16[2,256,512]{2,1,0:T(8,128)(2,1)S(1)}, u32[]{:S(2)}, u32[]{:S(2)}) collective-permute-start(bf16[2,256,512]{2,1,0:T(8,128)(2,1)S(1)} %copy-done.57), channel_id=1, source_target_pairs={{0,10},{2,8},{4,14},{6,12},{8,2},{10,0},{12,6},{14,4},{1,11},{3,9}... | collective-permute-start | bytes 1572872 | tf_op jit(solution)/shard_map/ppermute | solution.py:91
  340.1 34.8 %collective-permute-start.23 = (bf16[2,256,512]{2,1,0:T(8,128)(2,1)S(1)}, bf16[2,256,512]{2,1,0:T(8,128)(2,1)S(1)}, u32[]{:S(2)}, u32[]{:S(2)}) collective-permute-start(bf16[2,256,512]{2,1,0:T(8,128)(2,1)S(1)} %copy-done.55), channel_id=1, source_target_pairs={{0,14},{2,12},{4,10},{6,8},{8,6},{10,4},{12,2},{14,0},{1,15},{3,13... | collective-permute-start | bytes 1572872 | tf_op jit(solution)/shard_map/ppermute | solution.py:91
  342.3 45.1 %collective-permute-start.24 = (bf16[2,256,512]{2,1,0:T(8,128)(2,1)S(1)}, bf16[2,256,512]{2,1,0:T(8,128)(2,1)S(1)}, u32[]{:S(2)}, u32[]{:S(2)}) collective-permute-start(bf16[2,256,512]{2,1,0:T(8,128)(2,1)S(1)} %copy-done.53), channel_id=1, source_target_pairs={{0,2},{2,0},{4,6},{6,4},{8,10},{10,8},{12,14},{14,12},{1,3},{3,1},... | collective-permute-start | bytes 1572872 | tf_op jit(solution)/shard_map/ppermute | solution.py:91
  344.1 43.4 %collective-permute-start.25 = (bf16[2,256,512]{2,1,0:T(8,128)(2,1)S(1)}, bf16[2,256,512]{2,1,0:T(8,128)(2,1)S(1)}, u32[]{:S(2)}, u32[]{:S(2)}) collective-permute-start(bf16[2,256,512]{2,1,0:T(8,128)(2,1)S(1)} %copy-done.51), channel_id=1, source_target_pairs={{0,6},{2,4},{4,2},{6,0},{8,14},{10,12},{12,10},{14,8},{1,7},{3,5},... | collective-permute-start | bytes 1572872 | tf_op jit(solution)/shard_map/ppermute | solution.py:91
  345.4 58.2 %collective-permute-start.29 = (bf16[512,2048]{1,0:T(8,128)(2,1)}, bf16[512,2048]{1,0:T(8,128)(2,1)}, u32[]{:S(2)}, u32[]{:S(2)}) collective-permute-start(bf16[512,2048]{1,0:T(8,128)(2,1)} %shard_map.258), channel_id=1, source_target_pairs={{0,16},{16,0},{1,17},{17,1},{2,18},{18,2},{3,19},{19,3},{4,20},{20... | collective-permute-start | bytes 6291464 | tf_op jit(solution)/shard_map/ppermute | solution.py:81
  388.9 42.8 %collective-permute-start.27 = (bf16[64,4608]{1,0:T(8,128)(2,1)}, bf16[64,4608]{1,0:T(8,128)(2,1)}, u32[]{:S(2)}, u32[]{:S(2)}) collective-permute-start(bf16[64,4608]{1,0:T(8,128)(2,1)} %get-tuple-element.273), channel_id=1, source_target_pairs={{0,8},{2,10},{4,12},{6,14},{8,0},{10,2},{12,4},{14,6},{1,9},{3,11}... | collective-permute-start | bytes 1769480 | tf_op jit(solution)/shard_map/ppermute | solution.py:81
  391.6 40.0 %collective-permute-start.28 = (bf16[64,4608]{1,0:T(8,128)(2,1)}, bf16[64,4608]{1,0:T(8,128)(2,1)}, u32[]{:S(2)}, u32[]{:S(2)}) collective-permute-start(bf16[64,4608]{1,0:T(8,128)(2,1)} %get-tuple-element.272), channel_id=1, source_target_pairs={{0,12},{2,14},{4,8},{6,10},{8,4},{10,6},{12,0},{14,2},{1,13},{3,15... | collective-permute-start | bytes 1769480 | tf_op jit(solution)/shard_map/ppermute | solution.py:81
  398.3 100.7 %collective-permute-start.14 = (bf16[512,1024]{1,0:T(8,128)(2,1)S(1)}, bf16[512,1024]{1,0:T(8,128)(2,1)}, u32[]{:S(2)}, u32[]{:S(2)}) collective-permute-start(bf16[512,1024]{1,0:T(8,128)(2,1)S(1)} %shard_map.252), channel_id=1, source_target_pairs={{0,1},{1,0},{2,3},{3,2},{4,5},{5,4},{6,7},{7,6},{8,9},{9,8},{10,11... | collective-permute-start | bytes 3145736 | tf_op jit(solution)/shard_map/ppermute | solution.py:75
  455.7 42.4 %collective-permute-start.32 = (bf16[512,1024]{1,0:T(8,128)(2,1)S(1)}, bf16[512,1024]{1,0:T(8,128)(2,1)S(1)}, u32[]{:S(2)}, u32[]{:S(2)}) collective-permute-start(bf16[512,1024]{1,0:T(8,128)(2,1)S(1)} %add_convert_fusion.5), channel_id=1, source_target_pairs={{0,1},{1,0},{2,3},{3,2},{4,5},{5,4},{6,7},{7,6},{8,9},{9,8},{10,11... | collective-permute-start | bytes 3145736 | tf_op jit(solution)/shard_map/ppermute | solution.py:75
  509.0 32.2 %collective-permute-start.42 = (bf16[64,3072]{1,0:T(8,128)(2,1)S(1)}, bf16[64,3072]{1,0:T(8,128)(2,1)S(1)}, u32[]{:S(2)}, u32[]{:S(2)}) collective-permute-start(bf16[64,3072]{1,0:T(8,128)(2,1)S(1)} %get-tuple-element.276), channel_id=1, source_target_pairs={{0,4},{2,6},{4,0},{6,2},{8,12},{10,14},{12,8},{14,10},{1,5},{3,7},... | collective-permute-start | bytes 1179656 | tf_op jit(solution)/shard_map/ppermute | solution.py:81
  509.1 32.1 %collective-permute-start.43 = (bf16[64,3072]{1,0:T(8,128)(2,1)S(1)}, bf16[64,3072]{1,0:T(8,128)(2,1)S(1)}, u32[]{:S(2)}, u32[]{:S(2)}) collective-permute-start(bf16[64,3072]{1,0:T(8,128)(2,1)S(1)} %get-tuple-element.278), channel_id=1, source_target_pairs={{0,8},{2,10},{4,12},{6,14},{8,0},{10,2},{12,4},{14,6},{1,9},{3,11}... | collective-permute-start | bytes 1179656 | tf_op jit(solution)/shard_map/ppermute | solution.py:81
  (128 other events, 2187.1 us)
Sparse Core Ops, SparseCore 0:
  97.7 79.6 all-gather.1

commit v9 on v8

--- a/solution.py
+++ b/solution.py
@@ -111,7 +111,7 @@
     place = place_in(masks)
     kept = rows_at(addends, place, rows)
     for turn in range(1, size):
-        sent = total(rows_at(addends, place ^ turn, rows))
+        sent = picked_sum(addends, place ^ turn, rows)
         kept = kept + [swap(sent, "ctx", turn * masks[0])]
     return kept
 
@@ -132,6 +132,30 @@
         blocks = [join(list(pair), 0, (place >> bit) % 2) for pair in pairs]
         bit += 1
     return blocks[0]
+
+
+def picked_sum_kernel(which_ref, *refs):
+    refs[-1][...] = sum(ref[...].astype(F32) for ref in refs[:-1]).astype(BF16)
+
+
+def picked_sum(addends, block, rows):
+    if rows % 16 != 0:
+        return total(rows_at(addends, block, rows))
+    width = addends[0].shape[1]
+    step = width // 4 if width % 512 == 0 else width // 2
+    picked = pl.BlockSpec((rows, step), lambda i, w: (w[0], i))
+    return pl.pallas_call(
+        picked_sum_kernel,
+        grid_spec=pltpu.PrefetchScalarGridSpec(
+            num_scalar_prefetch=1,
+            grid=(width // step,),
+            in_specs=[picked] * len(addends),
+            out_specs=pl.BlockSpec((rows, step), lambda i, w: (0, i)),
+        ),
+        out_shape=jax.ShapeDtypeStruct((rows, width), BF16),
+        compiler_params=pltpu.CompilerParams(vmem_limit_bytes=VMEM_LIMIT),
+        cost_estimate=CHEAP,
+    )(jnp.reshape(block, (1,)).astype(jnp.int32), *addends)
 
 
 def product_kernel(count, *refs):
@@ -639,7 +663,7 @@
     k_pieces = pieces_of(key_weight, "shard")
     v_pieces = pieces_of(value_weight, "shard")
     packed_pieces = pieces_of(packed, "shard")
-    own_rest = jnp.concatenate([w_query, w_out.T, w_down.T], axis=1)
+    (own_rest,) = tie(jnp.concatenate([w_query, w_out.T, w_down.T], axis=1))
     own_gate_up = jnp.concatenate([w_gate, w_up], axis=1)
 
     turns = jnp.arange(count, dtype=jnp.int32)
@@ -677,8 +701,8 @@
     half_rest = own_rest
     if shard_count == 2:
         half_rest = lax.dynamic_slice_in_dim(own_rest, bit * (depth // 2), depth // 2, 0)
-    half_rest, own_gate_up, packed_pieces[-1], k_pieces[-1], v_pieces[-1] = tie(
-        half_rest, own_gate_up, packed_pieces[-1], k_pieces[-1], v_pieces[-1]
+    half_rest, own_rest, own_gate_up, packed_pieces[-1], k_pieces[-1], v_pieces[-1] = tie(
+        half_rest, own_rest, own_gate_up, packed_pieces[-1], k_pieces[-1], v_pieces[-1]
     )
     cosine, sine, meta, factor_one, k_pieces[-1] = tie(
         cosine, sine, meta, factor_one, k_pieces[-1]
@@ -775,14 +799,15 @@
     if shard_count == 2:
         first, second = straight[-1], straight[0]
         normed_late, returned[first] = tie(normed_two, returned[first])
-        units_a = [split_product(home, pairs_a(normed_late)), got_a]
-        units_a = halve(units_a, near_axis)
-        normed_late, upstream_late, returned[second] = tie(
-            normed_two, cotangent, returned[second]
+        kept_a = split_product(home, pairs_a(normed_late))
+        normed_late, upstream_late, kept_a, returned[second] = tie(
+            normed_two, cotangent, kept_a, returned[second]
         )
         kept_b = split_product((bit, 2 + bit), pairs_b(normed_late, upstream_late))
+        units_a = halve([kept_a, got_a], near_axis)
+        d_queries, kept_b = tie(d_queries, kept_b)
         units_b = [kept_b, got_b]
-        units_b_away = total(rows_at(units_b, 1 - shard, depth // 2))
+        units_b_away = picked_sum(units_b, 1 - shard, depth // 2)
         units_b = rows_at(units_b, shard, depth // 2) + [swap(units_b_away, "shard")]
     else:
         units_a = halve(scattered(pairs_a(normed_two)), near_axis)

time: 631 us -> 615 us (0.975)
  other arithmetic: 102 us -> 50 us
  waiting for transfers between devices: 266 us -> 296 us
  starting transfers between devices: 94.6 us -> 79.3 us
  Pallas kernels: 90.7 us -> 104 us
  local copies, waits for them, and re-layouts: 31.7 us -> 39 us
    select_n x18, other arithmetic: 56.6 us -> 13.8 us  [join(): jnp.where(index == 0, jnp.concatenate(pieces, dim), jnp.concatenate(piece...]
    ppermute x37, waiting for transfers between devices: 157 us -> 187 us  [swap(): return lax.ppermute(value, axis, [(i, i ^ level) for i in range(count)])]
    ppermute x37, starting transfers between devices: 66.7 us -> 51.8 us  [swap(): return lax.ppermute(value, axis, [(i, i ^ level) for i in range(count)])]
    pallas_call x0 -> x10, Pallas kernels: none -> 12.6 us  [picked_sum(): pl.pallas_call(picked_sum_kernel, grid_spec=pltpu.PrefetchScalarGridSpec(...]
    convert_element_type x10 -> x6, other arithmetic: 15.7 us -> 8.07 us  [total(): return sum((a.astype(F32) for a in addends)).astype(BF16)]
  transfers between devices with their start and end apart: 59 -> 59, of which waited for: 24 -> 24; matrix products, arithmetic and copies ran while one was open for 20% -> 11% of each run, Pallas kernels for 12% -> 15%
where the time goes in v9:
time: 615 us; the launch traced here: 606 us
  waiting for transfers between devices  296 us (48%)
  Pallas kernels  104 us (17%)
  starting transfers between devices  79.3 us (13%)
  other arithmetic  50 us (8%)
  local copies, waits for them, and re-layouts  39 us (6%)
  matrix products  21.1 us (3%)
  between operations  15.8 us (3%)
    ppermute x37, waiting for transfers between devices, swap(): return lax.ppermute(value, axis, [(i, i ^ level) for i in range(count)])  187 us
    ppermute x14, waiting for transfers between devices, exchange(): done[d] = lax.ppermute(values[d], 'ctx', [(i, i ^ d) for i in range(count)])  99.8 us
    ppermute x37, starting transfers between devices, swap(): return lax.ppermute(value, axis, [(i, i ^ level) for i in range(count)])  51.8 us
    pallas_call x8, Pallas kernels, split_product(): pl.pallas_call(functools.partial(split_product_kernel, spans), grid_spec=...  32.1 us
    unnamed x186, local copies, waits for them, and re-layouts  26.3 us
    ppermute x14, starting transfers between devices, exchange(): done[d] = lax.ppermute(values[d], 'ctx', [(i, i ^ d) for i in range(count)])  22 us
    pallas_call x1, Pallas kernels, attend_back(): pl.pallas_call(functools.partial(backward_kernel, docs, count), grid_spec...  20 us
    dot_general x4, matrix products, dot(): return jnp.dot(a, b, preferred_element_type=F32)  14.1 us
  transfers between devices with their start and end apart: 59, of which 24 were waited for; matrix products, arithmetic and copies ran while one was open for 11% of the time, Pallas kernels for 15%

profile of v9, /device:TPU:0, one launch (start us, length us, event | category | flops | bytes accessed | tf_op | source)
XLA Modules:
  0.0 605.6 jit_solution(8743466057636099850)
XLA Ops:
  30.3 7.6 %collective-permute-done.2.refs_3_ = bf16[512,512]{1,0:T(8,128)(2,1)} collective-permute-done((bf16[512,512]{1,0:T(8,128)(2,1)}, bf16[512,512]{1,0:T(8,128)(2,1)}, u32[]{:S(2)}, u32[]{:S(2)}) %collective-permute-start.2) | collective-permute-done | bytes 524320 | tf_op jit(solution)/shard_map/ppermute | solution.py:48
  40.5 8.0 %shard_map.246 = (f32[512,512]{1,0:T(8,128)}, bf16[512,1024]{1,0:T(8,128)(2,1)}, bf16[512,1024]{1,0:T(8,128)(2,1)}, bf16[256,1024]{1,0:T(8,128)(2,1)}, bf16[256,...) custom-call(s32[20]{0:T(128)S(1)} %concatenate.244.meta_ref, ...), custom_call_target="tpu_custom_call" | custom-call | flops 1000 | bytes 1000 | tf_op jit(solution)/shard_map/pallas_call | solution.py:308
  57.7 31.4 %collective-permute-done.3.refs_8_.refs_9_ = bf16[256,1024]{1,0:T(8,128)(2,1)S(1)} collective-permute-done((bf16[256,1024]{1,0:T(8,128)(2,1)}, bf16[256,1024]{1,0:T(8,128)(2,1)S(1)}, u32[]{:S(2)}, u32[]{:S(2)}) %collective-permute-start.3) | collective-permute-done | bytes 524320 | tf_op jit(solution)/shard_map/ppermute | solution.py:91
  89.1 11.5 %collective-permute-done.5.refs_0_.refs_1_ = bf16[256,1024]{1,0:T(8,128)(2,1)S(1)} collective-permute-done((bf16[256,1024]{1,0:T(8,128)(2,1)}, bf16[256,1024]{1,0:T(8,128)(2,1)S(1)}, u32[]{:S(2)}, u32[]{:S(2)}) %collective-permute-start.5) | collective-permute-done | bytes 524320 | tf_op jit(solution)/shard_map/ppermute | solution.py:91
  106.1 35.3 %collective-permute-done.11 = bf16[256,3584]{1,0:T(8,128)(2,1)} collective-permute-done((bf16[256,3584]{1,0:T(8,128)(2,1)}, bf16[256,3584]{1,0:T(8,128)(2,1)}, u32[]{:S(2)}, u32[]{:S(2)}) %collective-permute-start.11) | collective-permute-done | bytes 1835040 | tf_op jit(solution)/shard_map/ppermute | solution.py:81
  156.3 10.5 %shard_map.248 = (f32[512,1024]{1,0:T(8,128)}, bf16[512,1024]{1,0:T(8,128)(2,1)S(1)}, f32[512,1024]{1,0:T(8,128)}) custom-call(s32[20]{0:T(128)S(1)} %concatenate.244.meta_ref, bf16[512,1024]{1,0:T(8,128)(2,1)S(1)} %shard_map.247.q_ref, bf16[512,1024]{1,0:T(8,128)(2,1)} %get-tuple-element.145.k_ref.v_ref, bf16[512,1024]{1,0:T(8,128)(2,1)} %get-tuple-element.145.k_ref.v_ref, ...), custom_call_target="tpu_custom_call" | custom-call | flops 1000 | bytes 1000 | tf_op jit(solution)/shard_map/pallas_call | solution.py:572
  173.1 5.8 fusion.47
  193.8 5.9 shard_map.251
  208.9 20.0 %shard_map.253 = (f32[512,1024]{1,0:T(8,128)}, f32[2,512,512]{2,1,0:T(8,128)}, bf16[2,256,512]{2,1,0:T(8,128)(2,1)S(1)}, bf16[2,256,512]{2,1,0:T(8,128)(2,1)}, b...) custom-call(s32[20]{0:T(128)S(1)} %concatenate.244.meta_ref, ...), custom_call_target="tpu_custom_call" | custom-call | flops 1000 | bytes 1000 | tf_op jit(solution)/shard_map/pallas_call | solution.py:601
  236.3 20.8 %collective-permute-done.15.refs_1_ = bf16[2,256,512]{2,1,0:T(8,128)(2,1)S(1)} collective-permute-done((bf16[2,256,512]{2,1,0:T(8,128)(2,1)}, bf16[2,256,512]{2,1,0:T(8,128)(2,1)S(1)}, u32[]{:S(2)}, u32[]{:S(2)}) %collective-permute-start.15) | collective-permute-done | bytes 524320 | tf_op jit(solution)/shard_map/ppermute | solution.py:91
  313.7 23.6 %collective-permute-done.22.refs_4_ = bf16[2,256,512]{2,1,0:T(8,128)(2,1)S(1)} collective-permute-done((bf16[2,256,512]{2,1,0:T(8,128)(2,1)S(1)}, bf16[2,256,512]{2,1,0:T(8,128)(2,1)S(1)}, u32[]{:S(2)}, u32[]{:S(2)}) %collective-permute-start.22) | collective-permute-done | bytes 524320 | tf_op jit(solution)/shard_map/ppermute | solution.py:91
  337.4 12.5 %collective-permute-done.24.refs_0_ = bf16[2,256,512]{2,1,0:T(8,128)(2,1)S(1)} collective-permute-done((bf16[2,256,512]{2,1,0:T(8,128)(2,1)S(1)}, bf16[2,256,512]{2,1,0:T(8,128)(2,1)S(1)}, u32[]{:S(2)}, u32[]{:S(2)}) %collective-permute-start.24) | collective-permute-done | bytes 524320 | tf_op jit(solution)/shard_map/ppermute | solution.py:91
  376.1 27.5 %collective-permute-done.27 = bf16[64,4608]{1,0:T(8,128)(2,1)} collective-permute-done((bf16[64,4608]{1,0:T(8,128)(2,1)}, bf16[64,4608]{1,0:T(8,128)(2,1)}, u32[]{:S(2)}, u32[]{:S(2)}) %collective-permute-start.27) | collective-permute-done | bytes 589856 | tf_op jit(solution)/shard_map/ppermute | solution.py:81
  409.3 7.9 %collective-permute-start.34 = (bf16[64,2304]{1,0:T(8,128)(2,1)S(1)}, bf16[64,2304]{1,0:T(8,128)(2,1)S(1)}, u32[]{:S(2)}, u32[]{:S(2)}) collective-permute-start(bf16[64,2304]{1,0:T(8,128)(2,1)S(1)} %get-tuple-element.208), channel_id=1, source_target_pairs={{0,8},{2,10},{4,12},{6,14},{8,0},{10,2},{12,4},{14,6},{1,9},{3,11}... | collective-permute-start | bytes 884744 | tf_op jit(solution)/shard_map/ppermute | solution.py:81
  429.3 7.3 %collective-permute-done.34 = bf16[64,2304]{1,0:T(8,128)(2,1)S(1)} collective-permute-done((bf16[64,2304]{1,0:T(8,128)(2,1)S(1)}, bf16[64,2304]{1,0:T(8,128)(2,1)S(1)}, u32[]{:S(2)}, u32[]{:S(2)}) %collective-permute-start.34) | collective-permute-done | bytes 294944 | tf_op jit(solution)/shard_map/ppermute | solution.py:81
  445.6 12.0 %collective-permute-done.37 = bf16[64,2304]{1,0:T(8,128)(2,1)S(1)} collective-permute-done((bf16[64,2304]{1,0:T(8,128)(2,1)S(1)}, bf16[64,2304]{1,0:T(8,128)(2,1)S(1)}, u32[]{:S(2)}, u32[]{:S(2)}) %collective-permute-start.37) | collective-permute-done | bytes 294944 | tf_op jit(solution)/shard_map/ppermute | solution.py:81
  459.4 6.1 %collective-permute-done.38 = bf16[64,2304]{1,0:T(8,128)(2,1)S(1)} collective-permute-done((bf16[64,2304]{1,0:T(8,128)(2,1)S(1)}, bf16[64,2304]{1,0:T(8,128)(2,1)S(1)}, u32[]{:S(2)}, u32[]{:S(2)}) %collective-permute-start.38) | collective-permute-done | bytes 294944 | tf_op jit(solution)/shard_map/ppermute | solution.py:81
  466.9 16.5 %collective-permute-done.40 = bf16[256,2304]{1,0:T(8,128)(2,1)S(1)} collective-permute-done((bf16[256,2304]{1,0:T(8,128)(2,1)S(1)}, bf16[256,2304]{1,0:T(8,128)(2,1)S(1)}, u32[]{:S(2)}, u32[]{:S(2)}) %collective-permute-start.40) | collective-permute-done | bytes 1179680 | tf_op jit(solution)/shard_map/ppermute | solution.py:81
  497.7 19.7 %collective-permute-done.46 = f32[18,128]{1,0:T(8,128)S(1)} collective-permute-done((f32[18,128]{1,0:T(8,128)S(1)}, f32[18,128]{1,0:T(8,128)S(1)}, u32[]{:S(2)}, u32[]{:S(2)}) %collective-permute-start.46) | collective-permute-done | bytes 9248 | tf_op jit(solution)/shard_map/ppermute | solution.py:81
  517.4 11.4 %collective-permute-done.43 = bf16[64,3072]{1,0:T(8,128)(2,1)S(1)} collective-permute-done((bf16[64,3072]{1,0:T(8,128)(2,1)S(1)}, bf16[64,3072]{1,0:T(8,128)(2,1)S(1)}, u32[]{:S(2)}, u32[]{:S(2)}) %collective-permute-start.43) | collective-permute-done | bytes 393248 | tf_op jit(solution)/shard_map/ppermute | solution.py:81
  534.9 8.7 %collective-permute-done.50 = f32[18,128]{1,0:T(8,128)S(1)} collective-permute-done((f32[18,128]{1,0:T(8,128)S(1)}, f32[18,128]{1,0:T(8,128)S(1)}, u32[]{:S(2)}, u32[]{:S(2)}) %collective-permute-start.50) | collective-permute-done | bytes 9248 | tf_op jit(solution)/shard_map/ppermute | solution.py:81
  558.9 6.6 %collective-permute-done.54 = bf16[64,1536]{1,0:T(8,128)(2,1)S(1)} collective-permute-done((bf16[64,1536]{1,0:T(8,128)(2,1)S(1)}, bf16[64,1536]{1,0:T(8,128)(2,1)S(1)}, u32[]{:S(2)}, u32[]{:S(2)}) %collective-permute-start.54) | collective-permute-done | bytes 196640 | tf_op jit(solution)/shard_map/ppermute | solution.py:81
  565.5 8.4 %collective-permute-done.53 = bf16[64,1536]{1,0:T(8,128)(2,1)S(1)} collective-permute-done((bf16[64,1536]{1,0:T(8,128)(2,1)S(1)}, bf16[64,1536]{1,0:T(8,128)(2,1)S(1)}, u32[]{:S(2)}, u32[]{:S(2)}) %collective-permute-start.53) | collective-permute-done | bytes 196640 | tf_op jit(solution)/shard_map/ppermute | solution.py:81
  583.5 10.6 %collective-permute-done.56 = bf16[256,1536]{1,0:T(8,128)(2,1)} collective-permute-done((bf16[256,1536]{1,0:T(8,128)(2,1)S(1)}, bf16[256,1536]{1,0:T(8,128)(2,1)}, u32[]{:S(2)}, u32[]{:S(2)}) %collective-permute-start.56) | collective-permute-done | bytes 786464 | tf_op jit(solution)/shard_map/ppermute | solution.py:81
  (412 shorter events, 254.0 us)
Async XLA Ops:
  7.2 165.9 %all-gather.2.cloned.1.call-start = ((), (), s32[]{:S(2)}) async-start(), calls=%async_computation | async-start | bytes 9437184 | tf_op jit(solution)/shard_map/all_gather | solution.py:718
  37.9 62.6 %collective-permute-start.7 = (bf16[256,3584]{1,0:T(8,128)(2,1)}, bf16[256,3584]{1,0:T(8,128)(2,1)}, u32[]{:S(2)}, u32[]{:S(2)}) collective-permute-start(bf16[256,3584]{1,0:T(8,128)(2,1)} %constant_dynamic-slice_fusion), channel_id=1, source_target_pairs={{0,16},{16,0},{1,17},{17,1},{2,18},{18,2},{3,19},{19,3},{4,20},{20... | collective-permute-start | bytes 5505032 | tf_op jit(solution)/shard_map/ppermute | solution.py:81
  50.9 38.2 %collective-permute-start.3 = (bf16[256,1024]{1,0:T(8,128)(2,1)}, bf16[256,1024]{1,0:T(8,128)(2,1)S(1)}, u32[]{:S(2)}, u32[]{:S(2)}) collective-permute-start(bf16[256,1024]{1,0:T(8,128)(2,1)} %get-tuple-element.130), channel_id=1, source_target_pairs={{0,10},{2,8},{4,14},{6,12},{8,2},{10,0},{12,6},{14,4},{1,11},{3,9}... | collective-permute-start | bytes 1572872 | tf_op jit(solution)/shard_map/ppermute | solution.py:91
  54.6 34.5 %collective-permute-start.4 = (bf16[256,1024]{1,0:T(8,128)(2,1)}, bf16[256,1024]{1,0:T(8,128)(2,1)S(1)}, u32[]{:S(2)}, u32[]{:S(2)}) collective-permute-start(bf16[256,1024]{1,0:T(8,128)(2,1)} %get-tuple-element.131), channel_id=1, source_target_pairs={{0,14},{2,12},{4,10},{6,8},{8,6},{10,4},{12,2},{14,0},{1,15},{3,13... | collective-permute-start | bytes 1572872 | tf_op jit(solution)/shard_map/ppermute | solution.py:91
  55.9 44.6 %collective-permute-start.5 = (bf16[256,1024]{1,0:T(8,128)(2,1)}, bf16[256,1024]{1,0:T(8,128)(2,1)S(1)}, u32[]{:S(2)}, u32[]{:S(2)}) collective-permute-start(bf16[256,1024]{1,0:T(8,128)(2,1)} %get-tuple-element.132), channel_id=1, source_target_pairs={{0,2},{2,0},{4,6},{6,4},{8,10},{10,8},{12,14},{14,12},{1,3},{3,1},... | collective-permute-start | bytes 1572872 | tf_op jit(solution)/shard_map/ppermute | solution.py:91
  57.4 43.2 %collective-permute-start.6 = (bf16[256,1024]{1,0:T(8,128)(2,1)}, bf16[256,1024]{1,0:T(8,128)(2,1)S(1)}, u32[]{:S(2)}, u32[]{:S(2)}) collective-permute-start(bf16[256,1024]{1,0:T(8,128)(2,1)} %get-tuple-element.133), channel_id=1, source_target_pairs={{0,6},{2,4},{4,2},{6,0},{8,14},{10,12},{12,10},{14,8},{1,7},{3,5},... | collective-permute-start | bytes 1572872 | tf_op jit(solution)/shard_map/ppermute | solution.py:91
  100.6 40.8 %collective-permute-start.11 = (bf16[256,3584]{1,0:T(8,128)(2,1)}, bf16[256,3584]{1,0:T(8,128)(2,1)}, u32[]{:S(2)}, u32[]{:S(2)}) collective-permute-start(bf16[256,3584]{1,0:T(8,128)(2,1)} %collective-permute-done.7), channel_id=1, source_target_pairs={{0,2},{2,0},{4,6},{6,4},{8,10},{10,8},{12,14},{14,12},{1,3},{3,1},... | collective-permute-start | bytes 5505032 | tf_op jit(solution)/shard_map/ppermute | solution.py:81
  102.1 54.2 %collective-permute-start.8 = (bf16[256,1024]{1,0:T(8,128)(2,1)}, bf16[256,1024]{1,0:T(8,128)(2,1)S(1)}, u32[]{:S(2)}, u32[]{:S(2)}) collective-permute-start(bf16[256,1024]{1,0:T(8,128)(2,1)} %copy-done.68), channel_id=1, source_target_pairs={{0,8},{2,10},{4,12},{6,14},{8,0},{10,2},{12,4},{14,6},{1,9},{3,11}... | collective-permute-start | bytes 1572872 | tf_op jit(solution)/shard_map/ppermute | solution.py:91
  103.4 52.8 %collective-permute-start.9 = (bf16[256,1024]{1,0:T(8,128)(2,1)}, bf16[256,1024]{1,0:T(8,128)(2,1)S(1)}, u32[]{:S(2)}, u32[]{:S(2)}) collective-permute-start(bf16[256,1024]{1,0:T(8,128)(2,1)} %copy-done.67), channel_id=1, source_target_pairs={{0,12},{2,14},{4,8},{6,10},{8,4},{10,6},{12,0},{14,2},{1,13},{3,15... | collective-permute-start | bytes 1572872 | tf_op jit(solution)/shard_map/ppermute | solution.py:91
  105.6 50.6 %collective-permute-start.10 = (bf16[256,1024]{1,0:T(8,128)(2,1)S(1)}, bf16[256,1024]{1,0:T(8,128)(2,1)S(1)}, u32[]{:S(2)}, u32[]{:S(2)}) collective-permute-start(bf16[256,1024]{1,0:T(8,128)(2,1)S(1)} %copy-done.66), channel_id=1, source_target_pairs={{0,4},{2,6},{4,0},{6,2},{8,12},{10,14},{12,8},{14,10},{1,5},{3,7},... | collective-permute-start | bytes 1572872 | tf_op jit(solution)/shard_map/ppermute | solution.py:91
  200.0 68.5 %collective-permute-start.18 = (bf16[512,2304]{1,0:T(8,128)(2,1)}, bf16[512,2304]{1,0:T(8,128)(2,1)}, u32[]{:S(2)}, u32[]{:S(2)}) collective-permute-start(bf16[512,2304]{1,0:T(8,128)(2,1)} %shard_map.249), channel_id=1, source_target_pairs={{0,16},{16,0},{1,17},{17,1},{2,18},{18,2},{3,19},{19,3},{4,20},{20... | collective-permute-start | bytes 7077896 | tf_op jit(solution)/shard_map/ppermute | solution.py:81
  201.5 70.9 %collective-permute-start.20 = (bf16[512,2304]{1,0:T(8,128)(2,1)}, bf16[512,2304]{1,0:T(8,128)(2,1)}, u32[]{:S(2)}, u32[]{:S(2)}) collective-permute-start(bf16[512,2304]{1,0:T(8,128)(2,1)} %shard_map.250), channel_id=1, source_target_pairs={{0,2},{2,0},{4,6},{6,4},{8,10},{10,8},{12,14},{14,12},{1,3},{3,1},... | collective-permute-start | bytes 7077896 | tf_op jit(solution)/shard_map/ppermute | solution.py:81
  302.0 35.4 %collective-permute-start.22 = (bf16[2,256,512]{2,1,0:T(8,128)(2,1)S(1)}, bf16[2,256,512]{2,1,0:T(8,128)(2,1)S(1)}, u32[]{:S(2)}, u32[]{:S(2)}) collective-permute-start(bf16[2,256,512]{2,1,0:T(8,128)(2,1)S(1)} %copy-done.64), channel_id=1, source_target_pairs={{0,10},{2,8},{4,14},{6,12},{8,2},{10,0},{12,6},{14,4},{1,11},{3,9}... | collective-permute-start | bytes 1572872 | tf_op jit(solution)/shard_map/ppermute | solution.py:91
  302.0 35.4 %collective-permute-start.23 = (bf16[2,256,512]{2,1,0:T(8,128)(2,1)S(1)}, bf16[2,256,512]{2,1,0:T(8,128)(2,1)S(1)}, u32[]{:S(2)}, u32[]{:S(2)}) collective-permute-start(bf16[2,256,512]{2,1,0:T(8,128)(2,1)S(1)} %copy-done.62), channel_id=1, source_target_pairs={{0,14},{2,12},{4,10},{6,8},{8,6},{10,4},{12,2},{14,0},{1,15},{3,13... | collective-permute-start | bytes 1572872 | tf_op jit(solution)/shard_map/ppermute | solution.py:91
  304.8 45.0 %collective-permute-start.24 = (bf16[2,256,512]{2,1,0:T(8,128)(2,1)S(1)}, bf16[2,256,512]{2,1,0:T(8,128)(2,1)S(1)}, u32[]{:S(2)}, u32[]{:S(2)}) collective-permute-start(bf16[2,256,512]{2,1,0:T(8,128)(2,1)S(1)} %copy-done.60), channel_id=1, source_target_pairs={{0,2},{2,0},{4,6},{6,4},{8,10},{10,8},{12,14},{14,12},{1,3},{3,1},... | collective-permute-start | bytes 1572872 | tf_op jit(solution)/shard_map/ppermute | solution.py:91
  305.1 44.8 %collective-permute-start.25 = (bf16[2,256,512]{2,1,0:T(8,128)(2,1)S(1)}, bf16[2,256,512]{2,1,0:T(8,128)(2,1)S(1)}, u32[]{:S(2)}, u32[]{:S(2)}) collective-permute-start(bf16[2,256,512]{2,1,0:T(8,128)(2,1)S(1)} %copy-done.58), channel_id=1, source_target_pairs={{0,6},{2,4},{4,2},{6,0},{8,14},{10,12},{12,10},{14,8},{1,7},{3,5},... | collective-permute-start | bytes 1572872 | tf_op jit(solution)/shard_map/ppermute | solution.py:91
  307.9 61.6 %collective-permute-start.29 = (bf16[512,2048]{1,0:T(8,128)(2,1)}, bf16[512,2048]{1,0:T(8,128)(2,1)}, u32[]{:S(2)}, u32[]{:S(2)}) collective-permute-start(bf16[512,2048]{1,0:T(8,128)(2,1)} %shard_map.260), channel_id=1, source_target_pairs={{0,16},{16,0},{1,17},{17,1},{2,18},{18,2},{3,19},{19,3},{4,20},{20... | collective-permute-start | bytes 6291464 | tf_op jit(solution)/shard_map/ppermute | solution.py:81
  354.4 49.2 %collective-permute-start.27 = (bf16[64,4608]{1,0:T(8,128)(2,1)}, bf16[64,4608]{1,0:T(8,128)(2,1)}, u32[]{:S(2)}, u32[]{:S(2)}) collective-permute-start(bf16[64,4608]{1,0:T(8,128)(2,1)} %shard_map.262), channel_id=1, source_target_pairs={{0,8},{2,10},{4,12},{6,14},{8,0},{10,2},{12,4},{14,6},{1,9},{3,11}... | collective-permute-start | bytes 1769480 | tf_op jit(solution)/shard_map/ppermute | solution.py:81
  355.9 47.7 %collective-permute-start.26 = (bf16[64,4608]{1,0:T(8,128)(2,1)}, bf16[64,4608]{1,0:T(8,128)(2,1)}, u32[]{:S(2)}, u32[]{:S(2)}) collective-permute-start(bf16[64,4608]{1,0:T(8,128)(2,1)} %shard_map.261), channel_id=1, source_target_pairs={{0,4},{2,6},{4,0},{6,2},{8,12},{10,14},{12,8},{14,10},{1,5},{3,7},... | collective-permute-start | bytes 1769480 | tf_op jit(solution)/shard_map/ppermute | solution.py:81
  363.8 120.3 %collective-permute-start.14 = (bf16[512,1024]{1,0:T(8,128)(2,1)S(1)}, bf16[512,1024]{1,0:T(8,128)(2,1)}, u32[]{:S(2)}, u32[]{:S(2)}) collective-permute-start(bf16[512,1024]{1,0:T(8,128)(2,1)S(1)} %shard_map.252), channel_id=1, source_target_pairs={{0,1},{1,0},{2,3},{3,2},{4,5},{5,4},{6,7},{7,6},{8,9},{9,8},{10,11... | collective-permute-start | bytes 3145736 | tf_op jit(solution)/shard_map/ppermute | solution.py:75
  371.8 35.9 %collective-permute-start.30 = (bf16[256,2048]{1,0:T(8,128)(2,1)S(1)}, bf16[256,2048]{1,0:T(8,128)(2,1)S(1)}, u32[]{:S(2)}, u32[]{:S(2)}) collective-permute-start(bf16[256,2048]{1,0:T(8,128)(2,1)S(1)} %shard_map.265), channel_id=1, source_target_pairs={{0,2},{2,0},{4,6},{6,4},{8,10},{10,8},{12,14},{14,12},{1,3},{3,1},... | collective-permute-start | bytes 3145736 | tf_op jit(solution)/shard_map/ppermute | solution.py:81
  423.2 42.7 %collective-permute-start.32 = (bf16[512,1024]{1,0:T(8,128)(2,1)S(1)}, bf16[512,1024]{1,0:T(8,128)(2,1)S(1)}, u32[]{:S(2)}, u32[]{:S(2)}) collective-permute-start(bf16[512,1024]{1,0:T(8,128)(2,1)S(1)} %add_convert_fusion.3), channel_id=1, source_target_pairs={{0,1},{1,0},{2,3},{3,2},{4,5},{5,4},{6,7},{7,6},{8,9},{9,8},{10,11... | collective-permute-start | bytes 3145736 | tf_op jit(solution)/shard_map/ppermute | solution.py:75
  489.2 39.9 %collective-permute-start.41 = (bf16[256,2304]{1,0:T(8,128)(2,1)S(1)}, bf16[256,2304]{1,0:T(8,128)(2,1)S(1)}, u32[]{:S(2)}, u32[]{:S(2)}) collective-permute-start(bf16[256,2304]{1,0:T(8,128)(2,1)S(1)} %maximum_select_fusion.7), channel_id=1, source_target_pairs={{0,2},{2,0},{4,6},{6,4},{8,10},{10,8},{12,14},{14,12},{1,3},{3,1},... | collective-permute-start | bytes 3538952 | tf_op jit(solution)/shard_map/ppermute | solution.py:81
  491.1 37.7 %collective-permute-start.43 = (bf16[64,3072]{1,0:T(8,128)(2,1)S(1)}, bf16[64,3072]{1,0:T(8,128)(2,1)S(1)}, u32[]{:S(2)}, u32[]{:S(2)}) collective-permute-start(bf16[64,3072]{1,0:T(8,128)(2,1)S(1)} %shard_map.270), channel_id=1, source_target_pairs={{0,8},{2,10},{4,12},{6,14},{8,0},{10,2},{12,4},{14,6},{1,9},{3,11}... | collective-permute-start | bytes 1179656 | tf_op jit(solution)/shard_map/ppermute | solution.py:81
  (128 other events, 1845.8 us)
Sparse Core Ops, SparseCore 0:
  57.8 88.5 all-gather.1

commit v10 on v9

--- a/solution.py
+++ b/solution.py
@@ -659,10 +659,8 @@
     crossing = [d for d in far + near if d % 2 == 1]
     straight = [d for d in far + near if d % 2 == 0]
 
-    packed = jnp.concatenate([gain_in, gain_post, gain_q, gain_k])
     k_pieces = pieces_of(key_weight, "shard")
     v_pieces = pieces_of(value_weight, "shard")
-    packed_pieces = pieces_of(packed, "shard")
     (own_rest,) = tie(jnp.concatenate([w_query, w_out.T, w_down.T], axis=1))
     own_gate_up = jnp.concatenate([w_gate, w_up], axis=1)
 
@@ -696,6 +694,9 @@
 
     inputs = tokens.astype(F32)
     normal_one, factor_one = rms_parts(inputs)
+    factor_one, gain_in = tie(factor_one, gain_in)
+    packed = jnp.concatenate([gain_in, gain_post, gain_q, gain_k])
+    packed_pieces = pieces_of(packed, "shard")
 
     bit = place_in(near_axis)
     half_rest = own_rest
@@ -780,9 +781,6 @@
     d_normed_two = pair_total(
         product_nt((d_gate, full_gate_up, 0), (d_up, full_gate_up, 1))
     )
-    hidden, d_normed_two = tie(hidden, d_normed_two)
-    mixed_part = product_nt((hidden, full_down_t, 0))
-    mixed = (residual + pair_total(mixed_part)).astype(BF16)
     grad_post = jnp.sum(d_normed_two * normal_two, axis=0)
     d_residual = cotangent.astype(F32) + rms_back(
         d_normed_two * scale_post, normal_two, factor_two
@@ -856,15 +854,15 @@
 
     units_a = double(units_a, far_axis)
     key_value_grad = halve(key_value_grad, near_axis)
-    units_a, units_b, key_value_grad[-1], out_query[-1] = tie(
-        units_a, units_b, key_value_grad[-1], out_query[-1]
+    d_normed = pair_total(
+        dot_nt(d_q_pre, full_query) + dot_nt(d_k_pre, full_key) + dot_nt(d_v_pre, full_value)
+    )
+    units_a, units_b, key_value_grad[-1], out_query[-1], d_normed = tie(
+        units_a, units_b, key_value_grad[-1], out_query[-1], d_normed
     )
 
     units_b = double(units_b, far_axis)
     owned_a = double(units_a, near_axis)
-    d_normed = pair_total(
-        dot_nt(d_q_pre, full_query) + dot_nt(d_k_pre, full_key) + dot_nt(d_v_pre, full_value)
-    )
     grad_in = jnp.sum(d_normed * normal_one, axis=0)
     input_grad = d_residual + rms_back(d_normed * scale_in, normal_one, factor_one)
     once = jnp.where(lax.axis_index("tp") == 0, 1.0, 0.0)
@@ -892,13 +890,15 @@
     rest_chain = total(halve(rest_chain, far_axis))
     gain_grads = gain_grads + swap(gain_grads, "tp")
     gain_grads = gain_grads + swap(gain_grads, "ctx", masks[0])
-    owned_b, rest_chain, gain_grads = tie(owned_b, rest_chain, gain_grads)
+    owned_b, rest_chain, gain_grads, hidden = tie(owned_b, rest_chain, gain_grads, hidden)
 
     cut = rest_chain.shape[1] // 2
     rest_a, rest_b = rest_chain[:, :cut], rest_chain[:, cut:]
     rest_a = double(rest_a, far_axis)
     gain_grads = gain_grads + swap(gain_grads, "ctx", masks[1])
-    rest_a, rest_b, gain_grads = tie(rest_a, rest_b, gain_grads)
+    mixed_part = product_nt((hidden, full_down_t, 0))
+    mixed = (residual + pair_total(mixed_part)).astype(BF16)
+    rest_a, rest_b, gain_grads, mixed = tie(rest_a, rest_b, gain_grads, mixed)
 
     rest_b = double(rest_b, far_axis)
     rest_a = double(rest_a, near_axis)

time: 615 us -> 594 us (0.966)
  waiting for transfers between devices: 296 us -> 280 us
    ppermute x37, waiting for transfers between devices: 187 us -> 168 us  [swap(): return lax.ppermute(value, axis, [(i, i ^ level) for i in range(count)])]
    unnamed x186 -> x182, local copies, waits for them, and re-layouts: 26.3 us -> 27 us
  transfers between devices with their start and end apart: 59 -> 59, of which waited for: 24 -> 23; matrix products, arithmetic and copies ran while one was open for 11% -> 11% of each run, Pallas kernels for 15% -> 15%
where the time goes in v10:
time: 594 us; the launch traced here: 584 us
  waiting for transfers between devices  280 us (47%)
  Pallas kernels  104 us (18%)
  starting transfers between devices  73.2 us (12%)
  other arithmetic  49.8 us (8%)
  local copies, waits for them, and re-layouts  39.7 us (7%)
  matrix products  21.1 us (4%)
  between operations  15.7 us (3%)
    ppermute x37, waiting for transfers between devices, swap(): return lax.ppermute(value, axis, [(i, i ^ level) for i in range(count)])  168 us
    ppermute x14, waiting for transfers between devices, exchange(): done[d] = lax.ppermute(values[d], 'ctx', [(i, i ^ d) for i in range(count)])  100 us
    ppermute x37, starting transfers between devices, swap(): return lax.ppermute(value, axis, [(i, i ^ level) for i in range(count)])  45.8 us
    pallas_call x8, Pallas kernels, split_product(): pl.pallas_call(functools.partial(split_product_kernel, spans), grid_spec=...  32.1 us
    unnamed x182, local copies, waits for them, and re-layouts  27 us
    ppermute x14, starting transfers between devices, exchange(): done[d] = lax.ppermute(values[d], 'ctx', [(i, i ^ d) for i in range(count)])  22 us
    pallas_call x1, Pallas kernels, attend_back(): pl.pallas_call(functools.partial(backward_kernel, docs, count), grid_spec...  20 us
    select_n x18, other arithmetic, join(): jnp.where(index == 0, jnp.concatenate(pieces, dim), jnp.concatenate(piece...  14.6 us
  transfers between devices with their start and end apart: 59, of which 23 were waited for; matrix products, arithmetic and copies ran while one was open for 11% of the time, Pallas kernels for 15%

profile of v10, /device:TPU:0, one launch (start us, length us, event | category | flops | bytes accessed | tf_op | source)
XLA Modules:
  0.0 583.9 jit_solution(18314502314587584432)
XLA Ops:
  29.9 9.5 %collective-permute-done.2.refs_3_ = bf16[512,512]{1,0:T(8,128)(2,1)} collective-permute-done((bf16[512,512]{1,0:T(8,128)(2,1)}, bf16[512,512]{1,0:T(8,128)(2,1)}, u32[]{:S(2)}, u32[]{:S(2)}) %collective-permute-start.2) | collective-permute-done | bytes 524320 | tf_op jit(solution)/shard_map/ppermute | solution.py:48
  41.6 8.0 %shard_map.246 = (f32[512,512]{1,0:T(8,128)}, bf16[512,1024]{1,0:T(8,128)(2,1)}, bf16[512,1024]{1,0:T(8,128)(2,1)}, bf16[256,1024]{1,0:T(8,128)(2,1)}, bf16[256,...) custom-call(s32[20]{0:T(128)S(1)} %concatenate.244.meta_ref, ...), custom_call_target="tpu_custom_call" | custom-call | flops 1000 | bytes 1000 | tf_op jit(solution)/shard_map/pallas_call | solution.py:308
  58.8 31.4 %collective-permute-done.3.refs_8_.refs_9_ = bf16[256,1024]{1,0:T(8,128)(2,1)S(1)} collective-permute-done((bf16[256,1024]{1,0:T(8,128)(2,1)}, bf16[256,1024]{1,0:T(8,128)(2,1)S(1)}, u32[]{:S(2)}, u32[]{:S(2)}) %collective-permute-start.3) | collective-permute-done | bytes 524320 | tf_op jit(solution)/shard_map/ppermute | solution.py:91
  90.2 11.5 %collective-permute-done.5.refs_0_.refs_1_ = bf16[256,1024]{1,0:T(8,128)(2,1)S(1)} collective-permute-done((bf16[256,1024]{1,0:T(8,128)(2,1)}, bf16[256,1024]{1,0:T(8,128)(2,1)S(1)}, u32[]{:S(2)}, u32[]{:S(2)}) %collective-permute-start.5) | collective-permute-done | bytes 524320 | tf_op jit(solution)/shard_map/ppermute | solution.py:91
  107.3 35.3 %collective-permute-done.11 = bf16[256,3584]{1,0:T(8,128)(2,1)} collective-permute-done((bf16[256,3584]{1,0:T(8,128)(2,1)}, bf16[256,3584]{1,0:T(8,128)(2,1)}, u32[]{:S(2)}, u32[]{:S(2)}) %collective-permute-start.11) | collective-permute-done | bytes 1835040 | tf_op jit(solution)/shard_map/ppermute | solution.py:81
  157.4 10.5 %shard_map.248 = (f32[512,1024]{1,0:T(8,128)}, bf16[512,1024]{1,0:T(8,128)(2,1)S(1)}, f32[512,1024]{1,0:T(8,128)}) custom-call(s32[20]{0:T(128)S(1)} %concatenate.244.meta_ref, bf16[512,1024]{1,0:T(8,128)(2,1)S(1)} %shard_map.247.q_ref, bf16[512,1024]{1,0:T(8,128)(2,1)} %get-tuple-element.150.k_ref.v_ref, bf16[512,1024]{1,0:T(8,128)(2,1)} %get-tuple-element.150.k_ref.v_ref, ...), custom_call_target="tpu_custom_call" | custom-call | flops 1000 | bytes 1000 | tf_op jit(solution)/shard_map/pallas_call | solution.py:572
  174.2 5.8 fusion.47
  184.8 5.1 shard_map.249
  194.9 6.1 %shard_map.251 = bf16[512,1024]{1,0:T(8,128)(2,1)S(1)} custom-call(bf16[512,1536]{1,0:T(8,128)(2,1)S(1)} %get-tuple-element.161.refs_1_.refs_0_, bf16[1024,3072]{1,0:T(8,128)(2,1)} %all-gather.2.cloned.1.call-done.refs_1_.refs_3_, bf16[512,1536]{1,0:T(8,128)(2,1)S(1)} %get-tuple-element.162.refs_3_.refs_1_.refs_2_, ...), custom_call_target="tpu_custom_call" | custom-call | flops 1000 | bytes 1000 | tf_op jit(solution)/shard_map/pallas_call | solution.py:176
  209.3 20.0 %shard_map.252 = (f32[512,1024]{1,0:T(8,128)}, f32[2,512,512]{2,1,0:T(8,128)}, bf16[2,256,512]{2,1,0:T(8,128)(2,1)S(1)}, bf16[2,256,512]{2,1,0:T(8,128)(2,1)}, b...) custom-call(s32[20]{0:T(128)S(1)} %concatenate.244.meta_ref, ...), custom_call_target="tpu_custom_call" | custom-call | flops 1000 | bytes 1000 | tf_op jit(solution)/shard_map/pallas_call | solution.py:601
  236.7 20.8 %collective-permute-done.14.refs_1_ = bf16[2,256,512]{2,1,0:T(8,128)(2,1)S(1)} collective-permute-done((bf16[2,256,512]{2,1,0:T(8,128)(2,1)}, bf16[2,256,512]{2,1,0:T(8,128)(2,1)S(1)}, u32[]{:S(2)}, u32[]{:S(2)}) %collective-permute-start.14) | collective-permute-done | bytes 524320 | tf_op jit(solution)/shard_map/ppermute | solution.py:91
  313.9 23.8 %collective-permute-done.21.refs_4_ = bf16[2,256,512]{2,1,0:T(8,128)(2,1)S(1)} collective-permute-done((bf16[2,256,512]{2,1,0:T(8,128)(2,1)S(1)}, bf16[2,256,512]{2,1,0:T(8,128)(2,1)S(1)}, u32[]{:S(2)}, u32[]{:S(2)}) %collective-permute-start.21) | collective-permute-done | bytes 524320 | tf_op jit(solution)/shard_map/ppermute | solution.py:91
  337.8 12.5 %collective-permute-done.23.refs_0_ = bf16[2,256,512]{2,1,0:T(8,128)(2,1)S(1)} collective-permute-done((bf16[2,256,512]{2,1,0:T(8,128)(2,1)S(1)}, bf16[2,256,512]{2,1,0:T(8,128)(2,1)S(1)}, u32[]{:S(2)}, u32[]{:S(2)}) %collective-permute-start.23) | collective-permute-done | bytes 524320 | tf_op jit(solution)/shard_map/ppermute | solution.py:91
  362.0 5.4 shard_map.263
  374.1 29.9 %collective-permute-done.26 = bf16[64,4608]{1,0:T(8,128)(2,1)} collective-permute-done((bf16[64,4608]{1,0:T(8,128)(2,1)}, bf16[64,4608]{1,0:T(8,128)(2,1)}, u32[]{:S(2)}, u32[]{:S(2)}) %collective-permute-start.26) | collective-permute-done | bytes 589856 | tf_op jit(solution)/shard_map/ppermute | solution.py:81
  419.8 8.2 %collective-permute-done.31 = bf16[64,2304]{1,0:T(8,128)(2,1)S(1)} collective-permute-done((bf16[64,2304]{1,0:T(8,128)(2,1)S(1)}, bf16[64,2304]{1,0:T(8,128)(2,1)S(1)}, u32[]{:S(2)}, u32[]{:S(2)}) %collective-permute-start.31) | collective-permute-done | bytes 294944 | tf_op jit(solution)/shard_map/ppermute | solution.py:81
  428.0 5.2 collective-permute-done.32
  444.5 9.2 %collective-permute-done.36 = bf16[64,2304]{1,0:T(8,128)(2,1)S(1)} collective-permute-done((bf16[64,2304]{1,0:T(8,128)(2,1)S(1)}, bf16[64,2304]{1,0:T(8,128)(2,1)S(1)}, u32[]{:S(2)}, u32[]{:S(2)}) %collective-permute-start.36) | collective-permute-done | bytes 294944 | tf_op jit(solution)/shard_map/ppermute | solution.py:81
  453.9 5.2 collective-permute-done.37
  473.7 20.1 %collective-permute-done.45 = f32[18,128]{1,0:T(8,128)S(1)} collective-permute-done((f32[18,128]{1,0:T(8,128)S(1)}, f32[18,128]{1,0:T(8,128)S(1)}, u32[]{:S(2)}, u32[]{:S(2)}) %collective-permute-start.45) | collective-permute-done | bytes 9248 | tf_op jit(solution)/shard_map/ppermute | solution.py:81
  493.8 9.3 %collective-permute-done.42 = bf16[64,3072]{1,0:T(8,128)(2,1)S(1)} collective-permute-done((bf16[64,3072]{1,0:T(8,128)(2,1)S(1)}, bf16[64,3072]{1,0:T(8,128)(2,1)S(1)}, u32[]{:S(2)}, u32[]{:S(2)}) %collective-permute-start.42) | collective-permute-done | bytes 393248 | tf_op jit(solution)/shard_map/ppermute | solution.py:81
  537.2 6.6 %collective-permute-done.54 = bf16[64,1536]{1,0:T(8,128)(2,1)S(1)} collective-permute-done((bf16[64,1536]{1,0:T(8,128)(2,1)S(1)}, bf16[64,1536]{1,0:T(8,128)(2,1)S(1)}, u32[]{:S(2)}, u32[]{:S(2)}) %collective-permute-start.54) | collective-permute-done | bytes 196640 | tf_op jit(solution)/shard_map/ppermute | solution.py:81
  543.8 8.4 %collective-permute-done.53 = bf16[64,1536]{1,0:T(8,128)(2,1)S(1)} collective-permute-done((bf16[64,1536]{1,0:T(8,128)(2,1)S(1)}, bf16[64,1536]{1,0:T(8,128)(2,1)S(1)}, u32[]{:S(2)}, u32[]{:S(2)}) %collective-permute-start.53) | collective-permute-done | bytes 196640 | tf_op jit(solution)/shard_map/ppermute | solution.py:81
  561.2 11.2 %collective-permute-done.56 = bf16[256,1536]{1,0:T(8,128)(2,1)} collective-permute-done((bf16[256,1536]{1,0:T(8,128)(2,1)S(1)}, bf16[256,1536]{1,0:T(8,128)(2,1)}, u32[]{:S(2)}, u32[]{:S(2)}) %collective-permute-start.56) | collective-permute-done | bytes 786464 | tf_op jit(solution)/shard_map/ppermute | solution.py:81
  (408 shorter events, 249.1 us)
Async XLA Ops:
  7.2 167.0 %all-gather.2.cloned.1.call-start = ((), (), s32[]{:S(2)}) async-start(), calls=%async_computation | async-start | bytes 9437184 | tf_op jit(solution)/shard_map/all_gather | solution.py:719
  39.4 62.3 %collective-permute-start.7 = (bf16[256,3584]{1,0:T(8,128)(2,1)}, bf16[256,3584]{1,0:T(8,128)(2,1)}, u32[]{:S(2)}, u32[]{:S(2)}) collective-permute-start(bf16[256,3584]{1,0:T(8,128)(2,1)} %constant_dynamic-slice_fusion), channel_id=1, source_target_pairs={{0,16},{16,0},{1,17},{17,1},{2,18},{18,2},{3,19},{19,3},{4,20},{20... | collective-permute-start | bytes 5505032 | tf_op jit(solution)/shard_map/ppermute | solution.py:81
  52.1 38.2 %collective-permute-start.3 = (bf16[256,1024]{1,0:T(8,128)(2,1)}, bf16[256,1024]{1,0:T(8,128)(2,1)S(1)}, u32[]{:S(2)}, u32[]{:S(2)}) collective-permute-start(bf16[256,1024]{1,0:T(8,128)(2,1)} %get-tuple-element.135), channel_id=1, source_target_pairs={{0,10},{2,8},{4,14},{6,12},{8,2},{10,0},{12,6},{14,4},{1,11},{3,9}... | collective-permute-start | bytes 1572872 | tf_op jit(solution)/shard_map/ppermute | solution.py:91
  55.7 34.5 %collective-permute-start.4 = (bf16[256,1024]{1,0:T(8,128)(2,1)}, bf16[256,1024]{1,0:T(8,128)(2,1)S(1)}, u32[]{:S(2)}, u32[]{:S(2)}) collective-permute-start(bf16[256,1024]{1,0:T(8,128)(2,1)} %get-tuple-element.136), channel_id=1, source_target_pairs={{0,14},{2,12},{4,10},{6,8},{8,6},{10,4},{12,2},{14,0},{1,15},{3,13... | collective-permute-start | bytes 1572872 | tf_op jit(solution)/shard_map/ppermute | solution.py:91
  57.1 44.6 %collective-permute-start.5 = (bf16[256,1024]{1,0:T(8,128)(2,1)}, bf16[256,1024]{1,0:T(8,128)(2,1)S(1)}, u32[]{:S(2)}, u32[]{:S(2)}) collective-permute-start(bf16[256,1024]{1,0:T(8,128)(2,1)} %get-tuple-element.137), channel_id=1, source_target_pairs={{0,2},{2,0},{4,6},{6,4},{8,10},{10,8},{12,14},{14,12},{1,3},{3,1},... | collective-permute-start | bytes 1572872 | tf_op jit(solution)/shard_map/ppermute | solution.py:91
  58.5 43.2 %collective-permute-start.6 = (bf16[256,1024]{1,0:T(8,128)(2,1)}, bf16[256,1024]{1,0:T(8,128)(2,1)S(1)}, u32[]{:S(2)}, u32[]{:S(2)}) collective-permute-start(bf16[256,1024]{1,0:T(8,128)(2,1)} %get-tuple-element.138), channel_id=1, source_target_pairs={{0,6},{2,4},{4,2},{6,0},{8,14},{10,12},{12,10},{14,8},{1,7},{3,5},... | collective-permute-start | bytes 1572872 | tf_op jit(solution)/shard_map/ppermute | solution.py:91
  101.7 40.8 %collective-permute-start.11 = (bf16[256,3584]{1,0:T(8,128)(2,1)}, bf16[256,3584]{1,0:T(8,128)(2,1)}, u32[]{:S(2)}, u32[]{:S(2)}) collective-permute-start(bf16[256,3584]{1,0:T(8,128)(2,1)} %collective-permute-done.7), channel_id=1, source_target_pairs={{0,2},{2,0},{4,6},{6,4},{8,10},{10,8},{12,14},{14,12},{1,3},{3,1},... | collective-permute-start | bytes 5505032 | tf_op jit(solution)/shard_map/ppermute | solution.py:81
  103.2 54.1 %collective-permute-start.8 = (bf16[256,1024]{1,0:T(8,128)(2,1)}, bf16[256,1024]{1,0:T(8,128)(2,1)S(1)}, u32[]{:S(2)}, u32[]{:S(2)}) collective-permute-start(bf16[256,1024]{1,0:T(8,128)(2,1)} %copy-done.70), channel_id=1, source_target_pairs={{0,8},{2,10},{4,12},{6,14},{8,0},{10,2},{12,4},{14,6},{1,9},{3,11}... | collective-permute-start | bytes 1572872 | tf_op jit(solution)/shard_map/ppermute | solution.py:91
  104.5 52.8 %collective-permute-start.9 = (bf16[256,1024]{1,0:T(8,128)(2,1)}, bf16[256,1024]{1,0:T(8,128)(2,1)S(1)}, u32[]{:S(2)}, u32[]{:S(2)}) collective-permute-start(bf16[256,1024]{1,0:T(8,128)(2,1)} %copy-done.69), channel_id=1, source_target_pairs={{0,12},{2,14},{4,8},{6,10},{8,4},{10,6},{12,0},{14,2},{1,13},{3,15... | collective-permute-start | bytes 1572872 | tf_op jit(solution)/shard_map/ppermute | solution.py:91
  106.8 50.5 %collective-permute-start.10 = (bf16[256,1024]{1,0:T(8,128)(2,1)S(1)}, bf16[256,1024]{1,0:T(8,128)(2,1)S(1)}, u32[]{:S(2)}, u32[]{:S(2)}) collective-permute-start(bf16[256,1024]{1,0:T(8,128)(2,1)S(1)} %copy-done.68), channel_id=1, source_target_pairs={{0,4},{2,6},{4,0},{6,2},{8,12},{10,14},{12,8},{14,10},{1,5},{3,7},... | collective-permute-start | bytes 1572872 | tf_op jit(solution)/shard_map/ppermute | solution.py:91
  201.2 67.7 %collective-permute-start.17 = (bf16[512,2304]{1,0:T(8,128)(2,1)}, bf16[512,2304]{1,0:T(8,128)(2,1)}, u32[]{:S(2)}, u32[]{:S(2)}) collective-permute-start(bf16[512,2304]{1,0:T(8,128)(2,1)} %shard_map.249), channel_id=1, source_target_pairs={{0,16},{16,0},{1,17},{17,1},{2,18},{18,2},{3,19},{19,3},{4,20},{20... | collective-permute-start | bytes 7077896 | tf_op jit(solution)/shard_map/ppermute | solution.py:81
  202.7 70.1 %collective-permute-start.19 = (bf16[512,2304]{1,0:T(8,128)(2,1)}, bf16[512,2304]{1,0:T(8,128)(2,1)}, u32[]{:S(2)}, u32[]{:S(2)}) collective-permute-start(bf16[512,2304]{1,0:T(8,128)(2,1)} %shard_map.250), channel_id=1, source_target_pairs={{0,2},{2,0},{4,6},{6,4},{8,10},{10,8},{12,14},{14,12},{1,3},{3,1},... | collective-permute-start | bytes 7077896 | tf_op jit(solution)/shard_map/ppermute | solution.py:81
  302.4 35.4 %collective-permute-start.21 = (bf16[2,256,512]{2,1,0:T(8,128)(2,1)S(1)}, bf16[2,256,512]{2,1,0:T(8,128)(2,1)S(1)}, u32[]{:S(2)}, u32[]{:S(2)}) collective-permute-start(bf16[2,256,512]{2,1,0:T(8,128)(2,1)S(1)} %copy-done.66), channel_id=1, source_target_pairs={{0,10},{2,8},{4,14},{6,12},{8,2},{10,0},{12,6},{14,4},{1,11},{3,9}... | collective-permute-start | bytes 1572872 | tf_op jit(solution)/shard_map/ppermute | solution.py:91
  302.4 35.4 %collective-permute-start.22 = (bf16[2,256,512]{2,1,0:T(8,128)(2,1)S(1)}, bf16[2,256,512]{2,1,0:T(8,128)(2,1)S(1)}, u32[]{:S(2)}, u32[]{:S(2)}) collective-permute-start(bf16[2,256,512]{2,1,0:T(8,128)(2,1)S(1)} %copy-done.64), channel_id=1, source_target_pairs={{0,14},{2,12},{4,10},{6,8},{8,6},{10,4},{12,2},{14,0},{1,15},{3,13... | collective-permute-start | bytes 1572872 | tf_op jit(solution)/shard_map/ppermute | solution.py:91
  305.2 45.0 %collective-permute-start.23 = (bf16[2,256,512]{2,1,0:T(8,128)(2,1)S(1)}, bf16[2,256,512]{2,1,0:T(8,128)(2,1)S(1)}, u32[]{:S(2)}, u32[]{:S(2)}) collective-permute-start(bf16[2,256,512]{2,1,0:T(8,128)(2,1)S(1)} %copy-done.62), channel_id=1, source_target_pairs={{0,2},{2,0},{4,6},{6,4},{8,10},{10,8},{12,14},{14,12},{1,3},{3,1},... | collective-permute-start | bytes 1572872 | tf_op jit(solution)/shard_map/ppermute | solution.py:91
  305.5 44.8 %collective-permute-start.24 = (bf16[2,256,512]{2,1,0:T(8,128)(2,1)S(1)}, bf16[2,256,512]{2,1,0:T(8,128)(2,1)S(1)}, u32[]{:S(2)}, u32[]{:S(2)}) collective-permute-start(bf16[2,256,512]{2,1,0:T(8,128)(2,1)S(1)} %copy-done.60), channel_id=1, source_target_pairs={{0,6},{2,4},{4,2},{6,0},{8,14},{10,12},{12,10},{14,8},{1,7},{3,5},... | collective-permute-start | bytes 1572872 | tf_op jit(solution)/shard_map/ppermute | solution.py:91
  308.2 59.2 %collective-permute-start.28 = (bf16[512,2048]{1,0:T(8,128)(2,1)}, bf16[512,2048]{1,0:T(8,128)(2,1)}, u32[]{:S(2)}, u32[]{:S(2)}) collective-permute-start(bf16[512,2048]{1,0:T(8,128)(2,1)} %shard_map.259), channel_id=1, source_target_pairs={{0,16},{16,0},{1,17},{17,1},{2,18},{18,2},{3,19},{19,3},{4,20},{20... | collective-permute-start | bytes 6291464 | tf_op jit(solution)/shard_map/ppermute | solution.py:81
  354.7 49.3 %collective-permute-start.26 = (bf16[64,4608]{1,0:T(8,128)(2,1)}, bf16[64,4608]{1,0:T(8,128)(2,1)}, u32[]{:S(2)}, u32[]{:S(2)}) collective-permute-start(bf16[64,4608]{1,0:T(8,128)(2,1)} %shard_map.261), channel_id=1, source_target_pairs={{0,8},{2,10},{4,12},{6,14},{8,0},{10,2},{12,4},{14,6},{1,9},{3,11}... | collective-permute-start | bytes 1769480 | tf_op jit(solution)/shard_map/ppermute | solution.py:81
  356.3 47.8 %collective-permute-start.25 = (bf16[64,4608]{1,0:T(8,128)(2,1)}, bf16[64,4608]{1,0:T(8,128)(2,1)}, u32[]{:S(2)}, u32[]{:S(2)}) collective-permute-start(bf16[64,4608]{1,0:T(8,128)(2,1)} %shard_map.260), channel_id=1, source_target_pairs={{0,4},{2,6},{4,0},{6,2},{8,12},{10,14},{12,8},{14,10},{1,5},{3,7},... | collective-permute-start | bytes 1769480 | tf_op jit(solution)/shard_map/ppermute | solution.py:81
  369.8 38.3 %collective-permute-start.29 = (bf16[256,2048]{1,0:T(8,128)(2,1)S(1)}, bf16[256,2048]{1,0:T(8,128)(2,1)S(1)}, u32[]{:S(2)}, u32[]{:S(2)}) collective-permute-start(bf16[256,2048]{1,0:T(8,128)(2,1)S(1)} %shard_map.264), channel_id=1, source_target_pairs={{0,2},{2,0},{4,6},{6,4},{8,10},{10,8},{12,14},{14,12},{1,3},{3,1},... | collective-permute-start | bytes 3145736 | tf_op jit(solution)/shard_map/ppermute | solution.py:81
  372.5 35.5 %collective-permute-start.30 = (bf16[512,1024]{1,0:T(8,128)(2,1)S(1)}, bf16[512,1024]{1,0:T(8,128)(2,1)S(1)}, u32[]{:S(2)}, u32[]{:S(2)}) collective-permute-start(bf16[512,1024]{1,0:T(8,128)(2,1)S(1)} %shard_map.265), channel_id=1, source_target_pairs={{0,16},{16,0},{1,17},{17,1},{2,18},{18,2},{3,19},{19,3},{4,20},{20... | collective-permute-start | bytes 3145736 | tf_op jit(solution)/shard_map/ppermute | solution.py:81
  465.1 38.2 %collective-permute-start.40 = (bf16[256,2304]{1,0:T(8,128)(2,1)S(1)}, bf16[256,2304]{1,0:T(8,128)(2,1)S(1)}, u32[]{:S(2)}, u32[]{:S(2)}) collective-permute-start(bf16[256,2304]{1,0:T(8,128)(2,1)S(1)} %maximum_select_fusion.7), channel_id=1, source_target_pairs={{0,2},{2,0},{4,6},{6,4},{8,10},{10,8},{12,14},{14,12},{1,3},{3,1},... | collective-permute-start | bytes 3538952 | tf_op jit(solution)/shard_map/ppermute | solution.py:81
  468.0 35.1 %collective-permute-start.42 = (bf16[64,3072]{1,0:T(8,128)(2,1)S(1)}, bf16[64,3072]{1,0:T(8,128)(2,1)S(1)}, u32[]{:S(2)}, u32[]{:S(2)}) collective-permute-start(bf16[64,3072]{1,0:T(8,128)(2,1)S(1)} %shard_map.269), channel_id=1, source_target_pairs={{0,8},{2,10},{4,12},{6,14},{8,0},{10,2},{12,4},{14,6},{1,9},{3,11}... | collective-permute-start | bytes 1179656 | tf_op jit(solution)/shard_map/ppermute | solution.py:81
  468.7 34.5 %collective-permute-start.41 = (bf16[64,3072]{1,0:T(8,128)(2,1)S(1)}, bf16[64,3072]{1,0:T(8,128)(2,1)S(1)}, u32[]{:S(2)}, u32[]{:S(2)}) collective-permute-start(bf16[64,3072]{1,0:T(8,128)(2,1)S(1)} %shard_map.268), channel_id=1, source_target_pairs={{0,4},{2,6},{4,0},{6,2},{8,12},{10,14},{12,8},{14,10},{1,5},{3,7},... | collective-permute-start | bytes 1179656 | tf_op jit(solution)/shard_map/ppermute | solution.py:81
  (126 other events, 1704.2 us)
Sparse Core Ops, SparseCore 0:
  58.9 88.9 all-gather.1

commit v11 on v10

--- a/solution.py
+++ b/solution.py
@@ -661,7 +661,7 @@
 
     k_pieces = pieces_of(key_weight, "shard")
     v_pieces = pieces_of(value_weight, "shard")
-    (own_rest,) = tie(jnp.concatenate([w_query, w_out.T, w_down.T], axis=1))
+    (own_rest,) = tie(jnp.concatenate([w_down.T, w_query, w_out.T], axis=1))
     own_gate_up = jnp.concatenate([w_gate, w_up], axis=1)
 
     turns = jnp.arange(count, dtype=jnp.int32)
@@ -743,12 +743,13 @@
         full_rest = join([own_rest, other_rest], 0, shard)
     else:
         full_rest = lax.all_gather(half_rest, "shard", axis=0, tiled=True)
-    full_query = full_rest[:, :heads_width]
-    full_out_t = full_rest[:, heads_width : 2 * heads_width]
-    full_down_t = full_rest[:, 2 * heads_width :]
+    full_query = full_rest[:, units : units + heads_width]
     q_pre = dot(normed_input, full_query)
     queries = rope(q_pre, cosine, sine, scale_q)
-    queries, full_out_t = settle(held, straight, queries, full_out_t)
+    queries, full_rest = settle(held, straight, queries, full_rest)
+    full_down_t = full_rest[:, :units]
+    full_query = full_rest[:, units : units + heads_width]
+    full_out_t = full_rest[:, units + heads_width :]
     held = [held[d] for d in range(1, count)]
     attended, attn_out, lse = attend(meta, docs, queries, key_value, held)
 
@@ -796,12 +797,13 @@
     exchange(given, returned, straight)
     if shard_count == 2:
         first, second = straight[-1], straight[0]
-        normed_late, returned[first] = tie(normed_two, returned[first])
+        normed_late, d_queries = tie(normed_two, d_queries)
         kept_a = split_product(home, pairs_a(normed_late))
-        normed_late, upstream_late, kept_a, returned[second] = tie(
-            normed_two, cotangent, kept_a, returned[second]
+        normed_late, upstream_late, kept_a, returned[first] = tie(
+            normed_late, cotangent, kept_a, returned[first]
         )
         kept_b = split_product((bit, 2 + bit), pairs_b(normed_late, upstream_late))
+        kept_a, kept_b, returned[second] = tie(kept_a, kept_b, returned[second])
         units_a = halve([kept_a, got_a], near_axis)
         d_queries, kept_b = tie(d_queries, kept_b)
         units_b = [kept_b, got_b]
@@ -890,15 +892,22 @@
     rest_chain = total(halve(rest_chain, far_axis))
     gain_grads = gain_grads + swap(gain_grads, "tp")
     gain_grads = gain_grads + swap(gain_grads, "ctx", masks[0])
-    owned_b, rest_chain, gain_grads, hidden = tie(owned_b, rest_chain, gain_grads, hidden)
+    grad_gate = owned_a[:, :units].astype(F32)
+    owned_b, rest_chain, gain_grads, hidden, grad_gate = tie(
+        owned_b, rest_chain, gain_grads, hidden, grad_gate
+    )
 
     cut = rest_chain.shape[1] // 2
     rest_a, rest_b = rest_chain[:, :cut], rest_chain[:, cut:]
     rest_a = double(rest_a, far_axis)
     gain_grads = gain_grads + swap(gain_grads, "ctx", masks[1])
-    mixed_part = product_nt((hidden, full_down_t, 0))
+    mixed_part = product_nt((hidden, full_rest, 0))
     mixed = (residual + pair_total(mixed_part)).astype(BF16)
-    rest_a, rest_b, gain_grads, mixed = tie(rest_a, rest_b, gain_grads, mixed)
+    grad_up = jnp.concatenate([owned_a[:, units:], owned_b[:, :middle]], axis=1).astype(F32)
+    grad_down = owned_b[:, middle:].astype(F32).T
+    rest_a, rest_b, gain_grads, mixed, grad_up, grad_down = tie(
+        rest_a, rest_b, gain_grads, mixed, grad_up, grad_down
+    )
 
     rest_b = double(rest_b, far_axis)
     rest_a = double(rest_a, near_axis)
@@ -910,7 +919,6 @@
     if shard_count == 2:
         gain_grads = gain_grads + swap(gain_grads, "shard")
     gain_grads = gain_grads.reshape(-1)
-    owned_up = jnp.concatenate([owned_a[:, units:], owned_b[:, :middle]], axis=1)
     own_gains = []
     for lo, size in ((0, model), (model, model), (2 * model, HEAD), (2 * model + HEAD, HEAD)):
         size = size // shard_count
@@ -922,9 +930,9 @@
         rest_a[:, heads_width:].astype(F32),
         rest_b[:, heads_width:].astype(F32),
         rest_a[:, :heads_width].astype(F32).T,
-        owned_a[:, :units].astype(F32),
-        owned_up.astype(F32),
-        owned_b[:, middle:].astype(F32).T,
+        grad_gate,
+        grad_up,
+        grad_down,
         *own_gains,
     )
 

time: 594 us -> 588 us (0.990)
  waiting for transfers between devices: 280 us -> 265 us
    ppermute x37, waiting for transfers between devices: 168 us -> 160 us  [swap(): return lax.ppermute(value, axis, [(i, i ^ level) for i in range(count)])]
    ppermute x14, waiting for transfers between devices: 100 us -> 93.5 us  [exchange(): done[d] = lax.ppermute(values[d], 'ctx', [(i, i ^ d) for i in range(count)])]
    unnamed x182 -> x186, local copies, waits for them, and re-layouts: 27 us -> 31 us
  transfers between devices with their start and end apart: 59 -> 59, of which waited for: 23 -> 24; matrix products, arithmetic and copies ran while one was open for 11% -> 12% of each run, Pallas kernels for 15% -> 15%
where the time goes in v11:
time: 588 us; the launch traced here: 577 us
  waiting for transfers between devices  265 us (45%)
  Pallas kernels  105 us (18%)
  starting transfers between devices  73.5 us (12%)
  other arithmetic  52.4 us (9%)
  local copies, waits for them, and re-layouts  39.4 us (7%)
  matrix products  26.4 us (4%)
  between operations  15.6 us (3%)
    ppermute x37, waiting for transfers between devices, swap(): return lax.ppermute(value, axis, [(i, i ^ level) for i in range(count)])  160 us
    ppermute x14, waiting for transfers between devices, exchange(): done[d] = lax.ppermute(values[d], 'ctx', [(i, i ^ d) for i in range(count)])  93.5 us
    ppermute x37, starting transfers between devices, swap(): return lax.ppermute(value, axis, [(i, i ^ level) for i in range(count)])  45.9 us
    pallas_call x8, Pallas kernels, split_product(): pl.pallas_call(functools.partial(split_product_kernel, spans), grid_spec=...  32.1 us
    unnamed x186, local copies, waits for them, and re-layouts  31 us
    ppermute x14, starting transfers between devices, exchange(): done[d] = lax.ppermute(values[d], 'ctx', [(i, i ^ d) for i in range(count)])  22.2 us
    pallas_call x1, Pallas kernels, attend_back(): pl.pallas_call(functools.partial(backward_kernel, docs, count), grid_spec...  19.9 us
    dot_general x4, matrix products, dot(): return jnp.dot(a, b, preferred_element_type=F32)  17.7 us
  transfers between devices with their start and end apart: 59, of which 24 were waited for; matrix products, arithmetic and copies ran while one was open for 12% of the time, Pallas kernels for 15%

profile of v11, /device:TPU:0, one launch (start us, length us, event | category | flops | bytes accessed | tf_op | source)
XLA Modules:
  0.0 577.4 jit_solution(1005181748346218576)
XLA Ops:
  30.9 8.4 %collective-permute-done.2.refs_3_ = bf16[512,512]{1,0:T(8,128)(2,1)S(1)} collective-permute-done((bf16[512,512]{1,0:T(8,128)(2,1)}, bf16[512,512]{1,0:T(8,128)(2,1)S(1)}, u32[]{:S(2)}, u32[]{:S(2)}) %collective-permute-start.2) | collective-permute-done | bytes 524320 | tf_op jit(solution)/shard_map/ppermute | solution.py:48
  41.5 8.0 %shard_map.246 = (f32[512,512]{1,0:T(8,128)}, bf16[512,1024]{1,0:T(8,128)(2,1)}, bf16[512,1024]{1,0:T(8,128)(2,1)}, bf16[256,1024]{1,0:T(8,128)(2,1)}, bf16[256,...) custom-call(s32[20]{0:T(128)S(1)} %concatenate.244.meta_ref, ...), custom_call_target="tpu_custom_call" | custom-call | flops 1000 | bytes 1000 | tf_op jit(solution)/shard_map/pallas_call | solution.py:308
  57.2 31.4 %collective-permute-done.3.refs_8_.refs_9_ = bf16[256,1024]{1,0:T(8,128)(2,1)S(1)} collective-permute-done((bf16[256,1024]{1,0:T(8,128)(2,1)}, bf16[256,1024]{1,0:T(8,128)(2,1)S(1)}, u32[]{:S(2)}, u32[]{:S(2)}) %collective-permute-start.3) | collective-permute-done | bytes 524320 | tf_op jit(solution)/shard_map/ppermute | solution.py:91
  88.6 11.5 %collective-permute-done.5.refs_0_.refs_1_ = bf16[256,1024]{1,0:T(8,128)(2,1)S(1)} collective-permute-done((bf16[256,1024]{1,0:T(8,128)(2,1)}, bf16[256,1024]{1,0:T(8,128)(2,1)S(1)}, u32[]{:S(2)}, u32[]{:S(2)}) %collective-permute-start.5) | collective-permute-done | bytes 524320 | tf_op jit(solution)/shard_map/ppermute | solution.py:91
  105.7 35.2 %collective-permute-done.11 = bf16[256,3584]{1,0:T(8,128)(2,1)} collective-permute-done((bf16[256,3584]{1,0:T(8,128)(2,1)}, bf16[256,3584]{1,0:T(8,128)(2,1)}, u32[]{:S(2)}, u32[]{:S(2)}) %collective-permute-start.11) | collective-permute-done | bytes 1835040 | tf_op jit(solution)/shard_map/ppermute | solution.py:81
  155.5 10.3 %shard_map.248 = (f32[512,1024]{1,0:T(8,128)}, bf16[512,1024]{1,0:T(8,128)(2,1)S(1)}, f32[512,1024]{1,0:T(8,128)}) custom-call(s32[20]{0:T(128)S(1)} %concatenate.244.meta_ref, bf16[512,1024]{1,0:T(8,128)(2,1)S(1)} %shard_map.247.q_ref, bf16[512,1024]{1,0:T(8,128)(2,1)} %get-tuple-element.156.k_ref.v_ref, bf16[512,1024]{1,0:T(8,128)(2,1)} %get-tuple-element.156.k_ref.v_ref, ...), custom_call_target="tpu_custom_call" | custom-call | flops 1000 | bytes 1000 | tf_op jit(solution)/shard_map/pallas_call | solution.py:572
  176.6 5.8 %fusion.57 = f32[512,3072]{1,0:T(8,128)S(1)} fusion(bf16[512,1024]{1,0:T(8,128)(2,1)S(1)} %multiply_convert_fusion.3.refs_0_.refs_2_, bf16[1024,3072]{1,0:T(8,128)(2,1)} %all-gather.2.cloned.1.call-done.refs_1_.refs_3_), kind=kOutput, calls=%fused_computation.147 | convolution fusion | flops 3221225472 | bytes 13631488 | tf_op jit(solution)/shard_map/dot_general | solution.py:30
  187.2 5.1 shard_map.249
  197.3 6.1 %shard_map.251 = bf16[512,1024]{1,0:T(8,128)(2,1)S(1)} custom-call(bf16[512,1536]{1,0:T(8,128)(2,1)S(1)} %get-tuple-element.167.refs_1_.refs_0_, bf16[1024,3072]{1,0:T(8,128)(2,1)} %all-gather.2.cloned.1.call-done.refs_1_.refs_3_, bf16[512,1536]{1,0:T(8,128)(2,1)S(1)} %get-tuple-element.168.refs_3_.refs_1_.refs_2_, ...), custom_call_target="tpu_custom_call" | custom-call | flops 1000 | bytes 1000 | tf_op jit(solution)/shard_map/pallas_call | solution.py:176
  212.9 19.9 %shard_map.252 = (f32[512,1024]{1,0:T(8,128)}, f32[2,512,512]{2,1,0:T(8,128)}, bf16[2,256,512]{2,1,0:T(8,128)(2,1)S(1)}, bf16[2,256,512]{2,1,0:T(8,128)(2,1)}, b...) custom-call(s32[20]{0:T(128)S(1)} %concatenate.244.meta_ref, ...), custom_call_target="tpu_custom_call" | custom-call | flops 1000 | bytes 1000 | tf_op jit(solution)/shard_map/pallas_call | solution.py:601
  241.6 5.0 shard_map.253.refs_0_
  246.6 14.3 %collective-permute-done.14.refs_1_ = bf16[2,256,512]{2,1,0:T(8,128)(2,1)S(1)} collective-permute-done((bf16[2,256,512]{2,1,0:T(8,128)(2,1)}, bf16[2,256,512]{2,1,0:T(8,128)(2,1)S(1)}, u32[]{:S(2)}, u32[]{:S(2)}) %collective-permute-start.14) | collective-permute-done | bytes 524320 | tf_op jit(solution)/shard_map/ppermute | solution.py:91
  311.1 23.8 %collective-permute-done.21.refs_4_ = bf16[2,256,512]{2,1,0:T(8,128)(2,1)S(1)} collective-permute-done((bf16[2,256,512]{2,1,0:T(8,128)(2,1)S(1)}, bf16[2,256,512]{2,1,0:T(8,128)(2,1)S(1)}, u32[]{:S(2)}, u32[]{:S(2)}) %collective-permute-start.21) | collective-permute-done | bytes 524320 | tf_op jit(solution)/shard_map/ppermute | solution.py:91
  334.8 12.5 %collective-permute-done.23.refs_0_ = bf16[2,256,512]{2,1,0:T(8,128)(2,1)S(1)} collective-permute-done((bf16[2,256,512]{2,1,0:T(8,128)(2,1)S(1)}, bf16[2,256,512]{2,1,0:T(8,128)(2,1)S(1)}, u32[]{:S(2)}, u32[]{:S(2)}) %collective-permute-start.23) | collective-permute-done | bytes 524320 | tf_op jit(solution)/shard_map/ppermute | solution.py:91
  363.4 5.3 shard_map.263
  375.5 25.5 %collective-permute-done.26 = bf16[64,4608]{1,0:T(8,128)(2,1)} collective-permute-done((bf16[64,4608]{1,0:T(8,128)(2,1)}, bf16[64,4608]{1,0:T(8,128)(2,1)}, u32[]{:S(2)}, u32[]{:S(2)}) %collective-permute-start.26) | collective-permute-done | bytes 589856 | tf_op jit(solution)/shard_map/ppermute | solution.py:81
  415.7 9.2 %collective-permute-done.31 = bf16[64,2304]{1,0:T(8,128)(2,1)S(1)} collective-permute-done((bf16[64,2304]{1,0:T(8,128)(2,1)S(1)}, bf16[64,2304]{1,0:T(8,128)(2,1)S(1)}, u32[]{:S(2)}, u32[]{:S(2)}) %collective-permute-start.31) | collective-permute-done | bytes 294944 | tf_op jit(solution)/shard_map/ppermute | solution.py:81
  425.0 5.2 collective-permute-done.32
  441.7 9.1 %collective-permute-done.36 = bf16[64,2304]{1,0:T(8,128)(2,1)S(1)} collective-permute-done((bf16[64,2304]{1,0:T(8,128)(2,1)S(1)}, bf16[64,2304]{1,0:T(8,128)(2,1)S(1)}, u32[]{:S(2)}, u32[]{:S(2)}) %collective-permute-start.36) | collective-permute-done | bytes 294944 | tf_op jit(solution)/shard_map/ppermute | solution.py:81
  450.9 5.2 collective-permute-done.37
  470.7 20.1 %collective-permute-done.45 = f32[18,128]{1,0:T(8,128)S(1)} collective-permute-done((f32[18,128]{1,0:T(8,128)S(1)}, f32[18,128]{1,0:T(8,128)S(1)}, u32[]{:S(2)}, u32[]{:S(2)}) %collective-permute-start.45) | collective-permute-done | bytes 9248 | tf_op jit(solution)/shard_map/ppermute | solution.py:81
  490.8 9.3 %collective-permute-done.42 = bf16[64,3072]{1,0:T(8,128)(2,1)S(1)} collective-permute-done((bf16[64,3072]{1,0:T(8,128)(2,1)S(1)}, bf16[64,3072]{1,0:T(8,128)(2,1)S(1)}, u32[]{:S(2)}, u32[]{:S(2)}) %collective-permute-start.42) | collective-permute-done | bytes 393248 | tf_op jit(solution)/shard_map/ppermute | solution.py:81
  535.5 8.7 %collective-permute-done.53 = bf16[64,1536]{1,0:T(8,128)(2,1)} collective-permute-done((bf16[64,1536]{1,0:T(8,128)(2,1)S(1)}, bf16[64,1536]{1,0:T(8,128)(2,1)}, u32[]{:S(2)}, u32[]{:S(2)}) %collective-permute-start.53) | collective-permute-done | bytes 196640 | tf_op jit(solution)/shard_map/ppermute | solution.py:81
  554.4 11.4 %collective-permute-done.56 = bf16[256,1536]{1,0:T(8,128)(2,1)} collective-permute-done((bf16[256,1536]{1,0:T(8,128)(2,1)S(1)}, bf16[256,1536]{1,0:T(8,128)(2,1)}, u32[]{:S(2)}, u32[]{:S(2)}) %collective-permute-start.56) | collective-permute-done | bytes 786464 | tf_op jit(solution)/shard_map/ppermute | solution.py:81
  (410 shorter events, 255.3 us)
Async XLA Ops:
  7.2 168.4 %all-gather.2.cloned.1.call-start = ((), (), s32[]{:S(2)}) async-start(), calls=%async_computation | async-start | bytes 9437184 | tf_op jit(solution)/shard_map/all_gather | solution.py:719
  39.3 60.8 %collective-permute-start.7 = (bf16[256,3584]{1,0:T(8,128)(2,1)}, bf16[256,3584]{1,0:T(8,128)(2,1)}, u32[]{:S(2)}, u32[]{:S(2)}) collective-permute-start(bf16[256,3584]{1,0:T(8,128)(2,1)} %constant_dynamic-slice_fusion), channel_id=1, source_target_pairs={{0,16},{16,0},{1,17},{17,1},{2,18},{18,2},{3,19},{19,3},{4,20},{20... | collective-permute-start | bytes 5505032 | tf_op jit(solution)/shard_map/ppermute | solution.py:81
  50.4 38.2 %collective-permute-start.3 = (bf16[256,1024]{1,0:T(8,128)(2,1)}, bf16[256,1024]{1,0:T(8,128)(2,1)S(1)}, u32[]{:S(2)}, u32[]{:S(2)}) collective-permute-start(bf16[256,1024]{1,0:T(8,128)(2,1)} %get-tuple-element.141), channel_id=1, source_target_pairs={{0,10},{2,8},{4,14},{6,12},{8,2},{10,0},{12,6},{14,4},{1,11},{3,9}... | collective-permute-start | bytes 1572872 | tf_op jit(solution)/shard_map/ppermute | solution.py:91
  54.1 34.5 %collective-permute-start.4 = (bf16[256,1024]{1,0:T(8,128)(2,1)}, bf16[256,1024]{1,0:T(8,128)(2,1)S(1)}, u32[]{:S(2)}, u32[]{:S(2)}) collective-permute-start(bf16[256,1024]{1,0:T(8,128)(2,1)} %get-tuple-element.142), channel_id=1, source_target_pairs={{0,14},{2,12},{4,10},{6,8},{8,6},{10,4},{12,2},{14,0},{1,15},{3,13... | collective-permute-start | bytes 1572872 | tf_op jit(solution)/shard_map/ppermute | solution.py:91
  55.5 44.7 %collective-permute-start.5 = (bf16[256,1024]{1,0:T(8,128)(2,1)}, bf16[256,1024]{1,0:T(8,128)(2,1)S(1)}, u32[]{:S(2)}, u32[]{:S(2)}) collective-permute-start(bf16[256,1024]{1,0:T(8,128)(2,1)} %get-tuple-element.143), channel_id=1, source_target_pairs={{0,2},{2,0},{4,6},{6,4},{8,10},{10,8},{12,14},{14,12},{1,3},{3,1},... | collective-permute-start | bytes 1572872 | tf_op jit(solution)/shard_map/ppermute | solution.py:91
  57.0 43.2 %collective-permute-start.6 = (bf16[256,1024]{1,0:T(8,128)(2,1)}, bf16[256,1024]{1,0:T(8,128)(2,1)S(1)}, u32[]{:S(2)}, u32[]{:S(2)}) collective-permute-start(bf16[256,1024]{1,0:T(8,128)(2,1)} %get-tuple-element.144), channel_id=1, source_target_pairs={{0,6},{2,4},{4,2},{6,0},{8,14},{10,12},{12,10},{14,8},{1,7},{3,5},... | collective-permute-start | bytes 1572872 | tf_op jit(solution)/shard_map/ppermute | solution.py:91
  100.2 40.7 %collective-permute-start.11 = (bf16[256,3584]{1,0:T(8,128)(2,1)}, bf16[256,3584]{1,0:T(8,128)(2,1)}, u32[]{:S(2)}, u32[]{:S(2)}) collective-permute-start(bf16[256,3584]{1,0:T(8,128)(2,1)} %collective-permute-done.7), channel_id=1, source_target_pairs={{0,2},{2,0},{4,6},{6,4},{8,10},{10,8},{12,14},{14,12},{1,3},{3,1},... | collective-permute-start | bytes 5505032 | tf_op jit(solution)/shard_map/ppermute | solution.py:81
  101.6 53.9 %collective-permute-start.8 = (bf16[256,1024]{1,0:T(8,128)(2,1)}, bf16[256,1024]{1,0:T(8,128)(2,1)S(1)}, u32[]{:S(2)}, u32[]{:S(2)}) collective-permute-start(bf16[256,1024]{1,0:T(8,128)(2,1)} %copy-done.70), channel_id=1, source_target_pairs={{0,8},{2,10},{4,12},{6,14},{8,0},{10,2},{12,4},{14,6},{1,9},{3,11}... | collective-permute-start | bytes 1572872 | tf_op jit(solution)/shard_map/ppermute | solution.py:91
  102.9 52.5 %collective-permute-start.9 = (bf16[256,1024]{1,0:T(8,128)(2,1)}, bf16[256,1024]{1,0:T(8,128)(2,1)S(1)}, u32[]{:S(2)}, u32[]{:S(2)}) collective-permute-start(bf16[256,1024]{1,0:T(8,128)(2,1)} %copy-done.69), channel_id=1, source_target_pairs={{0,12},{2,14},{4,8},{6,10},{8,4},{10,6},{12,0},{14,2},{1,13},{3,15... | collective-permute-start | bytes 1572872 | tf_op jit(solution)/shard_map/ppermute | solution.py:91
  105.2 50.3 %collective-permute-start.10 = (bf16[256,1024]{1,0:T(8,128)(2,1)S(1)}, bf16[256,1024]{1,0:T(8,128)(2,1)S(1)}, u32[]{:S(2)}, u32[]{:S(2)}) collective-permute-start(bf16[256,1024]{1,0:T(8,128)(2,1)S(1)} %copy-done.68), channel_id=1, source_target_pairs={{0,4},{2,6},{4,0},{6,2},{8,12},{10,14},{12,8},{14,10},{1,5},{3,7},... | collective-permute-start | bytes 1572872 | tf_op jit(solution)/shard_map/ppermute | solution.py:91
  203.6 62.3 %collective-permute-start.17 = (bf16[512,2304]{1,0:T(8,128)(2,1)}, bf16[512,2304]{1,0:T(8,128)(2,1)}, u32[]{:S(2)}, u32[]{:S(2)}) collective-permute-start(bf16[512,2304]{1,0:T(8,128)(2,1)} %shard_map.249), channel_id=1, source_target_pairs={{0,16},{16,0},{1,17},{17,1},{2,18},{18,2},{3,19},{19,3},{4,20},{20... | collective-permute-start | bytes 7077896 | tf_op jit(solution)/shard_map/ppermute | solution.py:81
  205.1 64.8 %collective-permute-start.19 = (bf16[512,2304]{1,0:T(8,128)(2,1)}, bf16[512,2304]{1,0:T(8,128)(2,1)}, u32[]{:S(2)}, u32[]{:S(2)}) collective-permute-start(bf16[512,2304]{1,0:T(8,128)(2,1)} %shard_map.250), channel_id=1, source_target_pairs={{0,2},{2,0},{4,6},{6,4},{8,10},{10,8},{12,14},{14,12},{1,3},{3,1},... | collective-permute-start | bytes 7077896 | tf_op jit(solution)/shard_map/ppermute | solution.py:81
  299.4 35.4 %collective-permute-start.21 = (bf16[2,256,512]{2,1,0:T(8,128)(2,1)S(1)}, bf16[2,256,512]{2,1,0:T(8,128)(2,1)S(1)}, u32[]{:S(2)}, u32[]{:S(2)}) collective-permute-start(bf16[2,256,512]{2,1,0:T(8,128)(2,1)S(1)} %copy-done.66), channel_id=1, source_target_pairs={{0,10},{2,8},{4,14},{6,12},{8,2},{10,0},{12,6},{14,4},{1,11},{3,9}... | collective-permute-start | bytes 1572872 | tf_op jit(solution)/shard_map/ppermute | solution.py:91
  299.4 35.4 %collective-permute-start.22 = (bf16[2,256,512]{2,1,0:T(8,128)(2,1)S(1)}, bf16[2,256,512]{2,1,0:T(8,128)(2,1)S(1)}, u32[]{:S(2)}, u32[]{:S(2)}) collective-permute-start(bf16[2,256,512]{2,1,0:T(8,128)(2,1)S(1)} %copy-done.64), channel_id=1, source_target_pairs={{0,14},{2,12},{4,10},{6,8},{8,6},{10,4},{12,2},{14,0},{1,15},{3,13... | collective-permute-start | bytes 1572872 | tf_op jit(solution)/shard_map/ppermute | solution.py:91
  302.2 45.0 %collective-permute-start.23 = (bf16[2,256,512]{2,1,0:T(8,128)(2,1)S(1)}, bf16[2,256,512]{2,1,0:T(8,128)(2,1)S(1)}, u32[]{:S(2)}, u32[]{:S(2)}) collective-permute-start(bf16[2,256,512]{2,1,0:T(8,128)(2,1)S(1)} %copy-done.62), channel_id=1, source_target_pairs={{0,2},{2,0},{4,6},{6,4},{8,10},{10,8},{12,14},{14,12},{1,3},{3,1},... | collective-permute-start | bytes 1572872 | tf_op jit(solution)/shard_map/ppermute | solution.py:91
  302.5 44.8 %collective-permute-start.24 = (bf16[2,256,512]{2,1,0:T(8,128)(2,1)S(1)}, bf16[2,256,512]{2,1,0:T(8,128)(2,1)S(1)}, u32[]{:S(2)}, u32[]{:S(2)}) collective-permute-start(bf16[2,256,512]{2,1,0:T(8,128)(2,1)S(1)} %copy-done.60), channel_id=1, source_target_pairs={{0,6},{2,4},{4,2},{6,0},{8,14},{10,12},{12,10},{14,8},{1,7},{3,5},... | collective-permute-start | bytes 1572872 | tf_op jit(solution)/shard_map/ppermute | solution.py:91
  305.3 63.4 %collective-permute-start.28 = (bf16[512,2048]{1,0:T(8,128)(2,1)}, bf16[512,2048]{1,0:T(8,128)(2,1)}, u32[]{:S(2)}, u32[]{:S(2)}) collective-permute-start(bf16[512,2048]{1,0:T(8,128)(2,1)} %shard_map.259), channel_id=1, source_target_pairs={{0,16},{16,0},{1,17},{17,1},{2,18},{18,2},{3,19},{19,3},{4,20},{20... | collective-permute-start | bytes 6291464 | tf_op jit(solution)/shard_map/ppermute | solution.py:81
  351.8 49.2 %collective-permute-start.26 = (bf16[64,4608]{1,0:T(8,128)(2,1)}, bf16[64,4608]{1,0:T(8,128)(2,1)}, u32[]{:S(2)}, u32[]{:S(2)}) collective-permute-start(bf16[64,4608]{1,0:T(8,128)(2,1)} %shard_map.261), channel_id=1, source_target_pairs={{0,8},{2,10},{4,12},{6,14},{8,0},{10,2},{12,4},{14,6},{1,9},{3,11}... | collective-permute-start | bytes 1769480 | tf_op jit(solution)/shard_map/ppermute | solution.py:81
  353.4 47.7 %collective-permute-start.25 = (bf16[64,4608]{1,0:T(8,128)(2,1)}, bf16[64,4608]{1,0:T(8,128)(2,1)}, u32[]{:S(2)}, u32[]{:S(2)}) collective-permute-start(bf16[64,4608]{1,0:T(8,128)(2,1)} %shard_map.260), channel_id=1, source_target_pairs={{0,4},{2,6},{4,0},{6,2},{8,12},{10,14},{12,8},{14,10},{1,5},{3,7},... | collective-permute-start | bytes 1769480 | tf_op jit(solution)/shard_map/ppermute | solution.py:81
  371.2 33.9 %collective-permute-start.29 = (bf16[256,2048]{1,0:T(8,128)(2,1)S(1)}, bf16[256,2048]{1,0:T(8,128)(2,1)S(1)}, u32[]{:S(2)}, u32[]{:S(2)}) collective-permute-start(bf16[256,2048]{1,0:T(8,128)(2,1)S(1)} %shard_map.264), channel_id=1, source_target_pairs={{0,2},{2,0},{4,6},{6,4},{8,10},{10,8},{12,14},{14,12},{1,3},{3,1},... | collective-permute-start | bytes 3145736 | tf_op jit(solution)/shard_map/ppermute | solution.py:81
  374.0 31.1 %collective-permute-start.30 = (bf16[512,1024]{1,0:T(8,128)(2,1)S(1)}, bf16[512,1024]{1,0:T(8,128)(2,1)S(1)}, u32[]{:S(2)}, u32[]{:S(2)}) collective-permute-start(bf16[512,1024]{1,0:T(8,128)(2,1)S(1)} %shard_map.265), channel_id=1, source_target_pairs={{0,16},{16,0},{1,17},{17,1},{2,18},{18,2},{3,19},{19,3},{4,20},{20... | collective-permute-start | bytes 3145736 | tf_op jit(solution)/shard_map/ppermute | solution.py:81
  462.1 38.2 %collective-permute-start.40 = (bf16[256,2304]{1,0:T(8,128)(2,1)S(1)}, bf16[256,2304]{1,0:T(8,128)(2,1)S(1)}, u32[]{:S(2)}, u32[]{:S(2)}) collective-permute-start(bf16[256,2304]{1,0:T(8,128)(2,1)S(1)} %maximum_select_fusion.7), channel_id=1, source_target_pairs={{0,2},{2,0},{4,6},{6,4},{8,10},{10,8},{12,14},{14,12},{1,3},{3,1},... | collective-permute-start | bytes 3538952 | tf_op jit(solution)/shard_map/ppermute | solution.py:81
  465.0 35.2 %collective-permute-start.42 = (bf16[64,3072]{1,0:T(8,128)(2,1)S(1)}, bf16[64,3072]{1,0:T(8,128)(2,1)S(1)}, u32[]{:S(2)}, u32[]{:S(2)}) collective-permute-start(bf16[64,3072]{1,0:T(8,128)(2,1)S(1)} %shard_map.269), channel_id=1, source_target_pairs={{0,8},{2,10},{4,12},{6,14},{8,0},{10,2},{12,4},{14,6},{1,9},{3,11}... | collective-permute-start | bytes 1179656 | tf_op jit(solution)/shard_map/ppermute | solution.py:81
  465.7 34.5 %collective-permute-start.41 = (bf16[64,3072]{1,0:T(8,128)(2,1)S(1)}, bf16[64,3072]{1,0:T(8,128)(2,1)S(1)}, u32[]{:S(2)}, u32[]{:S(2)}) collective-permute-start(bf16[64,3072]{1,0:T(8,128)(2,1)S(1)} %shard_map.268), channel_id=1, source_target_pairs={{0,4},{2,6},{4,0},{6,2},{8,12},{10,14},{12,8},{14,10},{1,5},{3,7},... | collective-permute-start | bytes 1179656 | tf_op jit(solution)/shard_map/ppermute | solution.py:81
  (128 other events, 1725.0 us)
Sparse Core Ops, SparseCore 0:
  57.3 90.4 all-gather.1
